TPU v7x, 32 devices: a whole 2x2x4 slice. The times are simulated.
32 devices in a mesh: ctx: 16 (over z, y, core), wa: 2 (over x).
Axes of the slice: x: 2, y: 2, z: 4, core: 2. Of those that a mesh axis runs over, the one named last changes fastest.
Arguments:
- ids: int32 [32768], P('ctx'), may hold values from 0 to 274
- targets: int32 [32768], P('ctx'), may hold values from 0 to 274
- doc_lengths: int32 [4], replicated, may hold values from 1 to 16384, 32768 in all
- block_of: int32 [16], replicated, may hold values from 0 to 15, each once
- embed: bfloat16 [275, 100], replicated, may hold values from -6 to 6
- w_in: bfloat16 [100, 4, 2048], P(None, None, 'wa'), may hold values from -0.625 to 0.625
- b_in: float32 [4, 2048], P(None, 'wa'), may hold values from -6.5 to 12.5
- w_out: bfloat16 [2048, 275], P('wa'), may hold values from -0.5 to 0.5
- b_out: float32 [275], replicated, may hold values from -3 to 3
Outputs:
- hidden_out: bfloat16 [32768, 2048], P('ctx', 'wa')
- loss: float32 [], replicated
- grad_embed: float32 [275, 100], replicated
- grad_w_in: float32 [100, 4, 2048], P(None, None, 'wa')
- grad_b_in: float32 [4, 2048], P(None, 'wa')
- grad_w_out: float32 [2048, 275], P('wa')
- grad_b_out: float32 [275], replicated
Inputs may be any that keep to these rules, and one draw needn't show every extreme that they name: `doc_lengths`: the documents are laid end to end from position 0 and fill the stream. Device d of ctx holds stream block block_of[d]; each block once.
All inputs are finite; a program needn't handle non-finite values.
Results may differ from a plain program's by a relative error of at most 0.0019.
Values may be sent and summed in bfloat16 or wider, within the bound.
No kernel may reach another device: no remote copies, remote signals or barrier semaphores. Data moves between devices by JAX's collectives and lax.ppermute only.
A program may use at most 192 MiB of HBM per device.

v0:
```python
import jax
import jax.numpy as jnp
from jax import lax
from jax.sharding import PartitionSpec as P


def doubling_scan(decay, source, reverse):
    rows, width = decay.shape
    prods, sums = (decay, source)
    stride = 1
    while stride < rows:
        ones = jnp.ones((stride, width), jnp.float32)
        zeros = jnp.zeros((stride, width), jnp.float32)
        if reverse:
            moved_p = jnp.concatenate([prods[stride:], ones], axis=0)
            moved_s = jnp.concatenate([sums[stride:], zeros], axis=0)
        else:
            moved_p = jnp.concatenate([ones, prods[:-stride]], axis=0)
            moved_s = jnp.concatenate([zeros, sums[:-stride]], axis=0)
        sums = prods * moved_s + sums
        prods = prods * moved_p
        stride = stride * 2
    return (prods, sums)


def body(ids, targets, doc_lengths, block_of, embed, w_in, b_in, w_out, b_out):
    highest = lax.Precision.HIGHEST
    blocks = lax.axis_size("ctx")
    own_index = lax.axis_index("ctx")
    tok_rows = ids.shape[0]
    shard_width = w_in.shape[2]
    vocab_size = embed.shape[0]
    total_tokens = tok_rows * blocks
    block_ids = jnp.arange(blocks, dtype=jnp.int32)
    own_block = jnp.sum(jnp.where(block_ids == own_index, block_of, 0))
    positions = own_block * tok_rows + jnp.arange(tok_rows, dtype=jnp.int32)
    starts = jnp.cumsum(doc_lengths) - doc_lengths
    resets = jnp.any(positions[:, None] == starts[None, :], axis=1).astype(jnp.float32)
    keep_mask = (1.0 - resets)[:, None]
    vocab_ids = jnp.arange(vocab_size, dtype=jnp.int32)
    id_table = (ids[:, None] == vocab_ids[None, :]).astype(jnp.bfloat16)
    feats = jnp.dot(id_table, embed, preferred_element_type=jnp.float32).astype(jnp.bfloat16)
    gates = jnp.einsum("te,egh->tgh", feats, w_in, preferred_element_type=jnp.float32) + b_in[None]
    in_gate = jax.nn.sigmoid(gates[:, 0])
    forget = jax.nn.sigmoid(gates[:, 1] + 3.0)
    candidate = jnp.tanh(gates[:, 2])
    out_gate = jax.nn.sigmoid(gates[:, 3])
    decay = forget * keep_mask
    prods, sums = doubling_scan(decay, in_gate * candidate, False)
    reorder = (block_of[None, :] == block_ids[:, None]).astype(jnp.float32)
    span_decay, span_state = (
        lax.all_gather(prods[-1:], "ctx", axis=0, tiled=True),
        lax.all_gather(sums[-1:], "ctx", axis=0, tiled=True),
    )
    stream_decay = jnp.dot(reorder, span_decay, precision=highest)
    stream_state = jnp.dot(reorder, span_state, precision=highest)
    ends_decay, ends_state = doubling_scan(stream_decay, stream_state, False)
    before_own = (block_ids == own_block - 1).astype(jnp.float32)
    cell_in = jnp.dot(before_own[None, :], ends_state, precision=highest)
    cells = sums + prods * cell_in
    tanh_cells = jnp.tanh(cells)
    hidden_low = (out_gate * tanh_cells).astype(jnp.bfloat16)
    target_table = (targets[:, None] == vocab_ids[None, :]).astype(jnp.float32)
    hidden_all, w_all = (
        lax.all_gather(hidden_low, "wa", axis=1, tiled=True),
        lax.all_gather(w_out, "wa", axis=0, tiled=True),
    )
    logits = jnp.dot(hidden_all, w_all, preferred_element_type=jnp.float32) + b_out
    log_total = jax.nn.logsumexp(logits, axis=1)
    loss_local = jnp.sum(log_total - jnp.sum(logits * target_table, axis=1))
    probs = jnp.exp(logits - log_total[:, None])
    logit_grad = ((probs - target_table) / total_tokens).astype(jnp.bfloat16)
    hidden_grad = jnp.dot(logit_grad, w_out.T, preferred_element_type=jnp.float32)
    grad_w_out = jnp.dot(hidden_low.T, logit_grad, preferred_element_type=jnp.float32)
    grad_b_out = jnp.sum(logit_grad.astype(jnp.float32), axis=0)
    out_grad = hidden_grad * tanh_cells
    cell_source = hidden_grad * out_gate * (1.0 - tanh_cells * tanh_cells)
    next_decay = jnp.concatenate([decay[1:], jnp.ones((1, shard_width), jnp.float32)], axis=0)
    back_prods, back_sums = doubling_scan(next_decay, cell_source, True)
    head_state = decay[:1] * back_sums[:1]
    span_back = lax.all_gather(head_state, "ctx", axis=0, tiled=True)
    stream_back = jnp.dot(reorder, span_back, precision=highest)
    later_decay, later_state = doubling_scan(stream_decay, stream_back, True)
    after_own = (block_ids == own_block + 1).astype(jnp.float32)
    cell_carry = jnp.dot(after_own[None, :], later_state, precision=highest)
    cell_grad = back_sums + back_prods * cell_carry
    prev_cells = jnp.concatenate([cell_in, cells[:-1]], axis=0)
    grad_input = cell_grad * candidate * in_gate * (1.0 - in_gate)
    grad_forget = cell_grad * keep_mask * prev_cells * forget * (1.0 - forget)
    grad_candidate = cell_grad * in_gate * (1.0 - candidate * candidate)
    grad_output = out_grad * out_gate * (1.0 - out_gate)
    gate_grad = jnp.stack([grad_input, grad_forget, grad_candidate, grad_output], axis=1).astype(
        jnp.bfloat16
    )
    grad_w_in = jnp.einsum("te,tgh->egh", feats, gate_grad, preferred_element_type=jnp.float32)
    grad_b_in = jnp.sum(gate_grad.astype(jnp.float32), axis=0)
    feat_grad = jnp.einsum("tgh,egh->te", gate_grad, w_in, preferred_element_type=jnp.float32)
    embed_local = jnp.dot(id_table.astype(jnp.float32).T, feat_grad, precision=highest)
    summed = lax.psum((grad_w_in, grad_b_in, grad_w_out, grad_b_out, loss_local), "ctx")
    grad_embed = lax.psum(embed_local, ("ctx", "wa"))
    loss = summed[4] / total_tokens
    return (hidden_low, loss, grad_embed, summed[0], summed[1], summed[2], summed[3])


def solution(mesh):
    placed = (
        P("ctx"),
        P("ctx"),
        P(),
        P(),
        P(),
        P(None, None, "wa"),
        P(None, "wa"),
        P("wa", None),
        P(),
    )
    return jax.shard_map(
        body,
        mesh=mesh,
        in_specs=placed,
        out_specs=(
            P("ctx", "wa"),
            P(),
            P(),
            P(None, None, "wa"),
            P(None, "wa"),
            P("wa", None),
            P(),
        ),
        check_vma=False,
    )
```

profile of v0, /device:TPU:0, one launch (start us, length us, event | category | flops | bytes accessed | tf_op | source)
XLA Modules:
  0.0 1139.0 jit_solution(2331868919142472721)
XLA Ops:
  14.0 14.3 %convolution_add_fusion = f32[2048,4,1024]{2,0,1:T(8,128)} fusion(bf16[2048,100,1]{0,1,2:T(8,128)(2,1)S(1)} %fusion.25, f32[4,1024]{1,0:T(4,128)} %param.15, bf16[100,4,1024]{2,1,0:T(4,128)(2,1)S(1)} %copy-done), kind=kOutput, calls=%fused_computation.1 | convolution fusion | flops 1686110208 | bytes 34799616 | tf_op jit(solution)/shard_map/te,egh->tgh/dot_general | solution.py:43
  36.0 14.8 %multiply_add_fusion.23 = (f32[2048,1024]{1,0:T(8,128)}, f32[2048,1024]{1,0:T(8,128)S(1)}) fusion(f32[2047,1024]{1,0:T(8,128)S(1)} %bitcast.127, f32[2048]{0:T(1024)S(1)} %convert_subtract_fusion, f32[2048,4,1024]{2,0,1:T(8,128)} %convolution_add_fusion), kind=kLoop, calls=%fused_computation.64 | loop fusion | flops 23068672 | bytes 50335744 | tf_op jit(solution)/shard_map/add | solution.py:20
  59.3 19.0 %multiply_add_fusion.22 = (f32[2048,1024]{1,0:T(8,128)}, f32[2048,1024]{1,0:T(8,128)}) fusion(f32[2048,1024]{1,0:T(8,128)} %get-tuple-element.91, f32[2046,1024]{1,0:T(8,128)} %bitcast.106, f32[2048,1024]{1,0:T(8,128)} %copy-done.1, f32[2047,1024]{1,0:T(8,128)} %get-tuple-element.98), kind=kLoop, calls=%fused_computation.63 | loop fusion | flops 6291456 | bytes 50319360 | tf_op jit(solution)/shard_map/add | solution.py:20
  78.3 19.2 %multiply_add_fusion.21 = (f32[2048,1024]{1,0:T(8,128)}, f32[2048,1024]{1,0:T(8,128)}) fusion(f32[2048,1024]{1,0:T(8,128)} %get-tuple-element.89, f32[2044,1024]{1,0:T(8,128)} %bitcast.108, f32[2048,1024]{1,0:T(8,128)} %get-tuple-element.90, f32[2046,1024]{1,0:T(8,128)} %bitcast.109), kind=kLoop, calls=%fused_computation.62 | loop fusion | flops 6291456 | bytes 50307072 | tf_op jit(solution)/shard_map/add | solution.py:20
  105.8 19.0 %multiply_add_fusion.20 = (f32[2048,1024]{1,0:T(8,128)}, f32[2048,1024]{1,0:T(8,128)}) fusion(f32[2048,1024]{1,0:T(8,128)} %get-tuple-element.87, f32[2040,1024]{1,0:T(8,128)} %slice.289, f32[2048,1024]{1,0:T(8,128)} %get-tuple-element.88, f32[2044,1024]{1,0:T(8,128)} %bitcast.107), kind=kLoop, calls=%fused_computation.61 | loop fusion | flops 6291456 | bytes 50282496 | tf_op jit(solution)/shard_map/add | solution.py:20
  137.5 18.7 %multiply_add_fusion.19 = (f32[2048,1024]{1,0:T(8,128)}, f32[2048,1024]{1,0:T(8,128)}) fusion(f32[2048,1024]{1,0:T(8,128)} %get-tuple-element.85, f32[2032,1024]{1,0:T(8,128)} %slice.290, f32[2048,1024]{1,0:T(8,128)} %get-tuple-element.86, f32[2040,1024]{1,0:T(8,128)} %slice.277), kind=kLoop, calls=%fused_computation.60 | loop fusion | flops 6291456 | bytes 50233344 | tf_op jit(solution)/shard_map/add | solution.py:20
  169.1 19.0 %multiply_add_fusion.18 = (f32[2048,1024]{1,0:T(8,128)}, f32[2048,1024]{1,0:T(8,128)}) fusion(f32[2048,1024]{1,0:T(8,128)} %get-tuple-element.83, f32[2016,1024]{1,0:T(8,128)} %slice.291, f32[2048,1024]{1,0:T(8,128)} %get-tuple-element.84, f32[2032,1024]{1,0:T(8,128)} %slice.278), kind=kLoop, calls=%fused_computation.59 | loop fusion | flops 6291456 | bytes 50135040 | tf_op jit(solution)/shard_map/add | solution.py:20
  200.8 18.6 %multiply_add_fusion.17 = (f32[2048,1024]{1,0:T(8,128)}, f32[2048,1024]{1,0:T(8,128)}) fusion(f32[2048,1024]{1,0:T(8,128)} %get-tuple-element.81, f32[1984,1024]{1,0:T(8,128)} %slice.292, f32[2048,1024]{1,0:T(8,128)} %get-tuple-element.82, f32[2016,1024]{1,0:T(8,128)} %slice.279), kind=kLoop, calls=%fused_computation.58 | loop fusion | flops 6291456 | bytes 49938432 | tf_op jit(solution)/shard_map/add | solution.py:20
  231.8 18.5 %multiply_add_fusion.16 = (f32[2048,1024]{1,0:T(8,128)}, f32[2048,1024]{1,0:T(8,128)}) fusion(f32[2048,1024]{1,0:T(8,128)} %get-tuple-element.79, f32[1920,1024]{1,0:T(8,128)} %slice.293, f32[2048,1024]{1,0:T(8,128)} %get-tuple-element.80, f32[1984,1024]{1,0:T(8,128)} %slice.280), kind=kLoop, calls=%fused_computation.57 | loop fusion | flops 6291456 | bytes 49545216 | tf_op jit(solution)/shard_map/add | solution.py:20
  261.9 18.6 %multiply_add_fusion.15 = (f32[2048,1024]{1,0:T(8,128)}, f32[2048,1024]{1,0:T(8,128)}) fusion(f32[2048,1024]{1,0:T(8,128)} %get-tuple-element.77, f32[1792,1024]{1,0:T(8,128)} %slice.294, f32[2048,1024]{1,0:T(8,128)} %get-tuple-element.78, f32[1920,1024]{1,0:T(8,128)} %slice.281), kind=kLoop, calls=%fused_computation.56 | loop fusion | flops 6291456 | bytes 48758784 | tf_op jit(solution)/shard_map/add | solution.py:20
  291.7 18.3 %multiply_add_fusion.14 = (f32[2048,1024]{1,0:T(8,128)}, f32[2048,1024]{1,0:T(8,128)}) fusion(f32[2048,1024]{1,0:T(8,128)} %get-tuple-element.75, f32[1536,1024]{1,0:T(8,128)} %slice.295, f32[2048,1024]{1,0:T(8,128)} %get-tuple-element.76, f32[1792,1024]{1,0:T(8,128)} %slice.282), kind=kLoop, calls=%fused_computation.55 | loop fusion | flops 6291456 | bytes 47185920 | tf_op jit(solution)/shard_map/add | solution.py:20
  317.8 13.6 %multiply_add_fusion.13 = (f32[2048,1024]{1,0:T(8,128)}, f32[2048,1024]{1,0:T(8,128)}) fusion(f32[2048,1024]{1,0:T(8,128)} %get-tuple-element.73, f32[1024,1024]{1,0:T(8,128)S(1)} %slice.296, f32[2048,1024]{1,0:T(8,128)} %get-tuple-element.74, f32[1536,1024]{1,0:T(8,128)} %slice.283), kind=kLoop, calls=%fused_computation.54 | loop fusion | flops 6291456 | bytes 44040192 | tf_op jit(solution)/shard_map/add | solution.py:20
  332.1 23.0 %all-gather.1 = f32[16,1,1024]{2,1,0:T(1,128)S(1)} all-gather(f32[1,1,1024]{2,1,0:T(1,128)S(1)} %slice_bitcast_fusion), channel_id=1, replica_groups=mesh['ctx'=16,'wa'=2] {'ctx'}, dimensions={0}, use_global_device_ids=true | all-gather | bytes 69632 | tf_op jit(solution)/shard_map/all_gather | solution.py:53
  367.3 17.6 %all-gather = f32[16,1,1024]{2,1,0:T(1,128)S(1)} all-gather(f32[1,1,1024]{2,1,0:T(1,128)S(1)} %slice_bitcast_fusion.1), channel_id=1, replica_groups=mesh['ctx'=16,'wa'=2] {'ctx'}, dimensions={0}, use_global_device_ids=true | all-gather | bytes 69632 | tf_op jit(solution)/shard_map/all_gather | solution.py:52
  385.9 13.8 %multiply_convert_fusion.3 = (bf16[2048,1024]{1,0:T(8,128)(2,1)}, f32[2048,1024]{1,0:T(8,128)}) fusion(f32[2048,4,1024]{2,0,1:T(8,128)} %convolution_add_fusion, f32[2048,1024]{1,0:T(8,128)} %get-tuple-element.71, f32[2048,1024]{1,0:T(8,128)} %pad_multiply_fusion.9, f32[1024]{0:T(1024)S(1)} %bitcast.133), kind=kLoop, calls=%fused_computation.51 | loop fusion | flops 14680064 | bytes 37752832 | tf_op jit(solution)/shard_map/convert_element_type | solution.py:62
  416.9 85.5 %all-gather.6.cloned.1.call-done = bf16[2048,2048]{1,0:T(8,128)(2,1)} async-done(((bf16[2048,1024]{1,0:T(8,128)(2,1)}), bf16[2048,2048]{1,0:T(8,128)(2,1)}) %all-gather.6.cloned.1.call-update) | async-done | bytes 8388624 | tf_op jit(solution)/shard_map/all_gather | solution.py:65
  513.8 12.2 %subtract_multiply_fusion = (f32[2048,1024]{1,0:T(8,128)}, bf16[2048,1,1024]{2,0,1:T(8,128)(2,1)}) fusion(f32[2048,1024]{1,0:T(8,128)} %get-tuple-element.66, f32[2048,4,1024]{2,0,1:T(8,128)} %convolution_add_fusion, bf16[2048,275]{0,1:T(8,128)(2,1)S(1)} %get-tuple-element.36, bf16[1024,275]{0,1:T(8,128)(2,1)S(1)} %copy-done.16), kind=kOutput, calls=%fused_computation.41 | convolution fusion | flops 1178599424 | bytes 31049728 | tf_op jit(solution)/shard_map/dot_general | solution.py:73
  553.4 13.0 %multiply_add_fusion.10 = f32[2048,1024]{1,0:T(8,128)} fusion(f32[2048,1024]{1,0:T(8,128)} %multiply_add_fusion.11, f32[2046,1024]{1,0:T(8,128)} %slice.319, f32[2047,1024]{1,0:T(8,128)} %copy-done.2, f32[2047,1024]{1,0:T(8,128)S(1)} %bitcast.103), kind=kLoop, calls=%fused_computation.39 | loop fusion | flops 6291456 | bytes 41926656 | tf_op jit(solution)/shard_map/add | solution.py:20
  575.1 21.9 %multiply_add_fusion.9 = (f32[2048,1024]{1,0:T(8,128)}, f32[2048,1024]{1,0:T(8,128)}) fusion(f32[2048,1024]{1,0:T(8,128)} %multiply_add_fusion.10, f32[2044,1024]{1,0:T(8,128)} %slice.320, f32[2046,1024]{1,0:T(8,128)} %slice_multiply_fusion, f32[2047,1024]{1,0:T(8,128)} %copy-done.2, f32[2047,1024]{1,0:T(8,128)} %get-tuple-element.97), kind=kLoop, calls=%fused_computation.38 | loop fusion | flops 8388608 | bytes 58687488 | tf_op jit(solution)/shard_map/add | solution.py:20
  609.8 19.1 %multiply_add_fusion.8 = (f32[2048,1024]{1,0:T(8,128)}, f32[2048,1024]{1,0:T(8,128)}) fusion(f32[2048,1024]{1,0:T(8,128)} %get-tuple-element.61, f32[2040,1024]{1,0:T(8,128)} %slice.321, f32[2048,1024]{1,0:T(8,128)} %get-tuple-element.62, f32[2044,1024]{1,0:T(8,128)} %slice.310), kind=kLoop, calls=%fused_computation.37 | loop fusion | flops 6291456 | bytes 50282496 | tf_op jit(solution)/shard_map/add | solution.py:20
  641.6 19.1 %multiply_add_fusion.7 = (f32[2048,1024]{1,0:T(8,128)}, f32[2048,1024]{1,0:T(8,128)}) fusion(f32[2048,1024]{1,0:T(8,128)} %get-tuple-element.59, f32[2032,1024]{1,0:T(8,128)} %slice.322, f32[2048,1024]{1,0:T(8,128)} %get-tuple-element.60, f32[2040,1024]{1,0:T(8,128)} %slice.311), kind=kLoop, calls=%fused_computation.36 | loop fusion | flops 6291456 | bytes 50233344 | tf_op jit(solution)/shard_map/add | solution.py:20
  673.5 19.0 %multiply_add_fusion.6 = (f32[2048,1024]{1,0:T(8,128)}, f32[2048,1024]{1,0:T(8,128)}) fusion(f32[2048,1024]{1,0:T(8,128)} %get-tuple-element.57, f32[2016,1024]{1,0:T(8,128)} %slice.323, f32[2048,1024]{1,0:T(8,128)} %get-tuple-element.58, f32[2032,1024]{1,0:T(8,128)} %slice.312), kind=kLoop, calls=%fused_computation.35 | loop fusion | flops 6291456 | bytes 50135040 | tf_op jit(solution)/shard_map/add | solution.py:20
  705.3 19.0 %multiply_add_fusion.5 = (f32[2048,1024]{1,0:T(8,128)}, f32[2048,1024]{1,0:T(8,128)}) fusion(f32[2048,1024]{1,0:T(8,128)} %get-tuple-element.55, f32[1984,1024]{1,0:T(8,128)} %slice.324, f32[2048,1024]{1,0:T(8,128)} %get-tuple-element.56, f32[2016,1024]{1,0:T(8,128)} %slice.313), kind=kLoop, calls=%fused_computation.34 | loop fusion | flops 6291456 | bytes 49938432 | tf_op jit(solution)/shard_map/add | solution.py:20
  736.7 18.7 %multiply_add_fusion.4 = (f32[2048,1024]{1,0:T(8,128)}, f32[2048,1024]{1,0:T(8,128)}) fusion(f32[2048,1024]{1,0:T(8,128)} %get-tuple-element.53, f32[1920,1024]{1,0:T(8,128)} %slice.325, f32[2048,1024]{1,0:T(8,128)} %get-tuple-element.54, f32[1984,1024]{1,0:T(8,128)} %slice.314), kind=kLoop, calls=%fused_computation.33 | loop fusion | flops 6291456 | bytes 49545216 | tf_op jit(solution)/shard_map/add | solution.py:20
  764.8 15.1 %multiply_add_fusion.3 = (f32[2048,1024]{1,0:T(8,128)}, f32[2048,1024]{1,0:T(8,128)}) fusion(f32[2048,1024]{1,0:T(8,128)} %get-tuple-element.51, f32[1792,1024]{1,0:T(8,128)S(1)} %slice.326, f32[2048,1024]{1,0:T(8,128)} %get-tuple-element.52, f32[1920,1024]{1,0:T(8,128)} %slice.315), kind=kLoop, calls=%fused_computation.32 | loop fusion | flops 6291456 | bytes 48758784 | tf_op jit(solution)/shard_map/add | solution.py:20
  790.6 13.0 %multiply_add_fusion.2 = (f32[2048,1024]{1,0:T(8,128)}, f32[2048,1024]{1,0:T(8,128)}) fusion(f32[2048,1024]{1,0:T(8,128)} %get-tuple-element.49, f32[1536,1024]{1,0:T(8,128)} %slice.327, f32[2048,1024]{1,0:T(8,128)S(1)} %copy-done.6, f32[1792,1024]{1,0:T(8,128)} %slice.316), kind=kLoop, calls=%fused_computation.31 | loop fusion | flops 6291456 | bytes 47185920 | tf_op jit(solution)/shard_map/add | solution.py:20
  825.9 21.5 %all-gather.2 = f32[16,1,1024]{2,1,0:T(1,128)S(1)} all-gather(f32[1,1,1024]{2,1,0:T(1,128)S(1)} %fusion.53), channel_id=1, replica_groups=mesh['ctx'=16,'wa'=2] {'ctx'}, dimensions={0}, use_global_device_ids=true | all-gather | bytes 69632 | tf_op jit(solution)/shard_map/all_gather | solution.py:81
  850.5 18.3 %fusion.18 = (bf16[2048,1,1024]{2,0,1:T(8,128)(2,1)}, f32[2048,1024]{1,0:T(8,128)}) fusion(f32[2048,4,1024]{2,0,1:T(8,128)} %convolution_add_fusion, f32[2048,1024]{1,0:T(8,128)} %get-tuple-element.45, f32[1024]{0:T(1024)S(1)} %bitcast.134, f32[2048,1024]{1,0:T(8,128)} %get-tuple-element.46, f32[1024,1024]{1,0:T(8,128)S(1)} %slice.329), kind=kLoop, calls=%fused_computation.78 | loop fusion | flops 23068672 | bytes 50335744 | tf_op jit(solution)/shard_map/stack | solution.py:92
  868.8 15.3 %fusion.21 = (bf16[2048,1,1024]{2,0,1:T(8,128)(2,1)S(1)}, bf16[2048,1,1024]{2,0,1:T(8,128)(2,1)S(1)}) fusion(f32[2047,1024]{1,0:T(8,128)} %bitcast.126, f32[1,1024]{1,0:T(1,128)S(1)} %copy-done.21, f32[2048,1024]{1,0:T(8,128)} %get-tuple-element.40, f32[2048]{0:T(1024)S(1)} %copy-done.19, f32[2048,4,1024]{2,0,1:T(8,128)} %convolution_add_fusion), kind=kLoop, calls=%fused_computation.81 | loop fusion | flops 39845888 | bytes 50339840 | tf_op jit(solution)/shard_map/stack | solution.py:92
  917.3 58.3 %all-reduce.59 = (f32[]{:T(128)}, f32[4,1024]{1,0:T(4,128)}, f32[275]{0:T(512)}) all-reduce(f32[]{:T(128)} %get-tuple-element.63, f32[4,1024]{1,0:T(4,128)S(1)} %get-tuple-element.37, f32[275]{0:T(512)S(1)} %copy-done.23), channel_id=1, replica_groups=mesh['ctx'=16,'wa'=2] {'ctx'}, use_global_device_ids=true, to_apply=%region_7.8 | all-reduce | flops 4372 | bytes 34976 | tf_op jit(solution)/shard_map/psum | solution.py:99
  976.2 25.3 %all-reduce.66.cloned.1.call-done = (f32[100,4,1024]{2,0,1:T(8,128)}, f32[1024,275]{0,1:T(8,128)}) async-done(((f32[100,4,1024]{2,0,1:T(8,128)}, f32[1024,275]{0,1:T(8,128)}), (f32[100,4,1024]{2,0,1:T(8,128)}, f32[1024,275]{0,1:T(8,128)})) %all-reduce.66.cloned.1.call-update) | async-done | bytes 2764816 | tf_op jit(solution)/shard_map/psum | solution.py:99
  1005.1 122.0 %all-reduce.64.cloned.1.call-done = f32[275,100]{1,0:T(8,128)} async-done(((f32[275,100]{1,0:T(8,128)}), f32[275,100]{1,0:T(8,128)}) %all-reduce.64.cloned.1.call-update) | async-done | bytes 110016 | tf_op jit(solution)/shard_map/psum | solution.py:100
  (199 shorter events, 338.8 us)
Async XLA Ops:
  7.2 409.7 %all-gather.8.cloned.1.call-start = ((), (), s32[]{:S(2)}) async-start(), calls=%async_computation.1 | async-start | bytes 1720320 | tf_op jit(solution)/shard_map/all_gather | solution.py:66
  7.9 494.4 %all-gather.6.cloned.1.call-start = ((), (), s32[]{:S(2)}) async-start(), calls=%async_computation | async-start | bytes 12582912 | tf_op jit(solution)/shard_map/all_gather | solution.py:65
  12.2 23.9 %copy-start.18 = (f32[2048]{0:T(1024)}, f32[2048]{0:T(1024)S(1)}, u32[]{:S(2)}) copy-start(f32[2048]{0:T(1024)S(1)} %convert_subtract_fusion) | copy-start | bytes 24580
  13.9 14.4 %copy-start.14 = (bf16[2048,100,1]{0,1,2:T(8,128)(2,1)}, bf16[2048,100,1]{0,1,2:T(8,128)(2,1)S(1)}, u32[]{:S(2)}) copy-start(bf16[2048,100,1]{0,1,2:T(8,128)(2,1)S(1)} %fusion.25) | copy-start | bytes 1228804
  50.8 8.5 copy-start.1
  124.8 8.5 slice-start.6
  124.8 8.5 slice-start.7
  156.2 8.4 slice-start.9
  317.8 37.3 %copy-start.24 = (s32[16]{0:T(128)S(1)}, s32[16]{0:T(128)}, u32[]{:S(2)}) copy-start(s32[16]{0:T(128)} %param.12) | copy-start | bytes 196
  385.9 13.8 %copy-start.20 = (f32[1,1024]{1,0:T(1,128)}, f32[1,1024]{1,0:T(1,128)S(1)}, u32[]{:S(2)}) copy-start(f32[1,1024]{1,0:T(1,128)S(1)} %fusion.47) | copy-start | bytes 12292
  399.8 601.7 %all-reduce.66.cloned.1.call-start = ((), (), s32[]{:S(2)}) async-start(), calls=%async_computation.3 | async-start | bytes 5701632 | tf_op jit(solution)/shard_map/psum | solution.py:99
  409.3 93.1 %copy-start.27 = (f32[275]{0:T(512)S(1)}, f32[275]{0:T(512)}, u32[]{:S(2)}) copy-start(f32[275]{0:T(512)} %param.17) | copy-start | bytes 3304
  416.9 91.9 %copy-start.22 = (s32[2048]{0:T(1024)S(1)}, s32[2048]{0:T(1024)}, u32[]{:S(2)}) copy-start(s32[2048]{0:T(1024)} %param.10) | copy-start | bytes 24580
  502.3 9.1 copy-start.10
  511.5 23.3 %slice-start = ((s8[8388608]{0:T(1024)(128)(4,1)}), s8[4194304]{0:T(1024)(128)(4,1)S(1)}, s32[]{:S(2)}) async-start(s8[8388608]{0:T(1024)(128)(4,1)} %bitcast.102), calls=%async_computation.4 | async-start | bytes 8388608
  513.8 20.9 %slice-start.1 = ((s8[8388608]{0:T(1024)(128)(4,1)}), s8[4194304]{0:T(1024)(128)(4,1)S(1)}, s32[]{:S(2)}) async-start(s8[8388608]{0:T(1024)(128)(4,1)} %bitcast.102), calls=%async_computation.5 | async-start | bytes 8388608
  597.0 8.5 slice-start.2
  597.0 8.5 slice-start.3
  628.9 8.5 slice-start.4
  628.9 8.5 slice-start.5
  660.6 8.5 slice-start.10
  660.6 8.5 slice-start.11
  813.5 33.9 %copy-start.25 = (s32[16]{0:T(128)S(1)}, s32[16]{0:T(128)}, u32[]{:S(2)}) copy-start(s32[16]{0:T(128)} %param.12) | copy-start | bytes 196
  813.5 34.1 %copy-start.13 = (f32[16,1024]{1,0:T(8,128)S(1)}, f32[16,1024]{1,0:T(8,128)}, u32[]{:S(2)}) copy-start(f32[16,1024]{1,0:T(8,128)} %copy-done.12) | copy-start | bytes 196612
  813.5 34.1 %copy-start.17 = (f32[15,1024]{1,0:T(8,128)S(1)}, f32[15,1024]{1,0:T(8,128)}, u32[]{:S(2)}) copy-start(f32[15,1024]{1,0:T(8,128)} %get-tuple-element.99) | copy-start | bytes 184324
  850.4 18.3 %copy-start.19 = (f32[2048]{0:T(1024)S(1)}, f32[2048]{0:T(1024)}, u32[]{:S(2)}) copy-start(f32[2048]{0:T(1024)} %copy-done.18) | copy-start | bytes 24580
  850.5 18.3 %copy-start.21 = (f32[1,1024]{1,0:T(1,128)S(1)}, f32[1,1024]{1,0:T(1,128)}, u32[]{:S(2)}) copy-start(f32[1,1024]{1,0:T(1,128)} %copy-done.20) | copy-start | bytes 12292
  868.8 15.3 %copy-start.11 = (bf16[2048,1,1024]{2,0,1:T(8,128)(2,1)S(1)}, bf16[2048,1,1024]{2,0,1:T(8,128)(2,1)}, u32[]{:S(2)}) copy-start(bf16[2048,1,1024]{2,0,1:T(8,128)(2,1)} %get-tuple-element.39) | copy-start | bytes 12582916
  884.1 14.7 %copy-start.15 = (bf16[2048,100,1]{0,1,2:T(8,128)(2,1)S(1)}, bf16[2048,100,1]{0,1,2:T(8,128)(2,1)}, u32[]{:S(2)}) copy-start(bf16[2048,100,1]{0,1,2:T(8,128)(2,1)} %copy-done.14) | copy-start | bytes 1228804
  902.7 11.8 %copy-start.26 = (s32[2048]{0:T(1024)S(1)}, s32[2048]{0:T(1024)}, u32[]{:S(2)}) copy-start(s32[2048]{0:T(1024)} %param.9) | copy-start | bytes 24580
  902.7 14.5 %copy-start.23 = (f32[275]{0:T(512)S(1)}, f32[275]{0:T(512)}, u32[]{:S(2)}) copy-start(f32[275]{0:T(512)} %get-tuple-element.35) | copy-start | bytes 3304
  902.7 224.4 %all-reduce.64.cloned.1.call-start = ((), (), s32[]{:S(2)}) async-start(), calls=%async_computation.2 | async-start | bytes 286720 | tf_op jit(solution)/shard_map/psum | solution.py:100
  (20 other events, 134.5 us)
Sparse Core Ops, SparseCore 0:
  9.6 25.0 all-gather.7
  399.9 102.3 all-gather.5
  902.8 98.5 all-reduce.65
  1007.4 119.6 all-reduce.63
where the time goes:
time: 1150 us; the launch traced here: 1140 us
  other arithmetic  463 us (40%)
  local copies, waits for them, and re-layouts  247 us (21%)
  waiting for transfers between devices  233 us (20%)
  blocking collectives  120 us (10%)
  matrix products  56 us (5%)
  between operations  18.3 us (2%)
    add x27, other arithmetic, doubling_scan(): sums = prods * moved_s + sums  377 us
    psum x1, waiting for transfers between devices, body(): grad_embed = lax.psum(embed_local, ('ctx', 'wa'))  122 us
    all_gather x1, waiting for transfers between devices, body(): lax.all_gather(hidden_low, 'wa', axis=1, tiled=True)  85.5 us
    slice x15, local copies, waits for them, and re-layouts, doubling_scan(): moved_s = jnp.concatenate([sums[stride:], zeros], axis=0)  83.9 us
    slice x9, local copies, waits for them, and re-layouts, doubling_scan(): moved_s = jnp.concatenate([zeros, sums[:-stride]], axis=0)  58.8 us
    psum x1, blocking collectives, body(): lax.psum((grad_w_in, grad_b_in, grad_w_out, grad_b_out, loss_local), 'ctx')  58.3 us
    slice x13, local copies, waits for them, and re-layouts, doubling_scan(): moved_p = jnp.concatenate([prods[stride:], ones], axis=0)  40.7 us
    another operation x2, other arithmetic, body(): jnp.stack([grad_input, grad_forget, grad_candidate, grad_output], axis=1)  33.6 us
  transfers between devices with their start and end apart: 4, of which 3 were waited for; matrix products, arithmetic and copies ran while one was open for 33% of the time, Pallas kernels for 0%

commit v1 on v0

v1 whole, which is shorter than its diff:
```python
import functools

import jax
import jax.numpy as jnp
from jax import lax
from jax.experimental import pallas as pl
from jax.experimental.pallas import tpu as pltpu
from jax.sharding import PartitionSpec as P

SUB = 8
LANE = 128
WBLK = 256
VMEM = 52 * 1024 * 1024
RESET_PULL = -30000.0
F32 = jnp.float32
BF16 = jnp.bfloat16


def ceil_to(value, step):
    return -(-value // step) * step


def params(steps=1):
    return pltpu.CompilerParams(dimension_semantics=("arbitrary",) * steps, vmem_limit_bytes=VMEM)


def whole(shape):
    zeros = (0,) * len(shape)
    return pl.BlockSpec(shape, lambda *_: zeros)


def smem():
    return pl.BlockSpec(memory_space=pltpu.SMEM)


def stages_of(count):
    stages, bit, number = [], 1, 0
    while bit < count:
        if number >= 2 and bit * 2 < count:
            stages.append([bit, 2 * bit, 3 * bit])
            bit *= 4
        else:
            stages.append([bit])
            bit *= 2
        number += 1
    return stages


def swap(value, axis, mask):
    count = lax.axis_size(axis)
    return lax.ppermute(value, axis, [(k, k ^ mask) for k in range(count)])


def gather_xor(value, axis):
    out = value[None]
    for masks in stages_of(lax.axis_size(axis)):
        out = jnp.concatenate([out] + [swap(out, axis, mask) for mask in masks], axis=0)
    return out


def slot_of(xor_index, count):
    place, size, bit = 0, count, 1
    for masks in stages_of(count):
        ways = len(masks) + 1
        size = size // ways
        place = place + ((xor_index // bit) % ways) * size
        bit = bit * ways
    return place


def scatter_sum(chunks, axis):
    count = lax.axis_size(axis)
    value = chunks
    for masks in stages_of(count):
        ways = len(masks) + 1
        value = value.reshape((ways, value.shape[0] // ways) + value.shape[1:])
        moved = [swap(value[k + 1], axis, mask) for k, mask in enumerate(masks)]
        total = value[0]
        for part in moved:
            total = total + part
        value = total
    return value[0]


def gather_chunks(chunk, axis):
    value = chunk[None]
    for masks in reversed(stages_of(lax.axis_size(axis))):
        value = jnp.concatenate([value] + [swap(value, axis, mask) for mask in masks], axis=0)
    return value


def feats_kernel(starts, base, ids, table, feats, onehot):
    vocab, toks = onehot.shape
    seg = toks // SUB
    hits = lax.broadcasted_iota(jnp.int32, (vocab, toks), 0) == ids[...]
    table_t = hits.astype(F32).astype(BF16)
    onehot[...] = table_t
    rows = lax.dot_general(table_t, table[...], (((0,), (0,)), ((), ())), preferred_element_type=F32)
    width = rows.shape[1]
    row = lax.broadcasted_iota(jnp.int32, (toks, width), 0)
    col = lax.broadcasted_iota(jnp.int32, (toks, width), 1)
    position = base[0] + (row % SUB) * seg + row // SUB
    hit = position == starts[0]
    for k in range(1, starts.shape[0]):
        hit = hit | (position == starts[k])
    mark = jnp.where(hit & (col == 103), 1.0, 0.0)
    feats[...] = (rows + mark).astype(BF16)


def gate_kernel(feats, w, decay, source, out, seg_p, seg_s, block_ps):
    toks = feats.shape[0]
    rows = 128
    width = decay.shape[1]

    def chunk(k, carry):
        prod, total = carry
        at = pl.multiple_of(k * rows, rows)
        fe = feats[pl.ds(at, rows), :]
        gate = [jnp.dot(fe, w[g], preferred_element_type=F32) for g in range(4)]
        in_gate = 0.5 * jnp.tanh(gate[0]) + 0.5
        forget = 0.5 * jnp.tanh(gate[1]) + 0.5
        cand = jnp.tanh(gate[2])
        src = in_gate * cand
        decay[pl.ds(at, rows), :] = forget
        source[pl.ds(at, rows), :] = src
        out[pl.ds(at, rows), :] = 0.5 * jnp.tanh(gate[3]) + 0.5
        for r in range(rows // SUB):
            d = forget[r * SUB:(r + 1) * SUB]
            total = d * total + src[r * SUB:(r + 1) * SUB]
            prod = prod * d
        return prod, total

    prod, total = lax.fori_loop(
        0, toks // rows, chunk, (jnp.ones((SUB, width), F32), jnp.zeros((SUB, width), F32))
    )
    seg_p[...] = prod
    seg_s[...] = total
    p_all, s_all = prod[0:1], total[0:1]
    for s in range(1, SUB):
        s_all = prod[s:s + 1] * s_all + total[s:s + 1]
        p_all = prod[s:s + 1] * p_all
    block_ps[0:1, :] = p_all
    block_ps[1:2, :] = s_all


def cell_kernel(
    order, meta, d_o, x_o, o_o, d_x, x_x, o_x, ps_all, sp_o, ss_o, sp_x, ss_x, wt_o, wt_x, bias, tgt,
    prev, hid, lgrad, src, go, h_seg, h_blk, b_grad, loss,
    c_o, c_x, pcum, hs_o, hs_x, hb_o, hb_x, q, u, hg, gacc, *, total_tokens,
):
    k = pl.program_id(0)
    steps = hid.shape[1]
    rows = steps * SUB
    width = d_o.shape[1]
    vocab = wt_o.shape[0]

    @pl.when(k == 0)
    def _():
        me, own = meta[0], meta[1]

        def earlier(b, c):
            pair = ps_all[order[b] ^ me]
            return pair[0:1] * c + pair[1:2]

        c = lax.fori_loop(0, own, earlier, jnp.zeros((1, ps_all.shape[2]), F32))
        for ref, sp, ss, at in ((c_o, sp_o, ss_o, 0), (c_x, sp_x, ss_x, width)):
            one = c[:, at:at + ref.shape[1]]
            for s in range(SUB):
                ref[s:s + 1, :] = one
                one = sp[s:s + 1, :] * one + ss[s:s + 1, :]
        pcum[...] = jnp.ones_like(pcum)
        h_seg[...] = jnp.zeros_like(h_seg)
        gacc[...] = jnp.zeros_like(gacc)
        loss[...] = jnp.zeros_like(loss)

    def spread(ref, r, value):
        for b in range(ref.shape[0]):
            ref[b, pl.ds(r, SUB, stride=steps), :] = value[:, b * LANE:(b + 1) * LANE]

    def own_step(r, c):
        at = pl.multiple_of(r * SUB, SUB)
        prev[pl.ds(at, SUB), :] = c
        c = d_o[pl.ds(at, SUB), :] * c + x_o[pl.ds(at, SUB), :]
        t = jnp.tanh(c)
        o = o_o[pl.ds(at, SUB), :]
        h = o * t
        q[pl.ds(at, SUB), :] = o - h * t
        u[pl.ds(at, SUB), :] = h - h * o
        spread(hs_o, r, h)
        return c

    def other_step(r, c):
        at = pl.multiple_of(r * SUB, SUB)
        c = d_x[pl.ds(at, SUB), :] * c + x_x[pl.ds(at, SUB), :]
        spread(hs_x, r, o_x[pl.ds(at, SUB), :] * jnp.tanh(c))
        return c

    c_o[...] = lax.fori_loop(0, steps, own_step, c_o[...], unroll=4)
    c_x[...] = lax.fori_loop(0, steps, other_step, c_x[...], unroll=4)
    for low, high in ((hb_o, hs_o), (hb_x, hs_x)):
        for b in range(high.shape[0]):
            low[:, b * LANE:(b + 1) * LANE] = high[b].astype(BF16)
    hid[...] = hb_o[...].reshape(SUB, steps, width)
    nt = (((1,), (1,)), ((), ()))
    logits = lax.dot_general(hb_o[...], wt_o[...], nt, preferred_element_type=F32)
    logits = logits + lax.dot_general(hb_x[...], wt_x[...], nt, preferred_element_type=F32)
    logits = logits + bias[...]
    target = lax.broadcasted_iota(jnp.int32, (rows, vocab), 1) == tgt[...].reshape(rows, 1)
    top = jnp.max(logits, axis=1, keepdims=True)
    power = jnp.exp(logits - top)
    norm = jnp.sum(power, axis=1, keepdims=True)
    picked = jnp.sum(jnp.where(target, logits, 0.0), axis=1, keepdims=True)
    loss[...] += jnp.sum(top + jnp.log(norm) - picked, keepdims=True)
    probs = power / norm
    grad = ((probs - jnp.where(target, 1.0, 0.0)) * (1.0 / total_tokens)).astype(BF16)
    lgrad[...] = grad.reshape(SUB, steps, vocab)
    gacc[...] += jnp.sum(grad.astype(F32).reshape(rows // SUB, SUB, vocab), axis=0)
    back = jnp.dot(grad, wt_o[...], preferred_element_type=F32)
    for b in range(hg.shape[0]):
        hg[b] = back[:, b * LANE:(b + 1) * LANE]

    def back_step(pair, carry):
        pc, acc = carry
        outs = []
        for half in range(2):
            r = pair * 2 + half
            at = pl.multiple_of(r * SUB, SUB)
            g = jnp.concatenate([hg[b, pl.ds(r, SUB, stride=steps), :] for b in range(hg.shape[0])], axis=1)
            s = g * q[pl.ds(at, SUB), :]
            src[pl.ds(at, SUB), :] = s
            outs.append(g * u[pl.ds(at, SUB), :])
            pc = pc * d_o[pl.ds(at, SUB), :]
            acc = acc + pc * s
        at = pl.multiple_of(pair * 2 * SUB, 2 * SUB)
        go[pl.ds(at, 2 * SUB), :] = jnp.concatenate(outs, axis=0).astype(BF16)
        return pc, acc

    pc, acc = lax.fori_loop(0, steps // 2, back_step, (pcum[...], h_seg[...]), unroll=2)
    pcum[...] = pc
    h_seg[...] = acc

    @pl.when(k == pl.num_programs(0) - 1)
    def _():
        b_grad[...] = jnp.sum(gacc[...], axis=0, keepdims=True)
        head = h_seg[SUB - 1:SUB, :]
        for s in range(SUB - 2, -1, -1):
            head = h_seg[s:s + 1, :] + sp_o[s:s + 1, :] * head
        h_blk[...] = head


def decoder_grad_kernel(meta, lgrad, hid, out, *, count):
    j = pl.program_id(0)
    tn = (((0,), (0,)), ((), ()))
    grad = lax.dot_general(lgrad[...], hid[...], tn, preferred_element_type=F32)
    vocab = grad.shape[0]
    cols = grad.shape[1] // LANE
    part = out.shape[1]
    splits = count // (pl.num_programs(0) * cols)
    for c in range(cols):
        for e in range(splits):
            if e * part >= vocab:
                continue
            size = min(part, vocab - e * part)
            slot = slot_of(((j * cols + c) * splits + e) ^ meta[0], count)
            piece = grad[e * part:e * part + size, c * LANE:(c + 1) * LANE]
            if size < part:
                piece = jnp.concatenate([piece, jnp.zeros((part - size, LANE), F32)], axis=0)
            out[slot] = piece


def input_grad_kernel(
    order, meta, feats, w, prev, src, go, onehot, table_t, h_all, ps_all, seg_p, h_seg, b_grad, loss,
    out, out_e,
    gg, hn, eacc, *, count, part,
):
    j = pl.program_id(0)
    toks = feats.shape[0]
    rows = 128
    width = prev.shape[1]
    vocab = onehot.shape[0]
    me, own = meta[0], meta[1]

    def later(i, g):
        slot = order[count - 1 - i] ^ me
        return h_all[slot] + ps_all[slot][0:1] * g

    one = lax.fori_loop(0, count - 1 - own, later, jnp.zeros((1, width), F32))
    for s in range(SUB - 1, -1, -1):
        hn[s:s + 1, :] = one
        one = h_seg[s:s + 1, :] + seg_p[s:s + 1, :] * one

    def chunk(i, later_grad):
        at = pl.multiple_of((toks // rows - 1 - i) * rows, rows)
        fe = feats[pl.ds(at, rows), :]
        gate = [jnp.dot(fe, w[g], preferred_element_type=F32) for g in range(3)]
        in_gate = 0.5 * jnp.tanh(gate[0]) + 0.5
        decay = 0.5 * jnp.tanh(gate[1]) + 0.5
        cand = jnp.tanh(gate[2])
        source = in_gate * cand
        given = src[pl.ds(at, rows), :]
        cell, carried = [], []
        for r in range(rows // SUB - 1, -1, -1):
            g = given[r * SUB:(r + 1) * SUB] + later_grad
            later_grad = decay[r * SUB:(r + 1) * SUB] * g
            cell.append(g)
            carried.append(later_grad)
        g = jnp.concatenate(cell[::-1], axis=0)
        h = jnp.concatenate(carried[::-1], axis=0)
        gg[pl.ds(at, rows), 0:width] = (g * (source - source * in_gate)).astype(BF16)
        gg[pl.ds(at, rows), width:2 * width] = (h * prev[pl.ds(at, rows), :] * (1.0 - decay)).astype(BF16)
        gg[pl.ds(at, rows), 2 * width:3 * width] = (g * (in_gate - source * cand)).astype(BF16)
        return later_grad

    lax.fori_loop(0, toks // rows, chunk, hn[...])
    gg[:, 3 * width:4 * width] = go[...]
    both = (((1,), (1,)), ((), ()))
    cols = width // LANE
    splits = count // (pl.num_programs(0) * cols)
    part_e = jnp.zeros((vocab, feats.shape[1]), F32)
    for gate in range(4):
        total = jnp.dot(onehot[...], gg[:, gate * width:(gate + 1) * width], preferred_element_type=F32)
        high = total.astype(BF16)
        low = (total - high.astype(F32)).astype(BF16)
        wide = jnp.dot(table_t[...], high, preferred_element_type=F32)
        wide = wide + jnp.dot(table_t[...], low, preferred_element_type=F32)
        for c in range(cols):
            for e in range(splits):
                if e * part >= wide.shape[0]:
                    continue
                size = min(part, wide.shape[0] - e * part)
                slot = slot_of(((j * cols + c) * splits + e) ^ me, count)
                out[slot, gate * part:gate * part + size, :] = wide[
                    e * part:e * part + size, c * LANE:(c + 1) * LANE
                ]
        back = lax.dot_general(high, w[gate], both, preferred_element_type=F32)
        back = back + lax.dot_general(low, w[gate], both, preferred_element_type=F32)
        part_e = part_e + (back if gate == 2 else 2.0 * back)

    @pl.when(j == 0)
    def _():
        eacc[...] = jnp.zeros_like(eacc)

    eacc[0:vocab, 0:feats.shape[1]] += part_e

    @pl.when(j == pl.num_programs(0) - 1)
    def _():
        for k in range(3):
            size = min(LANE, vocab - k * LANE)
            eacc[vocab + k:vocab + k + 1, 0:size] = b_grad[:, k * LANE:k * LANE + size]
        eacc[vocab + 3:vocab + 4, 0:1] = loss[...]
        per = out_e.shape[1]
        for p in range(count):
            out_e[slot_of(p ^ me, count)] = eacc[p * per:(p + 1) * per, :]


def finish_kernel(meta, chunks, w_grad, b_grad, e_grad, o_grad, loss, eacc, *, part, vocab, emb, shards, total_tokens):
    count = chunks.shape[0]
    me = meta[0]
    width = w_grad.shape[2]
    cols = width // LANE
    splits = count // cols
    per = chunks.shape[1] - 4 * part
    for c in range(cols):
        lanes = slice(c * LANE, (c + 1) * LANE)
        for e in range(splits):
            slot = slot_of((c * splits + e) ^ me, count)
            size = max(0, min(part, emb - e * part))
            for gate in range(4):
                if size:
                    w_grad[gate, e * part:e * part + size, lanes] = chunks[slot, gate * part:gate * part + size, :]
                if e * part <= emb < (e + 1) * part:
                    at = gate * part + emb - e * part
                    b_grad[gate:gate + 1, lanes] = chunks[slot, at:at + 1, :]
    for p in range(count):
        eacc[p * per:(p + 1) * per, :] = chunks[slot_of(p ^ me, count), 4 * part:4 * part + per, :]
    e_grad[...] = eacc[0:e_grad.shape[0], 0:emb]
    for k in range(3):
        size = min(LANE, o_grad.shape[1] - k * LANE)
        o_grad[:, k * LANE:k * LANE + size] = eacc[vocab + k:vocab + k + 1, 0:size] * (1.0 / shards)
    loss[...] = eacc[vocab + 3:vocab + 4, 0:1] * (1.0 / (shards * total_tokens))


def decoder_finish_kernel(meta, chunks, out):
    count = chunks.shape[0]
    me = meta[0]
    cols = out.shape[1] // LANE
    splits = count // cols
    part = chunks.shape[1]
    for c in range(cols):
        for e in range(splits):
            size = max(0, min(part, out.shape[0] - e * part))
            if size:
                slot = slot_of((c * splits + e) ^ me, count)
                out[e * part:e * part + size, c * LANE:(c + 1) * LANE] = chunks[slot, 0:size, :]


def fetch_others(value, wa, own_core):
    half = value.shape[0] // 2
    mine = lax.dynamic_slice_in_dim(value, own_core * half, half, 0)
    fetched = []
    for shift in range(1, wa):
        got = lax.ppermute(mine, "wa", [(k, (k - shift) % wa) for k in range(wa)])
        other = swap(got, "ctx", 1)
        first = jnp.where(own_core == 0, got, other)
        second = jnp.where(own_core == 0, other, got)
        fetched.append(jnp.concatenate([first, second], axis=0))
    return fetched


def body(ids, targets, doc_lengths, block_of, embed, w_in, b_in, w_out, b_out):
    count = lax.axis_size("ctx")
    wa = lax.axis_size("wa")
    me = lax.axis_index("ctx").astype(jnp.int32)
    toks = ids.shape[0]
    seg = toks // SUB
    emb, gates, width = w_in.shape
    other = width * (wa - 1)
    vocab = embed.shape[0]
    vpad = ceil_to(vocab, 32)
    total_tokens = toks * count
    block_ids = jnp.arange(count, dtype=jnp.int32)
    own_block = jnp.sum(jnp.where(block_ids == me, block_of, 0))
    order = jnp.sum(jnp.where(block_of[None, :] == block_ids[:, None], block_ids[None, :], 0), axis=1)
    meta = jnp.stack([me, own_block])
    base = (own_block * toks)[None]
    starts = jnp.cumsum(doc_lengths) - doc_lengths

    kdim = ceil_to(emb + 4, 16)
    scale = jnp.array([0.5, 0.5, 1.0, 0.5], F32)
    shift = jnp.array([0.0, 3.0, 0.0, 0.0], F32)
    b_eff = (b_in + shift[:, None]) * scale[:, None]
    b_hi = lax.reduce_precision(b_eff, 8, 7)
    b_mid = lax.reduce_precision(b_eff - b_hi, 8, 7)
    b_lo = b_eff - b_hi - b_mid
    pull = jnp.broadcast_to(jnp.array([0.0, RESET_PULL, 0.0, 0.0], F32)[:, None], (gates, width))
    extra = jnp.stack([b_hi, b_mid, b_lo, pull], axis=1)
    main = jnp.transpose(w_in, (1, 0, 2)).astype(F32) * scale[:, None, None]
    fill = jnp.zeros((gates, kdim - emb - 4, width), F32)
    w_own = jnp.concatenate([main, extra, fill], axis=1).astype(BF16)
    table = jnp.pad(embed, ((0, vpad - vocab), (0, kdim - emb)))
    table = jnp.where((jnp.arange(kdim) >= emb) & (jnp.arange(kdim) < emb + 3), jnp.ones((), BF16), table)
    wt_own = jnp.pad(w_out.T, ((0, vpad - vocab), (0, 0)))
    core = me % 2
    w_oth = jnp.concatenate(fetch_others(w_own, wa, core), axis=2)
    wt_oth = jnp.concatenate(fetch_others(wt_own, wa, core), axis=1)
    bias_out = jnp.pad(b_out, (0, vpad - vocab), constant_values=-1e30)[None]
    ids_p = ids.reshape(SUB, seg).T.reshape(1, toks)
    tgt = targets.reshape(SUB, seg, 1)

    feats, onehot = pl.pallas_call(
        feats_kernel,
        in_specs=[smem(), smem(), whole((1, toks)), whole((vpad, kdim))],
        out_specs=[whole((toks, kdim)), whole((vpad, toks))],
        out_shape=[jax.ShapeDtypeStruct((toks, kdim), BF16), jax.ShapeDtypeStruct((vpad, toks), BF16)],
        compiler_params=pltpu.CompilerParams(vmem_limit_bytes=VMEM),
        name="feats",
    )(starts, base, ids_p, table)

    def gate_call(w, name):
        wide = w.shape[2]
        column = lambda rows: pl.BlockSpec((rows, WBLK), lambda j: (0, j))
        shape = lambda rows: jax.ShapeDtypeStruct((rows, wide), F32)
        return pl.pallas_call(
            gate_kernel,
            grid=(wide // WBLK,),
            in_specs=[whole((toks, kdim)), pl.BlockSpec((gates, kdim, WBLK), lambda j: (0, 0, j))],
            out_specs=[column(toks)] * 3 + [column(SUB)] * 2 + [column(2)],
            out_shape=[shape(toks)] * 3 + [shape(SUB)] * 2 + [shape(2)],
            compiler_params=params(),
            cost_estimate=pl.CostEstimate(
                flops=8 * toks * kdim * wide, bytes_accessed=12 * toks * wide, transcendentals=4 * toks * wide
            ),
            name=name,
        )(feats, w)

    d_o, x_o, o_o, sp_o, ss_o, ps = gate_call(w_own, "gates_own")
    ps_x = [ps] + [
        lax.ppermute(ps, "wa", [(k, (k - s) % wa) for k in range(wa)]) for s in range(1, wa)
    ]
    ps_all = gather_xor(jnp.concatenate(ps_x, axis=1), "ctx")
    d_x, x_x, o_x, sp_x, ss_x, _ = gate_call(w_oth, "gates_other")

    steps = 32
    rows = steps * SUB
    row_block = lambda wide: pl.BlockSpec((rows, wide), lambda k: (k, 0))
    nat_block = lambda wide: pl.BlockSpec((SUB, steps, wide), lambda k: (0, k, 0))
    prev, hid, lgrad, src, go, h_seg, h_blk, b_grad, loss = pl.pallas_call(
        functools.partial(cell_kernel, total_tokens=total_tokens),
        grid=(seg // steps,),
        in_specs=[smem(), smem()]
        + [row_block(width)] * 3
        + [row_block(other)] * 3
        + [whole(ps_all.shape)]
        + [whole((SUB, width))] * 2
        + [whole((SUB, other))] * 2
        + [whole((vpad, width)), whole((vpad, other)), whole((1, vpad)), nat_block(1)],
        out_specs=[
            row_block(width), nat_block(width), nat_block(vpad), row_block(width), row_block(width),
            whole((SUB, width)), whole((1, width)), whole((1, vpad)), whole((1, 1)),
        ],
        out_shape=[
            jax.ShapeDtypeStruct((toks, width), F32),
            jax.ShapeDtypeStruct((SUB, seg, width), BF16),
            jax.ShapeDtypeStruct((SUB, seg, vpad), BF16),
            jax.ShapeDtypeStruct((toks, width), F32),
            jax.ShapeDtypeStruct((toks, width), BF16),
            jax.ShapeDtypeStruct((SUB, width), F32),
            jax.ShapeDtypeStruct((1, width), F32),
            jax.ShapeDtypeStruct((1, vpad), F32),
            jax.ShapeDtypeStruct((1, 1), F32),
        ],
        scratch_shapes=[
            pltpu.VMEM((SUB, width), F32), pltpu.VMEM((SUB, other), F32), pltpu.VMEM((SUB, width), F32),
            pltpu.VMEM((width // LANE, rows, LANE), F32), pltpu.VMEM((other // LANE, rows, LANE), F32),
            pltpu.VMEM((rows, width), BF16), pltpu.VMEM((rows, other), BF16),
            pltpu.VMEM((rows, width), F32), pltpu.VMEM((rows, width), F32),
            pltpu.VMEM((width // LANE, rows, LANE), F32),
            pltpu.VMEM((SUB, vpad), F32),
        ],
        compiler_params=params(),
        name="cells",
    )(order, meta, d_o, x_o, o_o, d_x, x_x, o_x, ps_all, sp_o, ss_o, sp_x, ss_x, wt_own, wt_oth, bias_out, tgt)

    hidden = hid.reshape(toks, width)
    h_all = gather_xor(h_blk, "ctx")

    cols = width // LANE
    splits = count // cols
    vpart = ceil_to(-(-vpad // splits), 8)
    w_out_chunks = pl.pallas_call(
        functools.partial(decoder_grad_kernel, count=count),
        grid=(width // WBLK,),
        in_specs=[smem(), whole((toks, vpad)), pl.BlockSpec((toks, WBLK), lambda j: (0, j))],
        out_specs=whole((count, vpart, LANE)),
        out_shape=jax.ShapeDtypeStruct((count, vpart, LANE), F32),
        compiler_params=params(),
        cost_estimate=pl.CostEstimate(
            flops=2 * toks * vpad * width, bytes_accessed=2 * toks * (width + vpad), transcendentals=0
        ),
        name="decoder_grad",
    )(meta, lgrad.reshape(toks, vpad), hidden)

    part = ceil_to(-(-kdim // splits), 8)
    per = ceil_to(-(-(vpad + 4) // count), 8)
    column = lambda size: pl.BlockSpec((size, WBLK), lambda j: (0, j))
    lead = lambda *size: pl.BlockSpec(size + (WBLK,), lambda j: (0, 0, j))
    w_chunks, e_chunks = pl.pallas_call(
        functools.partial(input_grad_kernel, count=count, part=part),
        grid=(width // WBLK,),
        in_specs=[
            smem(), smem(), whole((toks, kdim)), lead(gates, kdim), column(toks), column(toks), column(toks),
            whole((vpad, toks)), whole((kdim, vpad)), lead(count, 1), lead(count, 2), column(SUB), column(SUB),
            whole((1, vpad)), whole((1, 1)),
        ],
        out_specs=[whole((count, 4 * part, LANE)), whole((count, per, LANE))],
        out_shape=[
            jax.ShapeDtypeStruct((count, 4 * part, LANE), F32),
            jax.ShapeDtypeStruct((count, per, LANE), F32),
        ],
        scratch_shapes=[
            pltpu.VMEM((toks, 4 * WBLK), BF16), pltpu.VMEM((SUB, WBLK), F32), pltpu.VMEM((count * per, LANE), F32)
        ],
        compiler_params=params(),
        name="input_grad",
    )(order, meta, feats, w_own, prev, src, go, onehot, table.T, h_all, ps_all, sp_o, h_seg, b_grad, loss)

    bit = 1
    while bit < wa:
        e_chunks = e_chunks + swap(e_chunks, "wa", bit)
        bit *= 2
    out_chunk = gather_chunks(scatter_sum(w_out_chunks, "ctx"), "ctx")
    w_out_grad = pl.pallas_call(
        decoder_finish_kernel,
        in_specs=[smem(), whole(out_chunk.shape)],
        out_specs=whole((vpad, width)),
        out_shape=jax.ShapeDtypeStruct((vpad, width), F32),
        compiler_params=pltpu.CompilerParams(vmem_limit_bytes=VMEM),
        name="decoder_finish",
    )(meta, out_chunk)
    in_chunk = gather_chunks(scatter_sum(jnp.concatenate([w_chunks, e_chunks], axis=1), "ctx"), "ctx")
    w_grad, bi_grad, e_grad, bo_grad, loss_all = pl.pallas_call(
        functools.partial(
            finish_kernel, part=part, vocab=vpad, emb=emb, shards=wa, total_tokens=total_tokens
        ),
        in_specs=[smem(), whole(in_chunk.shape)],
        out_specs=[
            whole((gates, emb, width)), whole((gates, width)), whole((vocab, emb)), whole((1, vocab)), whole((1, 1))
        ],
        out_shape=[
            jax.ShapeDtypeStruct((gates, emb, width), F32),
            jax.ShapeDtypeStruct((gates, width), F32),
            jax.ShapeDtypeStruct((vocab, emb), F32),
            jax.ShapeDtypeStruct((1, vocab), F32),
            jax.ShapeDtypeStruct((1, 1), F32),
        ],
        scratch_shapes=[pltpu.VMEM((count * per, LANE), F32)],
        compiler_params=pltpu.CompilerParams(vmem_limit_bytes=VMEM),
        name="finish",
    )(meta, in_chunk)
    return (
        hidden,
        loss_all[0, 0],
        e_grad,
        jnp.transpose(w_grad, (1, 0, 2)),
        bi_grad,
        w_out_grad[:vocab].T,
        bo_grad[0],
    )


def solution(mesh):
    placed = (
        P("ctx"),
        P("ctx"),
        P(),
        P(),
        P(),
        P(None, None, "wa"),
        P(None, "wa"),
        P("wa", None),
        P(),
    )
    return jax.shard_map(
        body,
        mesh=mesh,
        in_specs=placed,
        out_specs=(
            P("ctx", "wa"),
            P(),
            P(),
            P(None, None, "wa"),
            P(None, "wa"),
            P("wa", None),
            P(),
        ),
        check_vma=False,
    )
```

time: 1150 us -> 257 us (0.22)
  other arithmetic: 463 us -> 7.61 us
  local copies, waits for them, and re-layouts: 247 us -> 11.3 us
  waiting for transfers between devices: 233 us -> 67.2 us
  Pallas kernels: 0 us -> 128 us
  blocking collectives: 120 us -> 0 us
  matrix products: 56 us -> 0 us
  starting transfers between devices: 0.37 us -> 40.1 us
  between operations: 18.3 us -> 1.91 us
    add x28 -> x5, other arithmetic: 377 us -> 0.28 us  [the longest x4 0.26 us: scatter_sum(): total = total + part]
    slice x46 -> x5, local copies, waits for them, and re-layouts: 222 us -> 0.14 us  [scatter_sum(): moved = [swap(value[k + 1], axis, mask) for k, mask in enumerate(masks)]]
    psum x2 -> x0, waiting for transfers between devices: 147 us -> none  [the longest x1 122 us: body(): grad_embed = lax.psum(embed_local, ('ctx', 'wa'))]
    pallas_call x0 -> x8, Pallas kernels: none -> 128 us  [the longest x1 43 us: body(): pl.pallas_call(functools.partial(cell_kernel, total_tokens=total_tokens),...]
    all_gather x2 -> x0, waiting for transfers between devices: 85.5 us -> none  [the longest x1 85.5 us: body(): lax.all_gather(hidden_low, 'wa', axis=1, tiled=True)]
    ppermute x0 -> x36, waiting for transfers between devices: none -> 67.2 us  [the longest x33 67.2 us: swap(): return lax.ppermute(value, axis, [(k, k ^ mask) for k in range(count)])]
    all_gather x3 -> x0, blocking collectives: 62.1 us -> none  [the longest x1 23 us: body(): lax.all_gather(sums[-1:], 'ctx', axis=0, tiled=True)]
    psum x1 -> x0, blocking collectives: 58.3 us -> none  [body(): lax.psum((grad_w_in, grad_b_in, grad_w_out, grad_b_out, loss_local), 'ctx')]
  transfers between devices with their start and end apart: 4 -> 36, of which waited for: 3 -> 23; matrix products, arithmetic and copies ran while one was open for 33% -> 4% of each run, Pallas kernels for 0% -> 25%
where the time goes in v1:
time: 257 us; the launch traced here: 256 us
  Pallas kernels  128 us (50%)
  waiting for transfers between devices  67.2 us (26%)
  starting transfers between devices  40.1 us (16%)
  local copies, waits for them, and re-layouts  11.3 us (4%)
  other arithmetic  7.61 us (3%)
    ppermute x33, waiting for transfers between devices, swap(): return lax.ppermute(value, axis, [(k, k ^ mask) for k in range(count)])  67.2 us
    pallas_call x1, Pallas kernels, body(): pl.pallas_call(functools.partial(cell_kernel, total_tokens=total_tokens),...  43 us
    pallas_call x1, Pallas kernels, body(): pl.pallas_call(functools.partial(input_grad_kernel, count=count, part=par...  39.8 us
    ppermute x33, starting transfers between devices, swap(): return lax.ppermute(value, axis, [(k, k ^ mask) for k in range(count)])  35 us
    pallas_call x2, Pallas kernels, gate_call(): pl.pallas_call(gate_kernel, grid=(wide // WBLK,), in_specs=[whole((toks,...  34.6 us
    unnamed x45, local copies, waits for them, and re-layouts  5.96 us
    pallas_call x1, Pallas kernels, body(): pl.pallas_call(functools.partial(decoder_grad_kernel, count=count), grid=...  5.14 us
  transfers between devices with their start and end apart: 36, of which 23 were waited for; matrix products, arithmetic and copies ran while one was open for 4% of the time, Pallas kernels for 25%

profile of v1, /device:TPU:0, one launch (start us, length us, event | category | flops | bytes accessed | tf_op | source)
XLA Modules:
  0.0 256.2 jit_solution(6495635532215315809)
XLA Ops:
  1.7 3.0 %collective-permute-start.8 = (bf16[144,1024]{1,0:T(8,128)(2,1)S(1)}, bf16[144,1024]{1,0:T(8,128)(2,1)}, u32[]{:S(2)}, u32[]{:S(2)}) collective-permute-start(bf16[144,1024]{1,0:T(8,128)(2,1)S(1)} %constant_dynamic-slice_fusion), channel_id=1, source_target_pairs={{0,1},{1,0},{2,3},{3,2},{4,5},{5,4},{6,7},{7,6},{8,9},{9,8},{10,11... | collective-permute-start | bytes 884744 | tf_op jit(solution)/shard_map/ppermute | solution.py:402
  12.4 17.3 %gates_own.1 = (f32[2048,1024]{1,0:T(8,128)}, f32[2048,1024]{1,0:T(8,128)}, f32[2048,1024]{1,0:T(8,128)}, f32[8,1024]{1,0:T(8,128)S(1)}, f32[8,1024]{1,0:T(8,128)S(1)}, /*index=5*/f32[2,1024]{1,0:T(2,128)S(1)}) custom-call(bf16[2048,112]{1,0:T(8,128)(2,1)S(1)} %get-tuple-element.36.feats, bf16[4,112,1024]{2,1,0:T(8,128)(2,1)S(1)} %concatenate.60.w), custom_call_target="tpu_custom_call" | custom-call | flops 1879048192 | bytes 25165824 | tf_op jit(solution)/shard_map/gates_own/pallas_call | solution.py:463
  29.7 2.0 collective-permute-start.2
  37.4 2.4 collective-permute-done.4
  39.8 3.7 %collective-permute-start.7 = (f32[4,2,2048]{2,1,0:T(2,128)S(1)}, f32[4,2,2048]{2,1,0:T(2,128)S(1)}, u32[]{:S(2)}, u32[]{:S(2)}) collective-permute-start(f32[4,2,2048]{2,1,0:T(2,128)S(1)} %pad_maximum_fusion.5), channel_id=1, source_target_pairs={{0,24},{2,26},{4,28},{6,30},{8,16},{10,18},{12,20},{14,22},{16,8},... | collective-permute-start | bytes 196616 | tf_op jit(solution)/shard_map/ppermute | solution.py:51
  44.3 3.8 %collective-permute-done.5 = f32[4,2,2048]{2,1,0:T(2,128)S(1)} collective-permute-done((f32[4,2,2048]{2,1,0:T(2,128)S(1)}, f32[4,2,2048]{2,1,0:T(2,128)S(1)}, u32[]{:S(2)}, u32[]{:S(2)}) %collective-permute-start.5) | collective-permute-done | bytes 65568 | tf_op jit(solution)/shard_map/ppermute | solution.py:51
  51.2 17.3 %gates_other.1 = (f32[2048,1024]{1,0:T(8,128)}, f32[2048,1024]{1,0:T(8,128)}, f32[2048,1024]{1,0:T(8,128)}, f32[8,1024]{1,0:T(8,128)S(1)}, f32[8,1024]{1,0:T(8,128)S(1)}, /*index=5*/f32[2,1024]{1,0:T(2,128)}) custom-call(bf16[2048,112]{1,0:T(8,128)(2,1)S(1)} %get-tuple-element.36.feats, bf16[4,112,1024]{2,1,0:T(8,128)(2,1)S(1)} %pad_maximum_fusion.1.w), custom_call_target="tpu_custom_call" | custom-call | flops 1879048192 | bytes 25165824 | tf_op jit(solution)/shard_map/gates_other/pallas_call | solution.py:463
  68.5 43.0 %cells.1 = (f32[2048,1024]{1,0:T(8,128)}, bf16[8,256,1024]{2,1,0:T(8,128)(2,1)}, bf16[8,256,288]{2,1,0:T(8,128)(2,1)}, f32[2048,1024]{1,0:T(8,128)}, bf16[2048,1...) custom-call(s32[16]{0:T(128)S(1)} %select_reduce_fusion.order, ...), custom_call_target="tpu_custom_call" | custom-call | tf_op jit(solution)/shard_map/cells/pallas_call | solution.py:487
  111.7 5.1 %decoder_grad.1 = f32[16,144,128]{2,1,0:T(8,128)S(1)} custom-call(s32[2]{0:T(128)S(1)} %pad_add_fusion.meta, bf16[2048,288]{1,0:T(8,128)(2,1)} %bitcast.38, bf16[2048,1024]{1,0:T(8,128)(2,1)} %bitcast.34), custom_call_target="tpu_custom_call" | custom-call | flops 1207959552 | bytes 5373952 | tf_op jit(solution)/shard_map/decoder_grad/pallas_call | solution.py:530
  118.9 2.2 collective-permute-done.11
  121.1 2.4 collective-permute-start.14
  125.6 2.0 collective-permute-done.12
  128.2 39.8 %input_grad.1 = (f32[16,224,128]{2,1,0:T(8,128)}, f32[16,24,128]{2,1,0:T(8,128)S(1)}) custom-call(s32[16]{0:T(128)S(1)} %select_reduce_fusion.order, s32[2]{0:T(128)S(1)} %pad_add_fusion.meta, bf16[2048,112]{1,0:T(8,128)(2,1)S(1)} %get-tuple-element.36.feats, bf16[4,112,1024]{2,1,0:T(8,128)(2,1)} %copy-done, f32[2048,1024]{1,0:T(8,128)} %get-tuple-element.49.prev, ...), custom_call_target="tpu_custom_call" | custom-call | tf_op jit(solution)/shard_map/input_grad/pallas_call | solution.py:547
  168.9 4.8 %collective-permute-done.15 = f32[16,24,128]{2,1,0:T(8,128)S(1)} collective-permute-done((f32[16,24,128]{2,1,0:T(8,128)S(1)}, f32[16,24,128]{2,1,0:T(8,128)S(1)}, u32[]{:S(2)}, u32[]{:S(2)}) %collective-permute-start.15) | collective-permute-done | bytes 196640 | tf_op jit(solution)/shard_map/ppermute | solution.py:51
  175.2 1.9 collective-permute-start.27
  177.1 7.7 %collective-permute-done.27 = f32[4,144,128]{2,1,0:T(8,128)S(1)} collective-permute-done((f32[4,144,128]{2,1,0:T(8,128)S(1)}, f32[4,144,128]{2,1,0:T(8,128)S(1)}, u32[]{:S(2)}, u32[]{:S(2)}) %collective-permute-start.27) | collective-permute-done | bytes 294944 | tf_op jit(solution)/shard_map/ppermute | solution.py:51
  187.9 2.0 collective-permute-start.30
  191.2 3.5 %collective-permute-done.30 = f32[1,144,128]{2,1,0:T(8,128)S(1)} collective-permute-done((f32[1,144,128]{2,1,0:T(8,128)S(1)}, f32[1,144,128]{2,1,0:T(8,128)S(1)}, u32[]{:S(2)}, u32[]{:S(2)}) %collective-permute-start.30) | collective-permute-done | bytes 73760 | tf_op jit(solution)/shard_map/ppermute | solution.py:51
  194.7 2.5 collective-permute-done.29
  197.2 2.2 collective-permute-start.33
  199.4 2.3 collective-permute-start.31
  201.8 2.2 collective-permute-start.20
  207.1 3.9 %collective-permute-done.18 = f32[1,248,128]{2,1,0:T(8,128)S(1)} collective-permute-done((f32[1,248,128]{2,1,0:T(8,128)S(1)}, f32[1,248,128]{2,1,0:T(8,128)S(1)}, u32[]{:S(2)}, u32[]{:S(2)}) %collective-permute-start.18) | collective-permute-done | bytes 127008 | tf_op jit(solution)/shard_map/ppermute | solution.py:51
  212.7 4.1 %collective-permute-done.19 = f32[1,248,128]{2,1,0:T(8,128)S(1)} collective-permute-done((f32[1,248,128]{2,1,0:T(8,128)S(1)}, f32[1,248,128]{2,1,0:T(8,128)S(1)}, u32[]{:S(2)}, u32[]{:S(2)}) %collective-permute-start.19) | collective-permute-done | bytes 127008 | tf_op jit(solution)/shard_map/ppermute | solution.py:51
  216.8 2.0 collective-permute-start.23
  218.8 2.5 collective-permute-start.21
  221.3 3.8 %collective-permute-done.23 = f32[1,248,128]{2,1,0:T(8,128)S(1)} collective-permute-done((f32[1,248,128]{2,1,0:T(8,128)S(1)}, f32[1,248,128]{2,1,0:T(8,128)S(1)}, u32[]{:S(2)}, u32[]{:S(2)}) %collective-permute-start.23) | collective-permute-done | bytes 127008 | tf_op jit(solution)/shard_map/ppermute | solution.py:51
  225.1 3.4 %collective-permute-done.22 = f32[1,248,128]{2,1,0:T(8,128)S(1)} collective-permute-done((f32[1,248,128]{2,1,0:T(8,128)S(1)}, f32[1,248,128]{2,1,0:T(8,128)S(1)}, u32[]{:S(2)}, u32[]{:S(2)}) %collective-permute-start.22) | collective-permute-done | bytes 127008 | tf_op jit(solution)/shard_map/ppermute | solution.py:51
  229.3 12.9 %collective-permute-done.24 = f32[4,248,128]{2,1,0:T(8,128)S(1)} collective-permute-done((f32[4,248,128]{2,1,0:T(8,128)S(1)}, f32[4,248,128]{2,1,0:T(8,128)S(1)}, u32[]{:S(2)}, u32[]{:S(2)}) %collective-permute-start.24) | collective-permute-done | bytes 507936 | tf_op jit(solution)/shard_map/ppermute | solution.py:51
  242.9 2.8 %collective-permute-done.35 = f32[8,144,128]{2,1,0:T(8,128)S(1)} collective-permute-done((f32[8,144,128]{2,1,0:T(8,128)S(1)}, f32[8,144,128]{2,1,0:T(8,128)S(1)}, u32[]{:S(2)}, u32[]{:S(2)}) %collective-permute-start.35) | collective-permute-done | bytes 589856 | tf_op jit(solution)/shard_map/ppermute | solution.py:51
  250.9 2.6 finish.1
  253.4 2.2 copy.58
  (151 shorter events, 41.1 us)
Async XLA Ops:
  1.7 46.4 %collective-permute-start.8 = (bf16[144,1024]{1,0:T(8,128)(2,1)S(1)}, bf16[144,1024]{1,0:T(8,128)(2,1)}, u32[]{:S(2)}, u32[]{:S(2)}) collective-permute-start(bf16[144,1024]{1,0:T(8,128)(2,1)S(1)} %constant_dynamic-slice_fusion), channel_id=1, source_target_pairs={{0,1},{1,0},{2,3},{3,2},{4,5},{5,4},{6,7},{7,6},{8,9},{9,8},{10,11... | collective-permute-start | bytes 884744 | tf_op jit(solution)/shard_map/ppermute | solution.py:402
  7.7 41.2 %collective-permute-start = (bf16[2,112,1024]{2,1,0:T(8,128)(2,1)S(1)}, bf16[2,112,1024]{2,1,0:T(8,128)(2,1)S(1)}, u32[]{:S(2)}, u32[]{:S(2)}) collective-permute-start(bf16[2,112,1024]{2,1,0:T(8,128)(2,1)S(1)} %constant_dynamic-slice_fusion.1), channel_id=1, source_target_pairs={{0,1},{1,0},{2,3},{3,2},{4,5},{5,4},{6,7},{7,6},{8,9},{9,8},{10,11... | collective-permute-start | bytes 1376264 | tf_op jit(solution)/shard_map/ppermute | solution.py:402
  29.7 4.8 %collective-permute-start.2 = (f32[2,1024]{1,0:T(2,128)S(1)}, f32[2,1024]{1,0:T(2,128)S(1)}, u32[]{:S(2)}, u32[]{:S(2)}) collective-permute-start(f32[2,1024]{1,0:T(2,128)S(1)} %get-tuple-element.43), channel_id=1, source_target_pairs={{0,1},{1,0},{2,3},{3,2},{4,5},{5,4},{6,7},{7,6},{8,9},{9,8},{10,11... | collective-permute-start | bytes 24584 | tf_op jit(solution)/shard_map/ppermute | solution.py:478
  35.8 4.0 %collective-permute-start.4 = (f32[2,2,2048]{2,1,0:T(2,128)S(1)}, f32[2,2,2048]{2,1,0:T(2,128)S(1)}, u32[]{:S(2)}, u32[]{:S(2)}) collective-permute-start(f32[2,2,2048]{2,1,0:T(2,128)S(1)} %pad_maximum_fusion.6), channel_id=1, source_target_pairs={{0,4},{2,6},{4,0},{6,2},{8,12},{10,14},{12,8},{14,10},{16,20},{18,... | collective-permute-start | bytes 98312 | tf_op jit(solution)/shard_map/ppermute | solution.py:51
  39.8 9.1 %collective-permute-start.7 = (f32[4,2,2048]{2,1,0:T(2,128)S(1)}, f32[4,2,2048]{2,1,0:T(2,128)S(1)}, u32[]{:S(2)}, u32[]{:S(2)}) collective-permute-start(f32[4,2,2048]{2,1,0:T(2,128)S(1)} %pad_maximum_fusion.5), channel_id=1, source_target_pairs={{0,24},{2,26},{4,28},{6,30},{8,16},{10,18},{12,20},{14,22},{16,8},... | collective-permute-start | bytes 196616 | tf_op jit(solution)/shard_map/ppermute | solution.py:51
  43.5 5.4 %collective-permute-start.6 = (f32[4,2,2048]{2,1,0:T(2,128)S(1)}, f32[4,2,2048]{2,1,0:T(2,128)S(1)}, u32[]{:S(2)}, u32[]{:S(2)}) collective-permute-start(f32[4,2,2048]{2,1,0:T(2,128)S(1)} %pad_maximum_fusion.5), channel_id=1, source_target_pairs={{0,16},{2,18},{4,20},{6,22},{8,24},{10,26},{12,28},{14,30},{16,0},... | collective-permute-start | bytes 196616 | tf_op jit(solution)/shard_map/ppermute | solution.py:51
  43.5 4.6 %collective-permute-start.5 = (f32[4,2,2048]{2,1,0:T(2,128)S(1)}, f32[4,2,2048]{2,1,0:T(2,128)S(1)}, u32[]{:S(2)}, u32[]{:S(2)}) collective-permute-start(f32[4,2,2048]{2,1,0:T(2,128)S(1)} %pad_maximum_fusion.5), channel_id=1, source_target_pairs={{0,8},{2,10},{4,12},{6,14},{8,0},{10,2},{12,4},{14,6},{16,24},{18,... | collective-permute-start | bytes 196616 | tf_op jit(solution)/shard_map/ppermute | solution.py:51
  111.6 5.8 %collective-permute-start.10 = (f32[1,1,1024]{2,1,0:T(1,128)S(1)}, f32[1,1,1024]{2,1,0:T(1,128)S(1)}, u32[]{:S(2)}, u32[]{:S(2)}) collective-permute-start(f32[1,1,1024]{2,1,0:T(1,128)S(1)} %bitcast.31), channel_id=1, source_target_pairs={{0,2},{2,0},{4,6},{6,4},{8,10},{10,8},{12,14},{14,12},{16,18},{18,... | collective-permute-start | bytes 12296 | tf_op jit(solution)/shard_map/ppermute | solution.py:51
  116.9 58.2 %collective-permute-start.26 = (f32[8,144,128]{2,1,0:T(8,128)S(1)}, f32[8,144,128]{2,1,0:T(8,128)S(1)}, u32[]{:S(2)}, u32[]{:S(2)}) collective-permute-start(f32[8,144,128]{2,1,0:T(8,128)S(1)} %slice.93), channel_id=1, source_target_pairs={{0,2},{2,0},{4,6},{6,4},{8,10},{10,8},{12,14},{14,12},{16,18},{18,... | collective-permute-start | bytes 1769480 | tf_op jit(solution)/shard_map/ppermute | solution.py:51
  117.4 3.7 %collective-permute-start.11 = (f32[2,1,1024]{2,1,0:T(1,128)S(1)}, f32[2,1,1024]{2,1,0:T(1,128)S(1)}, u32[]{:S(2)}, u32[]{:S(2)}) collective-permute-start(f32[2,1,1024]{2,1,0:T(1,128)S(1)} %pad_maximum_fusion.8), channel_id=1, source_target_pairs={{0,4},{2,6},{4,0},{6,2},{8,12},{10,14},{12,8},{14,10},{16,20},{18,... | collective-permute-start | bytes 24584 | tf_op jit(solution)/shard_map/ppermute | solution.py:51
  121.1 7.1 %collective-permute-start.14 = (f32[4,1,1024]{2,1,0:T(1,128)S(1)}, f32[4,1,1024]{2,1,0:T(1,128)S(1)}, u32[]{:S(2)}, u32[]{:S(2)}) collective-permute-start(f32[4,1,1024]{2,1,0:T(1,128)S(1)} %pad_maximum_fusion.7), channel_id=1, source_target_pairs={{0,24},{2,26},{4,28},{6,30},{8,16},{10,18},{12,20},{14,22},{16,8},... | collective-permute-start | bytes 49160 | tf_op jit(solution)/shard_map/ppermute | solution.py:51
  123.6 4.6 %collective-permute-start.13 = (f32[4,1,1024]{2,1,0:T(1,128)S(1)}, f32[4,1,1024]{2,1,0:T(1,128)S(1)}, u32[]{:S(2)}, u32[]{:S(2)}) collective-permute-start(f32[4,1,1024]{2,1,0:T(1,128)S(1)} %pad_maximum_fusion.7), channel_id=1, source_target_pairs={{0,16},{2,18},{4,20},{6,22},{8,24},{10,26},{12,28},{14,30},{16,0},... | collective-permute-start | bytes 49160 | tf_op jit(solution)/shard_map/ppermute | solution.py:51
  123.9 3.7 %collective-permute-start.12 = (f32[4,1,1024]{2,1,0:T(1,128)S(1)}, f32[4,1,1024]{2,1,0:T(1,128)S(1)}, u32[]{:S(2)}, u32[]{:S(2)}) collective-permute-start(f32[4,1,1024]{2,1,0:T(1,128)S(1)} %pad_maximum_fusion.7), channel_id=1, source_target_pairs={{0,8},{2,10},{4,12},{6,14},{8,0},{10,2},{12,4},{14,6},{16,24},{18,... | collective-permute-start | bytes 49160 | tf_op jit(solution)/shard_map/ppermute | solution.py:51
  168.0 5.7 %collective-permute-start.15 = (f32[16,24,128]{2,1,0:T(8,128)S(1)}, f32[16,24,128]{2,1,0:T(8,128)S(1)}, u32[]{:S(2)}, u32[]{:S(2)}) collective-permute-start(f32[16,24,128]{2,1,0:T(8,128)S(1)} %get-tuple-element.58), channel_id=1, source_target_pairs={{0,1},{1,0},{2,3},{3,2},{4,5},{5,4},{6,7},{7,6},{8,9},{9,8},{10,11... | collective-permute-start | bytes 589832 | tf_op jit(solution)/shard_map/ppermute | solution.py:51
  175.0 9.8 %collective-permute-start.16 = (f32[8,248,128]{2,1,0:T(8,128)S(1)}, f32[8,248,128]{2,1,0:T(8,128)S(1)}, u32[]{:S(2)}, u32[]{:S(2)}) collective-permute-start(f32[8,248,128]{2,1,0:T(8,128)S(1)} %pad_maximum_fusion), channel_id=1, source_target_pairs={{0,2},{2,0},{4,6},{6,4},{8,10},{10,8},{12,14},{14,12},{16,18},{18,... | collective-permute-start | bytes 3047432 | tf_op jit(solution)/shard_map/ppermute | solution.py:51
  175.2 9.6 %collective-permute-start.27 = (f32[4,144,128]{2,1,0:T(8,128)S(1)}, f32[4,144,128]{2,1,0:T(8,128)S(1)}, u32[]{:S(2)}, u32[]{:S(2)}) collective-permute-start(f32[4,144,128]{2,1,0:T(8,128)S(1)} %slice.95), channel_id=1, source_target_pairs={{0,4},{2,6},{4,0},{6,2},{8,12},{10,14},{12,8},{14,10},{16,20},{18,... | collective-permute-start | bytes 884744 | tf_op jit(solution)/shard_map/ppermute | solution.py:51
  185.0 16.7 %collective-permute-start.17 = (f32[4,248,128]{2,1,0:T(8,128)S(1)}, f32[4,248,128]{2,1,0:T(8,128)S(1)}, u32[]{:S(2)}, u32[]{:S(2)}) collective-permute-start(f32[4,248,128]{2,1,0:T(8,128)S(1)} %slice.87), channel_id=1, source_target_pairs={{0,4},{2,6},{4,0},{6,2},{8,12},{10,14},{12,8},{14,10},{16,20},{18,... | collective-permute-start | bytes 1523720 | tf_op jit(solution)/shard_map/ppermute | solution.py:51
  186.8 4.4 %collective-permute-start.28 = (f32[1,144,128]{2,1,0:T(8,128)S(1)}, f32[1,144,128]{2,1,0:T(8,128)S(1)}, u32[]{:S(2)}, u32[]{:S(2)}) collective-permute-start(f32[1,144,128]{2,1,0:T(8,128)S(1)} %get-tuple-element.115), channel_id=1, source_target_pairs={{0,8},{2,10},{4,12},{6,14},{8,0},{10,2},{12,4},{14,6},{16,24},{18,... | collective-permute-start | bytes 221192 | tf_op jit(solution)/shard_map/ppermute | solution.py:51
  187.9 6.8 %collective-permute-start.30 = (f32[1,144,128]{2,1,0:T(8,128)S(1)}, f32[1,144,128]{2,1,0:T(8,128)S(1)}, u32[]{:S(2)}, u32[]{:S(2)}) collective-permute-start(f32[1,144,128]{2,1,0:T(8,128)S(1)} %get-tuple-element.116), channel_id=1, source_target_pairs={{0,24},{2,26},{4,28},{6,30},{8,16},{10,18},{12,20},{14,22},{16,8},... | collective-permute-start | bytes 221192 | tf_op jit(solution)/shard_map/ppermute | solution.py:51
  189.9 7.2 %collective-permute-start.29 = (f32[1,144,128]{2,1,0:T(8,128)S(1)}, f32[1,144,128]{2,1,0:T(8,128)S(1)}, u32[]{:S(2)}, u32[]{:S(2)}) collective-permute-start(f32[1,144,128]{2,1,0:T(8,128)S(1)} %get-tuple-element.117), channel_id=1, source_target_pairs={{0,16},{2,18},{4,20},{6,22},{8,24},{10,26},{12,28},{14,30},{16,0},... | collective-permute-start | bytes 221192 | tf_op jit(solution)/shard_map/ppermute | solution.py:51
  197.2 6.9 %collective-permute-start.33 = (f32[1,144,128]{2,1,0:T(8,128)S(1)}, f32[1,144,128]{2,1,0:T(8,128)S(1)}, u32[]{:S(2)}, u32[]{:S(2)}) collective-permute-start(f32[1,144,128]{2,1,0:T(8,128)S(1)} %get-tuple-element.101), channel_id=1, source_target_pairs={{0,24},{2,26},{4,28},{6,30},{8,16},{10,18},{12,20},{14,22},{16,8},... | collective-permute-start | bytes 221192 | tf_op jit(solution)/shard_map/ppermute | solution.py:51
  199.3 7.0 %collective-permute-start.32 = (f32[1,144,128]{2,1,0:T(8,128)S(1)}, f32[1,144,128]{2,1,0:T(8,128)S(1)}, u32[]{:S(2)}, u32[]{:S(2)}) collective-permute-start(f32[1,144,128]{2,1,0:T(8,128)S(1)} %get-tuple-element.101), channel_id=1, source_target_pairs={{0,16},{2,18},{4,20},{6,22},{8,24},{10,26},{12,28},{14,30},{16,0},... | collective-permute-start | bytes 221192 | tf_op jit(solution)/shard_map/ppermute | solution.py:51
  199.4 7.3 %collective-permute-start.31 = (f32[1,144,128]{2,1,0:T(8,128)S(1)}, f32[1,144,128]{2,1,0:T(8,128)S(1)}, u32[]{:S(2)}, u32[]{:S(2)}) collective-permute-start(f32[1,144,128]{2,1,0:T(8,128)S(1)} %get-tuple-element.101), channel_id=1, source_target_pairs={{0,8},{2,10},{4,12},{6,14},{8,0},{10,2},{12,4},{14,6},{16,24},{18,... | collective-permute-start | bytes 221192 | tf_op jit(solution)/shard_map/ppermute | solution.py:51
  201.7 9.3 %collective-permute-start.18 = (f32[1,248,128]{2,1,0:T(8,128)S(1)}, f32[1,248,128]{2,1,0:T(8,128)S(1)}, u32[]{:S(2)}, u32[]{:S(2)}) collective-permute-start(f32[1,248,128]{2,1,0:T(8,128)S(1)} %get-tuple-element.110), channel_id=1, source_target_pairs={{0,8},{2,10},{4,12},{6,14},{8,0},{10,2},{12,4},{14,6},{16,24},{18,... | collective-permute-start | bytes 380936 | tf_op jit(solution)/shard_map/ppermute | solution.py:51
  201.8 10.9 %collective-permute-start.20 = (f32[1,248,128]{2,1,0:T(8,128)S(1)}, f32[1,248,128]{2,1,0:T(8,128)S(1)}, u32[]{:S(2)}, u32[]{:S(2)}) collective-permute-start(f32[1,248,128]{2,1,0:T(8,128)S(1)} %get-tuple-element.111), channel_id=1, source_target_pairs={{0,24},{2,26},{4,28},{6,30},{8,16},{10,18},{12,20},{14,22},{16,8},... | collective-permute-start | bytes 380936 | tf_op jit(solution)/shard_map/ppermute | solution.py:51
  204.1 12.7 %collective-permute-start.19 = (f32[1,248,128]{2,1,0:T(8,128)S(1)}, f32[1,248,128]{2,1,0:T(8,128)S(1)}, u32[]{:S(2)}, u32[]{:S(2)}) collective-permute-start(f32[1,248,128]{2,1,0:T(8,128)S(1)} %get-tuple-element.112), channel_id=1, source_target_pairs={{0,16},{2,18},{4,20},{6,22},{8,24},{10,26},{12,28},{14,30},{16,0},... | collective-permute-start | bytes 380936 | tf_op jit(solution)/shard_map/ppermute | solution.py:51
  206.7 35.6 %collective-permute-start.34 = (f32[4,144,128]{2,1,0:T(8,128)S(1)}, f32[4,144,128]{2,1,0:T(8,128)S(1)}, u32[]{:S(2)}, u32[]{:S(2)}) collective-permute-start(f32[4,144,128]{2,1,0:T(8,128)S(1)} %pad_maximum_fusion.4), channel_id=1, source_target_pairs={{0,4},{2,6},{4,0},{6,2},{8,12},{10,14},{12,8},{14,10},{16,20},{18,... | collective-permute-start | bytes 884744 | tf_op jit(solution)/shard_map/ppermute | solution.py:51
  216.8 8.3 %collective-permute-start.23 = (f32[1,248,128]{2,1,0:T(8,128)S(1)}, f32[1,248,128]{2,1,0:T(8,128)S(1)}, u32[]{:S(2)}, u32[]{:S(2)}) collective-permute-start(f32[1,248,128]{2,1,0:T(8,128)S(1)} %get-tuple-element.103), channel_id=1, source_target_pairs={{0,24},{2,26},{4,28},{6,30},{8,16},{10,18},{12,20},{14,22},{16,8},... | collective-permute-start | bytes 380936 | tf_op jit(solution)/shard_map/ppermute | solution.py:51
  218.8 9.7 %collective-permute-start.22 = (f32[1,248,128]{2,1,0:T(8,128)S(1)}, f32[1,248,128]{2,1,0:T(8,128)S(1)}, u32[]{:S(2)}, u32[]{:S(2)}) collective-permute-start(f32[1,248,128]{2,1,0:T(8,128)S(1)} %get-tuple-element.103), channel_id=1, source_target_pairs={{0,16},{2,18},{4,20},{6,22},{8,24},{10,26},{12,28},{14,30},{16,0},... | collective-permute-start | bytes 380936 | tf_op jit(solution)/shard_map/ppermute | solution.py:51
  218.8 9.7 %collective-permute-start.21 = (f32[1,248,128]{2,1,0:T(8,128)S(1)}, f32[1,248,128]{2,1,0:T(8,128)S(1)}, u32[]{:S(2)}, u32[]{:S(2)}) collective-permute-start(f32[1,248,128]{2,1,0:T(8,128)S(1)} %get-tuple-element.103), channel_id=1, source_target_pairs={{0,8},{2,10},{4,12},{6,14},{8,0},{10,2},{12,4},{14,6},{16,24},{18,... | collective-permute-start | bytes 380936 | tf_op jit(solution)/shard_map/ppermute | solution.py:51
  228.6 13.6 %collective-permute-start.24 = (f32[4,248,128]{2,1,0:T(8,128)S(1)}, f32[4,248,128]{2,1,0:T(8,128)S(1)}, u32[]{:S(2)}, u32[]{:S(2)}) collective-permute-start(f32[4,248,128]{2,1,0:T(8,128)S(1)} %pad_maximum_fusion.3), channel_id=1, source_target_pairs={{0,4},{2,6},{4,0},{6,2},{8,12},{10,14},{12,8},{14,10},{16,20},{18,... | collective-permute-start | bytes 1523720 | tf_op jit(solution)/shard_map/ppermute | solution.py:51
  242.2 7.2 %collective-permute-start.25 = (f32[8,248,128]{2,1,0:T(8,128)S(1)}, f32[8,248,128]{2,1,0:T(8,128)S(1)}, u32[]{:S(2)}, u32[]{:S(2)}) collective-permute-start(f32[8,248,128]{2,1,0:T(8,128)S(1)} %get-tuple-element.108), channel_id=1, source_target_pairs={{0,2},{2,0},{4,6},{6,4},{8,10},{10,8},{12,14},{14,12},{16,18},{18,... | collective-permute-start | bytes 3047432 | tf_op jit(solution)/shard_map/ppermute | solution.py:51
  (17 other events, 116.2 us)

commit v2 on v0

v2 whole, which is shorter than its diff:
```python
import functools

import jax
import jax.numpy as jnp
from jax import lax
from jax.experimental import pallas as pl
from jax.experimental.pallas import tpu as pltpu
from jax.sharding import PartitionSpec as P

CHAINS = 16
LANE = 128
F32 = jnp.float32
BF16 = jnp.bfloat16


def ceil_to(value, step):
    return -(-value // step) * step


def call(kernel, name, scalars, arrays, outs, scratch=(), limit=16, in_spaces=None, out_spaces=None, micros=1):
    spec = lambda m: m if isinstance(m, pl.BlockSpec) else pl.BlockSpec(memory_space=m)
    blocked = [m for m in in_spaces or [] if isinstance(m, pl.BlockSpec)]
    steps = micros[1] if blocked else None
    return pl.pallas_call(
        kernel,
        grid=(steps,) if blocked else (),
        in_specs=[spec(pltpu.SMEM)] * len(scalars) + [spec(m) for m in in_spaces or [pltpu.VMEM] * len(arrays)],
        out_specs=[spec(m) for m in out_spaces or [pltpu.VMEM] * len(outs)],
        out_shape=list(outs),
        scratch_shapes=list(scratch),
        compiler_params=pltpu.CompilerParams(vmem_limit_bytes=limit * 1024 * 1024),
        cost_estimate=pl.CostEstimate(
            flops=0, transcendentals=0, bytes_accessed=3000000 * (micros[0] if blocked else micros)
        ),
        name=name,
    )(*scalars, *arrays)


def near(value):
    return pltpu.with_memory_space_constraint(value, pltpu.VMEM)


def stages_of(count):
    stages, bit = [[1]], 2
    while bit < count:
        ways = min(8 if bit == 2 else 4, count // bit)
        stages.append([k * bit for k in range(1, ways)])
        bit *= ways
    return stages


def swap(value, axis, mask):
    count = lax.axis_size(axis)
    return lax.ppermute(value, axis, [(k, k ^ mask) for k in range(count)])


def all_of(value, axes):
    count = lax.axis_size(axes)
    return lax.all_to_all(jnp.broadcast_to(value[None], (count,) + value.shape), axes, 0, 0, tiled=True)


def slot_of(xor_index, count):
    place, size, bit = 0, count, 1
    for masks in stages_of(count):
        ways = len(masks) + 1
        size = size // ways
        place = place + ((xor_index // bit) % ways) * size
        bit = bit * ways
    return place


STEPS = 32766.0
BIAS = 90


def power_of_two(exponent):
    value = jnp.full(exponent.shape, 2.0 ** -BIAS, F32)
    for bit in range(7):
        on = ((exponent + BIAS) // (1 << bit)) % 2 == 1
        value = value * jnp.where(on, 2.0 ** (1 << bit), 1.0)
    return value


def coded_rows(groups):
    return ceil_to(sum(groups) + len(groups), 16)


def encode(value, groups):
    parts, exponents, at = [], [], 0
    for size in groups:
        part = value[at:at + size]
        most = jnp.max(jnp.abs(part), axis=0, keepdims=True)
        exponent = jnp.ceil(jnp.log2(jnp.maximum(most, 2.0 ** (1 - BIAS)))).astype(jnp.int32)
        exponent = jnp.clip(exponent, -BIAS, 127 - BIAS)
        parts.append(jnp.round(part * (STEPS / power_of_two(exponent))).astype(jnp.int32))
        exponents.append(exponent)
        at += size
    fill = coded_rows(groups) - at - len(groups)
    if fill:
        exponents.append(jnp.zeros((fill, value.shape[1]), jnp.int32))
    return jnp.concatenate(parts + exponents, axis=0).astype(jnp.int16)


def decode(code, groups):
    code = code.astype(jnp.int32)
    parts, at, total = [], 0, sum(groups)
    for k, size in enumerate(groups):
        unit = power_of_two(code[total + k:total + k + 1]) * (1.0 / STEPS)
        parts.append(code[at:at + size].astype(F32) * unit)
        at += size
    return jnp.concatenate(parts, axis=0)


def reduce_chunks(keeps, moved, groups, axis):
    stages = stages_of(lax.axis_size(axis))[1:]
    number = len(keeps)
    sizes = [k.shape[1] for k in keeps]
    rows, coded = sum(sizes), coded_rows(groups)
    half = keeps[0].shape[0]
    ways = len(stages[0]) + 1 if stages else 1
    code_shape = lambda size: jax.ShapeDtypeStruct((size, coded, LANE), jnp.int16)

    def first(*refs):
        ins, outs = refs[:2 * number], refs[2 * number:]
        for place in range(half):
            way, slot = place // (half // ways), place % (half // ways)
            parts = [ins[k][place] + ins[number + k][place] for k in range(number)]
            value = jnp.concatenate(parts, axis=0)
            outs[way][slot] = value if way == 0 else encode(value, groups)

    keep, *sends = call(
        first,
        "core_sum",
        [],
        list(keeps) + list(moved),
        [jax.ShapeDtypeStruct((half // ways, rows, LANE), F32)] + [code_shape(half // ways)] * (ways - 1),
        limit=24,
    )
    for k, masks in enumerate(stages):
        got = [swap(part, axis, mask) for part, mask in zip(sends, masks)]
        ways = len(stages[k + 1]) + 1 if k + 1 < len(stages) else 1
        size = keep.shape[0] // ways
        last = k + 1 == len(stages)

        def later(*refs):
            ins, outs = refs[:len(got) + 1], refs[len(got) + 1:]
            for way in range(ways):
                for slot in range(size):
                    value = ins[0][way * size + slot]
                    for ref in ins[1:]:
                        value = value + decode(ref[way * size + slot], groups)
                    outs[way][slot] = value if way == 0 and not last else encode(value, groups)

        kept = code_shape(size) if last else jax.ShapeDtypeStruct((size, rows, LANE), F32)
        keep, *sends = call(
            later, "chip_sum" + str(k), [], [keep] + got, [kept] + [code_shape(size)] * (ways - 1), limit=24
        )
    return keep


def gather_chunks(chunk, axis):
    value = chunk
    stages = stages_of(lax.axis_size(axis))
    for number, masks in enumerate(reversed(stages[1:])):
        parts = [value] + [swap(value, axis, mask) for mask in masks]
        size = value.shape[0]

        def kernel(*refs):
            for k, ref in enumerate(refs[:-1]):
                refs[-1][k * size:(k + 1) * size] = ref[...]

        shape = (size * len(parts),) + value.shape[1:]
        value = call(kernel, "chunk_join" + str(number), [], parts, [jax.ShapeDtypeStruct(shape, value.dtype)])[0]
    return value, swap(value, axis, 1)


def padded(value, rows, lanes, size):
    count = rows.stop - rows.start
    if count == 0:
        return jnp.zeros((size, LANE), F32)
    piece = value[rows, lanes]
    return piece if count == size else jnp.concatenate([piece, jnp.zeros((size - count, LANE), F32)], axis=0)


def store_pairs(keep, send, me, value_of, count, rows):
    first = me % 2 == 0
    for pair in range(count // 2):
        a, b = value_of(2 * pair), value_of(2 * pair + 1)
        slot = slot_of((2 * pair) ^ (me - me % 2), count)
        keep[slot, rows, :] = jnp.where(first, a, b)
        send[slot, rows, :] = jnp.where(first, b, a)


def tile(ref, index, blocks, kind=0, kinds=1):
    return ref.at[pl.ds(pl.multiple_of((index * kinds + kind) * blocks, blocks), blocks), :]


def spread(ref, value, first, blocks, kind=0, kinds=1):
    rows = value.shape[0]
    for b in range(blocks):
        place = pl.ds((first * kinds + kind) * blocks + b, rows, stride=kinds * blocks)
        ref[place, :] = value[:, b * LANE:(b + 1) * LANE]


def gathered(ref, first, rows, blocks, b, kind=0, kinds=1):
    return ref[pl.ds((first * kinds + kind) * blocks + b, rows, stride=kinds * blocks), :]


def stream_order(order, block_of):
    def place(d, carry):
        order[block_of[d]] = d
        return carry

    lax.fori_loop(0, block_of.shape[0], place, 0)
    return block_of[lax.axis_index("ctx")]


def segment_ends(ids, tab, toks, blocks, kinds):
    length = toks // CHAINS

    def step(r, carry):
        prod, total = list(carry[:CHAINS]), list(carry[CHAINS:])
        for s in range(CHAINS):
            at = ids[s * length + r]
            d = tile(tab, at, blocks, 0, kinds)[...]
            total[s] = d * total[s] + tile(tab, at, blocks, 1, kinds)[...]
            prod[s] = prod[s] * d
        return tuple(prod + total)

    first = [jnp.ones((blocks, LANE), F32)] * CHAINS + [jnp.zeros((blocks, LANE), F32)] * CHAINS
    carry = lax.fori_loop(0, length, step, tuple(first), unroll=2)
    return carry[:CHAINS], carry[CHAINS:]


def own_table_kernel(doc_lengths, block_of, ids, embed, w, marked, spots, tab, seg, ends, sem, *, vocab, blocks):
    toks = ids.shape[0]
    copy = pltpu.make_async_copy(ids, marked, sem)
    copy.start()
    gate = [jnp.dot(embed[...], w[g], preferred_element_type=F32) for g in range(3)]
    spread(tab, jax.nn.sigmoid(gate[1] + 3.0), 0, blocks, 0, 2)
    spread(tab, jax.nn.sigmoid(gate[0]) * jnp.tanh(gate[2]), 0, blocks, 1, 2)
    copy.wait()
    start = -block_of[lax.axis_index("ctx")] * toks
    for k in range(doc_lengths.shape[0]):
        inside = (start >= 0) & (start < toks)
        at = jnp.clip(start, 0, toks - 1)
        spot = jnp.where(inside, marked[at], 0)
        spots[k] = spot
        marked[at] = jnp.where(inside, vocab + k, marked[at])
        tile(tab, vocab + k, blocks, 0, 2)[...] = jnp.zeros((blocks, LANE), F32)
        tile(tab, vocab + k, blocks, 1, 2)[...] = tile(tab, spot, blocks, 1, 2)[...]
        start = start + doc_lengths[k]
    prod, total = segment_ends(marked, tab, toks, blocks, 2)
    p_all, s_all = prod[0], total[0]
    for s in range(CHAINS):
        seg[s, 0] = prod[s]
        seg[s, 1] = total[s]
        if s:
            s_all = prod[s] * s_all + total[s]
            p_all = prod[s] * p_all
    ends[0] = p_all
    ends[1] = s_all


def rest_table_kernel(ids, spots, embed, w, *refs, vocab, blocks, others):
    fetched = refs[:2 * others]
    outs = refs[2 * others:]
    o_tab, coef = outs[:2]
    toks = ids.shape[0]
    gate = [jnp.dot(embed[...], w[g], preferred_element_type=F32) for g in (0, 2, 3)]
    in_gate, cand = jax.nn.sigmoid(gate[0]), jnp.tanh(gate[1])
    source = in_gate * cand
    spread(o_tab, jax.nn.sigmoid(gate[2]), 0, blocks)
    spread(coef, source - source * in_gate, 0, blocks, 0, 2)
    spread(coef, in_gate - source * cand, 0, blocks, 1, 2)
    docs = spots.shape[0]
    for k in range(docs):
        tile(o_tab, vocab + k, blocks)[...] = tile(o_tab, spots[k], blocks)[...]
    first = lax.axis_index("ctx") % 2 == 0
    for p in range(others):
        direct, passed = fetched[2 * p:2 * p + 2]
        tab, seg = outs[2 + 2 * p:4 + 2 * p]

        def weights(g):
            mine, theirs = direct[g % 2], passed[g % 2]
            return jnp.where(first, mine, theirs) if g < 2 else jnp.where(first, theirs, mine)

        gate = [jnp.dot(embed[...], weights(g), preferred_element_type=F32) for g in range(4)]
        spread(tab, jax.nn.sigmoid(gate[1] + 3.0), 0, blocks, 0, 3)
        spread(tab, jax.nn.sigmoid(gate[0]) * jnp.tanh(gate[2]), 0, blocks, 1, 3)
        spread(tab, jax.nn.sigmoid(gate[3]), 0, blocks, 2, 3)
        for k in range(docs):
            tile(tab, vocab + k, blocks, 0, 3)[...] = jnp.zeros((blocks, LANE), F32)
            for kind in (1, 2):
                tile(tab, vocab + k, blocks, kind, 3)[...] = tile(tab, spots[k], blocks, kind, 3)[...]
        prod, total = segment_ends(ids, tab, toks, blocks, 3)
        for s in range(CHAINS):
            seg[s, 0] = prod[s]
            seg[s, 1] = total[s]


def cell_kernel(*refs, others, total_tokens, blocks):
    ids, block_of, ps_all, tab_o, o_tab, seg_o, wt_o, bias, tgt, ids_row = refs[:10]
    refs = refs[10:]
    tab_x, seg_x = refs[:others], refs[others:2 * others]
    halves = refs[2 * others:4 * others]
    refs = refs[4 * others:]
    hid, prev_out, src_out, lgrad, heads, head, o_sum, sums = refs[:8]
    order, prev, src, hs, low, low_x, wt_x, logits, pcum, sem, src_sems = refs[8:]
    toks = ids.shape[0]
    length = toks // CHAINS
    width = blocks * LANE
    vocab = wt_o.shape[0]
    own = stream_order(order, block_of)
    shards, mine = lax.axis_size("wa"), lax.axis_index("wa")
    nt = (((1,), (1,)), ((), ()))
    tn = (((0,), (0,)), ((), ()))

    def starts(piece, seg):
        def earlier(b, c):
            slot = order[b] * shards + (mine + piece) % shards
            return ps_all[slot, 0] * c + ps_all[slot, 1]

        c = lax.fori_loop(0, own, earlier, jnp.zeros((blocks, LANE), F32))
        out = []
        for s in range(CHAINS):
            out.append(c)
            c = seg[s, 0] * c + seg[s, 1]
        return tuple(out)

    def flatten(low):
        rows = 256

        def part(k, carry):
            at = pl.multiple_of(k * rows, rows)
            value = hs[pl.ds(at * blocks, rows * blocks), :]
            low[pl.ds(at, rows), :] = value.reshape(rows, width).astype(BF16)
            return carry

        lax.fori_loop(0, toks // rows, part, 0)

    def own_step(r, carry):
        cells, prods = list(carry[:CHAINS]), list(carry[CHAINS:])
        for s in range(CHAINS):
            t = s * length + r
            at = ids[t]
            d = tile(tab_o, at, blocks, 0, 2)[...]
            o = tile(o_tab, at, blocks)[...]
            tile(prev, t, blocks)[...] = cells[s]
            cells[s] = d * cells[s] + tile(tab_o, at, blocks, 1, 2)[...]
            prods[s] = prods[s] * d
            tile(pcum, t, blocks)[...] = prods[s]
            th = jnp.tanh(cells[s])
            h = o * th
            tile(hs, t, blocks)[...] = h
            tile(src, t, blocks)[...] = o - h * th
        return tuple(cells + prods)

    lax.fori_loop(0, length, own_step, starts(0, seg_o) + (jnp.ones((blocks, LANE), F32),) * CHAINS)
    save_prev = pltpu.make_async_copy(prev, prev_out, sem.at[1])
    save_prev.start()
    flatten(low)
    save = pltpu.make_async_copy(low, hid, sem.at[0])
    save.start()
    logits[...] = lax.dot_general(wt_o[...], low[...], nt, preferred_element_type=F32) + bias[...]
    first = lax.axis_index("ctx") % 2 == 0
    half = vocab // 2
    for p in range(others):
        tab = tab_x[p]
        direct, passed = halves[2 * p:2 * p + 2]
        wt_x[0:half, :] = jnp.where(first, direct[...], passed[...])
        wt_x[half:vocab, :] = jnp.where(first, passed[...], direct[...])

        def other_step(r, carry):
            cells = list(carry)
            for s in range(CHAINS):
                t = s * length + r
                at = ids[t]
                cells[s] = tile(tab, at, blocks, 0, 3)[...] * cells[s] + tile(tab, at, blocks, 1, 3)[...]
                tile(hs, t, blocks)[...] = tile(tab, at, blocks, 2, 3)[...] * jnp.tanh(cells[s])
            return tuple(cells)

        lax.fori_loop(0, length, other_step, starts(p + 1, seg_x[p]))
        flatten(low_x)
        logits[...] += lax.dot_general(wt_x[...], low_x[...], nt, preferred_element_type=F32)

    rows = 512

    def save_src(k):
        place = pl.ds(pl.multiple_of(k * rows * blocks, rows * blocks), rows * blocks)
        return pltpu.make_async_copy(src.at[place, :], src_out.at[place, :], src_sems.at[k])

    o_sum[...] = jnp.zeros_like(o_sum)

    def back(k, carry):
        loss, b_grad = carry
        at = pl.multiple_of(k * rows, rows)
        part = logits[:, pl.ds(at, rows)]
        target = lax.broadcasted_iota(jnp.int32, (vocab, rows), 0) == tgt[:, pl.ds(at, rows)]
        top = jnp.max(part, axis=0, keepdims=True)
        power = jnp.exp(part - top)
        norm = jnp.sum(power, axis=0, keepdims=True)
        picked = jnp.sum(jnp.where(target, part, 0.0), axis=0, keepdims=True)
        loss = loss + (top + jnp.log(norm) - picked)
        grad = ((power / norm - jnp.where(target, 1.0, 0.0)) * (1.0 / total_tokens)).astype(BF16)
        lgrad[:, pl.ds(at, rows)] = grad
        b_grad = b_grad + jnp.sum(grad.astype(F32).reshape(vocab, rows // LANE, LANE), axis=1)
        hg = lax.dot_general(grad, wt_o[...], tn, preferred_element_type=F32)
        chars = lax.broadcasted_iota(jnp.int32, (vocab, rows), 0) == ids_row[:, pl.ds(at, rows)]
        moment = (hg * low[pl.ds(at, rows), :].astype(F32)).astype(BF16)
        o_sum[...] += jnp.dot(chars.astype(F32).astype(BF16), moment, preferred_element_type=F32)
        for b in range(blocks):
            hs[pl.ds(at * blocks + b, rows, stride=blocks), :] = hg[:, b * LANE:(b + 1) * LANE]
        for q in range(rows // length):
            place = pl.ds((at + q * length) * blocks, length * blocks)
            grad_src = src[place, :] * hs[place, :]
            src[place, :] = grad_src
            ends = (pcum[place, :] * grad_src).reshape(length, blocks, LANE)
            tile(heads, k * (rows // length) + q, blocks)[...] = jnp.sum(ends, axis=0)
        save_src(k).start()
        return loss, b_grad

    loss, b_grad = lax.fori_loop(
        0, toks // rows, back, (jnp.zeros((1, rows), F32), jnp.zeros((vocab, LANE), F32))
    )
    lane = lax.broadcasted_iota(jnp.int32, (vocab, LANE), 1)
    row = lax.broadcasted_iota(jnp.int32, (vocab, LANE), 0)
    sums[...] = jnp.where(lane == LANE - 1, jnp.sum(b_grad, axis=1, keepdims=True), 0.0) + jnp.where(
        (lane == LANE - 2) & (row == 0), jnp.sum(loss, axis=1, keepdims=True), 0.0
    )
    save.wait()
    save_prev.wait()
    for k in range(toks // rows):
        save_src(k).wait()
    total = tile(heads, CHAINS - 1, blocks)[...]
    for s in range(CHAINS - 2, -1, -1):
        total = tile(heads, s, blocks)[...] + seg_o[s, 0] * total
    head[...] = total


def decoder_grad_kernel(lgrad, hid, keep, send, *, count, blocks):
    grad = jnp.dot(lgrad[...], hid[...], preferred_element_type=F32)
    vocab = grad.shape[0]
    part = keep.shape[1]
    splits = count // blocks

    def piece(q):
        c, e = q // splits, q % splits
        size = max(0, min(part, vocab - e * part))
        return padded(grad, slice(e * part, e * part + size), slice(c * LANE, (c + 1) * LANE), part)

    store_pairs(keep, send, lax.axis_index("ctx"), piece, count, slice(0, part))


def char_sum_kernel(
    ids, block_of, tab, seg, heads, h_all, ps_all, prev, src, sums, order, carry, *refs, copies, blocks
):
    number = pl.program_id(0)
    length = ids.shape[0] // CHAINS
    span = prev.shape[1] // blocks
    sets = [refs[2 * k:2 * k + 2] for k in range(copies)]

    @pl.when(number == 0)
    def _():
        for ref in refs:
            ref[...] = jnp.zeros_like(ref)
        own = stream_order(order, block_of)
        count = block_of.shape[0]
        shards, mine = lax.axis_size("wa"), lax.axis_index("wa")

        def from_later(i, g):
            slot = order[count - 1 - i]
            return h_all[slot] + ps_all[slot * shards + mine, 0] * g

        later = lax.fori_loop(0, count - 1 - own, from_later, jnp.zeros((blocks, LANE), F32))
        for s in range(CHAINS - 1, -1, -1):
            carry[s] = later
            later = tile(heads, s, blocks)[...] + seg[s, 0] * later

    def step(i, later):
        h = list(later)
        r = span - 1 - i
        for s in range(CHAINS):
            at = ids[s * length + (pl.num_programs(0) - 1 - number) * span + r]
            here = pl.ds(pl.multiple_of(r * blocks, blocks), blocks)
            g = src[s, here, :] + h[s]
            h[s] = tile(tab, at, blocks, 0, 2)[...] * g
            cell, forget = sets[s % copies]
            tile(cell, at, blocks)[...] += g
            tile(forget, at, blocks)[...] += g * prev[s, here, :]
        return tuple(h)

    ends = lax.fori_loop(0, span, step, tuple(carry[s] for s in range(CHAINS)))
    for s in range(CHAINS):
        carry[s] = ends[s]

    @pl.when(number == pl.num_programs(0) - 1)
    def _():
        for k in range(2):
            value = refs[k][...]
            for more in sets[1:]:
                value = value + more[k][...]
            sums[k] = value


def input_grad_kernel(
    spots, sums, o_sum, tab, o_tab, coef, w, table, extra, keep, send, keep_e, send_e, merged,
    *, count, part, vocab, blocks,
):
    rows = table.shape[0]
    width = blocks * LANE
    me = lax.axis_index("ctx")
    merged[...] = sums[...]
    for k in range(spots.shape[0]):
        tile(merged.at[0], spots[k], blocks)[...] += tile(merged.at[0], vocab + k, blocks)[...]
    pad = (rows - vocab) * blocks
    for q in range(2):
        merged[q, vocab * blocks:, :] = jnp.zeros((pad, LANE), F32)

    def units(value_of):
        return jnp.concatenate([value_of(b) for b in range(blocks)], axis=1)

    def column(q, b):
        return merged[q, pl.ds(b, rows, stride=blocks), :]

    def square(ref, b, kinds):
        value = gathered(ref, 0, rows, blocks, b, 0, kinds)
        return value - value * value

    parts = [
        units(lambda b: column(0, b) * gathered(coef, 0, rows, blocks, b, 0, 2)),
        units(lambda b: column(1, b) * square(tab, b, 2)),
        units(lambda b: column(0, b) * gathered(coef, 0, rows, blocks, b, 1, 2)),
        o_sum[...] * (1.0 - units(lambda b: gathered(o_tab, 0, rows, blocks, b))),
    ]
    both = (((1,), (1,)), ((), ()))
    tn = (((0,), (0,)), ((), ()))
    splits = count // blocks
    part_e = jnp.zeros((rows, w.shape[1]), F32)
    for gate in range(4):
        total = parts[gate]
        high = total.astype(BF16)
        low = (total - high.astype(F32)).astype(BF16)
        wide = lax.dot_general(table[...], high, tn, preferred_element_type=F32)
        wide = wide + lax.dot_general(table[...], low, tn, preferred_element_type=F32)

        def piece(q):
            c, e = q // splits, q % splits
            size = max(0, min(part, wide.shape[0] - e * part))
            return padded(wide, slice(e * part, e * part + size), slice(c * LANE, (c + 1) * LANE), part)

        store_pairs(keep, send, me, piece, count, slice(gate * part, (gate + 1) * part))
        part_e = part_e + lax.dot_general(high, w[gate], both, preferred_element_type=F32)
        part_e = part_e + lax.dot_general(low, w[gate], both, preferred_element_type=F32)
    per = keep_e.shape[1]
    wide_e = jnp.concatenate([part_e, jnp.zeros((rows, LANE - part_e.shape[1]), F32)], axis=1) + extra[...]
    wide_e = jnp.concatenate([wide_e, jnp.zeros((count * per - rows, LANE), F32)], axis=0)
    store_pairs(keep_e, send_e, me, lambda q: wide_e[q * per:(q + 1) * per, :], count, slice(0, per))


def finish_kernel(
    mine, theirs, w_grad, b_grad, e_grad, out_grad, o_grad, loss, eacc, *, groups, part, per, emb, shards, total_tokens
):
    count = 2 * mine.shape[0]
    me = lax.axis_index("ctx")
    first = me % 2 == 0
    pairs = {}

    def chunk(q, rows):
        pair = q - q % 2
        if pair not in pairs:
            slot = slot_of(pair ^ (me - me % 2), count)
            own, other = mine[slot].astype(jnp.int32), theirs[slot].astype(jnp.int32)
            pairs[pair] = [
                decode(jnp.where(first, own, other), groups), decode(jnp.where(first, other, own), groups)
            ]
        return pairs[pair][q % 2][rows]

    cols = w_grad.shape[2] // LANE
    splits = count // cols
    vpart = groups[-1]
    vocab = out_grad.shape[0]
    for c in range(cols):
        lanes = slice(c * LANE, (c + 1) * LANE)
        for e in range(splits):
            q = c * splits + e
            size = max(0, min(part, emb - e * part))
            for gate in range(4):
                if size:
                    w_grad[gate, e * part:e * part + size, lanes] = chunk(q, slice(gate * part, gate * part + size))
                if e * part <= emb < (e + 1) * part:
                    at = gate * part + emb - e * part
                    b_grad[gate:gate + 1, lanes] = chunk(q, slice(at, at + 1))
            size = max(0, min(vpart, vocab - e * vpart))
            if size:
                at = 4 * part + per
                out_grad[e * vpart:e * vpart + size, lanes] = chunk(q, slice(at, at + size))
    for p in range(count):
        eacc[p * per:(p + 1) * per, :] = chunk(p, slice(4 * part, 4 * part + per))
    e_grad[...] = eacc[0:vocab, 0:emb]
    for k in range(eacc.shape[0] // LANE):
        size = max(0, min(LANE, vocab - k * LANE))
        if size:
            flipped = jnp.transpose(eacc[k * LANE:(k + 1) * LANE, :], (1, 0))
            o_grad[:, k * LANE:k * LANE + size] = flipped[LANE - 1:LANE, 0:size] * (1.0 / shards)
    loss[...] = eacc[0:1, LANE - 2:LANE - 1] * (1.0 / (shards * total_tokens))


def half_of(value, core):
    half = value.shape[0] // 2
    return lax.dynamic_slice_in_dim(value, core * half, half, 0)


def from_others(value, wa):
    return [lax.ppermute(value, "wa", [(k, (k - s) % wa) for k in range(wa)]) for s in range(1, wa)]


def after(value, earlier):
    return lax.optimization_barrier((value, earlier))[0]


def body(ids, targets, doc_lengths, block_of, embed, w_in, b_in, w_out, b_out):
    count = lax.axis_size("ctx")
    wa = lax.axis_size("wa")
    toks = ids.shape[0]
    emb, gates, width = w_in.shape
    blocks = width // LANE
    vocab = embed.shape[0]
    docs = doc_lengths.shape[0]
    vpad = ceil_to(vocab + docs, 32)
    kdim = ceil_to(emb + 3, 16)
    total_tokens = toks * count
    core = lax.axis_index("ctx") % 2

    b_hi = lax.reduce_precision(b_in, 8, 7)
    b_mid = lax.reduce_precision(b_in - b_hi, 8, 7)
    extra_rows = jnp.stack([b_hi, b_mid, b_in - b_hi - b_mid], axis=1).astype(BF16)
    fill = jnp.zeros((gates, kdim - emb - 3, width), BF16)
    w_own = jnp.concatenate([jnp.transpose(w_in, (1, 0, 2)), extra_rows, fill], axis=1)
    ones_col = (jnp.arange(kdim) >= emb) & (jnp.arange(kdim) < emb + 3)
    ones_row = jnp.arange(vpad) < vocab
    table = jnp.pad(embed, ((0, vpad - vocab), (0, kdim - emb)))
    table = jnp.where(ones_col[None, :] & ones_row[:, None], jnp.ones((), BF16), table)

    chip = lambda *shape: pltpu.VMEM(shape, F32)
    hbm = lambda shape, kind: jax.ShapeDtypeStruct(shape, kind)
    smem = lambda shape: jax.ShapeDtypeStruct(shape, jnp.int32)
    tokens = (toks * blocks, LANE)

    marked, spots, tab, seg, ends = call(
        functools.partial(own_table_kernel, vocab=vocab, blocks=blocks),
        "tables_own",
        [doc_lengths, block_of],
        [ids, table, w_own],
        [smem((toks,)), smem((docs,)), chip(vpad * 2 * blocks, LANE), chip(CHAINS, 2, blocks, LANE),
         hbm((2, blocks, LANE), F32)],
        [pltpu.SemaphoreType.DMA],
        in_spaces=[pl.ANY, pltpu.VMEM, pltpu.VMEM],
        out_spaces=[pltpu.SMEM, pltpu.SMEM, pltpu.VMEM, pltpu.VMEM, pltpu.VMEM],
    )
    tab, seg = near(tab), near(seg)
    w_far = from_others(half_of(after(w_own, ends), core), wa)
    ps_all = all_of(ends, ("ctx", "wa"))
    w_far = [after(w, ps_all) for w in w_far]
    w_oth = [v for w in w_far for v in (w, swap(w, "ctx", 1))]
    wt_own = jnp.pad(after(w_out, ps_all).T, ((0, vpad - vocab), (0, 0)))
    wt_far = from_others(half_of(wt_own, core), wa)
    wt_oth = [v for w in wt_far for v in (w, swap(w, "ctx", 1))]
    bias_out = jnp.pad(b_out, (0, vpad - vocab), constant_values=-1e30)[:, None]
    others = wa - 1
    rest = call(
        functools.partial(rest_table_kernel, vocab=vocab, blocks=blocks, others=others),
        "tables_rest",
        [marked, spots],
        [table, w_own] + w_oth,
        [chip(vpad * blocks, LANE), chip(vpad * 2 * blocks, LANE)]
        + [chip(vpad * 3 * blocks, LANE), chip(CHAINS, 2, blocks, LANE)] * others,
        micros=6,
    )
    rest = [near(r) for r in rest]
    o_tab, coef = rest[:2]

    hid, prev, src, lgrad, heads, head, o_sum, extra = call(
        functools.partial(cell_kernel, others=others, total_tokens=total_tokens, blocks=blocks),
        "cells",
        [marked, block_of],
        [ps_all, tab, o_tab, seg, wt_own, bias_out, targets[None], ids[None]] + rest[2::2] + rest[3::2] + wt_oth,
        [
            hbm((toks, width), BF16), hbm(tokens, F32), hbm(tokens, F32),
            pltpu.VMEM((vpad, toks), BF16), chip(CHAINS * blocks, LANE), hbm((blocks, LANE), F32),
            chip(vpad, width), hbm((vpad, LANE), F32),
        ],
        [
            pltpu.SMEM((count,), jnp.int32), pltpu.VMEM(tokens, F32), pltpu.VMEM(tokens, F32),
            pltpu.VMEM(tokens, F32), pltpu.VMEM((toks, width), BF16),
            pltpu.VMEM((toks, width), BF16), pltpu.VMEM((vpad, width), BF16), pltpu.VMEM((vpad, toks), F32), pltpu.VMEM(tokens, F32),
            pltpu.SemaphoreType.DMA((2,)), pltpu.SemaphoreType.DMA((toks // 512,)),
        ],
        limit=48,
        out_spaces=[pl.ANY] * 3 + [pltpu.VMEM] * 5,
        micros=26,
    )
    lgrad, heads, o_sum = map(near, (lgrad, heads, o_sum))
    splits = count // blocks
    vpart = ceil_to(-(-vpad // splits), 8)
    half_chunks = lambda rows: [hbm((count // 2, rows, LANE), F32)] * 2
    copies = 4

    part = ceil_to(-(-kdim // splits), 8)
    per = ceil_to(-(-vpad // count), 8)
    h_all = all_of(head, "ctx")
    keep_o, send_o = call(
        functools.partial(decoder_grad_kernel, count=count, blocks=blocks),
        "decoder_grad",
        [],
        [lgrad, after(hid, h_all)],
        half_chunks(vpart),
        limit=20,
    )
    got_o = swap(send_o, "ctx", 1)
    length = toks // CHAINS
    span = 16
    block = pl.BlockSpec((CHAINS, span * blocks, LANE), lambda i: (0, length // span - 1 - i, 0))
    (sums,) = call(
        functools.partial(char_sum_kernel, copies=copies, blocks=blocks),
        "char_sums",
        [marked, block_of],
        [tab, seg, heads, h_all, ps_all] + [v.reshape(CHAINS, length * blocks, LANE) for v in (prev, src)],
        [chip(2, vpad * blocks, LANE)],
        [pltpu.SMEM((count,), jnp.int32), pltpu.VMEM((CHAINS, blocks, LANE), F32)]
        + [pltpu.VMEM((vpad * blocks, LANE), F32)] * (2 * copies),
        limit=24,
        in_spaces=[pltpu.VMEM] * 5 + [block] * 2,
        micros=(9, length // span),
    )
    keep, send, keep_e, send_e = call(
        functools.partial(input_grad_kernel, count=count, part=part, vocab=vocab, blocks=blocks),
        "input_grad",
        [spots],
        [near(sums), o_sum, tab, o_tab, coef, w_own, table, extra],
        half_chunks(4 * part) + half_chunks(per),
        [pltpu.VMEM((2, vpad * blocks, LANE), F32)],
        limit=24,
        micros=5,
    )
    bit = 1
    while bit < wa:
        keep_e, send_e = keep_e + swap(keep_e, "wa", bit), send_e + swap(send_e, "wa", bit)
        bit *= 2
    groups = [part] * gates + [per, vpart]
    chunk = reduce_chunks(
        [keep, keep_e, keep_o], [swap(send, "ctx", 1), swap(send_e, "ctx", 1), got_o], groups, "ctx"
    )
    mine, theirs = gather_chunks(chunk, "ctx")
    w_grad, bi_grad, e_grad, w_out_grad, bo_grad, loss = call(
        functools.partial(finish_kernel, groups=groups, part=part, per=per, emb=emb, shards=wa, total_tokens=total_tokens),
        "finish",
        [],
        [mine, theirs],
        [
            hbm((gates, emb, width), F32), hbm((gates, width), F32), hbm((vocab, emb), F32),
            hbm((vocab, width), F32), hbm((1, vocab), F32), hbm((1, 1), F32),
        ],
        [pltpu.VMEM((ceil_to(count * per, LANE), LANE), F32)],
    )
    return (
        hid,
        loss[0, 0],
        e_grad,
        jnp.transpose(w_grad, (1, 0, 2)),
        bi_grad,
        w_out_grad.T,
        bo_grad[0],
    )


def solution(mesh):
    placed = (
        P("ctx"),
        P("ctx"),
        P(),
        P(),
        P(),
        P(None, None, "wa"),
        P(None, "wa"),
        P("wa", None),
        P(),
    )
    return jax.shard_map(
        body,
        mesh=mesh,
        in_specs=placed,
        out_specs=(
            P("ctx", "wa"),
            P(),
            P(),
            P(None, None, "wa"),
            P(None, "wa"),
            P("wa", None),
            P(),
        ),
        check_vma=False,
    )
```

time: 1150 us -> 176 us (0.15)
  other arithmetic: 463 us -> 2.36 us
  local copies, waits for them, and re-layouts: 247 us -> 20.9 us
  waiting for transfers between devices: 233 us -> 38.6 us
  blocking collectives: 120 us -> 12 us
  Pallas kernels: 0 us -> 57.9 us
  matrix products: 56 us -> 0 us
  starting transfers between devices: 0.37 us -> 42 us
  between operations: 18.3 us -> 1.02 us
    add x28 -> x2, other arithmetic: 377 us -> 0.03 us  [the longest x1 0.01 us: body(): keep_e + swap(keep_e, 'wa', bit)]
    slice x46 -> x0, local copies, waits for them, and re-layouts: 222 us -> none  [the longest x15 83.9 us: doubling_scan(): moved_s = jnp.concatenate([sums[stride:], zeros], axis=0)]
    psum x2 -> x0, waiting for transfers between devices: 147 us -> none  [the longest x1 122 us: body(): grad_embed = lax.psum(embed_local, ('ctx', 'wa'))]
    all_gather x2 -> x0, waiting for transfers between devices: 85.5 us -> none  [the longest x1 85.5 us: body(): lax.all_gather(hidden_low, 'wa', axis=1, tiled=True)]
    all_gather x3 -> x0, blocking collectives: 62.1 us -> none  [the longest x1 23 us: body(): lax.all_gather(sums[-1:], 'ctx', axis=0, tiled=True)]
    psum x1 -> x0, blocking collectives: 58.3 us -> none  [body(): lax.psum((grad_w_in, grad_b_in, grad_w_out, grad_b_out, loss_local), 'ctx')]
    pallas_call x0 -> x10, Pallas kernels: none -> 57.9 us  [call(): pl.pallas_call(kernel, grid=(steps,) if blocked else (), in_specs=[spec(p...]
    dot_general x13 -> x0, matrix products: 56 us -> none  [the longest x1 14.3 us: body(): jnp.einsum('te,egh->tgh', feats, w_in, preferred_element_type=jnp.float32)]
  transfers between devices with their start and end apart: 4 -> 25, of which waited for: 3 -> 12; matrix products, arithmetic and copies ran while one was open for 33% -> 3% of each run, Pallas kernels for 0% -> 4%
where the time goes in v2:
time: 176 us; the launch traced here: 175 us
  Pallas kernels  57.9 us (33%)
  starting transfers between devices  42 us (24%)
  waiting for transfers between devices  38.6 us (22%)
  local copies, waits for them, and re-layouts  20.9 us (12%)
  blocking collectives  12 us (7%)
  other arithmetic  2.36 us (1%)
    pallas_call x10, Pallas kernels, call(): pl.pallas_call(kernel, grid=(steps,) if blocked else (), in_specs=[spec(p...  57.9 us
    ppermute x22, starting transfers between devices, swap(): return lax.ppermute(value, axis, [(k, k ^ mask) for k in range(count)])  32 us
    ppermute x22, waiting for transfers between devices, swap(): return lax.ppermute(value, axis, [(k, k ^ mask) for k in range(count)])  21.1 us
    unnamed x46, local copies, waits for them, and re-layouts  14.1 us
    all_to_all x1, blocking collectives, all_of(): lax.all_to_all(jnp.broadcast_to(value[None], (count,) + value.shape), axe...  12 us
    ppermute x2, waiting for transfers between devices, from_others(): lax.ppermute(value, 'wa', [(k, (k - s) % wa) for k in range(wa)])  9.39 us
    all_to_all x1, waiting for transfers between devices, all_of(): lax.all_to_all(jnp.broadcast_to(value[None], (count,) + value.shape), axe...  8.11 us
    all_to_all x1, starting transfers between devices, all_of(): lax.all_to_all(jnp.broadcast_to(value[None], (count,) + value.shape), axe...  7.3 us
  transfers between devices with their start and end apart: 25, of which 12 were waited for; matrix products, arithmetic and copies ran while one was open for 3% of the time, Pallas kernels for 4%

profile of v2, /device:TPU:0, one launch (start us, length us, event | category | flops | bytes accessed | tf_op | source)
XLA Modules:
  0.0 174.8 jit_solution(9867523705123727276)
XLA Ops:
  4.7 4.9 %tables_own.1 = (s32[2048]{0:T(1024)S(1)}, s32[4]{0:T(128)S(1)}, f32[4608,128]{1,0:T(8,128)S(1)}, f32[16,2,8,128]{3,2,1,0:T(8,128)S(1)}, f32[2,8,128]{2,1,0:T(8,128)S(1)}) custom-call(s32[4]{0:T(128)S(1)} %copy-done.18, s32[16]{0:T(128)S(1)} %copy-done.14, s32[2048]{0:T(1024)S(1)} %copy-done.13, bf16[288,112]{1,0:T(8,128)(2,1)S(1)} %and_select_fusion.embed.table, ...), custom_call_target="tpu_custom_call" | custom-call | bytes 3000000 | tf_op jit(solution)/shard_map/tables_own/pallas_call | solution.py:24
  11.5 7.3 %all-to-all-start = ((f32[32,2,8,128]{3,2,1,0:T(8,128)}), f32[32,2,8,128]{3,2,1,0:T(8,128)S(1)}, u32[]{:S(2)}, u32[]{:S(2)}) async-start(f32[32,2,8,128]{3,2,1,0:T(8,128)} %broadcast_in_dim.32), calls=%async_computation | async-start | bytes 524288 | tf_op jit(solution)/shard_map/all_to_all | solution.py:59
  19.6 1.8 %collective-permute-start = (bf16[2,112,1024]{2,1,0:T(8,128)(2,1)}, bf16[2,112,1024]{2,1,0:T(8,128)(2,1)}, u32[]{:S(2)}, u32[]{:S(2)}) collective-permute-start(bf16[2,112,1024]{2,1,0:T(8,128)(2,1)} %constant_dynamic-slice_fusion.1), channel_id=1, source_target_pairs={{0,1},{1,0},{2,3},{3,2},{4,5},{5,4},{6,7},{7,6},{8,9},{9,8},{10,11... | collective-permute-start | bytes 1376264 | tf_op jit(solution)/shard_map/ppermute | solution.py:615
  21.4 8.1 %all-to-all-done.refs_2_.ps_all = f32[32,2,8,128]{3,2,1,0:T(8,128)S(1)} async-done(((f32[32,2,8,128]{3,2,1,0:T(8,128)}), f32[32,2,8,128]{3,2,1,0:T(8,128)S(1)}, u32[]{:S(2)}, u32[]{:S(2)}) %all-to-all-start) | async-done | bytes 262176 | tf_op jit(solution)/shard_map/all_to_all | solution.py:59
  31.5 3.5 %collective-permute-done.refs_0_ = bf16[2,112,1024]{2,1,0:T(8,128)(2,1)} collective-permute-done((bf16[2,112,1024]{2,1,0:T(8,128)(2,1)}, bf16[2,112,1024]{2,1,0:T(8,128)(2,1)}, u32[]{:S(2)}, u32[]{:S(2)}) %collective-permute-start) | collective-permute-done | bytes 458784 | tf_op jit(solution)/shard_map/ppermute | solution.py:615
  35.0 5.9 %collective-permute-done.2.refs_12_ = bf16[144,1024]{1,0:T(8,128)(2,1)S(1)} collective-permute-done((bf16[144,1024]{1,0:T(8,128)(2,1)S(1)}, bf16[144,1024]{1,0:T(8,128)(2,1)S(1)}, u32[]{:S(2)}, u32[]{:S(2)}) %collective-permute-start.2) | collective-permute-done | bytes 294944 | tf_op jit(solution)/shard_map/ppermute | solution.py:615
  41.7 1.9 %pad.13.refs_6_ = bf16[288,1024]{1,0:T(8,128)(2,1)} pad(bf16[275,1024]{1,0:T(8,128)(2,1)} %bitcast.23, bf16[]{:T(256)} %constant.13.clone.1), padding=0_13x0_0 | pad | bytes 1153026 | tf_op jit(solution)/shard_map/jit(_pad)/pad | solution.py:666
  44.5 5.9 %tables_rest.1 = (f32[2304,128]{1,0:T(8,128)S(1)}, f32[4608,128]{1,0:T(8,128)S(1)}, f32[6912,128]{1,0:T(8,128)S(1)}, f32[16,2,8,128]{3,2,1,0:T(8,128)S(1)}) custom-call(s32[2048]{0:T(1024)S(1)} %get-tuple-element.48.ids.refs_0_, s32[4]{0:T(128)S(1)} %copy-done.17, bf16[288,112]{1,0:T(8,128)(2,1)S(1)} %copy-done.6, bf16[4,112,1024]{2,1,0:T(8,128)(2,1)S(1)} %concatenate.4.w, ...), custom_call_target="tpu_custom_call" | custom-call | bytes 18000000 | tf_op jit(solution)/shard_map/tables_rest/pallas_call | solution.py:24
  51.2 28.2 %cells.1 = (bf16[2048,1024]{1,0:T(8,128)(2,1)}, f32[16384,128]{1,0:T(8,128)}, f32[16384,128]{1,0:T(8,128)}, bf16[288,2048]{1,0:T(8,128)(2,1)S(1)}, f32[128,128]{...) custom-call(s32[2048]{0:T(1024)} %copy-done.11, s32[16]{0:T(128)} %block_of.3, ...), custom_call_target="tpu_custom_call" | custom-call | bytes 78000000 | tf_op jit(solution)/shard_map/cells/pallas_call | solution.py:24
  80.1 12.0 %all_to_all.10.h_all = f32[16,8,128]{2,1,0:T(8,128)S(1)} all-to-all(f32[16,8,128]{2,1,0:T(8,128)S(1)} %broadcast_in_dim.36), channel_id=1, replica_groups=mesh['ctx'=16,'wa'=2] {'ctx'}, dimensions={0} | all-to-all | bytes 131072 | tf_op jit(solution)/shard_map/all_to_all | solution.py:59
  92.1 3.4 %copy-done = f32[16384,128]{1,0:T(8,128)S(1)} copy-done((f32[16384,128]{1,0:T(8,128)S(1)}, f32[16384,128]{1,0:T(8,128)}, u32[]{:S(2)}) %copy-start) | copy-done | bytes 8388632
  95.5 3.4 %copy-done.1 = f32[16384,128]{1,0:T(8,128)S(1)} copy-done((f32[16384,128]{1,0:T(8,128)S(1)}, f32[16384,128]{1,0:T(8,128)}, u32[]{:S(2)}) %copy-start.1) | copy-done | bytes 8388632
  99.8 9.2 %char_sums.1.sums = f32[2,2304,128]{2,1,0:T(8,128)S(1)} custom-call(s32[2048]{0:T(1024)S(1)} %copy-done.12, s32[16]{0:T(128)S(1)} %copy-done.15, f32[4608,128]{1,0:T(8,128)S(1)} %get-tuple-element.50.refs_3_.tab, f32[16,2,8,128]{3,2,1,0:T(8,128)S(1)} %copy-done.9, f32[128,128]{1,0:T(8,128)S(1)} %get-tuple-element.60.heads, ...), custom_call_target="tpu_custom_call" | custom-call | bytes 27000000 | tf_op jit(solution)/shard_map/char_sums/pallas_call | solution.py:24
  109.1 4.2 %input_grad.1 = (f32[8,224,128]{2,1,0:T(8,128)S(1)}, f32[8,224,128]{2,1,0:T(8,128)S(1)}, f32[8,24,128]{2,1,0:T(8,128)S(1)}, f32[8,24,128]{2,1,0:T(8,128)S(1)}) custom-call(s32[4]{0:T(128)S(1)} %copy-done.17, f32[2,2304,128]{2,1,0:T(8,128)S(1)} %char_sums.1.sums, f32[288,1024]{1,0:T(8,128)S(1)} %get-tuple-element.64.o_sum, ...), custom_call_target="tpu_custom_call" | custom-call | bytes 15000000 | tf_op jit(solution)/shard_map/input_grad/pallas_call | solution.py:24
  113.4 1.4 decoder_grad.1
  117.4 3.6 %collective-permute-done.6 = f32[8,24,128]{2,1,0:T(8,128)S(1)} collective-permute-done((f32[8,24,128]{2,1,0:T(8,128)S(1)}, f32[8,24,128]{2,1,0:T(8,128)S(1)}, u32[]{:S(2)}, u32[]{:S(2)}) %collective-permute-start.6) | collective-permute-done | bytes 98336 | tf_op jit(solution)/shard_map/ppermute | solution.py:54
  124.7 2.6 %collective-permute-start.11 = (s16[1,400,128]{2,1,0:T(8,128)(2,1)S(1)}, s16[1,400,128]{2,1,0:T(8,128)(2,1)S(1)}, u32[]{:S(2)}, u32[]{:S(2)}) collective-permute-start(s16[1,400,128]{2,1,0:T(8,128)(2,1)S(1)} %get-tuple-element.78), channel_id=1, source_target_pairs={{0,12},{2,14},{4,8},{6,10},{8,4},{10,6},{12,0},{14,2},{16,28},{18,... | collective-permute-start | bytes 307208 | tf_op jit(solution)/shard_map/ppermute | solution.py:54
  127.6 2.3 %collective-permute-start.13 = (s16[1,400,128]{2,1,0:T(8,128)(2,1)S(1)}, s16[1,400,128]{2,1,0:T(8,128)(2,1)S(1)}, u32[]{:S(2)}, u32[]{:S(2)}) collective-permute-start(s16[1,400,128]{2,1,0:T(8,128)(2,1)S(1)} %get-tuple-element.80), channel_id=1, source_target_pairs={{0,20},{2,22},{4,16},{6,18},{8,28},{10,30},{12,24},{14,26},{16,4},... | collective-permute-start | bytes 307208 | tf_op jit(solution)/shard_map/ppermute | solution.py:54
  130.9 4.1 %collective-permute-start.15 = (s16[1,400,128]{2,1,0:T(8,128)(2,1)S(1)}, s16[1,400,128]{2,1,0:T(8,128)(2,1)S(1)}, u32[]{:S(2)}, u32[]{:S(2)}) collective-permute-start(s16[1,400,128]{2,1,0:T(8,128)(2,1)S(1)} %get-tuple-element.82), channel_id=1, source_target_pairs={{0,28},{2,30},{4,24},{6,26},{8,20},{10,22},{12,16},{14,18},{16,12}... | collective-permute-start | bytes 307208 | tf_op jit(solution)/shard_map/ppermute | solution.py:54
  135.0 7.0 %collective-permute-done.12.refs_4_ = s16[1,400,128]{2,1,0:T(8,128)(2,1)S(1)} collective-permute-done((s16[1,400,128]{2,1,0:T(8,128)(2,1)S(1)}, s16[1,400,128]{2,1,0:T(8,128)(2,1)S(1)}, u32[]{:S(2)}, u32[]{:S(2)}) %collective-permute-start.12) | collective-permute-done | bytes 102432 | tf_op jit(solution)/shard_map/ppermute | solution.py:54
  142.0 2.3 %collective-permute-done.13.refs_5_ = s16[1,400,128]{2,1,0:T(8,128)(2,1)S(1)} collective-permute-done((s16[1,400,128]{2,1,0:T(8,128)(2,1)S(1)}, s16[1,400,128]{2,1,0:T(8,128)(2,1)S(1)}, u32[]{:S(2)}, u32[]{:S(2)}) %collective-permute-start.13) | collective-permute-done | bytes 102432 | tf_op jit(solution)/shard_map/ppermute | solution.py:54
  144.9 2.0 %collective-permute-start.22 = (s16[1,400,128]{2,1,0:T(8,128)(2,1)S(1)}, s16[1,400,128]{2,1,0:T(8,128)(2,1)S(1)}, u32[]{:S(2)}, u32[]{:S(2)}) collective-permute-start(s16[1,400,128]{2,1,0:T(8,128)(2,1)S(1)} %chip_sum0.1.refs_0_), channel_id=1, source_target_pairs={{0,28},{2,30},{4,24},{6,26},{8,20},{10,22},{12,16},{14,18},{16,12}... | collective-permute-start | bytes 307208 | tf_op jit(solution)/shard_map/ppermute | solution.py:54
  146.9 2.7 %collective-permute-start.21 = (s16[1,400,128]{2,1,0:T(8,128)(2,1)S(1)}, s16[1,400,128]{2,1,0:T(8,128)(2,1)S(1)}, u32[]{:S(2)}, u32[]{:S(2)}) collective-permute-start(s16[1,400,128]{2,1,0:T(8,128)(2,1)S(1)} %chip_sum0.1.refs_0_), channel_id=1, source_target_pairs={{0,24},{2,26},{4,28},{6,30},{8,16},{10,18},{12,20},{14,22},{16,8},... | collective-permute-start | bytes 307208 | tf_op jit(solution)/shard_map/ppermute | solution.py:54
  149.6 2.0 %collective-permute-start.20 = (s16[1,400,128]{2,1,0:T(8,128)(2,1)S(1)}, s16[1,400,128]{2,1,0:T(8,128)(2,1)S(1)}, u32[]{:S(2)}, u32[]{:S(2)}) collective-permute-start(s16[1,400,128]{2,1,0:T(8,128)(2,1)S(1)} %chip_sum0.1.refs_0_), channel_id=1, source_target_pairs={{0,20},{2,22},{4,16},{6,18},{8,28},{10,30},{12,24},{14,26},{16,4},... | collective-permute-start | bytes 307208 | tf_op jit(solution)/shard_map/ppermute | solution.py:54
  152.6 3.1 %collective-permute-start.18 = (s16[1,400,128]{2,1,0:T(8,128)(2,1)S(1)}, s16[1,400,128]{2,1,0:T(8,128)(2,1)S(1)}, u32[]{:S(2)}, u32[]{:S(2)}) collective-permute-start(s16[1,400,128]{2,1,0:T(8,128)(2,1)S(1)} %chip_sum0.1.refs_0_), channel_id=1, source_target_pairs={{0,12},{2,14},{4,8},{6,10},{8,4},{10,6},{12,0},{14,2},{16,28},{18,... | collective-permute-start | bytes 307208 | tf_op jit(solution)/shard_map/ppermute | solution.py:54
  155.6 5.2 %collective-permute-start.17 = (s16[1,400,128]{2,1,0:T(8,128)(2,1)S(1)}, s16[1,400,128]{2,1,0:T(8,128)(2,1)S(1)}, u32[]{:S(2)}, u32[]{:S(2)}) collective-permute-start(s16[1,400,128]{2,1,0:T(8,128)(2,1)S(1)} %chip_sum0.1.refs_0_), channel_id=1, source_target_pairs={{0,8},{2,10},{4,12},{6,14},{8,0},{10,2},{12,4},{14,6},{16,24},{18,... | collective-permute-start | bytes 307208 | tf_op jit(solution)/shard_map/ppermute | solution.py:54
  160.9 2.0 %collective-permute-start.16 = (s16[1,400,128]{2,1,0:T(8,128)(2,1)S(1)}, s16[1,400,128]{2,1,0:T(8,128)(2,1)S(1)}, u32[]{:S(2)}, u32[]{:S(2)}) collective-permute-start(s16[1,400,128]{2,1,0:T(8,128)(2,1)S(1)} %chip_sum0.1.refs_0_), channel_id=1, source_target_pairs={{0,4},{2,6},{4,0},{6,2},{8,12},{10,14},{12,8},{14,10},{16,20},{18,... | collective-permute-start | bytes 307208 | tf_op jit(solution)/shard_map/ppermute | solution.py:54
  162.9 1.7 collective-permute-done.20.refs_5_
  164.6 1.9 %collective-permute-done.19.refs_4_ = s16[1,400,128]{2,1,0:T(8,128)(2,1)S(1)} collective-permute-done((s16[1,400,128]{2,1,0:T(8,128)(2,1)S(1)}, s16[1,400,128]{2,1,0:T(8,128)(2,1)S(1)}, u32[]{:S(2)}, u32[]{:S(2)}) %collective-permute-start.19) | collective-permute-done | bytes 102432 | tf_op jit(solution)/shard_map/ppermute | solution.py:54
  167.6 2.3 %collective-permute-done.23.theirs = s16[8,400,128]{2,1,0:T(8,128)(2,1)S(1)} collective-permute-done((s16[8,400,128]{2,1,0:T(8,128)(2,1)S(1)}, s16[8,400,128]{2,1,0:T(8,128)(2,1)S(1)}, u32[]{:S(2)}, u32[]{:S(2)}) %collective-permute-start.23) | collective-permute-done | bytes 819232 | tf_op jit(solution)/shard_map/ppermute | solution.py:54
  170.0 2.1 %finish.1 = (f32[4,100,1024]{2,1,0:T(8,128)S(1)}, f32[4,1024]{1,0:T(4,128)}, f32[275,100]{1,0:T(8,128)}, f32[275,1024]{1,0:T(8,128)}, f32[1,275]{1,0:T(1,128)S(1)}, /*index=5*/f32[1,1]{1,0:T(1,128)}) custom-call(s16[8,400,128]{2,1,0:T(8,128)(2,1)S(1)} %chunk_join0.1.mine, s16[8,400,128]{2,1,0:T(8,128)(2,1)S(1)} %collective-permute-done.23.theirs), custom_call_target="tpu_custom_call" | custom-call | bytes 3000000 | tf_op jit(solution)/shard_map/finish/pallas_call | solution.py:24
  172.0 2.2 %copy.35 = f32[100,4,1024]{2,1,0:T(4,128)} copy(f32[100,4,1024]{2,0,1:T(8,128)S(1)} %bitcast.19) | data formatting | bytes 3276800
  (94 shorter events, 23.5 us)
Async XLA Ops:
  3.9 37.0 %copy-start.21 = (f32[275]{0:T(512)S(1)}, f32[275]{0:T(512)}, u32[]{:S(2)}) copy-start(f32[275]{0:T(512)} %param.17) | copy-start | bytes 3304
  10.8 39.6 %copy-start.11 = (s32[2048]{0:T(1024)}, s32[2048]{0:T(1024)S(1)}, u32[]{:S(2)}) copy-start(s32[2048]{0:T(1024)S(1)} %get-tuple-element.48.ids.refs_0_) | copy-start | bytes 24580
  10.8 32.9 %copy-start.17 = (s32[4]{0:T(128)S(1)}, s32[4]{0:T(128)}, u32[]{:S(2)}) copy-start(s32[4]{0:T(128)} %copy-done.16) | copy-start | bytes 52
  11.5 18.0 %all-to-all-start = ((f32[32,2,8,128]{3,2,1,0:T(8,128)}), f32[32,2,8,128]{3,2,1,0:T(8,128)S(1)}, u32[]{:S(2)}, u32[]{:S(2)}) async-start(f32[32,2,8,128]{3,2,1,0:T(8,128)} %broadcast_in_dim.32), calls=%async_computation | async-start | bytes 524288 | tf_op jit(solution)/shard_map/all_to_all | solution.py:59
  19.6 15.4 %collective-permute-start = (bf16[2,112,1024]{2,1,0:T(8,128)(2,1)}, bf16[2,112,1024]{2,1,0:T(8,128)(2,1)}, u32[]{:S(2)}, u32[]{:S(2)}) collective-permute-start(bf16[2,112,1024]{2,1,0:T(8,128)(2,1)} %constant_dynamic-slice_fusion.1), channel_id=1, source_target_pairs={{0,1},{1,0},{2,3},{3,2},{4,5},{5,4},{6,7},{7,6},{8,9},{9,8},{10,11... | collective-permute-start | bytes 1376264 | tf_op jit(solution)/shard_map/ppermute | solution.py:615
  29.5 20.9 %copy-start.3 = (f32[32,2,8,128]{3,2,1,0:T(8,128)}, f32[32,2,8,128]{3,2,1,0:T(8,128)S(1)}, u32[]{:S(2)}) copy-start(f32[32,2,8,128]{3,2,1,0:T(8,128)S(1)} %all-to-all-done.refs_2_.ps_all) | copy-start | bytes 786436
  29.5 21.6 %copy-start.9 = (f32[16,2,8,128]{3,2,1,0:T(8,128)S(1)}, f32[16,2,8,128]{3,2,1,0:T(8,128)}, u32[]{:S(2)}) copy-start(f32[16,2,8,128]{3,2,1,0:T(8,128)} %copy-done.8) | copy-start | bytes 393220
  30.7 10.3 %collective-permute-start.2 = (bf16[144,1024]{1,0:T(8,128)(2,1)S(1)}, bf16[144,1024]{1,0:T(8,128)(2,1)S(1)}, u32[]{:S(2)}, u32[]{:S(2)}) collective-permute-start(bf16[144,1024]{1,0:T(8,128)(2,1)S(1)} %constant_dynamic-slice_fusion), channel_id=1, source_target_pairs={{0,1},{1,0},{2,3},{3,2},{4,5},{5,4},{6,7},{7,6},{8,9},{9,8},{10,11... | collective-permute-start | bytes 884744 | tf_op jit(solution)/shard_map/ppermute | solution.py:615
  35.0 8.6 %collective-permute-start.1 = (bf16[2,112,1024]{2,1,0:T(8,128)(2,1)}, bf16[2,112,1024]{2,1,0:T(8,128)(2,1)S(1)}, u32[]{:S(2)}, u32[]{:S(2)}) collective-permute-start(bf16[2,112,1024]{2,1,0:T(8,128)(2,1)} %collective-permute-done.refs_0_), channel_id=1, source_target_pairs={{0,2},{2,0},{4,6},{6,4},{8,10},{10,8},{12,14},{14,12},{16,18},{18,... | collective-permute-start | bytes 1376264 | tf_op jit(solution)/shard_map/ppermute | solution.py:54
  40.9 9.5 %collective-permute-start.3 = (bf16[144,1024]{1,0:T(8,128)(2,1)S(1)}, bf16[144,1024]{1,0:T(8,128)(2,1)S(1)}, u32[]{:S(2)}, u32[]{:S(2)}) collective-permute-start(bf16[144,1024]{1,0:T(8,128)(2,1)S(1)} %collective-permute-done.2.refs_12_), channel_id=1, source_target_pairs={{0,2},{2,0},{4,6},{6,4},{8,10},{10,8},{12,14},{14,12},{16,18},{18,... | collective-permute-start | bytes 884744 | tf_op jit(solution)/shard_map/ppermute | solution.py:54
  51.2 41.0 %copy-start.12 = (s32[2048]{0:T(1024)S(1)}, s32[2048]{0:T(1024)}, u32[]{:S(2)}) copy-start(s32[2048]{0:T(1024)} %copy-done.11) | copy-start | bytes 24580
  51.2 41.0 %copy-start.15 = (s32[16]{0:T(128)S(1)}, s32[16]{0:T(128)}, u32[]{:S(2)}) copy-start(s32[16]{0:T(128)} %block_of.3) | copy-start | bytes 196
  113.3 9.1 %collective-permute-start.5 = (f32[8,224,128]{2,1,0:T(8,128)S(1)}, f32[8,224,128]{2,1,0:T(8,128)S(1)}, u32[]{:S(2)}, u32[]{:S(2)}) collective-permute-start(f32[8,224,128]{2,1,0:T(8,128)S(1)} %get-tuple-element.72), channel_id=1, source_target_pairs={{0,2},{2,0},{4,6},{6,4},{8,10},{10,8},{12,14},{14,12},{16,18},{18,... | collective-permute-start | bytes 2752520 | tf_op jit(solution)/shard_map/ppermute | solution.py:54
  114.8 7.6 %collective-permute-start.8 = (f32[8,144,128]{2,1,0:T(8,128)S(1)}, f32[8,144,128]{2,1,0:T(8,128)S(1)}, u32[]{:S(2)}, u32[]{:S(2)}) collective-permute-start(f32[8,144,128]{2,1,0:T(8,128)S(1)} %get-tuple-element.74), channel_id=1, source_target_pairs={{0,2},{2,0},{4,6},{6,4},{8,10},{10,8},{12,14},{14,12},{16,18},{18,... | collective-permute-start | bytes 1769480 | tf_op jit(solution)/shard_map/ppermute | solution.py:54
  115.4 5.7 %collective-permute-start.6 = (f32[8,24,128]{2,1,0:T(8,128)S(1)}, f32[8,24,128]{2,1,0:T(8,128)S(1)}, u32[]{:S(2)}, u32[]{:S(2)}) collective-permute-start(f32[8,24,128]{2,1,0:T(8,128)S(1)} %get-tuple-element.73), channel_id=1, source_target_pairs={{0,1},{1,0},{2,3},{3,2},{4,5},{5,4},{6,7},{7,6},{8,9},{9,8},{10,11... | collective-permute-start | bytes 294920 | tf_op jit(solution)/shard_map/ppermute | solution.py:54
  116.3 6.0 %collective-permute-start.4 = (f32[8,24,128]{2,1,0:T(8,128)S(1)}, f32[8,24,128]{2,1,0:T(8,128)S(1)}, u32[]{:S(2)}, u32[]{:S(2)}) collective-permute-start(f32[8,24,128]{2,1,0:T(8,128)S(1)} %get-tuple-element.68), channel_id=1, source_target_pairs={{0,1},{1,0},{2,3},{3,2},{4,5},{5,4},{6,7},{7,6},{8,9},{9,8},{10,11... | collective-permute-start | bytes 294920 | tf_op jit(solution)/shard_map/ppermute | solution.py:54
  121.1 1.4 collective-permute-start.7
  123.8 6.1 %collective-permute-start.9 = (s16[1,400,128]{2,1,0:T(8,128)(2,1)S(1)}, s16[1,400,128]{2,1,0:T(8,128)(2,1)S(1)}, u32[]{:S(2)}, u32[]{:S(2)}) collective-permute-start(s16[1,400,128]{2,1,0:T(8,128)(2,1)S(1)} %get-tuple-element.76), channel_id=1, source_target_pairs={{0,4},{2,6},{4,0},{6,2},{8,12},{10,14},{12,8},{14,10},{16,20},{18,... | collective-permute-start | bytes 307208 | tf_op jit(solution)/shard_map/ppermute | solution.py:54
  124.0 6.9 %collective-permute-start.10 = (s16[1,400,128]{2,1,0:T(8,128)(2,1)S(1)}, s16[1,400,128]{2,1,0:T(8,128)(2,1)S(1)}, u32[]{:S(2)}, u32[]{:S(2)}) collective-permute-start(s16[1,400,128]{2,1,0:T(8,128)(2,1)S(1)} %get-tuple-element.77), channel_id=1, source_target_pairs={{0,8},{2,10},{4,12},{6,14},{8,0},{10,2},{12,4},{14,6},{16,24},{18,... | collective-permute-start | bytes 307208 | tf_op jit(solution)/shard_map/ppermute | solution.py:54
  124.7 10.3 %collective-permute-start.11 = (s16[1,400,128]{2,1,0:T(8,128)(2,1)S(1)}, s16[1,400,128]{2,1,0:T(8,128)(2,1)S(1)}, u32[]{:S(2)}, u32[]{:S(2)}) collective-permute-start(s16[1,400,128]{2,1,0:T(8,128)(2,1)S(1)} %get-tuple-element.78), channel_id=1, source_target_pairs={{0,12},{2,14},{4,8},{6,10},{8,4},{10,6},{12,0},{14,2},{16,28},{18,... | collective-permute-start | bytes 307208 | tf_op jit(solution)/shard_map/ppermute | solution.py:54
  127.3 14.7 %collective-permute-start.12 = (s16[1,400,128]{2,1,0:T(8,128)(2,1)S(1)}, s16[1,400,128]{2,1,0:T(8,128)(2,1)S(1)}, u32[]{:S(2)}, u32[]{:S(2)}) collective-permute-start(s16[1,400,128]{2,1,0:T(8,128)(2,1)S(1)} %get-tuple-element.79), channel_id=1, source_target_pairs={{0,16},{2,18},{4,20},{6,22},{8,24},{10,26},{12,28},{14,30},{16,0},... | collective-permute-start | bytes 307208 | tf_op jit(solution)/shard_map/ppermute | solution.py:54
  127.6 16.7 %collective-permute-start.13 = (s16[1,400,128]{2,1,0:T(8,128)(2,1)S(1)}, s16[1,400,128]{2,1,0:T(8,128)(2,1)S(1)}, u32[]{:S(2)}, u32[]{:S(2)}) collective-permute-start(s16[1,400,128]{2,1,0:T(8,128)(2,1)S(1)} %get-tuple-element.80), channel_id=1, source_target_pairs={{0,20},{2,22},{4,16},{6,18},{8,28},{10,30},{12,24},{14,26},{16,4},... | collective-permute-start | bytes 307208 | tf_op jit(solution)/shard_map/ppermute | solution.py:54
  129.9 14.4 %collective-permute-start.14 = (s16[1,400,128]{2,1,0:T(8,128)(2,1)S(1)}, s16[1,400,128]{2,1,0:T(8,128)(2,1)S(1)}, u32[]{:S(2)}, u32[]{:S(2)}) collective-permute-start(s16[1,400,128]{2,1,0:T(8,128)(2,1)S(1)} %get-tuple-element.81), channel_id=1, source_target_pairs={{0,24},{2,26},{4,28},{6,30},{8,16},{10,18},{12,20},{14,22},{16,8},... | collective-permute-start | bytes 307208 | tf_op jit(solution)/shard_map/ppermute | solution.py:54
  130.9 13.4 %collective-permute-start.15 = (s16[1,400,128]{2,1,0:T(8,128)(2,1)S(1)}, s16[1,400,128]{2,1,0:T(8,128)(2,1)S(1)}, u32[]{:S(2)}, u32[]{:S(2)}) collective-permute-start(s16[1,400,128]{2,1,0:T(8,128)(2,1)S(1)} %get-tuple-element.82), channel_id=1, source_target_pairs={{0,28},{2,30},{4,24},{6,26},{8,20},{10,22},{12,16},{14,18},{16,12}... | collective-permute-start | bytes 307208 | tf_op jit(solution)/shard_map/ppermute | solution.py:54
  144.9 10.8 %collective-permute-start.22 = (s16[1,400,128]{2,1,0:T(8,128)(2,1)S(1)}, s16[1,400,128]{2,1,0:T(8,128)(2,1)S(1)}, u32[]{:S(2)}, u32[]{:S(2)}) collective-permute-start(s16[1,400,128]{2,1,0:T(8,128)(2,1)S(1)} %chip_sum0.1.refs_0_), channel_id=1, source_target_pairs={{0,28},{2,30},{4,24},{6,26},{8,20},{10,22},{12,16},{14,18},{16,12}... | collective-permute-start | bytes 307208 | tf_op jit(solution)/shard_map/ppermute | solution.py:54
  146.9 14.0 %collective-permute-start.21 = (s16[1,400,128]{2,1,0:T(8,128)(2,1)S(1)}, s16[1,400,128]{2,1,0:T(8,128)(2,1)S(1)}, u32[]{:S(2)}, u32[]{:S(2)}) collective-permute-start(s16[1,400,128]{2,1,0:T(8,128)(2,1)S(1)} %chip_sum0.1.refs_0_), channel_id=1, source_target_pairs={{0,24},{2,26},{4,28},{6,30},{8,16},{10,18},{12,20},{14,22},{16,8},... | collective-permute-start | bytes 307208 | tf_op jit(solution)/shard_map/ppermute | solution.py:54
  149.6 15.0 %collective-permute-start.20 = (s16[1,400,128]{2,1,0:T(8,128)(2,1)S(1)}, s16[1,400,128]{2,1,0:T(8,128)(2,1)S(1)}, u32[]{:S(2)}, u32[]{:S(2)}) collective-permute-start(s16[1,400,128]{2,1,0:T(8,128)(2,1)S(1)} %chip_sum0.1.refs_0_), channel_id=1, source_target_pairs={{0,20},{2,22},{4,16},{6,18},{8,28},{10,30},{12,24},{14,26},{16,4},... | collective-permute-start | bytes 307208 | tf_op jit(solution)/shard_map/ppermute | solution.py:54
  151.5 15.0 %collective-permute-start.19 = (s16[1,400,128]{2,1,0:T(8,128)(2,1)S(1)}, s16[1,400,128]{2,1,0:T(8,128)(2,1)S(1)}, u32[]{:S(2)}, u32[]{:S(2)}) collective-permute-start(s16[1,400,128]{2,1,0:T(8,128)(2,1)S(1)} %chip_sum0.1.refs_0_), channel_id=1, source_target_pairs={{0,16},{2,18},{4,20},{6,22},{8,24},{10,26},{12,28},{14,30},{16,0},... | collective-permute-start | bytes 307208 | tf_op jit(solution)/shard_map/ppermute | solution.py:54
  152.6 13.9 %collective-permute-start.18 = (s16[1,400,128]{2,1,0:T(8,128)(2,1)S(1)}, s16[1,400,128]{2,1,0:T(8,128)(2,1)S(1)}, u32[]{:S(2)}, u32[]{:S(2)}) collective-permute-start(s16[1,400,128]{2,1,0:T(8,128)(2,1)S(1)} %chip_sum0.1.refs_0_), channel_id=1, source_target_pairs={{0,12},{2,14},{4,8},{6,10},{8,4},{10,6},{12,0},{14,2},{16,28},{18,... | collective-permute-start | bytes 307208 | tf_op jit(solution)/shard_map/ppermute | solution.py:54
  155.6 11.9 %collective-permute-start.17 = (s16[1,400,128]{2,1,0:T(8,128)(2,1)S(1)}, s16[1,400,128]{2,1,0:T(8,128)(2,1)S(1)}, u32[]{:S(2)}, u32[]{:S(2)}) collective-permute-start(s16[1,400,128]{2,1,0:T(8,128)(2,1)S(1)} %chip_sum0.1.refs_0_), channel_id=1, source_target_pairs={{0,8},{2,10},{4,12},{6,14},{8,0},{10,2},{12,4},{14,6},{16,24},{18,... | collective-permute-start | bytes 307208 | tf_op jit(solution)/shard_map/ppermute | solution.py:54
  160.9 6.6 %collective-permute-start.16 = (s16[1,400,128]{2,1,0:T(8,128)(2,1)S(1)}, s16[1,400,128]{2,1,0:T(8,128)(2,1)S(1)}, u32[]{:S(2)}, u32[]{:S(2)}) collective-permute-start(s16[1,400,128]{2,1,0:T(8,128)(2,1)S(1)} %chip_sum0.1.refs_0_), channel_id=1, source_target_pairs={{0,4},{2,6},{4,0},{6,2},{8,12},{10,14},{12,8},{14,10},{16,20},{18,... | collective-permute-start | bytes 307208 | tf_op jit(solution)/shard_map/ppermute | solution.py:54
  167.6 2.4 %collective-permute-start.23 = (s16[8,400,128]{2,1,0:T(8,128)(2,1)S(1)}, s16[8,400,128]{2,1,0:T(8,128)(2,1)S(1)}, u32[]{:S(2)}, u32[]{:S(2)}) collective-permute-start(s16[8,400,128]{2,1,0:T(8,128)(2,1)S(1)} %chunk_join0.1.mine), channel_id=1, source_target_pairs={{0,2},{2,0},{4,6},{6,4},{8,10},{10,8},{12,14},{14,12},{16,18},{18,... | collective-permute-start | bytes 2457608 | tf_op jit(solution)/shard_map/ppermute | solution.py:54
  (15 other events, 62.5 us)

commit v3 on v2

--- a/solution.py
+++ b/solution.py
@@ -40,6 +40,10 @@
     return pltpu.with_memory_space_constraint(value, pltpu.VMEM)
 
 
+def far(value):
+    return pltpu.with_memory_space_constraint(value, pltpu.HBM)
+
+
 def stages_of(count):
     stages, bit = [[1]], 2
     while bit < count:
@@ -54,9 +58,8 @@
     return lax.ppermute(value, axis, [(k, k ^ mask) for k in range(count)])
 
 
-def all_of(value, axes):
-    count = lax.axis_size(axes)
-    return lax.all_to_all(jnp.broadcast_to(value[None], (count,) + value.shape), axes, 0, 0, tiled=True)
+def exchange(copies, axis):
+    return lax.all_to_all(copies, axis, 0, 0, tiled=True)
 
 
 def slot_of(xor_index, count):
@@ -232,10 +235,21 @@
     return carry[:CHAINS], carry[CHAINS:]
 
 
-def own_table_kernel(doc_lengths, block_of, ids, embed, w, marked, spots, tab, seg, ends, sem, *, vocab, blocks):
+def own_table_kernel(
+    doc_lengths, block_of, ids, embed, w, w_out, marked, spots, tab, seg, ends, w_far, wt, wt_far, sem, *, vocab, blocks
+):
     toks = ids.shape[0]
     copy = pltpu.make_async_copy(ids, marked, sem)
     copy.start()
+    core = lax.axis_index("ctx") % 2
+    shape = (wt.shape[0], w_out.shape[0])
+    same = lax.broadcasted_iota(jnp.int32, shape, 0) == lax.broadcasted_iota(jnp.int32, shape, 1)
+    turned = jnp.dot(same.astype(F32).astype(BF16), w_out[...], preferred_element_type=F32).astype(BF16)
+    wt[...] = turned
+    half = wt_far.shape[0]
+    wt_far[...] = jnp.where(core == 0, turned[0:half], turned[half:2 * half])
+    for g in range(w_far.shape[0]):
+        w_far[g] = w[core * w_far.shape[0] + g]
     gate = [jnp.dot(embed[...], w[g], preferred_element_type=F32) for g in range(3)]
     spread(tab, jax.nn.sigmoid(gate[1] + 3.0), 0, blocks, 0, 2)
     spread(tab, jax.nn.sigmoid(gate[0]) * jnp.tanh(gate[2]), 0, blocks, 1, 2)
@@ -258,70 +272,61 @@
         if s:
             s_all = prod[s] * s_all + total[s]
             p_all = prod[s] * p_all
-    ends[0] = p_all
-    ends[1] = s_all
-
-
-def rest_table_kernel(ids, spots, embed, w, *refs, vocab, blocks, others):
-    fetched = refs[:2 * others]
-    outs = refs[2 * others:]
-    o_tab, coef = outs[:2]
-    toks = ids.shape[0]
-    gate = [jnp.dot(embed[...], w[g], preferred_element_type=F32) for g in (0, 2, 3)]
-    in_gate, cand = jax.nn.sigmoid(gate[0]), jnp.tanh(gate[1])
-    source = in_gate * cand
-    spread(o_tab, jax.nn.sigmoid(gate[2]), 0, blocks)
-    spread(coef, source - source * in_gate, 0, blocks, 0, 2)
-    spread(coef, in_gate - source * cand, 0, blocks, 1, 2)
-    docs = spots.shape[0]
-    for k in range(docs):
+    for d in range(ends.shape[0]):
+        ends[d, 0] = p_all
+        ends[d, 1] = s_all
+
+
+def carry_kernel(block_of, ps_all, _, bias, carry, order):
+    own = stream_order(order, block_of)
+
+    def earlier(b, c):
+        return ps_all[order[b], 0] * c + ps_all[order[b], 1]
+
+    carry[...] = lax.fori_loop(0, own, earlier, jnp.zeros(carry.shape, F32))
+
+
+def rest_table_kernel(spots, embed, w, o_tab, *, vocab, blocks):
+    spread(o_tab, jax.nn.sigmoid(jnp.dot(embed[...], w[3], preferred_element_type=F32)), 0, blocks)
+    for k in range(spots.shape[0]):
         tile(o_tab, vocab + k, blocks)[...] = tile(o_tab, spots[k], blocks)[...]
+
+
+def other_table_kernel(spots, embed, direct, passed, tab, *, vocab, blocks):
     first = lax.axis_index("ctx") % 2 == 0
-    for p in range(others):
-        direct, passed = fetched[2 * p:2 * p + 2]
-        tab, seg = outs[2 + 2 * p:4 + 2 * p]
-
-        def weights(g):
-            mine, theirs = direct[g % 2], passed[g % 2]
-            return jnp.where(first, mine, theirs) if g < 2 else jnp.where(first, theirs, mine)
-
-        gate = [jnp.dot(embed[...], weights(g), preferred_element_type=F32) for g in range(4)]
-        spread(tab, jax.nn.sigmoid(gate[1] + 3.0), 0, blocks, 0, 3)
-        spread(tab, jax.nn.sigmoid(gate[0]) * jnp.tanh(gate[2]), 0, blocks, 1, 3)
-        spread(tab, jax.nn.sigmoid(gate[3]), 0, blocks, 2, 3)
-        for k in range(docs):
-            tile(tab, vocab + k, blocks, 0, 3)[...] = jnp.zeros((blocks, LANE), F32)
-            for kind in (1, 2):
-                tile(tab, vocab + k, blocks, kind, 3)[...] = tile(tab, spots[k], blocks, kind, 3)[...]
-        prod, total = segment_ends(ids, tab, toks, blocks, 3)
-        for s in range(CHAINS):
-            seg[s, 0] = prod[s]
-            seg[s, 1] = total[s]
+
+    def weights(g):
+        mine, theirs = direct[g % 2], passed[g % 2]
+        return jnp.where(first, mine, theirs) if g < 2 else jnp.where(first, theirs, mine)
+
+    gate = [jnp.dot(embed[...], weights(g), preferred_element_type=F32) for g in range(4)]
+    spread(tab, jax.nn.sigmoid(gate[1] + 3.0), 0, blocks, 0, 3)
+    spread(tab, jax.nn.sigmoid(gate[0]) * jnp.tanh(gate[2]), 0, blocks, 1, 3)
+    spread(tab, jax.nn.sigmoid(gate[3]), 0, blocks, 2, 3)
+    for k in range(spots.shape[0]):
+        tile(tab, vocab + k, blocks, 0, 3)[...] = jnp.zeros((blocks, LANE), F32)
+        for kind in (1, 2):
+            tile(tab, vocab + k, blocks, kind, 3)[...] = tile(tab, spots[k], blocks, kind, 3)[...]
 
 
 def cell_kernel(*refs, others, total_tokens, blocks):
-    ids, block_of, ps_all, tab_o, o_tab, seg_o, wt_o, bias, tgt, ids_row = refs[:10]
-    refs = refs[10:]
+    ids, tab_o, o_tab, seg_o, wt_o, bias, tgt, ids_row = refs[:8]
+    carries = refs[8:9 + others]
+    refs = refs[9 + others:]
     tab_x, seg_x = refs[:others], refs[others:2 * others]
     halves = refs[2 * others:4 * others]
     refs = refs[4 * others:]
-    hid, prev_out, src_out, lgrad, heads, head, o_sum, sums = refs[:8]
-    order, prev, src, hs, low, low_x, wt_x, logits, pcum, sem, src_sems = refs[8:]
+    hid, prev_out, src_out, keep_o, send_o, heads, head, o_sum, sums = refs[:9]
+    prev, src, hs, low, low_x, wt_x, logits, pcum, lgrad, sem, src_sems = refs[9:]
     toks = ids.shape[0]
     length = toks // CHAINS
     width = blocks * LANE
     vocab = wt_o.shape[0]
-    own = stream_order(order, block_of)
-    shards, mine = lax.axis_size("wa"), lax.axis_index("wa")
     nt = (((1,), (1,)), ((), ()))
     tn = (((0,), (0,)), ((), ()))
 
     def starts(piece, seg):
-        def earlier(b, c):
-            slot = order[b] * shards + (mine + piece) % shards
-            return ps_all[slot, 0] * c + ps_all[slot, 1]
-
-        c = lax.fori_loop(0, own, earlier, jnp.zeros((blocks, LANE), F32))
+        c = carries[piece][...]
         out = []
         for s in range(CHAINS):
             out.append(c)
@@ -356,7 +361,7 @@
             tile(src, t, blocks)[...] = o - h * th
         return tuple(cells + prods)
 
-    lax.fori_loop(0, length, own_step, starts(0, seg_o) + (jnp.ones((blocks, LANE), F32),) * CHAINS)
+    lax.fori_loop(0, length, own_step, starts(0, seg_o) + (jnp.ones((blocks, LANE), F32),) * CHAINS, unroll=2)
     save_prev = pltpu.make_async_copy(prev, prev_out, sem.at[1])
     save_prev.start()
     flatten(low)
@@ -390,7 +395,6 @@
         place = pl.ds(pl.multiple_of(k * rows * blocks, rows * blocks), rows * blocks)
         return pltpu.make_async_copy(src.at[place, :], src_out.at[place, :], src_sems.at[k])
 
-    o_sum[...] = jnp.zeros_like(o_sum)
 
     def back(k, carry):
         loss, b_grad = carry
@@ -406,9 +410,7 @@
         lgrad[:, pl.ds(at, rows)] = grad
         b_grad = b_grad + jnp.sum(grad.astype(F32).reshape(vocab, rows // LANE, LANE), axis=1)
         hg = lax.dot_general(grad, wt_o[...], tn, preferred_element_type=F32)
-        chars = lax.broadcasted_iota(jnp.int32, (vocab, rows), 0) == ids_row[:, pl.ds(at, rows)]
-        moment = (hg * low[pl.ds(at, rows), :].astype(F32)).astype(BF16)
-        o_sum[...] += jnp.dot(chars.astype(F32).astype(BF16), moment, preferred_element_type=F32)
+        low_x[pl.ds(at, rows), :] = (hg * low[pl.ds(at, rows), :].astype(F32)).astype(BF16)
         for b in range(blocks):
             hs[pl.ds(at * blocks + b, rows, stride=blocks), :] = hg[:, b * LANE:(b + 1) * LANE]
         for q in range(rows // length):
@@ -428,6 +430,19 @@
     sums[...] = jnp.where(lane == LANE - 1, jnp.sum(b_grad, axis=1, keepdims=True), 0.0) + jnp.where(
         (lane == LANE - 2) & (row == 0), jnp.sum(loss, axis=1, keepdims=True), 0.0
     )
+    grad_out = jnp.dot(lgrad[...], low[...], preferred_element_type=F32)
+    part = keep_o.shape[1]
+    count = head.shape[0]
+    splits = count // blocks
+
+    def piece(q):
+        c, e = q // splits, q % splits
+        size = max(0, min(part, vocab - e * part))
+        return padded(grad_out, slice(e * part, e * part + size), slice(c * LANE, (c + 1) * LANE), part)
+
+    store_pairs(keep_o, send_o, lax.axis_index("ctx"), piece, count, slice(0, part))
+    chars = lax.broadcasted_iota(jnp.int32, (vocab, toks), 0) == ids_row[...]
+    o_sum[...] = jnp.dot(chars.astype(F32).astype(BF16), low_x[...], preferred_element_type=F32)
     save.wait()
     save_prev.wait()
     for k in range(toks // rows):
@@ -435,21 +450,8 @@
     total = tile(heads, CHAINS - 1, blocks)[...]
     for s in range(CHAINS - 2, -1, -1):
         total = tile(heads, s, blocks)[...] + seg_o[s, 0] * total
-    head[...] = total
-
-
-def decoder_grad_kernel(lgrad, hid, keep, send, *, count, blocks):
-    grad = jnp.dot(lgrad[...], hid[...], preferred_element_type=F32)
-    vocab = grad.shape[0]
-    part = keep.shape[1]
-    splits = count // blocks
-
-    def piece(q):
-        c, e = q // splits, q % splits
-        size = max(0, min(part, vocab - e * part))
-        return padded(grad, slice(e * part, e * part + size), slice(c * LANE, (c + 1) * LANE), part)
-
-    store_pairs(keep, send, lax.axis_index("ctx"), piece, count, slice(0, part))
+    for d in range(head.shape[0]):
+        head[d] = total
 
 
 def char_sum_kernel(
@@ -466,11 +468,10 @@
             ref[...] = jnp.zeros_like(ref)
         own = stream_order(order, block_of)
         count = block_of.shape[0]
-        shards, mine = lax.axis_size("wa"), lax.axis_index("wa")
 
         def from_later(i, g):
             slot = order[count - 1 - i]
-            return h_all[slot] + ps_all[slot * shards + mine, 0] * g
+            return h_all[slot] + ps_all[slot, 0] * g
 
         later = lax.fori_loop(0, count - 1 - own, from_later, jnp.zeros((blocks, LANE), F32))
         for s in range(CHAINS - 1, -1, -1):
@@ -503,13 +504,8 @@
             sums[k] = value
 
 
-def input_grad_kernel(
-    spots, sums, o_sum, tab, o_tab, coef, w, table, extra, keep, send, keep_e, send_e, merged,
-    *, count, part, vocab, blocks,
-):
-    rows = table.shape[0]
-    width = blocks * LANE
-    me = lax.axis_index("ctx")
+def gate_sum_kernel(spots, sums, o_sum, embed, w, extra, high, low, keep_e, send_e, merged, *, count, vocab, blocks):
+    rows = high.shape[1]
     merged[...] = sums[...]
     for k in range(spots.shape[0]):
         tile(merged.at[0], spots[k], blocks)[...] += tile(merged.at[0], vocab + k, blocks)[...]
@@ -523,39 +519,47 @@
     def column(q, b):
         return merged[q, pl.ds(b, rows, stride=blocks), :]
 
-    def square(ref, b, kinds):
-        value = gathered(ref, 0, rows, blocks, b, 0, kinds)
-        return value - value * value
-
+    def gate_of(g):
+        return jnp.dot(embed[...], w[g], preferred_element_type=F32)
+
+    both = (((1,), (1,)), ((), ()))
+    in_gate, cand = jax.nn.sigmoid(gate_of(0)), jnp.tanh(gate_of(2))
+    forget = jax.nn.sigmoid(gate_of(1) + 3.0)
+    cell = units(lambda b: column(0, b))
+    source = in_gate * cand
     parts = [
-        units(lambda b: column(0, b) * gathered(coef, 0, rows, blocks, b, 0, 2)),
-        units(lambda b: column(1, b) * square(tab, b, 2)),
-        units(lambda b: column(0, b) * gathered(coef, 0, rows, blocks, b, 1, 2)),
-        o_sum[...] * (1.0 - units(lambda b: gathered(o_tab, 0, rows, blocks, b))),
+        lambda: cell * (source - source * in_gate),
+        lambda: units(lambda b: column(1, b)) * (forget - forget * forget),
+        lambda: cell * (in_gate - source * cand),
+        lambda: o_sum[...] * (1.0 - jax.nn.sigmoid(gate_of(3))),
     ]
-    both = (((1,), (1,)), ((), ()))
+    part_e = jnp.zeros((rows, w.shape[1]), F32)
+    for gate in range(4):
+        total = parts[gate]()
+        high[gate] = total.astype(BF16)
+        low[gate] = (total - high[gate].astype(F32)).astype(BF16)
+        part_e = part_e + lax.dot_general(high[gate], w[gate], both, preferred_element_type=F32)
+        part_e = part_e + lax.dot_general(low[gate], w[gate], both, preferred_element_type=F32)
+    per = keep_e.shape[1]
+    wide_e = jnp.concatenate([part_e, jnp.zeros((rows, LANE - part_e.shape[1]), F32)], axis=1) + extra[...]
+    wide_e = jnp.concatenate([wide_e, jnp.zeros((count * per - rows, LANE), F32)], axis=0)
+    me = lax.axis_index("ctx")
+    store_pairs(keep_e, send_e, me, lambda q: wide_e[q * per:(q + 1) * per, :], count, slice(0, per))
+
+
+def input_grad_kernel(high, low, table, keep, send, *, count, part, blocks):
     tn = (((0,), (0,)), ((), ()))
     splits = count // blocks
-    part_e = jnp.zeros((rows, w.shape[1]), F32)
     for gate in range(4):
-        total = parts[gate]
-        high = total.astype(BF16)
-        low = (total - high.astype(F32)).astype(BF16)
-        wide = lax.dot_general(table[...], high, tn, preferred_element_type=F32)
-        wide = wide + lax.dot_general(table[...], low, tn, preferred_element_type=F32)
+        wide = lax.dot_general(table[...], high[gate], tn, preferred_element_type=F32)
+        wide = wide + lax.dot_general(table[...], low[gate], tn, preferred_element_type=F32)
 
         def piece(q):
             c, e = q // splits, q % splits
             size = max(0, min(part, wide.shape[0] - e * part))
             return padded(wide, slice(e * part, e * part + size), slice(c * LANE, (c + 1) * LANE), part)
 
-        store_pairs(keep, send, me, piece, count, slice(gate * part, (gate + 1) * part))
-        part_e = part_e + lax.dot_general(high, w[gate], both, preferred_element_type=F32)
-        part_e = part_e + lax.dot_general(low, w[gate], both, preferred_element_type=F32)
-    per = keep_e.shape[1]
-    wide_e = jnp.concatenate([part_e, jnp.zeros((rows, LANE - part_e.shape[1]), F32)], axis=1) + extra[...]
-    wide_e = jnp.concatenate([wide_e, jnp.zeros((count * per - rows, LANE), F32)], axis=0)
-    store_pairs(keep_e, send_e, me, lambda q: wide_e[q * per:(q + 1) * per, :], count, slice(0, per))
+        store_pairs(keep, send, lax.axis_index("ctx"), piece, count, slice(gate * part, (gate + 1) * part))
 
 
 def finish_kernel(
@@ -587,7 +591,7 @@
             size = max(0, min(part, emb - e * part))
             for gate in range(4):
                 if size:
-                    w_grad[gate, e * part:e * part + size, lanes] = chunk(q, slice(gate * part, gate * part + size))
+                    w_grad[e * part:e * part + size, gate, lanes] = chunk(q, slice(gate * part, gate * part + size))
                 if e * part <= emb < (e + 1) * part:
                     at = gate * part + emb - e * part
                     b_grad[gate:gate + 1, lanes] = chunk(q, slice(at, at + 1))
@@ -647,76 +651,82 @@
     smem = lambda shape: jax.ShapeDtypeStruct(shape, jnp.int32)
     tokens = (toks * blocks, LANE)
 
-    marked, spots, tab, seg, ends = call(
+    bf = lambda *shape: pltpu.HBM(shape, BF16)
+    marked, spots, tab, seg, ends, w_far, wt_own, wt_far = call(
         functools.partial(own_table_kernel, vocab=vocab, blocks=blocks),
         "tables_own",
         [doc_lengths, block_of],
-        [ids, table, w_own],
-        [smem((toks,)), smem((docs,)), chip(vpad * 2 * blocks, LANE), chip(CHAINS, 2, blocks, LANE),
-         hbm((2, blocks, LANE), F32)],
+        [ids, table, w_own, w_out.T],
+        [smem((toks,)), smem((docs,)), chip(vpad * 2 * blocks, LANE), pltpu.HBM((CHAINS, 2, blocks, LANE), F32),
+         pltpu.HBM((count, 2, blocks, LANE), F32), bf(gates // 2, kdim, width), bf(vpad, width), bf(vpad // 2, width)],
         [pltpu.SemaphoreType.DMA],
-        in_spaces=[pl.ANY, pltpu.VMEM, pltpu.VMEM],
-        out_spaces=[pltpu.SMEM, pltpu.SMEM, pltpu.VMEM, pltpu.VMEM, pltpu.VMEM],
-    )
-    tab, seg = near(tab), near(seg)
-    w_far = from_others(half_of(after(w_own, ends), core), wa)
-    ps_all = all_of(ends, ("ctx", "wa"))
+        in_spaces=[pl.ANY, pltpu.VMEM, pltpu.VMEM, pltpu.VMEM],
+        out_spaces=[pltpu.SMEM, pltpu.SMEM] + [pltpu.VMEM] * 6,
+        micros=6,
+    )
+    tab = near(tab)
+    w_far, seg_x, wt_far = from_others(w_far, wa), from_others(seg, wa), from_others(wt_far, wa)
+    ps_all = exchange(ends, "ctx")
+    bias_out = jnp.pad(b_out, (0, vpad - vocab), constant_values=-1e30)[:, None]
+    (o_tab,) = call(
+        functools.partial(rest_table_kernel, vocab=vocab, blocks=blocks),
+        "tables_rest",
+        [spots],
+        [table, w_own],
+        [chip(vpad * blocks, LANE)],
+        micros=3,
+    )
+    o_tab = near(o_tab)
+    (carry,) = call(
+        carry_kernel, "carry", [block_of], [ps_all, o_tab, bias_out], [hbm((blocks, LANE), F32)],
+        [pltpu.SMEM((count,), jnp.int32)], in_spaces=[pltpu.VMEM, pltpu.VMEM, pl.ANY],
+    )
+    carries = [carry] + from_others(carry, wa)
     w_far = [after(w, ps_all) for w in w_far]
     w_oth = [v for w in w_far for v in (w, swap(w, "ctx", 1))]
-    wt_own = jnp.pad(after(w_out, ps_all).T, ((0, vpad - vocab), (0, 0)))
-    wt_far = from_others(half_of(wt_own, core), wa)
+    wt_far = [after(w, carry) for w in wt_far]
     wt_oth = [v for w in wt_far for v in (w, swap(w, "ctx", 1))]
-    bias_out = jnp.pad(b_out, (0, vpad - vocab), constant_values=-1e30)[:, None]
     others = wa - 1
-    rest = call(
-        functools.partial(rest_table_kernel, vocab=vocab, blocks=blocks, others=others),
-        "tables_rest",
-        [marked, spots],
-        [table, w_own] + w_oth,
-        [chip(vpad * blocks, LANE), chip(vpad * 2 * blocks, LANE)]
-        + [chip(vpad * 3 * blocks, LANE), chip(CHAINS, 2, blocks, LANE)] * others,
-        micros=6,
-    )
-    rest = [near(r) for r in rest]
-    o_tab, coef = rest[:2]
-
-    hid, prev, src, lgrad, heads, head, o_sum, extra = call(
-        functools.partial(cell_kernel, others=others, total_tokens=total_tokens, blocks=blocks),
-        "cells",
-        [marked, block_of],
-        [ps_all, tab, o_tab, seg, wt_own, bias_out, targets[None], ids[None]] + rest[2::2] + rest[3::2] + wt_oth,
-        [
-            hbm((toks, width), BF16), hbm(tokens, F32), hbm(tokens, F32),
-            pltpu.VMEM((vpad, toks), BF16), chip(CHAINS * blocks, LANE), hbm((blocks, LANE), F32),
-            chip(vpad, width), hbm((vpad, LANE), F32),
-        ],
-        [
-            pltpu.SMEM((count,), jnp.int32), pltpu.VMEM(tokens, F32), pltpu.VMEM(tokens, F32),
-            pltpu.VMEM(tokens, F32), pltpu.VMEM((toks, width), BF16),
-            pltpu.VMEM((toks, width), BF16), pltpu.VMEM((vpad, width), BF16), pltpu.VMEM((vpad, toks), F32), pltpu.VMEM(tokens, F32),
-            pltpu.SemaphoreType.DMA((2,)), pltpu.SemaphoreType.DMA((toks // 512,)),
-        ],
-        limit=48,
-        out_spaces=[pl.ANY] * 3 + [pltpu.VMEM] * 5,
-        micros=26,
-    )
-    lgrad, heads, o_sum = map(near, (lgrad, heads, o_sum))
+    tab_x = [
+        near(call(
+            functools.partial(other_table_kernel, vocab=vocab, blocks=blocks),
+            "tables_other",
+            [spots],
+            [table] + w_oth[2 * p:2 * p + 2],
+            [chip(vpad * 3 * blocks, LANE)],
+            micros=3,
+        )[0])
+        for p in range(others)
+    ]
+
     splits = count // blocks
     vpart = ceil_to(-(-vpad // splits), 8)
     half_chunks = lambda rows: [hbm((count // 2, rows, LANE), F32)] * 2
     copies = 4
-
+    hid, prev, src, keep_o, send_o, heads, head, o_sum, extra = call(
+        functools.partial(cell_kernel, others=others, total_tokens=total_tokens, blocks=blocks),
+        "cells",
+        [marked],
+        [tab, o_tab, seg, wt_own, bias_out, targets[None], ids[None]] + carries + tab_x + seg_x + wt_oth,
+        [
+            hbm((toks, width), BF16), hbm(tokens, F32), hbm(tokens, F32),
+            *half_chunks(vpart), chip(CHAINS * blocks, LANE), hbm((count, blocks, LANE), F32),
+            chip(vpad, width), hbm((vpad, LANE), F32),
+        ],
+        [
+            pltpu.VMEM(tokens, F32), pltpu.VMEM(tokens, F32), pltpu.VMEM(tokens, F32),
+            pltpu.VMEM((toks, width), BF16),
+            pltpu.VMEM((toks, width), BF16), pltpu.VMEM((vpad, width), BF16), pltpu.VMEM((vpad, toks), F32), pltpu.VMEM(tokens, F32),
+            pltpu.VMEM((vpad, toks), BF16), pltpu.SemaphoreType.DMA((2,)), pltpu.SemaphoreType.DMA((toks // 512,)),
+        ],
+        limit=52,
+        out_spaces=[pl.ANY] * 3 + [pltpu.VMEM] * 6,
+        micros=26,
+    )
+    heads, o_sum = near(heads), near(o_sum)
     part = ceil_to(-(-kdim // splits), 8)
     per = ceil_to(-(-vpad // count), 8)
-    h_all = all_of(head, "ctx")
-    keep_o, send_o = call(
-        functools.partial(decoder_grad_kernel, count=count, blocks=blocks),
-        "decoder_grad",
-        [],
-        [lgrad, after(hid, h_all)],
-        half_chunks(vpart),
-        limit=20,
-    )
+    h_all = exchange(head, "ctx")
     got_o = swap(send_o, "ctx", 1)
     length = toks // CHAINS
     span = 16
@@ -725,7 +735,7 @@
         functools.partial(char_sum_kernel, copies=copies, blocks=blocks),
         "char_sums",
         [marked, block_of],
-        [tab, seg, heads, h_all, ps_all] + [v.reshape(CHAINS, length * blocks, LANE) for v in (prev, src)],
+        [tab, seg, heads, h_all, ps_all] + [far(v.reshape(CHAINS, length * blocks, LANE)) for v in (prev, src)],
         [chip(2, vpad * blocks, LANE)],
         [pltpu.SMEM((count,), jnp.int32), pltpu.VMEM((CHAINS, blocks, LANE), F32)]
         + [pltpu.VMEM((vpad * blocks, LANE), F32)] * (2 * copies),
@@ -733,15 +743,24 @@
         in_spaces=[pltpu.VMEM] * 5 + [block] * 2,
         micros=(9, length // span),
     )
-    keep, send, keep_e, send_e = call(
-        functools.partial(input_grad_kernel, count=count, part=part, vocab=vocab, blocks=blocks),
-        "input_grad",
+    high, low, keep_e, send_e = call(
+        functools.partial(gate_sum_kernel, count=count, vocab=vocab, blocks=blocks),
+        "gate_sums",
         [spots],
-        [near(sums), o_sum, tab, o_tab, coef, w_own, table, extra],
-        half_chunks(4 * part) + half_chunks(per),
+        [near(sums), o_sum, table, w_own, extra],
+        [pltpu.VMEM((gates, vpad, width), BF16)] * 2 + half_chunks(per),
         [pltpu.VMEM((2, vpad * blocks, LANE), F32)],
         limit=24,
-        micros=5,
+        micros=3,
+    )
+    keep, send = call(
+        functools.partial(input_grad_kernel, count=count, part=part, blocks=blocks),
+        "input_grad",
+        [],
+        [near(high), near(low), table],
+        half_chunks(4 * part),
+        limit=24,
+        micros=3,
     )
     bit = 1
     while bit < wa:
@@ -758,7 +777,7 @@
         [],
         [mine, theirs],
         [
-            hbm((gates, emb, width), F32), hbm((gates, width), F32), hbm((vocab, emb), F32),
+            hbm((emb, gates, width), F32), hbm((gates, width), F32), hbm((vocab, emb), F32),
             hbm((vocab, width), F32), hbm((1, vocab), F32), hbm((1, 1), F32),
         ],
         [pltpu.VMEM((ceil_to(count * per, LANE), LANE), F32)],
@@ -767,7 +786,7 @@
         hid,
         loss[0, 0],
         e_grad,
-        jnp.transpose(w_grad, (1, 0, 2)),
+        w_grad,
         bi_grad,
         w_out_grad.T,
         bo_grad[0],

time: 176 us -> 157 us (0.89)
  local copies, waits for them, and re-layouts: 20.9 us -> 4.45 us
  waiting for transfers between devices: 38.6 us -> 32.1 us
  Pallas kernels: 57.9 us -> 59.9 us
    unnamed x46 -> x41, local copies, waits for them, and re-layouts: 14.1 us -> 3.58 us
    ppermute x2 -> x4, waiting for transfers between devices: 9.39 us -> 3.6 us  [from_others(): lax.ppermute(value, 'wa', [(k, (k - s) % wa) for k in range(wa)])]
    ppermute x2 -> x4, starting transfers between devices: 2.64 us -> 5.62 us  [from_others(): lax.ppermute(value, 'wa', [(k, (k - s) % wa) for k in range(wa)])]
    pallas_call x10 -> x12, Pallas kernels: 57.9 us -> 59.9 us  [call(): pl.pallas_call(kernel, grid=(steps,) if blocked else (), in_specs=[spec(p...]
    dynamic_slice x2 -> x0, local copies, waits for them, and re-layouts: 1.94 us -> none  [half_of(): return lax.dynamic_slice_in_dim(value, core * half, half, 0)]
    pad x1 -> x0, local copies, waits for them, and re-layouts: 1.92 us -> none  [body(): wt_own = jnp.pad(after(w_out, ps_all).T, ((0, vpad - vocab), (0, 0)))]
  transfers between devices with their start and end apart: 25 -> 27, of which waited for: 12 -> 12; matrix products, arithmetic and copies ran while one was open for 3% -> 0% of each run, Pallas kernels for 4% -> 2%
where the time goes in v3:
time: 157 us; the launch traced here: 156 us
  Pallas kernels  59.9 us (38%)
  starting transfers between devices  43.5 us (28%)
  waiting for transfers between devices  32.1 us (20%)
  blocking collectives  13.1 us (8%)
  local copies, waits for them, and re-layouts  4.45 us (3%)
  other arithmetic  2.42 us (2%)
    pallas_call x12, Pallas kernels, call(): pl.pallas_call(kernel, grid=(steps,) if blocked else (), in_specs=[spec(p...  59.9 us
    ppermute x22, starting transfers between devices, swap(): return lax.ppermute(value, axis, [(k, k ^ mask) for k in range(count)])  31.9 us
    ppermute x22, waiting for transfers between devices, swap(): return lax.ppermute(value, axis, [(k, k ^ mask) for k in range(count)])  21.1 us
    all_to_all x1, blocking collectives, exchange(): return lax.all_to_all(copies, axis, 0, 0, tiled=True)  13.1 us
    all_to_all x1, waiting for transfers between devices, exchange(): return lax.all_to_all(copies, axis, 0, 0, tiled=True)  7.34 us
    all_to_all x1, starting transfers between devices, exchange(): return lax.all_to_all(copies, axis, 0, 0, tiled=True)  5.93 us
    ppermute x4, starting transfers between devices, from_others(): lax.ppermute(value, 'wa', [(k, (k - s) % wa) for k in range(wa)])  5.62 us
    ppermute x4, waiting for transfers between devices, from_others(): lax.ppermute(value, 'wa', [(k, (k - s) % wa) for k in range(wa)])  3.6 us
  transfers between devices with their start and end apart: 27, of which 12 were waited for; matrix products, arithmetic and copies ran while one was open for 0% of the time, Pallas kernels for 2%

profile of v3, /device:TPU:0, one launch (start us, length us, event | category | flops | bytes accessed | tf_op | source)
XLA Modules:
  0.0 156.5 jit_solution(9529424777002578452)
XLA Ops:
  1.6 1.4 copy.36
  4.8 6.2 %tables_own.1 = (s32[2048]{0:T(1024)S(1)}, s32[4]{0:T(128)S(1)}, f32[4608,128]{1,0:T(8,128)S(1)}, f32[16,2,8,128]{3,2,1,0:T(8,128)}, f32[16,2,8,128]{3,2,1,0:T(8...) custom-call(s32[4]{0:T(128)S(1)} %copy-done.13, s32[16]{0:T(128)S(1)} %copy-done.12, ...), custom_call_target="tpu_custom_call" | custom-call | bytes 18000000 | tf_op jit(solution)/shard_map/tables_own/pallas_call | solution.py:24
  11.0 1.4 copy-done
  12.4 2.9 %collective-permute-start.1 = (bf16[2,112,1024]{2,1,0:T(8,128)(2,1)}, bf16[2,112,1024]{2,1,0:T(8,128)(2,1)S(1)}, u32[]{:S(2)}, u32[]{:S(2)}) collective-permute-start(bf16[2,112,1024]{2,1,0:T(8,128)(2,1)} %get-tuple-element.52), channel_id=1, source_target_pairs={{0,1},{1,0},{2,3},{3,2},{4,5},{5,4},{6,7},{7,6},{8,9},{9,8},{10,11... | collective-permute-start | bytes 1376264 | tf_op jit(solution)/shard_map/ppermute | solution.py:619
  15.3 5.9 %all-to-all-start = ((f32[16,2,8,128]{3,2,1,0:T(8,128)}), f32[16,2,8,128]{3,2,1,0:T(8,128)S(1)}, u32[]{:S(2)}, u32[]{:S(2)}) async-start(f32[16,2,8,128]{3,2,1,0:T(8,128)} %get-tuple-element.51), calls=%async_computation | async-start | bytes 262144 | tf_op jit(solution)/shard_map/all_to_all | solution.py:62
  21.8 7.3 %all-to-all-done.ps_all = f32[16,2,8,128]{3,2,1,0:T(8,128)S(1)} async-done(((f32[16,2,8,128]{3,2,1,0:T(8,128)}), f32[16,2,8,128]{3,2,1,0:T(8,128)S(1)}, u32[]{:S(2)}, u32[]{:S(2)}) %all-to-all-start) | async-done | bytes 131104 | tf_op jit(solution)/shard_map/all_to_all | solution.py:62
  32.4 1.8 %collective-permute-start.3 = (f32[16,2,8,128]{3,2,1,0:T(8,128)S(1)}, f32[16,2,8,128]{3,2,1,0:T(8,128)S(1)}, u32[]{:S(2)}, u32[]{:S(2)}) collective-permute-start(f32[16,2,8,128]{3,2,1,0:T(8,128)S(1)} %copy-done.5), channel_id=1, source_target_pairs={{0,1},{1,0},{2,3},{3,2},{4,5},{5,4},{6,7},{7,6},{8,9},{9,8},{10,11... | collective-permute-start | bytes 393224 | tf_op jit(solution)/shard_map/ppermute | solution.py:619
  34.5 1.6 tables_other.1.refs_10_
  36.0 2.3 %collective-permute-done.3.refs_11_ = f32[16,2,8,128]{3,2,1,0:T(8,128)S(1)} collective-permute-done((f32[16,2,8,128]{3,2,1,0:T(8,128)S(1)}, f32[16,2,8,128]{3,2,1,0:T(8,128)S(1)}, u32[]{:S(2)}, u32[]{:S(2)}) %collective-permute-start.3) | collective-permute-done | bytes 131104 | tf_op jit(solution)/shard_map/ppermute | solution.py:619
  39.1 27.6 %cells.1 = (bf16[2048,1024]{1,0:T(8,128)(2,1)}, f32[16384,128]{1,0:T(8,128)}, f32[16384,128]{1,0:T(8,128)}, f32[8,144,128]{2,1,0:T(8,128)}, f32[8,144,128]{2,1,0...) custom-call(s32[2048]{0:T(1024)} %copy-done.9, ...), custom_call_target="tpu_custom_call" | custom-call | bytes 78000000 | tf_op jit(solution)/shard_map/cells/pallas_call | solution.py:24
  66.7 13.1 %all_to_all.10.h_all = f32[16,8,128]{2,1,0:T(8,128)S(1)} all-to-all(f32[16,8,128]{2,1,0:T(8,128)} %get-tuple-element.58), channel_id=1, replica_groups=mesh['ctx'=16,'wa'=2] {'ctx'}, dimensions={0} | all-to-all | bytes 131072 | tf_op jit(solution)/shard_map/all_to_all | solution.py:62
  79.8 11.8 %char_sums.1.sums = f32[2,2304,128]{2,1,0:T(8,128)S(1)} custom-call(s32[2048]{0:T(1024)S(1)} %copy-done.10, s32[16]{0:T(128)S(1)} %copy-done.12, f32[4608,128]{1,0:T(8,128)S(1)} %copy-done.1, f32[16,2,8,128]{3,2,1,0:T(8,128)S(1)} %copy-done.6, f32[128,128]{1,0:T(8,128)S(1)} %get-tuple-element.57.heads, f32[16,8,128]{2,1,0:T(8,128)S(1)} %all_to_all.10.h_all, ...), custom_call_target="tpu_custom_call" | custom-call | bytes 27000000 | tf_op jit(solution)/shard_map/char_sums/pallas_call | solution.py:24
  91.6 4.1 %gate_sums.1 = (bf16[4,288,1024]{2,1,0:T(8,128)(2,1)S(1)}, bf16[4,288,1024]{2,1,0:T(8,128)(2,1)S(1)}, f32[8,24,128]{2,1,0:T(8,128)S(1)}, f32[8,24,128]{2,1,0:T(8,128)S(1)}) custom-call(s32[4]{0:T(128)S(1)} %get-tuple-element.48.spots, f32[2,2304,128]{2,1,0:T(8,128)S(1)} %char_sums.1.sums, f32[288,1024]{1,0:T(8,128)S(1)} %get-tuple-element.61.o_sum, ...), custom_call_target="tpu_custom_call" | custom-call | bytes 9000000 | tf_op jit(solution)/shard_map/gate_sums/pallas_call | solution.py:24
  95.7 1.3 input_grad.1
  97.6 1.5 collective-permute-start.8
  99.6 3.6 %collective-permute-done.8 = f32[8,24,128]{2,1,0:T(8,128)S(1)} collective-permute-done((f32[8,24,128]{2,1,0:T(8,128)S(1)}, f32[8,24,128]{2,1,0:T(8,128)S(1)}, u32[]{:S(2)}, u32[]{:S(2)}) %collective-permute-start.8) | collective-permute-done | bytes 98336 | tf_op jit(solution)/shard_map/ppermute | solution.py:58
  104.7 1.3 core_sum.1
  106.9 2.7 %collective-permute-start.13 = (s16[1,400,128]{2,1,0:T(8,128)(2,1)S(1)}, s16[1,400,128]{2,1,0:T(8,128)(2,1)S(1)}, u32[]{:S(2)}, u32[]{:S(2)}) collective-permute-start(s16[1,400,128]{2,1,0:T(8,128)(2,1)S(1)} %get-tuple-element.74), channel_id=1, source_target_pairs={{0,12},{2,14},{4,8},{6,10},{8,4},{10,6},{12,0},{14,2},{16,28},{18,... | collective-permute-start | bytes 307208 | tf_op jit(solution)/shard_map/ppermute | solution.py:58
  109.8 2.3 %collective-permute-start.15 = (s16[1,400,128]{2,1,0:T(8,128)(2,1)S(1)}, s16[1,400,128]{2,1,0:T(8,128)(2,1)S(1)}, u32[]{:S(2)}, u32[]{:S(2)}) collective-permute-start(s16[1,400,128]{2,1,0:T(8,128)(2,1)S(1)} %get-tuple-element.76), channel_id=1, source_target_pairs={{0,20},{2,22},{4,16},{6,18},{8,28},{10,30},{12,24},{14,26},{16,4},... | collective-permute-start | bytes 307208 | tf_op jit(solution)/shard_map/ppermute | solution.py:58
  113.2 4.0 %collective-permute-start.17 = (s16[1,400,128]{2,1,0:T(8,128)(2,1)S(1)}, s16[1,400,128]{2,1,0:T(8,128)(2,1)S(1)}, u32[]{:S(2)}, u32[]{:S(2)}) collective-permute-start(s16[1,400,128]{2,1,0:T(8,128)(2,1)S(1)} %get-tuple-element.78), channel_id=1, source_target_pairs={{0,28},{2,30},{4,24},{6,26},{8,20},{10,22},{12,16},{14,18},{16,12}... | collective-permute-start | bytes 307208 | tf_op jit(solution)/shard_map/ppermute | solution.py:58
  117.2 7.0 %collective-permute-done.14.refs_4_ = s16[1,400,128]{2,1,0:T(8,128)(2,1)S(1)} collective-permute-done((s16[1,400,128]{2,1,0:T(8,128)(2,1)S(1)}, s16[1,400,128]{2,1,0:T(8,128)(2,1)S(1)}, u32[]{:S(2)}, u32[]{:S(2)}) %collective-permute-start.14) | collective-permute-done | bytes 102432 | tf_op jit(solution)/shard_map/ppermute | solution.py:58
  124.2 2.2 %collective-permute-done.15.refs_5_ = s16[1,400,128]{2,1,0:T(8,128)(2,1)S(1)} collective-permute-done((s16[1,400,128]{2,1,0:T(8,128)(2,1)S(1)}, s16[1,400,128]{2,1,0:T(8,128)(2,1)S(1)}, u32[]{:S(2)}, u32[]{:S(2)}) %collective-permute-start.15) | collective-permute-done | bytes 102432 | tf_op jit(solution)/shard_map/ppermute | solution.py:58
  127.0 2.2 %collective-permute-start.24 = (s16[1,400,128]{2,1,0:T(8,128)(2,1)S(1)}, s16[1,400,128]{2,1,0:T(8,128)(2,1)S(1)}, u32[]{:S(2)}, u32[]{:S(2)}) collective-permute-start(s16[1,400,128]{2,1,0:T(8,128)(2,1)S(1)} %chip_sum0.1.refs_0_), channel_id=1, source_target_pairs={{0,28},{2,30},{4,24},{6,26},{8,20},{10,22},{12,16},{14,18},{16,12}... | collective-permute-start | bytes 307208 | tf_op jit(solution)/shard_map/ppermute | solution.py:58
  129.2 2.6 %collective-permute-start.23 = (s16[1,400,128]{2,1,0:T(8,128)(2,1)S(1)}, s16[1,400,128]{2,1,0:T(8,128)(2,1)S(1)}, u32[]{:S(2)}, u32[]{:S(2)}) collective-permute-start(s16[1,400,128]{2,1,0:T(8,128)(2,1)S(1)} %chip_sum0.1.refs_0_), channel_id=1, source_target_pairs={{0,24},{2,26},{4,28},{6,30},{8,16},{10,18},{12,20},{14,22},{16,8},... | collective-permute-start | bytes 307208 | tf_op jit(solution)/shard_map/ppermute | solution.py:58
  131.8 2.0 %collective-permute-start.22 = (s16[1,400,128]{2,1,0:T(8,128)(2,1)S(1)}, s16[1,400,128]{2,1,0:T(8,128)(2,1)S(1)}, u32[]{:S(2)}, u32[]{:S(2)}) collective-permute-start(s16[1,400,128]{2,1,0:T(8,128)(2,1)S(1)} %chip_sum0.1.refs_0_), channel_id=1, source_target_pairs={{0,20},{2,22},{4,16},{6,18},{8,28},{10,30},{12,24},{14,26},{16,4},... | collective-permute-start | bytes 307208 | tf_op jit(solution)/shard_map/ppermute | solution.py:58
  134.7 3.1 %collective-permute-start.20 = (s16[1,400,128]{2,1,0:T(8,128)(2,1)S(1)}, s16[1,400,128]{2,1,0:T(8,128)(2,1)S(1)}, u32[]{:S(2)}, u32[]{:S(2)}) collective-permute-start(s16[1,400,128]{2,1,0:T(8,128)(2,1)S(1)} %chip_sum0.1.refs_0_), channel_id=1, source_target_pairs={{0,12},{2,14},{4,8},{6,10},{8,4},{10,6},{12,0},{14,2},{16,28},{18,... | collective-permute-start | bytes 307208 | tf_op jit(solution)/shard_map/ppermute | solution.py:58
  137.8 5.1 %collective-permute-start.19 = (s16[1,400,128]{2,1,0:T(8,128)(2,1)S(1)}, s16[1,400,128]{2,1,0:T(8,128)(2,1)S(1)}, u32[]{:S(2)}, u32[]{:S(2)}) collective-permute-start(s16[1,400,128]{2,1,0:T(8,128)(2,1)S(1)} %chip_sum0.1.refs_0_), channel_id=1, source_target_pairs={{0,8},{2,10},{4,12},{6,14},{8,0},{10,2},{12,4},{14,6},{16,24},{18,... | collective-permute-start | bytes 307208 | tf_op jit(solution)/shard_map/ppermute | solution.py:58
  142.9 2.1 %collective-permute-start.18 = (s16[1,400,128]{2,1,0:T(8,128)(2,1)S(1)}, s16[1,400,128]{2,1,0:T(8,128)(2,1)S(1)}, u32[]{:S(2)}, u32[]{:S(2)}) collective-permute-start(s16[1,400,128]{2,1,0:T(8,128)(2,1)S(1)} %chip_sum0.1.refs_0_), channel_id=1, source_target_pairs={{0,4},{2,6},{4,0},{6,2},{8,12},{10,14},{12,8},{14,10},{16,20},{18,... | collective-permute-start | bytes 307208 | tf_op jit(solution)/shard_map/ppermute | solution.py:58
  145.0 1.7 %collective-permute-done.22.refs_5_ = s16[1,400,128]{2,1,0:T(8,128)(2,1)S(1)} collective-permute-done((s16[1,400,128]{2,1,0:T(8,128)(2,1)S(1)}, s16[1,400,128]{2,1,0:T(8,128)(2,1)S(1)}, u32[]{:S(2)}, u32[]{:S(2)}) %collective-permute-start.22) | collective-permute-done | bytes 102432 | tf_op jit(solution)/shard_map/ppermute | solution.py:58
  146.7 2.0 %collective-permute-done.21.refs_4_ = s16[1,400,128]{2,1,0:T(8,128)(2,1)S(1)} collective-permute-done((s16[1,400,128]{2,1,0:T(8,128)(2,1)S(1)}, s16[1,400,128]{2,1,0:T(8,128)(2,1)S(1)}, u32[]{:S(2)}, u32[]{:S(2)}) %collective-permute-start.21) | collective-permute-done | bytes 102432 | tf_op jit(solution)/shard_map/ppermute | solution.py:58
  149.8 2.3 %collective-permute-done.25.theirs = s16[8,400,128]{2,1,0:T(8,128)(2,1)S(1)} collective-permute-done((s16[8,400,128]{2,1,0:T(8,128)(2,1)S(1)}, s16[8,400,128]{2,1,0:T(8,128)(2,1)S(1)}, u32[]{:S(2)}, u32[]{:S(2)}) %collective-permute-start.25) | collective-permute-done | bytes 819232 | tf_op jit(solution)/shard_map/ppermute | solution.py:58
  152.1 3.8 %finish.1 = (f32[100,4,1024]{2,1,0:T(4,128)}, f32[4,1024]{1,0:T(4,128)}, f32[275,100]{1,0:T(8,128)}, f32[275,1024]{1,0:T(8,128)}, f32[1,275]{1,0:T(1,128)S(1)}, /*index=5*/f32[1,1]{1,0:T(1,128)}) custom-call(s16[8,400,128]{2,1,0:T(8,128)(2,1)S(1)} %chunk_join0.1.mine, s16[8,400,128]{2,1,0:T(8,128)(2,1)S(1)} %collective-permute-done.25.theirs), custom_call_target="tpu_custom_call" | custom-call | bytes 3000000 | tf_op jit(solution)/shard_map/finish/pallas_call | solution.py:24
  (90 shorter events, 15.2 us)
Async XLA Ops:
  3.0 26.2 %copy-start.18 = (f32[275]{0:T(512)S(1)}, f32[275]{0:T(512)}, u32[]{:S(2)}) copy-start(f32[275]{0:T(512)} %param.17) | copy-start | bytes 3304
  12.4 16.9 %copy-start.9 = (s32[2048]{0:T(1024)}, s32[2048]{0:T(1024)S(1)}, u32[]{:S(2)}) copy-start(s32[2048]{0:T(1024)S(1)} %get-tuple-element.46.refs_0_.ids) | copy-start | bytes 24580
  12.4 20.0 %copy-start.5 = (f32[16,2,8,128]{3,2,1,0:T(8,128)S(1)}, f32[16,2,8,128]{3,2,1,0:T(8,128)}, u32[]{:S(2)}) copy-start(f32[16,2,8,128]{3,2,1,0:T(8,128)} %get-tuple-element.49.refs_3_.seg) | copy-start | bytes 393220
  12.4 16.8 %collective-permute-start.1 = (bf16[2,112,1024]{2,1,0:T(8,128)(2,1)}, bf16[2,112,1024]{2,1,0:T(8,128)(2,1)S(1)}, u32[]{:S(2)}, u32[]{:S(2)}) collective-permute-start(bf16[2,112,1024]{2,1,0:T(8,128)(2,1)} %get-tuple-element.52), channel_id=1, source_target_pairs={{0,1},{1,0},{2,3},{3,2},{4,5},{5,4},{6,7},{7,6},{8,9},{9,8},{10,11... | collective-permute-start | bytes 1376264 | tf_op jit(solution)/shard_map/ppermute | solution.py:619
  15.3 13.9 %all-to-all-start = ((f32[16,2,8,128]{3,2,1,0:T(8,128)}), f32[16,2,8,128]{3,2,1,0:T(8,128)S(1)}, u32[]{:S(2)}, u32[]{:S(2)}) async-start(f32[16,2,8,128]{3,2,1,0:T(8,128)} %get-tuple-element.51), calls=%async_computation | async-start | bytes 262144 | tf_op jit(solution)/shard_map/all_to_all | solution.py:62
  21.2 11.1 %collective-permute-start.4 = (bf16[144,1024]{1,0:T(8,128)(2,1)}, bf16[144,1024]{1,0:T(8,128)(2,1)S(1)}, u32[]{:S(2)}, u32[]{:S(2)}) collective-permute-start(bf16[144,1024]{1,0:T(8,128)(2,1)} %get-tuple-element.54), channel_id=1, source_target_pairs={{0,1},{1,0},{2,3},{3,2},{4,5},{5,4},{6,7},{7,6},{8,9},{9,8},{10,11... | collective-permute-start | bytes 884744 | tf_op jit(solution)/shard_map/ppermute | solution.py:619
  29.2 5.3 %collective-permute-start.2 = (bf16[2,112,1024]{2,1,0:T(8,128)(2,1)S(1)}, bf16[2,112,1024]{2,1,0:T(8,128)(2,1)S(1)}, u32[]{:S(2)}, u32[]{:S(2)}) collective-permute-start(bf16[2,112,1024]{2,1,0:T(8,128)(2,1)S(1)} %collective-permute-done.1.direct), channel_id=1, source_target_pairs={{0,2},{2,0},{4,6},{6,4},{8,10},{10,8},{12,14},{14,12},{16,18},{18,... | collective-permute-start | bytes 1376264 | tf_op jit(solution)/shard_map/ppermute | solution.py:58
  32.3 6.0 %collective-permute-start.5 = (bf16[144,1024]{1,0:T(8,128)(2,1)S(1)}, bf16[144,1024]{1,0:T(8,128)(2,1)S(1)}, u32[]{:S(2)}, u32[]{:S(2)}) collective-permute-start(bf16[144,1024]{1,0:T(8,128)(2,1)S(1)} %collective-permute-done.4.refs_12_), channel_id=1, source_target_pairs={{0,2},{2,0},{4,6},{6,4},{8,10},{10,8},{12,14},{14,12},{16,18},{18,... | collective-permute-start | bytes 884744 | tf_op jit(solution)/shard_map/ppermute | solution.py:58
  32.4 6.0 %collective-permute-start.3 = (f32[16,2,8,128]{3,2,1,0:T(8,128)S(1)}, f32[16,2,8,128]{3,2,1,0:T(8,128)S(1)}, u32[]{:S(2)}, u32[]{:S(2)}) collective-permute-start(f32[16,2,8,128]{3,2,1,0:T(8,128)S(1)} %copy-done.5), channel_id=1, source_target_pairs={{0,1},{1,0},{2,3},{3,2},{4,5},{5,4},{6,7},{7,6},{8,9},{9,8},{10,11... | collective-permute-start | bytes 393224 | tf_op jit(solution)/shard_map/ppermute | solution.py:619
  34.2 4.2 %collective-permute-start = (f32[8,128]{1,0:T(8,128)S(1)}, f32[8,128]{1,0:T(8,128)S(1)}, u32[]{:S(2)}, u32[]{:S(2)}) collective-permute-start(f32[8,128]{1,0:T(8,128)S(1)} %carry.1.refs_8_), channel_id=1, source_target_pairs={{0,1},{1,0},{2,3},{3,2},{4,5},{5,4},{6,7},{7,6},{8,9},{9,8},{10,11... | collective-permute-start | bytes 12296 | tf_op jit(solution)/shard_map/ppermute | solution.py:619
  39.1 40.7 %copy-start.6 = (f32[16,2,8,128]{3,2,1,0:T(8,128)S(1)}, f32[16,2,8,128]{3,2,1,0:T(8,128)}, u32[]{:S(2)}) copy-start(f32[16,2,8,128]{3,2,1,0:T(8,128)} %get-tuple-element.49.refs_3_.seg) | copy-start | bytes 393220
  39.1 40.7 %copy-start.10 = (s32[2048]{0:T(1024)S(1)}, s32[2048]{0:T(1024)}, u32[]{:S(2)}) copy-start(s32[2048]{0:T(1024)} %copy-done.9) | copy-start | bytes 24580
  97.0 7.6 %collective-permute-start.7 = (f32[8,224,128]{2,1,0:T(8,128)S(1)}, f32[8,224,128]{2,1,0:T(8,128)S(1)}, u32[]{:S(2)}, u32[]{:S(2)}) collective-permute-start(f32[8,224,128]{2,1,0:T(8,128)S(1)} %get-tuple-element.68), channel_id=1, source_target_pairs={{0,2},{2,0},{4,6},{6,4},{8,10},{10,8},{12,14},{14,12},{16,18},{18,... | collective-permute-start | bytes 2752520 | tf_op jit(solution)/shard_map/ppermute | solution.py:58
  97.1 7.5 %collective-permute-start.10 = (f32[8,144,128]{2,1,0:T(8,128)S(1)}, f32[8,144,128]{2,1,0:T(8,128)S(1)}, u32[]{:S(2)}, u32[]{:S(2)}) collective-permute-start(f32[8,144,128]{2,1,0:T(8,128)S(1)} %copy-done.19), channel_id=1, source_target_pairs={{0,2},{2,0},{4,6},{6,4},{8,10},{10,8},{12,14},{14,12},{16,18},{18,... | collective-permute-start | bytes 1769480 | tf_op jit(solution)/shard_map/ppermute | solution.py:58
  97.6 5.7 %collective-permute-start.8 = (f32[8,24,128]{2,1,0:T(8,128)S(1)}, f32[8,24,128]{2,1,0:T(8,128)S(1)}, u32[]{:S(2)}, u32[]{:S(2)}) collective-permute-start(f32[8,24,128]{2,1,0:T(8,128)S(1)} %get-tuple-element.69), channel_id=1, source_target_pairs={{0,1},{1,0},{2,3},{3,2},{4,5},{5,4},{6,7},{7,6},{8,9},{9,8},{10,11... | collective-permute-start | bytes 294920 | tf_op jit(solution)/shard_map/ppermute | solution.py:58
  99.1 5.4 %collective-permute-start.6 = (f32[8,24,128]{2,1,0:T(8,128)S(1)}, f32[8,24,128]{2,1,0:T(8,128)S(1)}, u32[]{:S(2)}, u32[]{:S(2)}) collective-permute-start(f32[8,24,128]{2,1,0:T(8,128)S(1)} %get-tuple-element.66), channel_id=1, source_target_pairs={{0,1},{1,0},{2,3},{3,2},{4,5},{5,4},{6,7},{7,6},{8,9},{9,8},{10,11... | collective-permute-start | bytes 294920 | tf_op jit(solution)/shard_map/ppermute | solution.py:58
  103.3 1.4 collective-permute-start.9
  106.0 6.1 %collective-permute-start.11 = (s16[1,400,128]{2,1,0:T(8,128)(2,1)S(1)}, s16[1,400,128]{2,1,0:T(8,128)(2,1)S(1)}, u32[]{:S(2)}, u32[]{:S(2)}) collective-permute-start(s16[1,400,128]{2,1,0:T(8,128)(2,1)S(1)} %get-tuple-element.72), channel_id=1, source_target_pairs={{0,4},{2,6},{4,0},{6,2},{8,12},{10,14},{12,8},{14,10},{16,20},{18,... | collective-permute-start | bytes 307208 | tf_op jit(solution)/shard_map/ppermute | solution.py:58
  106.2 7.0 %collective-permute-start.12 = (s16[1,400,128]{2,1,0:T(8,128)(2,1)S(1)}, s16[1,400,128]{2,1,0:T(8,128)(2,1)S(1)}, u32[]{:S(2)}, u32[]{:S(2)}) collective-permute-start(s16[1,400,128]{2,1,0:T(8,128)(2,1)S(1)} %get-tuple-element.73), channel_id=1, source_target_pairs={{0,8},{2,10},{4,12},{6,14},{8,0},{10,2},{12,4},{14,6},{16,24},{18,... | collective-permute-start | bytes 307208 | tf_op jit(solution)/shard_map/ppermute | solution.py:58
  106.9 10.3 %collective-permute-start.13 = (s16[1,400,128]{2,1,0:T(8,128)(2,1)S(1)}, s16[1,400,128]{2,1,0:T(8,128)(2,1)S(1)}, u32[]{:S(2)}, u32[]{:S(2)}) collective-permute-start(s16[1,400,128]{2,1,0:T(8,128)(2,1)S(1)} %get-tuple-element.74), channel_id=1, source_target_pairs={{0,12},{2,14},{4,8},{6,10},{8,4},{10,6},{12,0},{14,2},{16,28},{18,... | collective-permute-start | bytes 307208 | tf_op jit(solution)/shard_map/ppermute | solution.py:58
  109.5 14.7 %collective-permute-start.14 = (s16[1,400,128]{2,1,0:T(8,128)(2,1)S(1)}, s16[1,400,128]{2,1,0:T(8,128)(2,1)S(1)}, u32[]{:S(2)}, u32[]{:S(2)}) collective-permute-start(s16[1,400,128]{2,1,0:T(8,128)(2,1)S(1)} %get-tuple-element.75), channel_id=1, source_target_pairs={{0,16},{2,18},{4,20},{6,22},{8,24},{10,26},{12,28},{14,30},{16,0},... | collective-permute-start | bytes 307208 | tf_op jit(solution)/shard_map/ppermute | solution.py:58
  109.8 16.7 %collective-permute-start.15 = (s16[1,400,128]{2,1,0:T(8,128)(2,1)S(1)}, s16[1,400,128]{2,1,0:T(8,128)(2,1)S(1)}, u32[]{:S(2)}, u32[]{:S(2)}) collective-permute-start(s16[1,400,128]{2,1,0:T(8,128)(2,1)S(1)} %get-tuple-element.76), channel_id=1, source_target_pairs={{0,20},{2,22},{4,16},{6,18},{8,28},{10,30},{12,24},{14,26},{16,4},... | collective-permute-start | bytes 307208 | tf_op jit(solution)/shard_map/ppermute | solution.py:58
  112.0 14.4 %collective-permute-start.16 = (s16[1,400,128]{2,1,0:T(8,128)(2,1)S(1)}, s16[1,400,128]{2,1,0:T(8,128)(2,1)S(1)}, u32[]{:S(2)}, u32[]{:S(2)}) collective-permute-start(s16[1,400,128]{2,1,0:T(8,128)(2,1)S(1)} %get-tuple-element.77), channel_id=1, source_target_pairs={{0,24},{2,26},{4,28},{6,30},{8,16},{10,18},{12,20},{14,22},{16,8},... | collective-permute-start | bytes 307208 | tf_op jit(solution)/shard_map/ppermute | solution.py:58
  113.2 13.3 %collective-permute-start.17 = (s16[1,400,128]{2,1,0:T(8,128)(2,1)S(1)}, s16[1,400,128]{2,1,0:T(8,128)(2,1)S(1)}, u32[]{:S(2)}, u32[]{:S(2)}) collective-permute-start(s16[1,400,128]{2,1,0:T(8,128)(2,1)S(1)} %get-tuple-element.78), channel_id=1, source_target_pairs={{0,28},{2,30},{4,24},{6,26},{8,20},{10,22},{12,16},{14,18},{16,12}... | collective-permute-start | bytes 307208 | tf_op jit(solution)/shard_map/ppermute | solution.py:58
  127.0 10.8 %collective-permute-start.24 = (s16[1,400,128]{2,1,0:T(8,128)(2,1)S(1)}, s16[1,400,128]{2,1,0:T(8,128)(2,1)S(1)}, u32[]{:S(2)}, u32[]{:S(2)}) collective-permute-start(s16[1,400,128]{2,1,0:T(8,128)(2,1)S(1)} %chip_sum0.1.refs_0_), channel_id=1, source_target_pairs={{0,28},{2,30},{4,24},{6,26},{8,20},{10,22},{12,16},{14,18},{16,12}... | collective-permute-start | bytes 307208 | tf_op jit(solution)/shard_map/ppermute | solution.py:58
  129.2 13.7 %collective-permute-start.23 = (s16[1,400,128]{2,1,0:T(8,128)(2,1)S(1)}, s16[1,400,128]{2,1,0:T(8,128)(2,1)S(1)}, u32[]{:S(2)}, u32[]{:S(2)}) collective-permute-start(s16[1,400,128]{2,1,0:T(8,128)(2,1)S(1)} %chip_sum0.1.refs_0_), channel_id=1, source_target_pairs={{0,24},{2,26},{4,28},{6,30},{8,16},{10,18},{12,20},{14,22},{16,8},... | collective-permute-start | bytes 307208 | tf_op jit(solution)/shard_map/ppermute | solution.py:58
  131.8 14.9 %collective-permute-start.22 = (s16[1,400,128]{2,1,0:T(8,128)(2,1)S(1)}, s16[1,400,128]{2,1,0:T(8,128)(2,1)S(1)}, u32[]{:S(2)}, u32[]{:S(2)}) collective-permute-start(s16[1,400,128]{2,1,0:T(8,128)(2,1)S(1)} %chip_sum0.1.refs_0_), channel_id=1, source_target_pairs={{0,20},{2,22},{4,16},{6,18},{8,28},{10,30},{12,24},{14,26},{16,4},... | collective-permute-start | bytes 307208 | tf_op jit(solution)/shard_map/ppermute | solution.py:58
  133.8 14.8 %collective-permute-start.21 = (s16[1,400,128]{2,1,0:T(8,128)(2,1)S(1)}, s16[1,400,128]{2,1,0:T(8,128)(2,1)S(1)}, u32[]{:S(2)}, u32[]{:S(2)}) collective-permute-start(s16[1,400,128]{2,1,0:T(8,128)(2,1)S(1)} %chip_sum0.1.refs_0_), channel_id=1, source_target_pairs={{0,16},{2,18},{4,20},{6,22},{8,24},{10,26},{12,28},{14,30},{16,0},... | collective-permute-start | bytes 307208 | tf_op jit(solution)/shard_map/ppermute | solution.py:58
  134.7 14.0 %collective-permute-start.20 = (s16[1,400,128]{2,1,0:T(8,128)(2,1)S(1)}, s16[1,400,128]{2,1,0:T(8,128)(2,1)S(1)}, u32[]{:S(2)}, u32[]{:S(2)}) collective-permute-start(s16[1,400,128]{2,1,0:T(8,128)(2,1)S(1)} %chip_sum0.1.refs_0_), channel_id=1, source_target_pairs={{0,12},{2,14},{4,8},{6,10},{8,4},{10,6},{12,0},{14,2},{16,28},{18,... | collective-permute-start | bytes 307208 | tf_op jit(solution)/shard_map/ppermute | solution.py:58
  137.8 11.8 %collective-permute-start.19 = (s16[1,400,128]{2,1,0:T(8,128)(2,1)S(1)}, s16[1,400,128]{2,1,0:T(8,128)(2,1)S(1)}, u32[]{:S(2)}, u32[]{:S(2)}) collective-permute-start(s16[1,400,128]{2,1,0:T(8,128)(2,1)S(1)} %chip_sum0.1.refs_0_), channel_id=1, source_target_pairs={{0,8},{2,10},{4,12},{6,14},{8,0},{10,2},{12,4},{14,6},{16,24},{18,... | collective-permute-start | bytes 307208 | tf_op jit(solution)/shard_map/ppermute | solution.py:58
  142.9 6.8 %collective-permute-start.18 = (s16[1,400,128]{2,1,0:T(8,128)(2,1)S(1)}, s16[1,400,128]{2,1,0:T(8,128)(2,1)S(1)}, u32[]{:S(2)}, u32[]{:S(2)}) collective-permute-start(s16[1,400,128]{2,1,0:T(8,128)(2,1)S(1)} %chip_sum0.1.refs_0_), channel_id=1, source_target_pairs={{0,4},{2,6},{4,0},{6,2},{8,12},{10,14},{12,8},{14,10},{16,20},{18,... | collective-permute-start | bytes 307208 | tf_op jit(solution)/shard_map/ppermute | solution.py:58
  149.7 2.4 %collective-permute-start.25 = (s16[8,400,128]{2,1,0:T(8,128)(2,1)S(1)}, s16[8,400,128]{2,1,0:T(8,128)(2,1)S(1)}, u32[]{:S(2)}, u32[]{:S(2)}) collective-permute-start(s16[8,400,128]{2,1,0:T(8,128)(2,1)S(1)} %chunk_join0.1.mine), channel_id=1, source_target_pairs={{0,2},{2,0},{4,6},{6,4},{8,10},{10,8},{12,14},{14,12},{16,18},{18,... | collective-permute-start | bytes 2457608 | tf_op jit(solution)/shard_map/ppermute | solution.py:58
  (15 other events, 70.0 us)

commit v4 on v3

--- a/solution.py
+++ b/solution.py
@@ -53,6 +53,15 @@
     return stages
 
 
+def gather_stages_of(count):
+    stages, bit = [[1]], 2
+    while bit < count:
+        ways = min(2 if bit == 2 else 4, count // bit)
+        stages.append([k * bit for k in range(1, ways)])
+        bit *= ways
+    return stages
+
+
 def swap(value, axis, mask):
     count = lax.axis_size(axis)
     return lax.ppermute(value, axis, [(k, k ^ mask) for k in range(count)])
@@ -62,9 +71,9 @@
     return lax.all_to_all(copies, axis, 0, 0, tiled=True)
 
 
-def slot_of(xor_index, count):
+def slot_of(xor_index, count, stages=None):
     place, size, bit = 0, count, 1
-    for masks in stages_of(count):
+    for masks in stages or stages_of(count):
         ways = len(masks) + 1
         size = size // ways
         place = place + ((xor_index // bit) % ways) * size
@@ -162,19 +171,23 @@
 
 
 def gather_chunks(chunk, axis):
-    value = chunk
-    stages = stages_of(lax.axis_size(axis))
+    stages = gather_stages_of(lax.axis_size(axis))
+    middle = ceil_to(chunk.shape[1] // 2, 16)
+    halves = [chunk[:, :middle], chunk[:, middle:]]
     for number, masks in enumerate(reversed(stages[1:])):
-        parts = [value] + [swap(value, axis, mask) for mask in masks]
-        size = value.shape[0]
-
-        def kernel(*refs):
-            for k, ref in enumerate(refs[:-1]):
-                refs[-1][k * size:(k + 1) * size] = ref[...]
-
-        shape = (size * len(parts),) + value.shape[1:]
-        value = call(kernel, "chunk_join" + str(number), [], parts, [jax.ShapeDtypeStruct(shape, value.dtype)])[0]
-    return value, swap(value, axis, 1)
+        for h in range(2):
+            value = halves[h]
+            parts = [value] + [swap(value, axis, mask) for mask in masks]
+            size = value.shape[0]
+
+            def kernel(*refs):
+                for k, ref in enumerate(refs[:-1]):
+                    refs[-1][k * size:(k + 1) * size] = ref[...]
+
+            shape = (size * len(parts),) + value.shape[1:]
+            out = jax.ShapeDtypeStruct(shape, value.dtype)
+            halves[h] = call(kernel, "chunk_join" + str(number), [], parts, [out])[0]
+    return halves + [swap(h, axis, 1) for h in halves]
 
 
 def padded(value, rows, lanes, size):
@@ -316,8 +329,8 @@
     tab_x, seg_x = refs[:others], refs[others:2 * others]
     halves = refs[2 * others:4 * others]
     refs = refs[4 * others:]
-    hid, prev_out, src_out, keep_o, send_o, heads, head, o_sum, sums = refs[:9]
-    prev, src, hs, low, low_x, wt_x, logits, pcum, lgrad, sem, src_sems = refs[9:]
+    hid, prev, src_out, keep_o, send_o, heads, head, o_sum, sums = refs[:9]
+    src, hs, low, low_x, wt_x, logits, pcum, lgrad, sem, src_sems = refs[9:]
     toks = ids.shape[0]
     length = toks // CHAINS
     width = blocks * LANE
@@ -362,10 +375,8 @@
         return tuple(cells + prods)
 
     lax.fori_loop(0, length, own_step, starts(0, seg_o) + (jnp.ones((blocks, LANE), F32),) * CHAINS, unroll=2)
-    save_prev = pltpu.make_async_copy(prev, prev_out, sem.at[1])
-    save_prev.start()
     flatten(low)
-    save = pltpu.make_async_copy(low, hid, sem.at[0])
+    save = pltpu.make_async_copy(low, hid, sem)
     save.start()
     logits[...] = lax.dot_general(wt_o[...], low[...], nt, preferred_element_type=F32) + bias[...]
     first = lax.axis_index("ctx") % 2 == 0
@@ -385,7 +396,7 @@
                 tile(hs, t, blocks)[...] = tile(tab, at, blocks, 2, 3)[...] * jnp.tanh(cells[s])
             return tuple(cells)
 
-        lax.fori_loop(0, length, other_step, starts(p + 1, seg_x[p]))
+        lax.fori_loop(0, length, other_step, starts(p + 1, seg_x[p]), unroll=2)
         flatten(low_x)
         logits[...] += lax.dot_general(wt_x[...], low_x[...], nt, preferred_element_type=F32)
 
@@ -406,7 +417,8 @@
         norm = jnp.sum(power, axis=0, keepdims=True)
         picked = jnp.sum(jnp.where(target, part, 0.0), axis=0, keepdims=True)
         loss = loss + (top + jnp.log(norm) - picked)
-        grad = ((power / norm - jnp.where(target, 1.0, 0.0)) * (1.0 / total_tokens)).astype(BF16)
+        share = power * ((1.0 / norm) * (1.0 / total_tokens))
+        grad = (share - jnp.where(target, 1.0 / total_tokens, 0.0)).astype(BF16)
         lgrad[:, pl.ds(at, rows)] = grad
         b_grad = b_grad + jnp.sum(grad.astype(F32).reshape(vocab, rows // LANE, LANE), axis=1)
         hg = lax.dot_general(grad, wt_o[...], tn, preferred_element_type=F32)
@@ -444,7 +456,6 @@
     chars = lax.broadcasted_iota(jnp.int32, (vocab, toks), 0) == ids_row[...]
     o_sum[...] = jnp.dot(chars.astype(F32).astype(BF16), low_x[...], preferred_element_type=F32)
     save.wait()
-    save_prev.wait()
     for k in range(toks // rows):
         save_src(k).wait()
     total = tile(heads, CHAINS - 1, blocks)[...]
@@ -459,7 +470,7 @@
 ):
     number = pl.program_id(0)
     length = ids.shape[0] // CHAINS
-    span = prev.shape[1] // blocks
+    span = src.shape[1] // blocks
     sets = [refs[2 * k:2 * k + 2] for k in range(copies)]
 
     @pl.when(number == 0)
@@ -482,13 +493,14 @@
         h = list(later)
         r = span - 1 - i
         for s in range(CHAINS):
-            at = ids[s * length + (pl.num_programs(0) - 1 - number) * span + r]
+            token = s * length + (pl.num_programs(0) - 1 - number) * span + r
+            at = ids[token]
             here = pl.ds(pl.multiple_of(r * blocks, blocks), blocks)
             g = src[s, here, :] + h[s]
             h[s] = tile(tab, at, blocks, 0, 2)[...] * g
             cell, forget = sets[s % copies]
             tile(cell, at, blocks)[...] += g
-            tile(forget, at, blocks)[...] += g * prev[s, here, :]
+            tile(forget, at, blocks)[...] += g * tile(prev, token, blocks)[...]
         return tuple(h)
 
     ends = lax.fori_loop(0, span, step, tuple(carry[s] for s in range(CHAINS)))
@@ -563,18 +575,22 @@
 
 
 def finish_kernel(
-    mine, theirs, w_grad, b_grad, e_grad, out_grad, o_grad, loss, eacc, *, groups, part, per, emb, shards, total_tokens
+    mine_a, mine_b, theirs_a, theirs_b, w_grad, b_grad, e_grad, out_grad, o_grad, loss, eacc, *, groups, part, per, emb, shards, total_tokens
 ):
-    count = 2 * mine.shape[0]
+    count = 2 * mine_a.shape[0]
     me = lax.axis_index("ctx")
     first = me % 2 == 0
     pairs = {}
+    stages = gather_stages_of(count)
 
     def chunk(q, rows):
         pair = q - q % 2
         if pair not in pairs:
-            slot = slot_of(pair ^ (me - me % 2), count)
-            own, other = mine[slot].astype(jnp.int32), theirs[slot].astype(jnp.int32)
+            slot = slot_of(pair ^ (me - me % 2), count, stages)
+            own, other = (
+                jnp.concatenate([a[slot].astype(jnp.int32), b[slot].astype(jnp.int32)], axis=0)
+                for a, b in ((mine_a, mine_b), (theirs_a, theirs_b))
+            )
             pairs[pair] = [
                 decode(jnp.where(first, own, other), groups), decode(jnp.where(first, other, own), groups)
             ]
@@ -709,38 +725,37 @@
         [marked],
         [tab, o_tab, seg, wt_own, bias_out, targets[None], ids[None]] + carries + tab_x + seg_x + wt_oth,
         [
-            hbm((toks, width), BF16), hbm(tokens, F32), hbm(tokens, F32),
+            hbm((toks, width), BF16), chip(*tokens), hbm(tokens, F32),
             *half_chunks(vpart), chip(CHAINS * blocks, LANE), hbm((count, blocks, LANE), F32),
             chip(vpad, width), hbm((vpad, LANE), F32),
         ],
         [
-            pltpu.VMEM(tokens, F32), pltpu.VMEM(tokens, F32), pltpu.VMEM(tokens, F32),
-            pltpu.VMEM((toks, width), BF16),
+            pltpu.VMEM(tokens, F32), pltpu.VMEM(tokens, F32), pltpu.VMEM((toks, width), BF16),
             pltpu.VMEM((toks, width), BF16), pltpu.VMEM((vpad, width), BF16), pltpu.VMEM((vpad, toks), F32), pltpu.VMEM(tokens, F32),
-            pltpu.VMEM((vpad, toks), BF16), pltpu.SemaphoreType.DMA((2,)), pltpu.SemaphoreType.DMA((toks // 512,)),
+            pltpu.VMEM((vpad, toks), BF16), pltpu.SemaphoreType.DMA, pltpu.SemaphoreType.DMA((toks // 512,)),
         ],
-        limit=52,
-        out_spaces=[pl.ANY] * 3 + [pltpu.VMEM] * 6,
+        limit=44,
+        out_spaces=[pl.ANY, pltpu.VMEM, pl.ANY] + [pltpu.VMEM] * 6,
         micros=26,
     )
-    heads, o_sum = near(heads), near(o_sum)
+    prev, heads, o_sum = near(prev), near(heads), near(o_sum)
     part = ceil_to(-(-kdim // splits), 8)
     per = ceil_to(-(-vpad // count), 8)
     h_all = exchange(head, "ctx")
     got_o = swap(send_o, "ctx", 1)
     length = toks // CHAINS
-    span = 16
+    span = 32
     block = pl.BlockSpec((CHAINS, span * blocks, LANE), lambda i: (0, length // span - 1 - i, 0))
     (sums,) = call(
         functools.partial(char_sum_kernel, copies=copies, blocks=blocks),
         "char_sums",
         [marked, block_of],
-        [tab, seg, heads, h_all, ps_all] + [far(v.reshape(CHAINS, length * blocks, LANE)) for v in (prev, src)],
+        [tab, seg, heads, h_all, ps_all, prev, far(src.reshape(CHAINS, length * blocks, LANE))],
         [chip(2, vpad * blocks, LANE)],
         [pltpu.SMEM((count,), jnp.int32), pltpu.VMEM((CHAINS, blocks, LANE), F32)]
         + [pltpu.VMEM((vpad * blocks, LANE), F32)] * (2 * copies),
         limit=24,
-        in_spaces=[pltpu.VMEM] * 5 + [block] * 2,
+        in_spaces=[pltpu.VMEM] * 6 + [block],
         micros=(9, length // span),
     )
     high, low, keep_e, send_e = call(
@@ -770,12 +785,12 @@
     chunk = reduce_chunks(
         [keep, keep_e, keep_o], [swap(send, "ctx", 1), swap(send_e, "ctx", 1), got_o], groups, "ctx"
     )
-    mine, theirs = gather_chunks(chunk, "ctx")
+    halves = gather_chunks(chunk, "ctx")
     w_grad, bi_grad, e_grad, w_out_grad, bo_grad, loss = call(
         functools.partial(finish_kernel, groups=groups, part=part, per=per, emb=emb, shards=wa, total_tokens=total_tokens),
         "finish",
         [],
-        [mine, theirs],
+        halves,
         [
             hbm((emb, gates, width), F32), hbm((gates, width), F32), hbm((vocab, emb), F32),
             hbm((vocab, width), F32), hbm((1, vocab), F32), hbm((1, 1), F32),

time: 157 us -> 151 us (0.962)
  Pallas kernels: 59.9 us -> 56 us
  starting transfers between devices: 43.5 us -> 40.2 us
    pallas_call x12 -> x15, Pallas kernels: 59.9 us -> 56 us  [call(): pl.pallas_call(kernel, grid=(steps,) if blocked else (), in_specs=[spec(p...]
    ppermute x22 -> x24, starting transfers between devices: 31.9 us -> 28.6 us  [swap(): return lax.ppermute(value, axis, [(k, k ^ mask) for k in range(count)])]
    ppermute x22 -> x24, waiting for transfers between devices: 21.1 us -> 22.5 us  [swap(): return lax.ppermute(value, axis, [(k, k ^ mask) for k in range(count)])]
  transfers between devices with their start and end apart: 27 -> 29, of which waited for: 12 -> 12; matrix products, arithmetic and copies ran while one was open for 0% -> 0% of each run, Pallas kernels for 2% -> 2%
where the time goes in v4:
time: 151 us
  Pallas kernels  56 us (37%)
  starting transfers between devices  40.2 us (27%)
  waiting for transfers between devices  33.5 us (22%)
  blocking collectives  13.1 us (9%)
  local copies, waits for them, and re-layouts  4.49 us (3%)
  other arithmetic  2.42 us (2%)
    pallas_call x15, Pallas kernels, call(): pl.pallas_call(kernel, grid=(steps,) if blocked else (), in_specs=[spec(p...  56 us
    ppermute x24, starting transfers between devices, swap(): return lax.ppermute(value, axis, [(k, k ^ mask) for k in range(count)])  28.6 us
    ppermute x24, waiting for transfers between devices, swap(): return lax.ppermute(value, axis, [(k, k ^ mask) for k in range(count)])  22.5 us
    all_to_all x1, blocking collectives, exchange(): return lax.all_to_all(copies, axis, 0, 0, tiled=True)  13.1 us
    all_to_all x1, waiting for transfers between devices, exchange(): return lax.all_to_all(copies, axis, 0, 0, tiled=True)  7.34 us
    all_to_all x1, starting transfers between devices, exchange(): return lax.all_to_all(copies, axis, 0, 0, tiled=True)  5.93 us
    ppermute x4, starting transfers between devices, from_others(): lax.ppermute(value, 'wa', [(k, (k - s) % wa) for k in range(wa)])  5.62 us
    unnamed x41, local copies, waits for them, and re-layouts  3.61 us
  transfers between devices with their start and end apart: 29, of which 12 were waited for; matrix products, arithmetic and copies ran while one was open for 0% of the time, Pallas kernels for 2%

profile of v4, /device:TPU:0, one launch (start us, length us, event | category | flops | bytes accessed | tf_op | source)
XLA Modules:
  0.0 150.6 jit_solution(18382605112847416708)
XLA Ops:
  1.6 1.4 copy.36
  4.8 6.2 %tables_own.1 = (s32[2048]{0:T(1024)S(1)}, s32[4]{0:T(128)S(1)}, f32[4608,128]{1,0:T(8,128)S(1)}, f32[16,2,8,128]{3,2,1,0:T(8,128)}, f32[16,2,8,128]{3,2,1,0:T(8...) custom-call(s32[4]{0:T(128)S(1)} %copy-done.13, s32[16]{0:T(128)S(1)} %copy-done.12, ...), custom_call_target="tpu_custom_call" | custom-call | bytes 18000000 | tf_op jit(solution)/shard_map/tables_own/pallas_call | solution.py:24
  11.0 1.4 copy-done
  12.4 2.9 %collective-permute-start.1 = (bf16[2,112,1024]{2,1,0:T(8,128)(2,1)}, bf16[2,112,1024]{2,1,0:T(8,128)(2,1)S(1)}, u32[]{:S(2)}, u32[]{:S(2)}) collective-permute-start(bf16[2,112,1024]{2,1,0:T(8,128)(2,1)} %get-tuple-element.52), channel_id=1, source_target_pairs={{0,1},{1,0},{2,3},{3,2},{4,5},{5,4},{6,7},{7,6},{8,9},{9,8},{10,11... | collective-permute-start | bytes 1376264 | tf_op jit(solution)/shard_map/ppermute | solution.py:635
  15.3 5.9 %all-to-all-start = ((f32[16,2,8,128]{3,2,1,0:T(8,128)}), f32[16,2,8,128]{3,2,1,0:T(8,128)S(1)}, u32[]{:S(2)}, u32[]{:S(2)}) async-start(f32[16,2,8,128]{3,2,1,0:T(8,128)} %get-tuple-element.51), calls=%async_computation | async-start | bytes 262144 | tf_op jit(solution)/shard_map/all_to_all | solution.py:71
  21.8 7.3 %all-to-all-done.ps_all = f32[16,2,8,128]{3,2,1,0:T(8,128)S(1)} async-done(((f32[16,2,8,128]{3,2,1,0:T(8,128)}), f32[16,2,8,128]{3,2,1,0:T(8,128)S(1)}, u32[]{:S(2)}, u32[]{:S(2)}) %all-to-all-start) | async-done | bytes 131104 | tf_op jit(solution)/shard_map/all_to_all | solution.py:71
  31.1 1.3 collective-permute-done.4.refs_12_
  32.4 1.8 %collective-permute-start.3 = (f32[16,2,8,128]{3,2,1,0:T(8,128)S(1)}, f32[16,2,8,128]{3,2,1,0:T(8,128)S(1)}, u32[]{:S(2)}, u32[]{:S(2)}) collective-permute-start(f32[16,2,8,128]{3,2,1,0:T(8,128)S(1)} %copy-done.5), channel_id=1, source_target_pairs={{0,1},{1,0},{2,3},{3,2},{4,5},{5,4},{6,7},{7,6},{8,9},{9,8},{10,11... | collective-permute-start | bytes 393224 | tf_op jit(solution)/shard_map/ppermute | solution.py:635
  34.5 1.6 %tables_other.1.refs_10_ = f32[6912,128]{1,0:T(8,128)S(1)} custom-call(s32[4]{0:T(128)S(1)} %get-tuple-element.48.spots, bf16[288,112]{1,0:T(8,128)(2,1)S(1)} %and_select_fusion.embed.table, bf16[2,112,1024]{2,1,0:T(8,128)(2,1)S(1)} %collective-permute-done.1.direct, bf16[2,112,1024]{2,1,0:T(8,128)(2,1)S(1)} %collective-permute-done.2.passed), custom_call_target="tpu_custom_call" | custom-call | bytes 9000000 | tf_op jit(solution)/shard_map/tables_other/pallas_call | solution.py:24
  36.0 2.3 %collective-permute-done.3.refs_11_ = f32[16,2,8,128]{3,2,1,0:T(8,128)S(1)} collective-permute-done((f32[16,2,8,128]{3,2,1,0:T(8,128)S(1)}, f32[16,2,8,128]{3,2,1,0:T(8,128)S(1)}, u32[]{:S(2)}, u32[]{:S(2)}) %collective-permute-start.3) | collective-permute-done | bytes 131104 | tf_op jit(solution)/shard_map/ppermute | solution.py:635
  39.1 26.4 %cells.1 = (bf16[2048,1024]{1,0:T(8,128)(2,1)}, f32[16384,128]{1,0:T(8,128)S(1)}, f32[16384,128]{1,0:T(8,128)}, f32[8,144,128]{2,1,0:T(8,128)}, f32[8,144,128]{2...) custom-call(s32[2048]{0:T(1024)} %copy-done.9, ...), custom_call_target="tpu_custom_call" | custom-call | bytes 78000000 | tf_op jit(solution)/shard_map/cells/pallas_call | solution.py:24
  65.5 13.1 %all_to_all.10.h_all = f32[16,8,128]{2,1,0:T(8,128)S(1)} all-to-all(f32[16,8,128]{2,1,0:T(8,128)} %get-tuple-element.58), channel_id=1, replica_groups=mesh['ctx'=16,'wa'=2] {'ctx'}, dimensions={0} | all-to-all | bytes 131072 | tf_op jit(solution)/shard_map/all_to_all | solution.py:71
  78.6 9.0 %char_sums.1.sums = f32[2,2304,128]{2,1,0:T(8,128)S(1)} custom-call(s32[2048]{0:T(1024)S(1)} %copy-done.10, s32[16]{0:T(128)S(1)} %copy-done.12, f32[4608,128]{1,0:T(8,128)S(1)} %copy-done.1, f32[16,2,8,128]{3,2,1,0:T(8,128)S(1)} %copy-done.6, f32[128,128]{1,0:T(8,128)S(1)} %get-tuple-element.57.heads, f32[16,8,128]{2,1,0:T(8,128)S(1)} %all_to_all.10.h_all, ...), custom_call_target="tpu_custom_call" | custom-call | bytes 27000000 | tf_op jit(solution)/shard_map/char_sums/pallas_call | solution.py:24
  87.6 4.1 %gate_sums.1 = (bf16[4,288,1024]{2,1,0:T(8,128)(2,1)S(1)}, bf16[4,288,1024]{2,1,0:T(8,128)(2,1)S(1)}, f32[8,24,128]{2,1,0:T(8,128)S(1)}, f32[8,24,128]{2,1,0:T(8,128)S(1)}) custom-call(s32[4]{0:T(128)S(1)} %get-tuple-element.48.spots, f32[2,2304,128]{2,1,0:T(8,128)S(1)} %char_sums.1.sums, f32[288,1024]{1,0:T(8,128)S(1)} %get-tuple-element.61.o_sum, ...), custom_call_target="tpu_custom_call" | custom-call | bytes 9000000 | tf_op jit(solution)/shard_map/gate_sums/pallas_call | solution.py:24
  91.7 1.3 input_grad.1
  93.6 1.5 collective-permute-start.8
  95.6 3.6 %collective-permute-done.8 = f32[8,24,128]{2,1,0:T(8,128)S(1)} collective-permute-done((f32[8,24,128]{2,1,0:T(8,128)S(1)}, f32[8,24,128]{2,1,0:T(8,128)S(1)}, u32[]{:S(2)}, u32[]{:S(2)}) %collective-permute-start.8) | collective-permute-done | bytes 98336 | tf_op jit(solution)/shard_map/ppermute | solution.py:67
  100.7 1.3 core_sum.1
  102.9 2.7 %collective-permute-start.13 = (s16[1,400,128]{2,1,0:T(8,128)(2,1)S(1)}, s16[1,400,128]{2,1,0:T(8,128)(2,1)S(1)}, u32[]{:S(2)}, u32[]{:S(2)}) collective-permute-start(s16[1,400,128]{2,1,0:T(8,128)(2,1)S(1)} %get-tuple-element.74), channel_id=1, source_target_pairs={{0,12},{2,14},{4,8},{6,10},{8,4},{10,6},{12,0},{14,2},{16,28},{18,... | collective-permute-start | bytes 307208 | tf_op jit(solution)/shard_map/ppermute | solution.py:67
  105.9 2.3 %collective-permute-start.15 = (s16[1,400,128]{2,1,0:T(8,128)(2,1)S(1)}, s16[1,400,128]{2,1,0:T(8,128)(2,1)S(1)}, u32[]{:S(2)}, u32[]{:S(2)}) collective-permute-start(s16[1,400,128]{2,1,0:T(8,128)(2,1)S(1)} %get-tuple-element.76), channel_id=1, source_target_pairs={{0,20},{2,22},{4,16},{6,18},{8,28},{10,30},{12,24},{14,26},{16,4},... | collective-permute-start | bytes 307208 | tf_op jit(solution)/shard_map/ppermute | solution.py:67
  109.1 4.1 %collective-permute-start.17 = (s16[1,400,128]{2,1,0:T(8,128)(2,1)S(1)}, s16[1,400,128]{2,1,0:T(8,128)(2,1)S(1)}, u32[]{:S(2)}, u32[]{:S(2)}) collective-permute-start(s16[1,400,128]{2,1,0:T(8,128)(2,1)S(1)} %get-tuple-element.78), channel_id=1, source_target_pairs={{0,28},{2,30},{4,24},{6,26},{8,20},{10,22},{12,16},{14,18},{16,12}... | collective-permute-start | bytes 307208 | tf_op jit(solution)/shard_map/ppermute | solution.py:67
  113.2 7.1 %collective-permute-done.14.refs_4_ = s16[1,400,128]{2,1,0:T(8,128)(2,1)S(1)} collective-permute-done((s16[1,400,128]{2,1,0:T(8,128)(2,1)S(1)}, s16[1,400,128]{2,1,0:T(8,128)(2,1)S(1)}, u32[]{:S(2)}, u32[]{:S(2)}) %collective-permute-start.14) | collective-permute-done | bytes 102432 | tf_op jit(solution)/shard_map/ppermute | solution.py:67
  120.3 2.3 %collective-permute-done.15.refs_5_ = s16[1,400,128]{2,1,0:T(8,128)(2,1)S(1)} collective-permute-done((s16[1,400,128]{2,1,0:T(8,128)(2,1)S(1)}, s16[1,400,128]{2,1,0:T(8,128)(2,1)S(1)}, u32[]{:S(2)}, u32[]{:S(2)}) %collective-permute-start.15) | collective-permute-done | bytes 102432 | tf_op jit(solution)/shard_map/ppermute | solution.py:67
  124.2 4.2 %collective-permute-start.19 = (s16[1,208,128]{2,1,0:T(8,128)(2,1)S(1)}, s16[1,208,128]{2,1,0:T(8,128)(2,1)S(1)}, u32[]{:S(2)}, u32[]{:S(2)}) collective-permute-start(s16[1,208,128]{2,1,0:T(8,128)(2,1)S(1)} %slice.8.refs_0_), channel_id=1, source_target_pairs={{0,16},{2,18},{4,20},{6,22},{8,24},{10,26},{12,28},{14,30},{16,0},... | collective-permute-start | bytes 159752 | tf_op jit(solution)/shard_map/ppermute | solution.py:67
  128.4 1.5 collective-permute-start.24
  129.9 2.0 %collective-permute-start.23 = (s16[1,192,128]{2,1,0:T(8,128)(2,1)S(1)}, s16[1,192,128]{2,1,0:T(8,128)(2,1)S(1)}, u32[]{:S(2)}, u32[]{:S(2)}) collective-permute-start(s16[1,192,128]{2,1,0:T(8,128)(2,1)S(1)} %slice.9.refs_0_), channel_id=1, source_target_pairs={{0,16},{2,18},{4,20},{6,22},{8,24},{10,26},{12,28},{14,30},{16,0},... | collective-permute-start | bytes 147464 | tf_op jit(solution)/shard_map/ppermute | solution.py:67
  133.7 2.7 %collective-permute-start.21 = (s16[4,208,128]{2,1,0:T(8,128)(2,1)S(1)}, s16[4,208,128]{2,1,0:T(8,128)(2,1)S(1)}, u32[]{:S(2)}, u32[]{:S(2)}) collective-permute-start(s16[4,208,128]{2,1,0:T(8,128)(2,1)S(1)} %chunk_join0.2.refs_0_), channel_id=1, source_target_pairs={{0,4},{2,6},{4,0},{6,2},{8,12},{10,14},{12,8},{14,10},{16,20},{18,... | collective-permute-start | bytes 638984 | tf_op jit(solution)/shard_map/ppermute | solution.py:67
  136.4 2.2 %collective-permute-start.25 = (s16[4,192,128]{2,1,0:T(8,128)(2,1)S(1)}, s16[4,192,128]{2,1,0:T(8,128)(2,1)S(1)}, u32[]{:S(2)}, u32[]{:S(2)}) collective-permute-start(s16[4,192,128]{2,1,0:T(8,128)(2,1)S(1)} %chunk_join0.3.refs_0_), channel_id=1, source_target_pairs={{0,4},{2,6},{4,0},{6,2},{8,12},{10,14},{12,8},{14,10},{16,20},{18,... | collective-permute-start | bytes 589832 | tf_op jit(solution)/shard_map/ppermute | solution.py:67
  138.7 3.6 %collective-permute-done.21.refs_1_ = s16[4,208,128]{2,1,0:T(8,128)(2,1)S(1)} collective-permute-done((s16[4,208,128]{2,1,0:T(8,128)(2,1)S(1)}, s16[4,208,128]{2,1,0:T(8,128)(2,1)S(1)}, u32[]{:S(2)}, u32[]{:S(2)}) %collective-permute-start.21) | collective-permute-done | bytes 213024 | tf_op jit(solution)/shard_map/ppermute | solution.py:67
  142.4 2.0 %collective-permute-done.25.refs_1_ = s16[4,192,128]{2,1,0:T(8,128)(2,1)S(1)} collective-permute-done((s16[4,192,128]{2,1,0:T(8,128)(2,1)S(1)}, s16[4,192,128]{2,1,0:T(8,128)(2,1)S(1)}, u32[]{:S(2)}, u32[]{:S(2)}) %collective-permute-start.25) | collective-permute-done | bytes 196640 | tf_op jit(solution)/shard_map/ppermute | solution.py:67
  144.5 1.7 %collective-permute-done.27.theirs_b = s16[8,192,128]{2,1,0:T(8,128)(2,1)S(1)} collective-permute-done((s16[8,192,128]{2,1,0:T(8,128)(2,1)S(1)}, s16[8,192,128]{2,1,0:T(8,128)(2,1)S(1)}, u32[]{:S(2)}, u32[]{:S(2)}) %collective-permute-start.27) | collective-permute-done | bytes 393248 | tf_op jit(solution)/shard_map/ppermute | solution.py:67
  146.3 3.8 %finish.1 = (f32[100,4,1024]{2,1,0:T(4,128)}, f32[4,1024]{1,0:T(4,128)}, f32[275,100]{1,0:T(8,128)}, f32[275,1024]{1,0:T(8,128)}, f32[1,275]{1,0:T(1,128)S(1)}, /*index=5*/f32[1,1]{1,0:T(1,128)}) custom-call(s16[8,208,128]{2,1,0:T(8,128)(2,1)S(1)} %chunk_join1.2.mine_a, s16[8,192,128]{2,1,0:T(8,128)(2,1)S(1)} %chunk_join1.3.mine_b, ...), custom_call_target="tpu_custom_call" | custom-call | bytes 3000000 | tf_op jit(solution)/shard_map/finish/pallas_call | solution.py:24
  (99 shorter events, 15.2 us)
Async XLA Ops:
  3.0 26.2 %copy-start.18 = (f32[275]{0:T(512)S(1)}, f32[275]{0:T(512)}, u32[]{:S(2)}) copy-start(f32[275]{0:T(512)} %param.17) | copy-start | bytes 3304
  12.4 16.8 %collective-permute-start.1 = (bf16[2,112,1024]{2,1,0:T(8,128)(2,1)}, bf16[2,112,1024]{2,1,0:T(8,128)(2,1)S(1)}, u32[]{:S(2)}, u32[]{:S(2)}) collective-permute-start(bf16[2,112,1024]{2,1,0:T(8,128)(2,1)} %get-tuple-element.52), channel_id=1, source_target_pairs={{0,1},{1,0},{2,3},{3,2},{4,5},{5,4},{6,7},{7,6},{8,9},{9,8},{10,11... | collective-permute-start | bytes 1376264 | tf_op jit(solution)/shard_map/ppermute | solution.py:635
  15.3 13.9 %all-to-all-start = ((f32[16,2,8,128]{3,2,1,0:T(8,128)}), f32[16,2,8,128]{3,2,1,0:T(8,128)S(1)}, u32[]{:S(2)}, u32[]{:S(2)}) async-start(f32[16,2,8,128]{3,2,1,0:T(8,128)} %get-tuple-element.51), calls=%async_computation | async-start | bytes 262144 | tf_op jit(solution)/shard_map/all_to_all | solution.py:71
  21.2 11.1 %collective-permute-start.4 = (bf16[144,1024]{1,0:T(8,128)(2,1)}, bf16[144,1024]{1,0:T(8,128)(2,1)S(1)}, u32[]{:S(2)}, u32[]{:S(2)}) collective-permute-start(bf16[144,1024]{1,0:T(8,128)(2,1)} %get-tuple-element.54), channel_id=1, source_target_pairs={{0,1},{1,0},{2,3},{3,2},{4,5},{5,4},{6,7},{7,6},{8,9},{9,8},{10,11... | collective-permute-start | bytes 884744 | tf_op jit(solution)/shard_map/ppermute | solution.py:635
  29.2 5.3 %collective-permute-start.2 = (bf16[2,112,1024]{2,1,0:T(8,128)(2,1)S(1)}, bf16[2,112,1024]{2,1,0:T(8,128)(2,1)S(1)}, u32[]{:S(2)}, u32[]{:S(2)}) collective-permute-start(bf16[2,112,1024]{2,1,0:T(8,128)(2,1)S(1)} %collective-permute-done.1.direct), channel_id=1, source_target_pairs={{0,2},{2,0},{4,6},{6,4},{8,10},{10,8},{12,14},{14,12},{16,18},{18,... | collective-permute-start | bytes 1376264 | tf_op jit(solution)/shard_map/ppermute | solution.py:67
  32.3 6.0 %collective-permute-start.5 = (bf16[144,1024]{1,0:T(8,128)(2,1)S(1)}, bf16[144,1024]{1,0:T(8,128)(2,1)S(1)}, u32[]{:S(2)}, u32[]{:S(2)}) collective-permute-start(bf16[144,1024]{1,0:T(8,128)(2,1)S(1)} %collective-permute-done.4.refs_12_), channel_id=1, source_target_pairs={{0,2},{2,0},{4,6},{6,4},{8,10},{10,8},{12,14},{14,12},{16,18},{18,... | collective-permute-start | bytes 884744 | tf_op jit(solution)/shard_map/ppermute | solution.py:67
  32.4 6.0 %collective-permute-start.3 = (f32[16,2,8,128]{3,2,1,0:T(8,128)S(1)}, f32[16,2,8,128]{3,2,1,0:T(8,128)S(1)}, u32[]{:S(2)}, u32[]{:S(2)}) collective-permute-start(f32[16,2,8,128]{3,2,1,0:T(8,128)S(1)} %copy-done.5), channel_id=1, source_target_pairs={{0,1},{1,0},{2,3},{3,2},{4,5},{5,4},{6,7},{7,6},{8,9},{9,8},{10,11... | collective-permute-start | bytes 393224 | tf_op jit(solution)/shard_map/ppermute | solution.py:635
  34.2 4.2 %collective-permute-start = (f32[8,128]{1,0:T(8,128)S(1)}, f32[8,128]{1,0:T(8,128)S(1)}, u32[]{:S(2)}, u32[]{:S(2)}) collective-permute-start(f32[8,128]{1,0:T(8,128)S(1)} %carry.1.refs_8_), channel_id=1, source_target_pairs={{0,1},{1,0},{2,3},{3,2},{4,5},{5,4},{6,7},{7,6},{8,9},{9,8},{10,11... | collective-permute-start | bytes 12296 | tf_op jit(solution)/shard_map/ppermute | solution.py:635
  39.1 39.5 %copy-start.6 = (f32[16,2,8,128]{3,2,1,0:T(8,128)S(1)}, f32[16,2,8,128]{3,2,1,0:T(8,128)}, u32[]{:S(2)}) copy-start(f32[16,2,8,128]{3,2,1,0:T(8,128)} %get-tuple-element.49.refs_3_.seg) | copy-start | bytes 393220
  39.1 39.5 %copy-start.10 = (s32[2048]{0:T(1024)S(1)}, s32[2048]{0:T(1024)}, u32[]{:S(2)}) copy-start(s32[2048]{0:T(1024)} %copy-done.9) | copy-start | bytes 24580
  93.0 7.6 %collective-permute-start.7 = (f32[8,224,128]{2,1,0:T(8,128)S(1)}, f32[8,224,128]{2,1,0:T(8,128)S(1)}, u32[]{:S(2)}, u32[]{:S(2)}) collective-permute-start(f32[8,224,128]{2,1,0:T(8,128)S(1)} %get-tuple-element.68), channel_id=1, source_target_pairs={{0,2},{2,0},{4,6},{6,4},{8,10},{10,8},{12,14},{14,12},{16,18},{18,... | collective-permute-start | bytes 2752520 | tf_op jit(solution)/shard_map/ppermute | solution.py:67
  93.1 7.5 %collective-permute-start.10 = (f32[8,144,128]{2,1,0:T(8,128)S(1)}, f32[8,144,128]{2,1,0:T(8,128)S(1)}, u32[]{:S(2)}, u32[]{:S(2)}) collective-permute-start(f32[8,144,128]{2,1,0:T(8,128)S(1)} %copy-done.19), channel_id=1, source_target_pairs={{0,2},{2,0},{4,6},{6,4},{8,10},{10,8},{12,14},{14,12},{16,18},{18,... | collective-permute-start | bytes 1769480 | tf_op jit(solution)/shard_map/ppermute | solution.py:67
  93.6 5.7 %collective-permute-start.8 = (f32[8,24,128]{2,1,0:T(8,128)S(1)}, f32[8,24,128]{2,1,0:T(8,128)S(1)}, u32[]{:S(2)}, u32[]{:S(2)}) collective-permute-start(f32[8,24,128]{2,1,0:T(8,128)S(1)} %get-tuple-element.69), channel_id=1, source_target_pairs={{0,1},{1,0},{2,3},{3,2},{4,5},{5,4},{6,7},{7,6},{8,9},{9,8},{10,11... | collective-permute-start | bytes 294920 | tf_op jit(solution)/shard_map/ppermute | solution.py:67
  95.1 5.4 %collective-permute-start.6 = (f32[8,24,128]{2,1,0:T(8,128)S(1)}, f32[8,24,128]{2,1,0:T(8,128)S(1)}, u32[]{:S(2)}, u32[]{:S(2)}) collective-permute-start(f32[8,24,128]{2,1,0:T(8,128)S(1)} %get-tuple-element.66), channel_id=1, source_target_pairs={{0,1},{1,0},{2,3},{3,2},{4,5},{5,4},{6,7},{7,6},{8,9},{9,8},{10,11... | collective-permute-start | bytes 294920 | tf_op jit(solution)/shard_map/ppermute | solution.py:67
  99.3 1.4 collective-permute-start.9
  102.0 6.1 %collective-permute-start.11 = (s16[1,400,128]{2,1,0:T(8,128)(2,1)S(1)}, s16[1,400,128]{2,1,0:T(8,128)(2,1)S(1)}, u32[]{:S(2)}, u32[]{:S(2)}) collective-permute-start(s16[1,400,128]{2,1,0:T(8,128)(2,1)S(1)} %get-tuple-element.72), channel_id=1, source_target_pairs={{0,4},{2,6},{4,0},{6,2},{8,12},{10,14},{12,8},{14,10},{16,20},{18,... | collective-permute-start | bytes 307208 | tf_op jit(solution)/shard_map/ppermute | solution.py:67
  102.3 6.9 %collective-permute-start.12 = (s16[1,400,128]{2,1,0:T(8,128)(2,1)S(1)}, s16[1,400,128]{2,1,0:T(8,128)(2,1)S(1)}, u32[]{:S(2)}, u32[]{:S(2)}) collective-permute-start(s16[1,400,128]{2,1,0:T(8,128)(2,1)S(1)} %get-tuple-element.73), channel_id=1, source_target_pairs={{0,8},{2,10},{4,12},{6,14},{8,0},{10,2},{12,4},{14,6},{16,24},{18,... | collective-permute-start | bytes 307208 | tf_op jit(solution)/shard_map/ppermute | solution.py:67
  102.9 10.3 %collective-permute-start.13 = (s16[1,400,128]{2,1,0:T(8,128)(2,1)S(1)}, s16[1,400,128]{2,1,0:T(8,128)(2,1)S(1)}, u32[]{:S(2)}, u32[]{:S(2)}) collective-permute-start(s16[1,400,128]{2,1,0:T(8,128)(2,1)S(1)} %get-tuple-element.74), channel_id=1, source_target_pairs={{0,12},{2,14},{4,8},{6,10},{8,4},{10,6},{12,0},{14,2},{16,28},{18,... | collective-permute-start | bytes 307208 | tf_op jit(solution)/shard_map/ppermute | solution.py:67
  105.5 14.7 %collective-permute-start.14 = (s16[1,400,128]{2,1,0:T(8,128)(2,1)S(1)}, s16[1,400,128]{2,1,0:T(8,128)(2,1)S(1)}, u32[]{:S(2)}, u32[]{:S(2)}) collective-permute-start(s16[1,400,128]{2,1,0:T(8,128)(2,1)S(1)} %get-tuple-element.75), channel_id=1, source_target_pairs={{0,16},{2,18},{4,20},{6,22},{8,24},{10,26},{12,28},{14,30},{16,0},... | collective-permute-start | bytes 307208 | tf_op jit(solution)/shard_map/ppermute | solution.py:67
  105.9 16.7 %collective-permute-start.15 = (s16[1,400,128]{2,1,0:T(8,128)(2,1)S(1)}, s16[1,400,128]{2,1,0:T(8,128)(2,1)S(1)}, u32[]{:S(2)}, u32[]{:S(2)}) collective-permute-start(s16[1,400,128]{2,1,0:T(8,128)(2,1)S(1)} %get-tuple-element.76), channel_id=1, source_target_pairs={{0,20},{2,22},{4,16},{6,18},{8,28},{10,30},{12,24},{14,26},{16,4},... | collective-permute-start | bytes 307208 | tf_op jit(solution)/shard_map/ppermute | solution.py:67
  108.1 14.4 %collective-permute-start.16 = (s16[1,400,128]{2,1,0:T(8,128)(2,1)S(1)}, s16[1,400,128]{2,1,0:T(8,128)(2,1)S(1)}, u32[]{:S(2)}, u32[]{:S(2)}) collective-permute-start(s16[1,400,128]{2,1,0:T(8,128)(2,1)S(1)} %get-tuple-element.77), channel_id=1, source_target_pairs={{0,24},{2,26},{4,28},{6,30},{8,16},{10,18},{12,20},{14,22},{16,8},... | collective-permute-start | bytes 307208 | tf_op jit(solution)/shard_map/ppermute | solution.py:67
  109.1 13.4 %collective-permute-start.17 = (s16[1,400,128]{2,1,0:T(8,128)(2,1)S(1)}, s16[1,400,128]{2,1,0:T(8,128)(2,1)S(1)}, u32[]{:S(2)}, u32[]{:S(2)}) collective-permute-start(s16[1,400,128]{2,1,0:T(8,128)(2,1)S(1)} %get-tuple-element.78), channel_id=1, source_target_pairs={{0,28},{2,30},{4,24},{6,26},{8,20},{10,22},{12,16},{14,18},{16,12}... | collective-permute-start | bytes 307208 | tf_op jit(solution)/shard_map/ppermute | solution.py:67
  123.1 8.7 %collective-permute-start.20 = (s16[1,208,128]{2,1,0:T(8,128)(2,1)S(1)}, s16[1,208,128]{2,1,0:T(8,128)(2,1)S(1)}, u32[]{:S(2)}, u32[]{:S(2)}) collective-permute-start(s16[1,208,128]{2,1,0:T(8,128)(2,1)S(1)} %slice.8.refs_0_), channel_id=1, source_target_pairs={{0,24},{2,26},{4,28},{6,30},{8,16},{10,18},{12,20},{14,22},{16,8},... | collective-permute-start | bytes 159752 | tf_op jit(solution)/shard_map/ppermute | solution.py:67
  124.2 9.5 %collective-permute-start.19 = (s16[1,208,128]{2,1,0:T(8,128)(2,1)S(1)}, s16[1,208,128]{2,1,0:T(8,128)(2,1)S(1)}, u32[]{:S(2)}, u32[]{:S(2)}) collective-permute-start(s16[1,208,128]{2,1,0:T(8,128)(2,1)S(1)} %slice.8.refs_0_), channel_id=1, source_target_pairs={{0,16},{2,18},{4,20},{6,22},{8,24},{10,26},{12,28},{14,30},{16,0},... | collective-permute-start | bytes 159752 | tf_op jit(solution)/shard_map/ppermute | solution.py:67
  128.4 5.3 %collective-permute-start.18 = (s16[1,208,128]{2,1,0:T(8,128)(2,1)S(1)}, s16[1,208,128]{2,1,0:T(8,128)(2,1)S(1)}, u32[]{:S(2)}, u32[]{:S(2)}) collective-permute-start(s16[1,208,128]{2,1,0:T(8,128)(2,1)S(1)} %slice.8.refs_0_), channel_id=1, source_target_pairs={{0,8},{2,10},{4,12},{6,14},{8,0},{10,2},{12,4},{14,6},{16,24},{18,... | collective-permute-start | bytes 159752 | tf_op jit(solution)/shard_map/ppermute | solution.py:67
  128.4 8.0 %collective-permute-start.24 = (s16[1,192,128]{2,1,0:T(8,128)(2,1)S(1)}, s16[1,192,128]{2,1,0:T(8,128)(2,1)S(1)}, u32[]{:S(2)}, u32[]{:S(2)}) collective-permute-start(s16[1,192,128]{2,1,0:T(8,128)(2,1)S(1)} %slice.9.refs_0_), channel_id=1, source_target_pairs={{0,24},{2,26},{4,28},{6,30},{8,16},{10,18},{12,20},{14,22},{16,8},... | collective-permute-start | bytes 147464 | tf_op jit(solution)/shard_map/ppermute | solution.py:67
  129.9 6.5 %collective-permute-start.23 = (s16[1,192,128]{2,1,0:T(8,128)(2,1)S(1)}, s16[1,192,128]{2,1,0:T(8,128)(2,1)S(1)}, u32[]{:S(2)}, u32[]{:S(2)}) collective-permute-start(s16[1,192,128]{2,1,0:T(8,128)(2,1)S(1)} %slice.9.refs_0_), channel_id=1, source_target_pairs={{0,16},{2,18},{4,20},{6,22},{8,24},{10,26},{12,28},{14,30},{16,0},... | collective-permute-start | bytes 147464 | tf_op jit(solution)/shard_map/ppermute | solution.py:67
  131.9 4.5 %collective-permute-start.22 = (s16[1,192,128]{2,1,0:T(8,128)(2,1)S(1)}, s16[1,192,128]{2,1,0:T(8,128)(2,1)S(1)}, u32[]{:S(2)}, u32[]{:S(2)}) collective-permute-start(s16[1,192,128]{2,1,0:T(8,128)(2,1)S(1)} %slice.9.refs_0_), channel_id=1, source_target_pairs={{0,8},{2,10},{4,12},{6,14},{8,0},{10,2},{12,4},{14,6},{16,24},{18,... | collective-permute-start | bytes 147464 | tf_op jit(solution)/shard_map/ppermute | solution.py:67
  133.7 8.6 %collective-permute-start.21 = (s16[4,208,128]{2,1,0:T(8,128)(2,1)S(1)}, s16[4,208,128]{2,1,0:T(8,128)(2,1)S(1)}, u32[]{:S(2)}, u32[]{:S(2)}) collective-permute-start(s16[4,208,128]{2,1,0:T(8,128)(2,1)S(1)} %chunk_join0.2.refs_0_), channel_id=1, source_target_pairs={{0,4},{2,6},{4,0},{6,2},{8,12},{10,14},{12,8},{14,10},{16,20},{18,... | collective-permute-start | bytes 638984 | tf_op jit(solution)/shard_map/ppermute | solution.py:67
  136.4 8.0 %collective-permute-start.25 = (s16[4,192,128]{2,1,0:T(8,128)(2,1)S(1)}, s16[4,192,128]{2,1,0:T(8,128)(2,1)S(1)}, u32[]{:S(2)}, u32[]{:S(2)}) collective-permute-start(s16[4,192,128]{2,1,0:T(8,128)(2,1)S(1)} %chunk_join0.3.refs_0_), channel_id=1, source_target_pairs={{0,4},{2,6},{4,0},{6,2},{8,12},{10,14},{12,8},{14,10},{16,20},{18,... | collective-permute-start | bytes 589832 | tf_op jit(solution)/shard_map/ppermute | solution.py:67
  142.4 3.9 %collective-permute-start.26 = (s16[8,208,128]{2,1,0:T(8,128)(2,1)S(1)}, s16[8,208,128]{2,1,0:T(8,128)(2,1)S(1)}, u32[]{:S(2)}, u32[]{:S(2)}) collective-permute-start(s16[8,208,128]{2,1,0:T(8,128)(2,1)S(1)} %chunk_join1.2.mine_a), channel_id=1, source_target_pairs={{0,2},{2,0},{4,6},{6,4},{8,10},{10,8},{12,14},{14,12},{16,18},{18,... | collective-permute-start | bytes 1277960 | tf_op jit(solution)/shard_map/ppermute | solution.py:67
  144.5 1.8 %collective-permute-start.27 = (s16[8,192,128]{2,1,0:T(8,128)(2,1)S(1)}, s16[8,192,128]{2,1,0:T(8,128)(2,1)S(1)}, u32[]{:S(2)}, u32[]{:S(2)}) collective-permute-start(s16[8,192,128]{2,1,0:T(8,128)(2,1)S(1)} %chunk_join1.3.mine_b), channel_id=1, source_target_pairs={{0,2},{2,0},{4,6},{6,4},{8,10},{10,8},{12,14},{14,12},{16,18},{18,... | collective-permute-start | bytes 1179656 | tf_op jit(solution)/shard_map/ppermute | solution.py:67
  (17 other events, 104.2 us)

commit v5 on v4

--- a/solution.py
+++ b/solution.py
@@ -93,8 +93,28 @@
     return value
 
 
-def coded_rows(groups):
+def section_rows(groups):
     return ceil_to(sum(groups) + len(groups), 16)
+
+
+def coded_rows(sections):
+    return sum(section_rows(groups) for groups in sections)
+
+
+def encode_all(value, sections):
+    parts, at = [], 0
+    for groups in sections:
+        parts.append(encode(value[at:at + sum(groups)], groups))
+        at += sum(groups)
+    return jnp.concatenate(parts, axis=0)
+
+
+def decode_all(code, sections):
+    parts, at = [], 0
+    for groups in sections:
+        parts.append(decode(code[at:at + section_rows(groups)], groups))
+        at += section_rows(groups)
+    return jnp.concatenate(parts, axis=0)
 
 
 def encode(value, groups):
@@ -107,7 +127,7 @@
         parts.append(jnp.round(part * (STEPS / power_of_two(exponent))).astype(jnp.int32))
         exponents.append(exponent)
         at += size
-    fill = coded_rows(groups) - at - len(groups)
+    fill = section_rows(groups) - at - len(groups)
     if fill:
         exponents.append(jnp.zeros((fill, value.shape[1]), jnp.int32))
     return jnp.concatenate(parts + exponents, axis=0).astype(jnp.int16)
@@ -123,11 +143,11 @@
     return jnp.concatenate(parts, axis=0)
 
 
-def reduce_chunks(keeps, moved, groups, axis):
+def reduce_chunks(keeps, moved, sections, axis):
     stages = stages_of(lax.axis_size(axis))[1:]
     number = len(keeps)
     sizes = [k.shape[1] for k in keeps]
-    rows, coded = sum(sizes), coded_rows(groups)
+    rows, coded = sum(sizes), coded_rows(sections)
     half = keeps[0].shape[0]
     ways = len(stages[0]) + 1 if stages else 1
     code_shape = lambda size: jax.ShapeDtypeStruct((size, coded, LANE), jnp.int16)
@@ -138,7 +158,7 @@
             way, slot = place // (half // ways), place % (half // ways)
             parts = [ins[k][place] + ins[number + k][place] for k in range(number)]
             value = jnp.concatenate(parts, axis=0)
-            outs[way][slot] = value if way == 0 else encode(value, groups)
+            outs[way][slot] = value if way == 0 else encode_all(value, sections)
 
     keep, *sends = call(
         first,
@@ -160,8 +180,8 @@
                 for slot in range(size):
                     value = ins[0][way * size + slot]
                     for ref in ins[1:]:
-                        value = value + decode(ref[way * size + slot], groups)
-                    outs[way][slot] = value if way == 0 and not last else encode(value, groups)
+                        value = value + decode_all(ref[way * size + slot], sections)
+                    outs[way][slot] = value if way == 0 and not last else encode_all(value, sections)
 
         kept = code_shape(size) if last else jax.ShapeDtypeStruct((size, rows, LANE), F32)
         keep, *sends = call(
@@ -170,24 +190,27 @@
     return keep
 
 
-def gather_chunks(chunk, axis):
+def gather_chunks(chunk, axis, apart):
     stages = gather_stages_of(lax.axis_size(axis))
     middle = ceil_to(chunk.shape[1] // 2, 16)
-    halves = [chunk[:, :middle], chunk[:, middle:]]
+    halves, tail = [chunk[:, :middle], chunk[:, middle:]], None
     for number, masks in enumerate(reversed(stages[1:])):
         for h in range(2):
             value = halves[h]
             parts = [value] + [swap(value, axis, mask) for mask in masks]
-            size = value.shape[0]
+            size, rows = value.shape[0], value.shape[1]
+            outs = [jax.ShapeDtypeStruct((size * len(parts), rows, LANE), value.dtype)]
+            if h == 1 and number == len(stages) - 2:
+                outs.append(jax.ShapeDtypeStruct((size * len(parts), apart, LANE), value.dtype))
 
             def kernel(*refs):
-                for k, ref in enumerate(refs[:-1]):
-                    refs[-1][k * size:(k + 1) * size] = ref[...]
-
-            shape = (size * len(parts),) + value.shape[1:]
-            out = jax.ShapeDtypeStruct(shape, value.dtype)
-            halves[h] = call(kernel, "chunk_join" + str(number), [], parts, [out])[0]
-    return halves + [swap(h, axis, 1) for h in halves]
+                for k in range(len(parts)):
+                    for out in refs[len(parts):]:
+                        out[k * size:(k + 1) * size] = refs[k][:, rows - out.shape[1]:, :]
+
+            got = call(kernel, "chunk_join" + str(number), [], parts, outs)
+            halves[h], tail = got[0], got[-1]
+    return halves + [swap(h, axis, 1) for h in halves], tail
 
 
 def padded(value, rows, lanes, size):
@@ -374,7 +397,7 @@
             tile(src, t, blocks)[...] = o - h * th
         return tuple(cells + prods)
 
-    lax.fori_loop(0, length, own_step, starts(0, seg_o) + (jnp.ones((blocks, LANE), F32),) * CHAINS, unroll=2)
+    lax.fori_loop(0, length, own_step, starts(0, seg_o) + (jnp.ones((blocks, LANE), F32),) * CHAINS, unroll=4)
     flatten(low)
     save = pltpu.make_async_copy(low, hid, sem)
     save.start()
@@ -396,11 +419,11 @@
                 tile(hs, t, blocks)[...] = tile(tab, at, blocks, 2, 3)[...] * jnp.tanh(cells[s])
             return tuple(cells)
 
-        lax.fori_loop(0, length, other_step, starts(p + 1, seg_x[p]), unroll=2)
+        lax.fori_loop(0, length, other_step, starts(p + 1, seg_x[p]), unroll=4)
         flatten(low_x)
         logits[...] += lax.dot_general(wt_x[...], low_x[...], nt, preferred_element_type=F32)
 
-    rows = 512
+    rows = 1024
 
     def save_src(k):
         place = pl.ds(pl.multiple_of(k * rows * blocks, rows * blocks), rows * blocks)
@@ -574,21 +597,21 @@
         store_pairs(keep, send, lax.axis_index("ctx"), piece, count, slice(gate * part, (gate + 1) * part))
 
 
-def finish_kernel(
-    mine_a, mine_b, theirs_a, theirs_b, w_grad, b_grad, e_grad, out_grad, o_grad, loss, eacc, *, groups, part, per, emb, shards, total_tokens
-):
+def finish_kernel(mine_a, mine_b, theirs_a, theirs_b, w_grad, b_grad, out_grad, *, groups, part, emb):
     count = 2 * mine_a.shape[0]
     me = lax.axis_index("ctx")
     first = me % 2 == 0
+    stages = gather_stages_of(count)
     pairs = {}
-    stages = gather_stages_of(count)
+    top = mine_a.shape[1]
+    rest = section_rows(groups) - top
 
     def chunk(q, rows):
         pair = q - q % 2
         if pair not in pairs:
             slot = slot_of(pair ^ (me - me % 2), count, stages)
             own, other = (
-                jnp.concatenate([a[slot].astype(jnp.int32), b[slot].astype(jnp.int32)], axis=0)
+                jnp.concatenate([a[slot].astype(jnp.int32), b[slot, 0:rest].astype(jnp.int32)], axis=0)
                 for a, b in ((mine_a, mine_b), (theirs_a, theirs_b))
             )
             pairs[pair] = [
@@ -613,10 +636,31 @@
                     b_grad[gate:gate + 1, lanes] = chunk(q, slice(at, at + 1))
             size = max(0, min(vpart, vocab - e * vpart))
             if size:
-                at = 4 * part + per
-                out_grad[e * vpart:e * vpart + size, lanes] = chunk(q, slice(at, at + size))
-    for p in range(count):
-        eacc[p * per:(p + 1) * per, :] = chunk(p, slice(4 * part, 4 * part + per))
+                out_grad[e * vpart:e * vpart + size, lanes] = chunk(q, slice(4 * part, 4 * part + size))
+
+
+def tree_sum(values):
+    while len(values) > 1:
+        values = [values[k] + values[k + 1] for k in range(0, len(values), 2)]
+    return values[0]
+
+
+def embed_finish_kernel(*refs, groups, shards, total_tokens):
+    codes, theirs_b = refs[:2 * shards - 1], refs[2 * shards - 1]
+    e_grad, o_grad, loss, eacc = refs[2 * shards:]
+    count = 2 * codes[0].shape[0]
+    me = lax.axis_index("ctx")
+    first = me % 2 == 0
+    stages = gather_stages_of(count)
+    per, rows = sum(groups), codes[0].shape[1]
+    for p in range(0, count, 2):
+        slot = slot_of(p ^ (me - me % 2), count, stages)
+        own = [codes[k if k == 0 else 2 * k - 1][slot] for k in range(shards)]
+        other = [theirs_b[slot, theirs_b.shape[1] - rows:]] + [codes[2 * k][slot] for k in range(1, shards)]
+        own, other = (tree_sum([decode(code, groups) for code in kind]) for kind in (own, other))
+        eacc[p * per:(p + 1) * per, :] = jnp.where(first, own, other)
+        eacc[(p + 1) * per:(p + 2) * per, :] = jnp.where(first, other, own)
+    vocab, emb = e_grad.shape
     e_grad[...] = eacc[0:vocab, 0:emb]
     for k in range(eacc.shape[0] // LANE):
         size = max(0, min(LANE, vocab - k * LANE))
@@ -718,7 +762,7 @@
     splits = count // blocks
     vpart = ceil_to(-(-vpad // splits), 8)
     half_chunks = lambda rows: [hbm((count // 2, rows, LANE), F32)] * 2
-    copies = 4
+    copies = 2
     hid, prev, src, keep_o, send_o, heads, head, o_sum, extra = call(
         functools.partial(cell_kernel, others=others, total_tokens=total_tokens, blocks=blocks),
         "cells",
@@ -732,7 +776,7 @@
         [
             pltpu.VMEM(tokens, F32), pltpu.VMEM(tokens, F32), pltpu.VMEM((toks, width), BF16),
             pltpu.VMEM((toks, width), BF16), pltpu.VMEM((vpad, width), BF16), pltpu.VMEM((vpad, toks), F32), pltpu.VMEM(tokens, F32),
-            pltpu.VMEM((vpad, toks), BF16), pltpu.SemaphoreType.DMA, pltpu.SemaphoreType.DMA((toks // 512,)),
+            pltpu.VMEM((vpad, toks), BF16), pltpu.SemaphoreType.DMA, pltpu.SemaphoreType.DMA((toks // 1024,)),
         ],
         limit=44,
         out_spaces=[pl.ANY, pltpu.VMEM, pl.ANY] + [pltpu.VMEM] * 6,
@@ -777,24 +821,29 @@
         limit=24,
         micros=3,
     )
-    bit = 1
-    while bit < wa:
-        keep_e, send_e = keep_e + swap(keep_e, "wa", bit), send_e + swap(send_e, "wa", bit)
-        bit *= 2
-    groups = [part] * gates + [per, vpart]
+    sections = [[part] * gates + [vpart], [per]]
+    apart = section_rows(sections[1])
     chunk = reduce_chunks(
-        [keep, keep_e, keep_o], [swap(send, "ctx", 1), swap(send_e, "ctx", 1), got_o], groups, "ctx"
-    )
-    halves = gather_chunks(chunk, "ctx")
-    w_grad, bi_grad, e_grad, w_out_grad, bo_grad, loss = call(
-        functools.partial(finish_kernel, groups=groups, part=part, per=per, emb=emb, shards=wa, total_tokens=total_tokens),
+        [keep, keep_o, keep_e], [swap(send, "ctx", 1), got_o, swap(send_e, "ctx", 1)], sections, "ctx"
+    )
+    halves, tail = gather_chunks(chunk, "ctx", apart)
+    far_tails = [swap(tail, "wa", mask) for mask in range(1, wa)]
+    w_grad, bi_grad, w_out_grad = call(
+        functools.partial(finish_kernel, groups=sections[0], part=part, emb=emb),
         "finish",
         [],
         halves,
-        [
-            hbm((emb, gates, width), F32), hbm((gates, width), F32), hbm((vocab, emb), F32),
-            hbm((vocab, width), F32), hbm((1, vocab), F32), hbm((1, 1), F32),
-        ],
+        [hbm((emb, gates, width), F32), hbm((gates, width), F32), hbm((vocab, width), F32)],
+        micros=4,
+    )
+    far_tails = [after(v, bi_grad) for v in far_tails]
+    tails = [tail] + [v for far_tail in far_tails for v in (far_tail, swap(far_tail, "ctx", 1))]
+    e_grad, bo_grad, loss = call(
+        functools.partial(embed_finish_kernel, groups=sections[1], shards=wa, total_tokens=total_tokens),
+        "embed_finish",
+        [],
+        tails + [halves[3]],
+        [hbm((vocab, emb), F32), hbm((1, vocab), F32), hbm((1, 1), F32)],
         [pltpu.VMEM((ceil_to(count * per, LANE), LANE), F32)],
     )
     return (

time: 151 us -> 148 us (0.980)
  waiting for transfers between devices: 33.5 us -> 31.7 us
    ppermute x24, waiting for transfers between devices: 22.5 us -> 20.9 us  [swap(): return lax.ppermute(value, axis, [(k, k ^ mask) for k in range(count)])]
    pallas_call x15 -> x16, Pallas kernels: 56 us -> 55.5 us  [call(): pl.pallas_call(kernel, grid=(steps,) if blocked else (), in_specs=[spec(p...]
  transfers between devices with their start and end apart: 29 -> 29, of which waited for: 12 -> 13; matrix products, arithmetic and copies ran while one was open for 0% -> 0% of each run, Pallas kernels for 2% -> 5%
where the time goes in v5:
time: 148 us
  Pallas kernels  55.5 us (38%)
  starting transfers between devices  39.8 us (27%)
  waiting for transfers between devices  31.7 us (21%)
  blocking collectives  13.1 us (9%)
  local copies, waits for them, and re-layouts  4.44 us (3%)
  other arithmetic  2.39 us (2%)
    pallas_call x16, Pallas kernels, call(): pl.pallas_call(kernel, grid=(steps,) if blocked else (), in_specs=[spec(p...  55.5 us
    ppermute x24, starting transfers between devices, swap(): return lax.ppermute(value, axis, [(k, k ^ mask) for k in range(count)])  28.2 us
    ppermute x24, waiting for transfers between devices, swap(): return lax.ppermute(value, axis, [(k, k ^ mask) for k in range(count)])  20.9 us
    all_to_all x1, blocking collectives, exchange(): return lax.all_to_all(copies, axis, 0, 0, tiled=True)  13.1 us
    all_to_all x1, waiting for transfers between devices, exchange(): return lax.all_to_all(copies, axis, 0, 0, tiled=True)  7.34 us
    all_to_all x1, starting transfers between devices, exchange(): return lax.all_to_all(copies, axis, 0, 0, tiled=True)  5.93 us
    ppermute x4, starting transfers between devices, from_others(): lax.ppermute(value, 'wa', [(k, (k - s) % wa) for k in range(wa)])  5.62 us
    unnamed x41, local copies, waits for them, and re-layouts  3.57 us
  transfers between devices with their start and end apart: 29, of which 13 were waited for; matrix products, arithmetic and copies ran while one was open for 0% of the time, Pallas kernels for 5%

profile of v5, /device:TPU:0, one launch (start us, length us, event | category | flops | bytes accessed | tf_op | source)
XLA Modules:
  0.0 148.0 jit_solution(2875617420959469812)
XLA Ops:
  1.6 1.4 copy.36
  4.8 6.2 %tables_own.1 = (s32[2048]{0:T(1024)S(1)}, s32[4]{0:T(128)S(1)}, f32[4608,128]{1,0:T(8,128)S(1)}, f32[16,2,8,128]{3,2,1,0:T(8,128)}, f32[16,2,8,128]{3,2,1,0:T(8...) custom-call(s32[4]{0:T(128)S(1)} %copy-done.13, s32[16]{0:T(128)S(1)} %copy-done.12, ...), custom_call_target="tpu_custom_call" | custom-call | bytes 18000000 | tf_op jit(solution)/shard_map/tables_own/pallas_call | solution.py:24
  11.0 1.4 copy-done
  12.4 2.9 %collective-permute-start.1 = (bf16[2,112,1024]{2,1,0:T(8,128)(2,1)}, bf16[2,112,1024]{2,1,0:T(8,128)(2,1)S(1)}, u32[]{:S(2)}, u32[]{:S(2)}) collective-permute-start(bf16[2,112,1024]{2,1,0:T(8,128)(2,1)} %get-tuple-element.55), channel_id=1, source_target_pairs={{0,1},{1,0},{2,3},{3,2},{4,5},{5,4},{6,7},{7,6},{8,9},{9,8},{10,11... | collective-permute-start | bytes 1376264 | tf_op jit(solution)/shard_map/ppermute | solution.py:679
  15.3 5.9 %all-to-all-start = ((f32[16,2,8,128]{3,2,1,0:T(8,128)}), f32[16,2,8,128]{3,2,1,0:T(8,128)S(1)}, u32[]{:S(2)}, u32[]{:S(2)}) async-start(f32[16,2,8,128]{3,2,1,0:T(8,128)} %get-tuple-element.54), calls=%async_computation | async-start | bytes 262144 | tf_op jit(solution)/shard_map/all_to_all | solution.py:71
  21.8 7.3 %all-to-all-done.ps_all = f32[16,2,8,128]{3,2,1,0:T(8,128)S(1)} async-done(((f32[16,2,8,128]{3,2,1,0:T(8,128)}), f32[16,2,8,128]{3,2,1,0:T(8,128)S(1)}, u32[]{:S(2)}, u32[]{:S(2)}) %all-to-all-start) | async-done | bytes 131104 | tf_op jit(solution)/shard_map/all_to_all | solution.py:71
  31.2 1.2 collective-permute-done.4.refs_12_
  32.4 1.8 %collective-permute-start.3 = (f32[16,2,8,128]{3,2,1,0:T(8,128)S(1)}, f32[16,2,8,128]{3,2,1,0:T(8,128)S(1)}, u32[]{:S(2)}, u32[]{:S(2)}) collective-permute-start(f32[16,2,8,128]{3,2,1,0:T(8,128)S(1)} %copy-done.5), channel_id=1, source_target_pairs={{0,1},{1,0},{2,3},{3,2},{4,5},{5,4},{6,7},{7,6},{8,9},{9,8},{10,11... | collective-permute-start | bytes 393224 | tf_op jit(solution)/shard_map/ppermute | solution.py:679
  34.5 1.6 %tables_other.1.refs_10_ = f32[6912,128]{1,0:T(8,128)S(1)} custom-call(s32[4]{0:T(128)S(1)} %get-tuple-element.51.spots, bf16[288,112]{1,0:T(8,128)(2,1)S(1)} %and_select_fusion.embed.table, bf16[2,112,1024]{2,1,0:T(8,128)(2,1)S(1)} %collective-permute-done.1.direct, bf16[2,112,1024]{2,1,0:T(8,128)(2,1)S(1)} %collective-permute-done.2.passed), custom_call_target="tpu_custom_call" | custom-call | bytes 9000000 | tf_op jit(solution)/shard_map/tables_other/pallas_call | solution.py:24
  36.0 2.3 %collective-permute-done.3.refs_11_ = f32[16,2,8,128]{3,2,1,0:T(8,128)S(1)} collective-permute-done((f32[16,2,8,128]{3,2,1,0:T(8,128)S(1)}, f32[16,2,8,128]{3,2,1,0:T(8,128)S(1)}, u32[]{:S(2)}, u32[]{:S(2)}) %collective-permute-start.3) | collective-permute-done | bytes 131104 | tf_op jit(solution)/shard_map/ppermute | solution.py:679
  39.1 24.1 %cells.1 = (bf16[2048,1024]{1,0:T(8,128)(2,1)}, f32[16384,128]{1,0:T(8,128)S(1)}, f32[16384,128]{1,0:T(8,128)}, f32[8,144,128]{2,1,0:T(8,128)}, f32[8,144,128]{2...) custom-call(s32[2048]{0:T(1024)} %copy-done.9, ...), custom_call_target="tpu_custom_call" | custom-call | bytes 78000000 | tf_op jit(solution)/shard_map/cells/pallas_call | solution.py:24
  63.2 13.1 %all_to_all.10.h_all = f32[16,8,128]{2,1,0:T(8,128)S(1)} all-to-all(f32[16,8,128]{2,1,0:T(8,128)} %get-tuple-element.61), channel_id=1, replica_groups=mesh['ctx'=16,'wa'=2] {'ctx'}, dimensions={0} | all-to-all | bytes 131072 | tf_op jit(solution)/shard_map/all_to_all | solution.py:71
  76.3 9.0 %char_sums.1.sums = f32[2,2304,128]{2,1,0:T(8,128)S(1)} custom-call(s32[2048]{0:T(1024)S(1)} %copy-done.10, s32[16]{0:T(128)S(1)} %copy-done.12, f32[4608,128]{1,0:T(8,128)S(1)} %copy-done.1, f32[16,2,8,128]{3,2,1,0:T(8,128)S(1)} %copy-done.6, f32[128,128]{1,0:T(8,128)S(1)} %get-tuple-element.60.heads, f32[16,8,128]{2,1,0:T(8,128)S(1)} %all_to_all.10.h_all, ...), custom_call_target="tpu_custom_call" | custom-call | bytes 27000000 | tf_op jit(solution)/shard_map/char_sums/pallas_call | solution.py:24
  85.3 4.1 %gate_sums.1 = (bf16[4,288,1024]{2,1,0:T(8,128)(2,1)S(1)}, bf16[4,288,1024]{2,1,0:T(8,128)(2,1)S(1)}, f32[8,24,128]{2,1,0:T(8,128)S(1)}, f32[8,24,128]{2,1,0:T(8,128)S(1)}) custom-call(s32[4]{0:T(128)S(1)} %get-tuple-element.51.spots, f32[2,2304,128]{2,1,0:T(8,128)S(1)} %char_sums.1.sums, f32[288,1024]{1,0:T(8,128)S(1)} %get-tuple-element.64.o_sum, ...), custom_call_target="tpu_custom_call" | custom-call | bytes 9000000 | tf_op jit(solution)/shard_map/gate_sums/pallas_call | solution.py:24
  89.4 1.3 input_grad.1
  91.4 2.9 %collective-permute-done.8.refs_5_ = f32[8,24,128]{2,1,0:T(8,128)S(1)} collective-permute-done((f32[8,24,128]{2,1,0:T(8,128)S(1)}, f32[8,24,128]{2,1,0:T(8,128)S(1)}, u32[]{:S(2)}, u32[]{:S(2)}) %collective-permute-start.8) | collective-permute-done | bytes 98336 | tf_op jit(solution)/shard_map/ppermute | solution.py:67
  94.3 1.3 core_sum.1
  96.4 2.7 %collective-permute-start.11 = (s16[1,416,128]{2,1,0:T(8,128)(2,1)S(1)}, s16[1,416,128]{2,1,0:T(8,128)(2,1)S(1)}, u32[]{:S(2)}, u32[]{:S(2)}) collective-permute-start(s16[1,416,128]{2,1,0:T(8,128)(2,1)S(1)} %get-tuple-element.77), channel_id=1, source_target_pairs={{0,12},{2,14},{4,8},{6,10},{8,4},{10,6},{12,0},{14,2},{16,28},{18,... | collective-permute-start | bytes 319496 | tf_op jit(solution)/shard_map/ppermute | solution.py:67
  99.3 2.3 %collective-permute-start.13 = (s16[1,416,128]{2,1,0:T(8,128)(2,1)S(1)}, s16[1,416,128]{2,1,0:T(8,128)(2,1)S(1)}, u32[]{:S(2)}, u32[]{:S(2)}) collective-permute-start(s16[1,416,128]{2,1,0:T(8,128)(2,1)S(1)} %get-tuple-element.79), channel_id=1, source_target_pairs={{0,20},{2,22},{4,16},{6,18},{8,28},{10,30},{12,24},{14,26},{16,4},... | collective-permute-start | bytes 319496 | tf_op jit(solution)/shard_map/ppermute | solution.py:67
  102.6 4.1 %collective-permute-start.15 = (s16[1,416,128]{2,1,0:T(8,128)(2,1)S(1)}, s16[1,416,128]{2,1,0:T(8,128)(2,1)S(1)}, u32[]{:S(2)}, u32[]{:S(2)}) collective-permute-start(s16[1,416,128]{2,1,0:T(8,128)(2,1)S(1)} %get-tuple-element.81), channel_id=1, source_target_pairs={{0,28},{2,30},{4,24},{6,26},{8,20},{10,22},{12,16},{14,18},{16,12}... | collective-permute-start | bytes 319496 | tf_op jit(solution)/shard_map/ppermute | solution.py:67
  106.8 7.5 %collective-permute-done.12.refs_4_ = s16[1,416,128]{2,1,0:T(8,128)(2,1)S(1)} collective-permute-done((s16[1,416,128]{2,1,0:T(8,128)(2,1)S(1)}, s16[1,416,128]{2,1,0:T(8,128)(2,1)S(1)}, u32[]{:S(2)}, u32[]{:S(2)}) %collective-permute-start.12) | collective-permute-done | bytes 106528 | tf_op jit(solution)/shard_map/ppermute | solution.py:67
  114.3 2.3 %collective-permute-done.13.refs_5_ = s16[1,416,128]{2,1,0:T(8,128)(2,1)S(1)} collective-permute-done((s16[1,416,128]{2,1,0:T(8,128)(2,1)S(1)}, s16[1,416,128]{2,1,0:T(8,128)(2,1)S(1)}, u32[]{:S(2)}, u32[]{:S(2)}) %collective-permute-start.13) | collective-permute-done | bytes 106528 | tf_op jit(solution)/shard_map/ppermute | solution.py:67
  118.4 4.4 %collective-permute-start.22 = (s16[1,208,128]{2,1,0:T(8,128)(2,1)S(1)}, s16[1,208,128]{2,1,0:T(8,128)(2,1)S(1)}, u32[]{:S(2)}, u32[]{:S(2)}) collective-permute-start(s16[1,208,128]{2,1,0:T(8,128)(2,1)S(1)} %get-tuple-element.91.refs_0_), channel_id=1, source_target_pairs={{0,16},{2,18},{4,20},{6,22},{8,24},{10,26},{12,28},{14,30},{16,0},... | collective-permute-start | bytes 159752 | tf_op jit(solution)/shard_map/ppermute | solution.py:67
  122.9 1.5 collective-permute-start.18
  124.3 2.0 %collective-permute-start.17 = (s16[1,208,128]{2,1,0:T(8,128)(2,1)S(1)}, s16[1,208,128]{2,1,0:T(8,128)(2,1)S(1)}, u32[]{:S(2)}, u32[]{:S(2)}) collective-permute-start(s16[1,208,128]{2,1,0:T(8,128)(2,1)S(1)} %get-tuple-element.92.refs_0_), channel_id=1, source_target_pairs={{0,16},{2,18},{4,20},{6,22},{8,24},{10,26},{12,28},{14,30},{16,0},... | collective-permute-start | bytes 159752 | tf_op jit(solution)/shard_map/ppermute | solution.py:67
  128.1 2.4 %collective-permute-start.24 = (s16[4,208,128]{2,1,0:T(8,128)(2,1)S(1)}, s16[4,208,128]{2,1,0:T(8,128)(2,1)S(1)}, u32[]{:S(2)}, u32[]{:S(2)}) collective-permute-start(s16[4,208,128]{2,1,0:T(8,128)(2,1)S(1)} %chunk_join0.3.refs_0_), channel_id=1, source_target_pairs={{0,4},{2,6},{4,0},{6,2},{8,12},{10,14},{12,8},{14,10},{16,20},{18,... | collective-permute-start | bytes 638984 | tf_op jit(solution)/shard_map/ppermute | solution.py:67
  131.1 2.3 %collective-permute-start.19 = (s16[4,208,128]{2,1,0:T(8,128)(2,1)S(1)}, s16[4,208,128]{2,1,0:T(8,128)(2,1)S(1)}, u32[]{:S(2)}, u32[]{:S(2)}) collective-permute-start(s16[4,208,128]{2,1,0:T(8,128)(2,1)S(1)} %chunk_join0.2.refs_0_), channel_id=1, source_target_pairs={{0,4},{2,6},{4,0},{6,2},{8,12},{10,14},{12,8},{14,10},{16,20},{18,... | collective-permute-start | bytes 638984 | tf_op jit(solution)/shard_map/ppermute | solution.py:67
  133.3 2.7 %collective-permute-done.24.refs_1_ = s16[4,208,128]{2,1,0:T(8,128)(2,1)S(1)} collective-permute-done((s16[4,208,128]{2,1,0:T(8,128)(2,1)S(1)}, s16[4,208,128]{2,1,0:T(8,128)(2,1)S(1)}, u32[]{:S(2)}, u32[]{:S(2)}) %collective-permute-start.24) | collective-permute-done | bytes 213024 | tf_op jit(solution)/shard_map/ppermute | solution.py:67
  136.2 2.8 %collective-permute-done.19.refs_1_ = s16[4,208,128]{2,1,0:T(8,128)(2,1)S(1)} collective-permute-done((s16[4,208,128]{2,1,0:T(8,128)(2,1)S(1)}, s16[4,208,128]{2,1,0:T(8,128)(2,1)S(1)}, u32[]{:S(2)}, u32[]{:S(2)}) %collective-permute-start.19) | collective-permute-done | bytes 213024 | tf_op jit(solution)/shard_map/ppermute | solution.py:67
  139.1 1.6 %collective-permute-start.20 = (s16[8,32,128]{2,1,0:T(8,128)(2,1)S(1)}, s16[8,32,128]{2,1,0:T(8,128)(2,1)S(1)}, u32[]{:S(2)}, u32[]{:S(2)}) collective-permute-start(s16[8,32,128]{2,1,0:T(8,128)(2,1)S(1)} %get-tuple-element.82.refs_0_), channel_id=1, source_target_pairs={{0,1},{1,0},{2,3},{3,2},{4,5},{5,4},{6,7},{7,6},{8,9},{9,8},{10,11... | collective-permute-start | bytes 196616 | tf_op jit(solution)/shard_map/ppermute | solution.py:67
  140.8 3.9 %finish.1 = (f32[100,4,1024]{2,1,0:T(4,128)}, f32[4,1024]{1,0:T(4,128)}, f32[275,1024]{1,0:T(8,128)}) custom-call(s16[8,208,128]{2,1,0:T(8,128)(2,1)S(1)} %chunk_join1.3.mine_a, s16[8,208,128]{2,1,0:T(8,128)(2,1)S(1)} %get-tuple-element.83.mine_b, s16[8,208,128]{2,1,0:T(8,128)(2,1)S(1)} %collective-permute-done.25.theirs_a, ...), custom_call_target="tpu_custom_call" | custom-call | bytes 12000000 | tf_op jit(solution)/shard_map/finish/pallas_call | solution.py:24
  145.9 1.4 embed_finish.1
  (97 shorter events, 15.3 us)
Async XLA Ops:
  3.0 26.2 %copy-start.18 = (f32[275]{0:T(512)S(1)}, f32[275]{0:T(512)}, u32[]{:S(2)}) copy-start(f32[275]{0:T(512)} %param.17) | copy-start | bytes 3304
  12.4 16.8 %collective-permute-start.1 = (bf16[2,112,1024]{2,1,0:T(8,128)(2,1)}, bf16[2,112,1024]{2,1,0:T(8,128)(2,1)S(1)}, u32[]{:S(2)}, u32[]{:S(2)}) collective-permute-start(bf16[2,112,1024]{2,1,0:T(8,128)(2,1)} %get-tuple-element.55), channel_id=1, source_target_pairs={{0,1},{1,0},{2,3},{3,2},{4,5},{5,4},{6,7},{7,6},{8,9},{9,8},{10,11... | collective-permute-start | bytes 1376264 | tf_op jit(solution)/shard_map/ppermute | solution.py:679
  15.3 13.9 %all-to-all-start = ((f32[16,2,8,128]{3,2,1,0:T(8,128)}), f32[16,2,8,128]{3,2,1,0:T(8,128)S(1)}, u32[]{:S(2)}, u32[]{:S(2)}) async-start(f32[16,2,8,128]{3,2,1,0:T(8,128)} %get-tuple-element.54), calls=%async_computation | async-start | bytes 262144 | tf_op jit(solution)/shard_map/all_to_all | solution.py:71
  21.2 11.1 %collective-permute-start.4 = (bf16[144,1024]{1,0:T(8,128)(2,1)}, bf16[144,1024]{1,0:T(8,128)(2,1)S(1)}, u32[]{:S(2)}, u32[]{:S(2)}) collective-permute-start(bf16[144,1024]{1,0:T(8,128)(2,1)} %get-tuple-element.57), channel_id=1, source_target_pairs={{0,1},{1,0},{2,3},{3,2},{4,5},{5,4},{6,7},{7,6},{8,9},{9,8},{10,11... | collective-permute-start | bytes 884744 | tf_op jit(solution)/shard_map/ppermute | solution.py:679
  29.2 5.3 %collective-permute-start.2 = (bf16[2,112,1024]{2,1,0:T(8,128)(2,1)S(1)}, bf16[2,112,1024]{2,1,0:T(8,128)(2,1)S(1)}, u32[]{:S(2)}, u32[]{:S(2)}) collective-permute-start(bf16[2,112,1024]{2,1,0:T(8,128)(2,1)S(1)} %collective-permute-done.1.direct), channel_id=1, source_target_pairs={{0,2},{2,0},{4,6},{6,4},{8,10},{10,8},{12,14},{14,12},{16,18},{18,... | collective-permute-start | bytes 1376264 | tf_op jit(solution)/shard_map/ppermute | solution.py:67
  32.3 6.0 %collective-permute-start.5 = (bf16[144,1024]{1,0:T(8,128)(2,1)S(1)}, bf16[144,1024]{1,0:T(8,128)(2,1)S(1)}, u32[]{:S(2)}, u32[]{:S(2)}) collective-permute-start(bf16[144,1024]{1,0:T(8,128)(2,1)S(1)} %collective-permute-done.4.refs_12_), channel_id=1, source_target_pairs={{0,2},{2,0},{4,6},{6,4},{8,10},{10,8},{12,14},{14,12},{16,18},{18,... | collective-permute-start | bytes 884744 | tf_op jit(solution)/shard_map/ppermute | solution.py:67
  32.4 6.0 %collective-permute-start.3 = (f32[16,2,8,128]{3,2,1,0:T(8,128)S(1)}, f32[16,2,8,128]{3,2,1,0:T(8,128)S(1)}, u32[]{:S(2)}, u32[]{:S(2)}) collective-permute-start(f32[16,2,8,128]{3,2,1,0:T(8,128)S(1)} %copy-done.5), channel_id=1, source_target_pairs={{0,1},{1,0},{2,3},{3,2},{4,5},{5,4},{6,7},{7,6},{8,9},{9,8},{10,11... | collective-permute-start | bytes 393224 | tf_op jit(solution)/shard_map/ppermute | solution.py:679
  34.2 4.2 %collective-permute-start = (f32[8,128]{1,0:T(8,128)S(1)}, f32[8,128]{1,0:T(8,128)S(1)}, u32[]{:S(2)}, u32[]{:S(2)}) collective-permute-start(f32[8,128]{1,0:T(8,128)S(1)} %carry.1.refs_8_), channel_id=1, source_target_pairs={{0,1},{1,0},{2,3},{3,2},{4,5},{5,4},{6,7},{7,6},{8,9},{9,8},{10,11... | collective-permute-start | bytes 12296 | tf_op jit(solution)/shard_map/ppermute | solution.py:679
  39.1 37.3 %copy-start.6 = (f32[16,2,8,128]{3,2,1,0:T(8,128)S(1)}, f32[16,2,8,128]{3,2,1,0:T(8,128)}, u32[]{:S(2)}) copy-start(f32[16,2,8,128]{3,2,1,0:T(8,128)} %get-tuple-element.52.refs_3_.seg) | copy-start | bytes 393220
  39.1 37.3 %copy-start.10 = (s32[2048]{0:T(1024)S(1)}, s32[2048]{0:T(1024)}, u32[]{:S(2)}) copy-start(s32[2048]{0:T(1024)} %copy-done.9) | copy-start | bytes 24580
  90.7 3.5 %collective-permute-start.6 = (f32[8,224,128]{2,1,0:T(8,128)S(1)}, f32[8,224,128]{2,1,0:T(8,128)S(1)}, u32[]{:S(2)}, u32[]{:S(2)}) collective-permute-start(f32[8,224,128]{2,1,0:T(8,128)S(1)} %get-tuple-element.71), channel_id=1, source_target_pairs={{0,2},{2,0},{4,6},{6,4},{8,10},{10,8},{12,14},{14,12},{16,18},{18,... | collective-permute-start | bytes 2752520 | tf_op jit(solution)/shard_map/ppermute | solution.py:67
  90.8 3.4 %collective-permute-start.7 = (f32[8,144,128]{2,1,0:T(8,128)S(1)}, f32[8,144,128]{2,1,0:T(8,128)S(1)}, u32[]{:S(2)}, u32[]{:S(2)}) collective-permute-start(f32[8,144,128]{2,1,0:T(8,128)S(1)} %copy-done.19), channel_id=1, source_target_pairs={{0,2},{2,0},{4,6},{6,4},{8,10},{10,8},{12,14},{14,12},{16,18},{18,... | collective-permute-start | bytes 1769480 | tf_op jit(solution)/shard_map/ppermute | solution.py:67
  91.3 2.9 %collective-permute-start.8 = (f32[8,24,128]{2,1,0:T(8,128)S(1)}, f32[8,24,128]{2,1,0:T(8,128)S(1)}, u32[]{:S(2)}, u32[]{:S(2)}) collective-permute-start(f32[8,24,128]{2,1,0:T(8,128)S(1)} %get-tuple-element.73), channel_id=1, source_target_pairs={{0,2},{2,0},{4,6},{6,4},{8,10},{10,8},{12,14},{14,12},{16,18},{18,... | collective-permute-start | bytes 294920 | tf_op jit(solution)/shard_map/ppermute | solution.py:67
  95.6 6.0 %collective-permute-start.9 = (s16[1,416,128]{2,1,0:T(8,128)(2,1)S(1)}, s16[1,416,128]{2,1,0:T(8,128)(2,1)S(1)}, u32[]{:S(2)}, u32[]{:S(2)}) collective-permute-start(s16[1,416,128]{2,1,0:T(8,128)(2,1)S(1)} %get-tuple-element.75), channel_id=1, source_target_pairs={{0,4},{2,6},{4,0},{6,2},{8,12},{10,14},{12,8},{14,10},{16,20},{18,... | collective-permute-start | bytes 319496 | tf_op jit(solution)/shard_map/ppermute | solution.py:67
  95.7 6.9 %collective-permute-start.10 = (s16[1,416,128]{2,1,0:T(8,128)(2,1)S(1)}, s16[1,416,128]{2,1,0:T(8,128)(2,1)S(1)}, u32[]{:S(2)}, u32[]{:S(2)}) collective-permute-start(s16[1,416,128]{2,1,0:T(8,128)(2,1)S(1)} %get-tuple-element.76), channel_id=1, source_target_pairs={{0,8},{2,10},{4,12},{6,14},{8,0},{10,2},{12,4},{14,6},{16,24},{18,... | collective-permute-start | bytes 319496 | tf_op jit(solution)/shard_map/ppermute | solution.py:67
  96.4 10.4 %collective-permute-start.11 = (s16[1,416,128]{2,1,0:T(8,128)(2,1)S(1)}, s16[1,416,128]{2,1,0:T(8,128)(2,1)S(1)}, u32[]{:S(2)}, u32[]{:S(2)}) collective-permute-start(s16[1,416,128]{2,1,0:T(8,128)(2,1)S(1)} %get-tuple-element.77), channel_id=1, source_target_pairs={{0,12},{2,14},{4,8},{6,10},{8,4},{10,6},{12,0},{14,2},{16,28},{18,... | collective-permute-start | bytes 319496 | tf_op jit(solution)/shard_map/ppermute | solution.py:67
  99.1 15.2 %collective-permute-start.12 = (s16[1,416,128]{2,1,0:T(8,128)(2,1)S(1)}, s16[1,416,128]{2,1,0:T(8,128)(2,1)S(1)}, u32[]{:S(2)}, u32[]{:S(2)}) collective-permute-start(s16[1,416,128]{2,1,0:T(8,128)(2,1)S(1)} %get-tuple-element.78), channel_id=1, source_target_pairs={{0,16},{2,18},{4,20},{6,22},{8,24},{10,26},{12,28},{14,30},{16,0},... | collective-permute-start | bytes 319496 | tf_op jit(solution)/shard_map/ppermute | solution.py:67
  99.3 17.3 %collective-permute-start.13 = (s16[1,416,128]{2,1,0:T(8,128)(2,1)S(1)}, s16[1,416,128]{2,1,0:T(8,128)(2,1)S(1)}, u32[]{:S(2)}, u32[]{:S(2)}) collective-permute-start(s16[1,416,128]{2,1,0:T(8,128)(2,1)S(1)} %get-tuple-element.79), channel_id=1, source_target_pairs={{0,20},{2,22},{4,16},{6,18},{8,28},{10,30},{12,24},{14,26},{16,4},... | collective-permute-start | bytes 319496 | tf_op jit(solution)/shard_map/ppermute | solution.py:67
  101.6 15.1 %collective-permute-start.14 = (s16[1,416,128]{2,1,0:T(8,128)(2,1)S(1)}, s16[1,416,128]{2,1,0:T(8,128)(2,1)S(1)}, u32[]{:S(2)}, u32[]{:S(2)}) collective-permute-start(s16[1,416,128]{2,1,0:T(8,128)(2,1)S(1)} %get-tuple-element.80), channel_id=1, source_target_pairs={{0,24},{2,26},{4,28},{6,30},{8,16},{10,18},{12,20},{14,22},{16,8},... | collective-permute-start | bytes 319496 | tf_op jit(solution)/shard_map/ppermute | solution.py:67
  102.6 14.0 %collective-permute-start.15 = (s16[1,416,128]{2,1,0:T(8,128)(2,1)S(1)}, s16[1,416,128]{2,1,0:T(8,128)(2,1)S(1)}, u32[]{:S(2)}, u32[]{:S(2)}) collective-permute-start(s16[1,416,128]{2,1,0:T(8,128)(2,1)S(1)} %get-tuple-element.81), channel_id=1, source_target_pairs={{0,28},{2,30},{4,24},{6,26},{8,20},{10,22},{12,16},{14,18},{16,12}... | collective-permute-start | bytes 319496 | tf_op jit(solution)/shard_map/ppermute | solution.py:67
  117.4 8.9 %collective-permute-start.23 = (s16[1,208,128]{2,1,0:T(8,128)(2,1)S(1)}, s16[1,208,128]{2,1,0:T(8,128)(2,1)S(1)}, u32[]{:S(2)}, u32[]{:S(2)}) collective-permute-start(s16[1,208,128]{2,1,0:T(8,128)(2,1)S(1)} %get-tuple-element.91.refs_0_), channel_id=1, source_target_pairs={{0,24},{2,26},{4,28},{6,30},{8,16},{10,18},{12,20},{14,22},{16,8},... | collective-permute-start | bytes 159752 | tf_op jit(solution)/shard_map/ppermute | solution.py:67
  118.4 9.7 %collective-permute-start.22 = (s16[1,208,128]{2,1,0:T(8,128)(2,1)S(1)}, s16[1,208,128]{2,1,0:T(8,128)(2,1)S(1)}, u32[]{:S(2)}, u32[]{:S(2)}) collective-permute-start(s16[1,208,128]{2,1,0:T(8,128)(2,1)S(1)} %get-tuple-element.91.refs_0_), channel_id=1, source_target_pairs={{0,16},{2,18},{4,20},{6,22},{8,24},{10,26},{12,28},{14,30},{16,0},... | collective-permute-start | bytes 159752 | tf_op jit(solution)/shard_map/ppermute | solution.py:67
  122.9 5.3 %collective-permute-start.21 = (s16[1,208,128]{2,1,0:T(8,128)(2,1)S(1)}, s16[1,208,128]{2,1,0:T(8,128)(2,1)S(1)}, u32[]{:S(2)}, u32[]{:S(2)}) collective-permute-start(s16[1,208,128]{2,1,0:T(8,128)(2,1)S(1)} %get-tuple-element.91.refs_0_), channel_id=1, source_target_pairs={{0,8},{2,10},{4,12},{6,14},{8,0},{10,2},{12,4},{14,6},{16,24},{18,... | collective-permute-start | bytes 159752 | tf_op jit(solution)/shard_map/ppermute | solution.py:67
  122.9 7.7 %collective-permute-start.18 = (s16[1,208,128]{2,1,0:T(8,128)(2,1)S(1)}, s16[1,208,128]{2,1,0:T(8,128)(2,1)S(1)}, u32[]{:S(2)}, u32[]{:S(2)}) collective-permute-start(s16[1,208,128]{2,1,0:T(8,128)(2,1)S(1)} %get-tuple-element.92.refs_0_), channel_id=1, source_target_pairs={{0,24},{2,26},{4,28},{6,30},{8,16},{10,18},{12,20},{14,22},{16,8},... | collective-permute-start | bytes 159752 | tf_op jit(solution)/shard_map/ppermute | solution.py:67
  124.3 6.5 %collective-permute-start.17 = (s16[1,208,128]{2,1,0:T(8,128)(2,1)S(1)}, s16[1,208,128]{2,1,0:T(8,128)(2,1)S(1)}, u32[]{:S(2)}, u32[]{:S(2)}) collective-permute-start(s16[1,208,128]{2,1,0:T(8,128)(2,1)S(1)} %get-tuple-element.92.refs_0_), channel_id=1, source_target_pairs={{0,16},{2,18},{4,20},{6,22},{8,24},{10,26},{12,28},{14,30},{16,0},... | collective-permute-start | bytes 159752 | tf_op jit(solution)/shard_map/ppermute | solution.py:67
  126.3 4.7 %collective-permute-start.16 = (s16[1,208,128]{2,1,0:T(8,128)(2,1)S(1)}, s16[1,208,128]{2,1,0:T(8,128)(2,1)S(1)}, u32[]{:S(2)}, u32[]{:S(2)}) collective-permute-start(s16[1,208,128]{2,1,0:T(8,128)(2,1)S(1)} %get-tuple-element.92.refs_0_), channel_id=1, source_target_pairs={{0,8},{2,10},{4,12},{6,14},{8,0},{10,2},{12,4},{14,6},{16,24},{18,... | collective-permute-start | bytes 159752 | tf_op jit(solution)/shard_map/ppermute | solution.py:67
  128.1 7.9 %collective-permute-start.24 = (s16[4,208,128]{2,1,0:T(8,128)(2,1)S(1)}, s16[4,208,128]{2,1,0:T(8,128)(2,1)S(1)}, u32[]{:S(2)}, u32[]{:S(2)}) collective-permute-start(s16[4,208,128]{2,1,0:T(8,128)(2,1)S(1)} %chunk_join0.3.refs_0_), channel_id=1, source_target_pairs={{0,4},{2,6},{4,0},{6,2},{8,12},{10,14},{12,8},{14,10},{16,20},{18,... | collective-permute-start | bytes 638984 | tf_op jit(solution)/shard_map/ppermute | solution.py:67
  131.1 7.9 %collective-permute-start.19 = (s16[4,208,128]{2,1,0:T(8,128)(2,1)S(1)}, s16[4,208,128]{2,1,0:T(8,128)(2,1)S(1)}, u32[]{:S(2)}, u32[]{:S(2)}) collective-permute-start(s16[4,208,128]{2,1,0:T(8,128)(2,1)S(1)} %chunk_join0.2.refs_0_), channel_id=1, source_target_pairs={{0,4},{2,6},{4,0},{6,2},{8,12},{10,14},{12,8},{14,10},{16,20},{18,... | collective-permute-start | bytes 638984 | tf_op jit(solution)/shard_map/ppermute | solution.py:67
  136.1 4.5 %collective-permute-start.25 = (s16[8,208,128]{2,1,0:T(8,128)(2,1)S(1)}, s16[8,208,128]{2,1,0:T(8,128)(2,1)S(1)}, u32[]{:S(2)}, u32[]{:S(2)}) collective-permute-start(s16[8,208,128]{2,1,0:T(8,128)(2,1)S(1)} %chunk_join1.3.mine_a), channel_id=1, source_target_pairs={{0,2},{2,0},{4,6},{6,4},{8,10},{10,8},{12,14},{14,12},{16,18},{18,... | collective-permute-start | bytes 1277960 | tf_op jit(solution)/shard_map/ppermute | solution.py:67
  139.0 1.8 %collective-permute-start.26 = (s16[8,208,128]{2,1,0:T(8,128)(2,1)S(1)}, s16[8,208,128]{2,1,0:T(8,128)(2,1)S(1)}, u32[]{:S(2)}, u32[]{:S(2)}) collective-permute-start(s16[8,208,128]{2,1,0:T(8,128)(2,1)S(1)} %get-tuple-element.83.mine_b), channel_id=1, source_target_pairs={{0,2},{2,0},{4,6},{6,4},{8,10},{10,8},{12,14},{14,12},{16,18},{18,... | collective-permute-start | bytes 1277960 | tf_op jit(solution)/shard_map/ppermute | solution.py:67
  139.1 5.6 %collective-permute-start.20 = (s16[8,32,128]{2,1,0:T(8,128)(2,1)S(1)}, s16[8,32,128]{2,1,0:T(8,128)(2,1)S(1)}, u32[]{:S(2)}, u32[]{:S(2)}) collective-permute-start(s16[8,32,128]{2,1,0:T(8,128)(2,1)S(1)} %get-tuple-element.82.refs_0_), channel_id=1, source_target_pairs={{0,1},{1,0},{2,3},{3,2},{4,5},{5,4},{6,7},{7,6},{8,9},{9,8},{10,11... | collective-permute-start | bytes 196616 | tf_op jit(solution)/shard_map/ppermute | solution.py:67
  144.7 1.3 collective-permute-start.27
  (17 other events, 99.7 us)

commit v6 on v5

--- a/solution.py
+++ b/solution.py
@@ -272,7 +272,8 @@
 
 
 def own_table_kernel(
-    doc_lengths, block_of, ids, embed, w, w_out, marked, spots, tab, seg, ends, w_far, wt, wt_far, sem, *, vocab, blocks
+    doc_lengths, block_of, ids, embed, w, w_out, marked, spots, tab_out, seg, ends, w_far, wt, wt_far, tab, sem, tab_sem,
+    *, vocab, blocks,
 ):
     toks = ids.shape[0]
     copy = pltpu.make_async_copy(ids, marked, sem)
@@ -300,6 +301,8 @@
         tile(tab, vocab + k, blocks, 0, 2)[...] = jnp.zeros((blocks, LANE), F32)
         tile(tab, vocab + k, blocks, 1, 2)[...] = tile(tab, spot, blocks, 1, 2)[...]
         start = start + doc_lengths[k]
+    save = pltpu.make_async_copy(tab, tab_out, tab_sem)
+    save.start()
     prod, total = segment_ends(marked, tab, toks, blocks, 2)
     p_all, s_all = prod[0], total[0]
     for s in range(CHAINS):
@@ -311,6 +314,7 @@
     for d in range(ends.shape[0]):
         ends[d, 0] = p_all
         ends[d, 1] = s_all
+    save.wait()
 
 
 def carry_kernel(block_of, ps_all, _, bias, carry, order):
@@ -717,11 +721,11 @@
         "tables_own",
         [doc_lengths, block_of],
         [ids, table, w_own, w_out.T],
-        [smem((toks,)), smem((docs,)), chip(vpad * 2 * blocks, LANE), pltpu.HBM((CHAINS, 2, blocks, LANE), F32),
+        [smem((toks,)), smem((docs,)), pltpu.HBM((vpad * 2 * blocks, LANE), F32), pltpu.HBM((CHAINS, 2, blocks, LANE), F32),
          pltpu.HBM((count, 2, blocks, LANE), F32), bf(gates // 2, kdim, width), bf(vpad, width), bf(vpad // 2, width)],
-        [pltpu.SemaphoreType.DMA],
+        [pltpu.VMEM((vpad * 2 * blocks, LANE), F32), pltpu.SemaphoreType.DMA, pltpu.SemaphoreType.DMA],
         in_spaces=[pl.ANY, pltpu.VMEM, pltpu.VMEM, pltpu.VMEM],
-        out_spaces=[pltpu.SMEM, pltpu.SMEM] + [pltpu.VMEM] * 6,
+        out_spaces=[pltpu.SMEM, pltpu.SMEM, pl.ANY] + [pltpu.VMEM] * 5,
         micros=6,
     )
     tab = near(tab)

time: 148 us -> 147 us (level)
    unnamed x41 -> x39, local copies, waits for them, and re-layouts: 3.57 us -> 2.17 us
where the time goes in v6:
time: 147 us; the launch traced here: 146 us
  Pallas kernels  55 us (37%)
  starting transfers between devices  40.1 us (27%)
  waiting for transfers between devices  31.6 us (21%)
  blocking collectives  13.1 us (9%)
  local copies, waits for them, and re-layouts  3.05 us (2%)
  other arithmetic  2.39 us (2%)
    pallas_call x16, Pallas kernels, call(): pl.pallas_call(kernel, grid=(steps,) if blocked else (), in_specs=[spec(p...  55 us
    ppermute x24, starting transfers between devices, swap(): return lax.ppermute(value, axis, [(k, k ^ mask) for k in range(count)])  28.4 us
    ppermute x24, waiting for transfers between devices, swap(): return lax.ppermute(value, axis, [(k, k ^ mask) for k in range(count)])  20.8 us
    all_to_all x1, blocking collectives, exchange(): return lax.all_to_all(copies, axis, 0, 0, tiled=True)  13.1 us
    all_to_all x1, waiting for transfers between devices, exchange(): return lax.all_to_all(copies, axis, 0, 0, tiled=True)  7.34 us
    all_to_all x1, starting transfers between devices, exchange(): return lax.all_to_all(copies, axis, 0, 0, tiled=True)  5.93 us
    ppermute x4, starting transfers between devices, from_others(): lax.ppermute(value, 'wa', [(k, (k - s) % wa) for k in range(wa)])  5.7 us
    ppermute x4, waiting for transfers between devices, from_others(): lax.ppermute(value, 'wa', [(k, (k - s) % wa) for k in range(wa)])  3.51 us
  transfers between devices with their start and end apart: 29, of which 13 were waited for; matrix products, arithmetic and copies ran while one was open for 0% of the time, Pallas kernels for 5%

profile of v6, /device:TPU:0, one launch (start us, length us, event | category | flops | bytes accessed | tf_op | source)
XLA Modules:
  0.0 146.3 jit_solution(16731937218991593428)
XLA Ops:
  1.6 1.4 copy.36
  4.8 5.7 %tables_own.1 = (s32[2048]{0:T(1024)S(1)}, s32[4]{0:T(128)S(1)}, f32[4608,128]{1,0:T(8,128)}, f32[16,2,8,128]{3,2,1,0:T(8,128)}, f32[16,2,8,128]{3,2,1,0:T(8,128...) custom-call(s32[4]{0:T(128)S(1)} %copy-done.12, s32[16]{0:T(128)S(1)} %copy-done.11, ...), custom_call_target="tpu_custom_call" | custom-call | bytes 18000000 | tf_op jit(solution)/shard_map/tables_own/pallas_call | solution.py:24
  10.5 3.0 %collective-permute-start.1 = (bf16[2,112,1024]{2,1,0:T(8,128)(2,1)}, bf16[2,112,1024]{2,1,0:T(8,128)(2,1)S(1)}, u32[]{:S(2)}, u32[]{:S(2)}) collective-permute-start(bf16[2,112,1024]{2,1,0:T(8,128)(2,1)} %get-tuple-element.55), channel_id=1, source_target_pairs={{0,1},{1,0},{2,3},{3,2},{4,5},{5,4},{6,7},{7,6},{8,9},{9,8},{10,11... | collective-permute-start | bytes 1376264 | tf_op jit(solution)/shard_map/ppermute | solution.py:683
  13.5 5.9 %all-to-all-start = ((f32[16,2,8,128]{3,2,1,0:T(8,128)}), f32[16,2,8,128]{3,2,1,0:T(8,128)S(1)}, u32[]{:S(2)}, u32[]{:S(2)}) async-start(f32[16,2,8,128]{3,2,1,0:T(8,128)} %get-tuple-element.54), calls=%async_computation | async-start | bytes 262144 | tf_op jit(solution)/shard_map/all_to_all | solution.py:71
  20.1 7.3 %all-to-all-done.ps_all = f32[16,2,8,128]{3,2,1,0:T(8,128)S(1)} async-done(((f32[16,2,8,128]{3,2,1,0:T(8,128)}), f32[16,2,8,128]{3,2,1,0:T(8,128)S(1)}, u32[]{:S(2)}, u32[]{:S(2)}) %all-to-all-start) | async-done | bytes 131104 | tf_op jit(solution)/shard_map/all_to_all | solution.py:71
  29.4 1.2 collective-permute-done.4.refs_12_
  30.6 1.8 %collective-permute-start.3 = (f32[16,2,8,128]{3,2,1,0:T(8,128)S(1)}, f32[16,2,8,128]{3,2,1,0:T(8,128)S(1)}, u32[]{:S(2)}, u32[]{:S(2)}) collective-permute-start(f32[16,2,8,128]{3,2,1,0:T(8,128)S(1)} %copy-done.4), channel_id=1, source_target_pairs={{0,1},{1,0},{2,3},{3,2},{4,5},{5,4},{6,7},{7,6},{8,9},{9,8},{10,11... | collective-permute-start | bytes 393224 | tf_op jit(solution)/shard_map/ppermute | solution.py:683
  32.7 1.6 %tables_other.1.refs_10_ = f32[6912,128]{1,0:T(8,128)S(1)} custom-call(s32[4]{0:T(128)S(1)} %get-tuple-element.51.spots, bf16[288,112]{1,0:T(8,128)(2,1)S(1)} %and_select_fusion.embed.table, bf16[2,112,1024]{2,1,0:T(8,128)(2,1)S(1)} %collective-permute-done.1.direct, bf16[2,112,1024]{2,1,0:T(8,128)(2,1)S(1)} %collective-permute-done.2.passed), custom_call_target="tpu_custom_call" | custom-call | bytes 9000000 | tf_op jit(solution)/shard_map/tables_other/pallas_call | solution.py:24
  34.2 2.3 %collective-permute-done.3.refs_11_ = f32[16,2,8,128]{3,2,1,0:T(8,128)S(1)} collective-permute-done((f32[16,2,8,128]{3,2,1,0:T(8,128)S(1)}, f32[16,2,8,128]{3,2,1,0:T(8,128)S(1)}, u32[]{:S(2)}, u32[]{:S(2)}) %collective-permute-start.3) | collective-permute-done | bytes 131104 | tf_op jit(solution)/shard_map/ppermute | solution.py:683
  37.3 24.2 %cells.1 = (bf16[2048,1024]{1,0:T(8,128)(2,1)}, f32[16384,128]{1,0:T(8,128)S(1)}, f32[16384,128]{1,0:T(8,128)}, f32[8,144,128]{2,1,0:T(8,128)}, f32[8,144,128]{2...) custom-call(s32[2048]{0:T(1024)} %copy-done.8, ...), custom_call_target="tpu_custom_call" | custom-call | bytes 78000000 | tf_op jit(solution)/shard_map/cells/pallas_call | solution.py:24
  61.5 13.1 %all_to_all.10.h_all = f32[16,8,128]{2,1,0:T(8,128)S(1)} all-to-all(f32[16,8,128]{2,1,0:T(8,128)} %get-tuple-element.61), channel_id=1, replica_groups=mesh['ctx'=16,'wa'=2] {'ctx'}, dimensions={0} | all-to-all | bytes 131072 | tf_op jit(solution)/shard_map/all_to_all | solution.py:71
  74.6 9.0 %char_sums.1.sums = f32[2,2304,128]{2,1,0:T(8,128)S(1)} custom-call(s32[2048]{0:T(1024)S(1)} %copy-done.9, s32[16]{0:T(128)S(1)} %copy-done.11, f32[4608,128]{1,0:T(8,128)S(1)} %copy-done, f32[16,2,8,128]{3,2,1,0:T(8,128)S(1)} %copy-done.5, f32[128,128]{1,0:T(8,128)S(1)} %get-tuple-element.60.heads, f32[16,8,128]{2,1,0:T(8,128)S(1)} %all_to_all.10.h_all, ...), custom_call_target="tpu_custom_call" | custom-call | bytes 27000000 | tf_op jit(solution)/shard_map/char_sums/pallas_call | solution.py:24
  83.6 4.1 %gate_sums.1 = (bf16[4,288,1024]{2,1,0:T(8,128)(2,1)S(1)}, bf16[4,288,1024]{2,1,0:T(8,128)(2,1)S(1)}, f32[8,24,128]{2,1,0:T(8,128)S(1)}, f32[8,24,128]{2,1,0:T(8,128)S(1)}) custom-call(s32[4]{0:T(128)S(1)} %get-tuple-element.51.spots, f32[2,2304,128]{2,1,0:T(8,128)S(1)} %char_sums.1.sums, f32[288,1024]{1,0:T(8,128)S(1)} %get-tuple-element.64.o_sum, ...), custom_call_target="tpu_custom_call" | custom-call | bytes 9000000 | tf_op jit(solution)/shard_map/gate_sums/pallas_call | solution.py:24
  87.7 1.3 input_grad.1
  89.6 2.9 %collective-permute-done.8.refs_5_ = f32[8,24,128]{2,1,0:T(8,128)S(1)} collective-permute-done((f32[8,24,128]{2,1,0:T(8,128)S(1)}, f32[8,24,128]{2,1,0:T(8,128)S(1)}, u32[]{:S(2)}, u32[]{:S(2)}) %collective-permute-start.8) | collective-permute-done | bytes 98336 | tf_op jit(solution)/shard_map/ppermute | solution.py:67
  92.5 1.3 core_sum.1
  94.6 2.8 %collective-permute-start.11 = (s16[1,416,128]{2,1,0:T(8,128)(2,1)S(1)}, s16[1,416,128]{2,1,0:T(8,128)(2,1)S(1)}, u32[]{:S(2)}, u32[]{:S(2)}) collective-permute-start(s16[1,416,128]{2,1,0:T(8,128)(2,1)S(1)} %get-tuple-element.77), channel_id=1, source_target_pairs={{0,12},{2,14},{4,8},{6,10},{8,4},{10,6},{12,0},{14,2},{16,28},{18,... | collective-permute-start | bytes 319496 | tf_op jit(solution)/shard_map/ppermute | solution.py:67
  97.5 2.3 %collective-permute-start.13 = (s16[1,416,128]{2,1,0:T(8,128)(2,1)S(1)}, s16[1,416,128]{2,1,0:T(8,128)(2,1)S(1)}, u32[]{:S(2)}, u32[]{:S(2)}) collective-permute-start(s16[1,416,128]{2,1,0:T(8,128)(2,1)S(1)} %get-tuple-element.79), channel_id=1, source_target_pairs={{0,20},{2,22},{4,16},{6,18},{8,28},{10,30},{12,24},{14,26},{16,4},... | collective-permute-start | bytes 319496 | tf_op jit(solution)/shard_map/ppermute | solution.py:67
  100.9 4.1 %collective-permute-start.15 = (s16[1,416,128]{2,1,0:T(8,128)(2,1)S(1)}, s16[1,416,128]{2,1,0:T(8,128)(2,1)S(1)}, u32[]{:S(2)}, u32[]{:S(2)}) collective-permute-start(s16[1,416,128]{2,1,0:T(8,128)(2,1)S(1)} %get-tuple-element.81), channel_id=1, source_target_pairs={{0,28},{2,30},{4,24},{6,26},{8,20},{10,22},{12,16},{14,18},{16,12}... | collective-permute-start | bytes 319496 | tf_op jit(solution)/shard_map/ppermute | solution.py:67
  105.0 7.5 %collective-permute-done.12.refs_4_ = s16[1,416,128]{2,1,0:T(8,128)(2,1)S(1)} collective-permute-done((s16[1,416,128]{2,1,0:T(8,128)(2,1)S(1)}, s16[1,416,128]{2,1,0:T(8,128)(2,1)S(1)}, u32[]{:S(2)}, u32[]{:S(2)}) %collective-permute-start.12) | collective-permute-done | bytes 106528 | tf_op jit(solution)/shard_map/ppermute | solution.py:67
  112.5 2.3 %collective-permute-done.13.refs_5_ = s16[1,416,128]{2,1,0:T(8,128)(2,1)S(1)} collective-permute-done((s16[1,416,128]{2,1,0:T(8,128)(2,1)S(1)}, s16[1,416,128]{2,1,0:T(8,128)(2,1)S(1)}, u32[]{:S(2)}, u32[]{:S(2)}) %collective-permute-start.13) | collective-permute-done | bytes 106528 | tf_op jit(solution)/shard_map/ppermute | solution.py:67
  116.7 4.4 %collective-permute-start.22 = (s16[1,208,128]{2,1,0:T(8,128)(2,1)S(1)}, s16[1,208,128]{2,1,0:T(8,128)(2,1)S(1)}, u32[]{:S(2)}, u32[]{:S(2)}) collective-permute-start(s16[1,208,128]{2,1,0:T(8,128)(2,1)S(1)} %get-tuple-element.91.refs_0_), channel_id=1, source_target_pairs={{0,16},{2,18},{4,20},{6,22},{8,24},{10,26},{12,28},{14,30},{16,0},... | collective-permute-start | bytes 159752 | tf_op jit(solution)/shard_map/ppermute | solution.py:67
  121.1 1.5 collective-permute-start.18
  122.5 2.0 %collective-permute-start.17 = (s16[1,208,128]{2,1,0:T(8,128)(2,1)S(1)}, s16[1,208,128]{2,1,0:T(8,128)(2,1)S(1)}, u32[]{:S(2)}, u32[]{:S(2)}) collective-permute-start(s16[1,208,128]{2,1,0:T(8,128)(2,1)S(1)} %get-tuple-element.92.refs_0_), channel_id=1, source_target_pairs={{0,16},{2,18},{4,20},{6,22},{8,24},{10,26},{12,28},{14,30},{16,0},... | collective-permute-start | bytes 159752 | tf_op jit(solution)/shard_map/ppermute | solution.py:67
  126.3 2.6 %collective-permute-start.24 = (s16[4,208,128]{2,1,0:T(8,128)(2,1)S(1)}, s16[4,208,128]{2,1,0:T(8,128)(2,1)S(1)}, u32[]{:S(2)}, u32[]{:S(2)}) collective-permute-start(s16[4,208,128]{2,1,0:T(8,128)(2,1)S(1)} %chunk_join0.3.refs_0_), channel_id=1, source_target_pairs={{0,4},{2,6},{4,0},{6,2},{8,12},{10,14},{12,8},{14,10},{16,20},{18,... | collective-permute-start | bytes 638984 | tf_op jit(solution)/shard_map/ppermute | solution.py:67
  129.3 2.3 %collective-permute-start.19 = (s16[4,208,128]{2,1,0:T(8,128)(2,1)S(1)}, s16[4,208,128]{2,1,0:T(8,128)(2,1)S(1)}, u32[]{:S(2)}, u32[]{:S(2)}) collective-permute-start(s16[4,208,128]{2,1,0:T(8,128)(2,1)S(1)} %chunk_join0.2.refs_0_), channel_id=1, source_target_pairs={{0,4},{2,6},{4,0},{6,2},{8,12},{10,14},{12,8},{14,10},{16,20},{18,... | collective-permute-start | bytes 638984 | tf_op jit(solution)/shard_map/ppermute | solution.py:67
  131.6 2.9 %collective-permute-done.24.refs_1_ = s16[4,208,128]{2,1,0:T(8,128)(2,1)S(1)} collective-permute-done((s16[4,208,128]{2,1,0:T(8,128)(2,1)S(1)}, s16[4,208,128]{2,1,0:T(8,128)(2,1)S(1)}, u32[]{:S(2)}, u32[]{:S(2)}) %collective-permute-start.24) | collective-permute-done | bytes 213024 | tf_op jit(solution)/shard_map/ppermute | solution.py:67
  134.6 2.7 %collective-permute-done.19.refs_1_ = s16[4,208,128]{2,1,0:T(8,128)(2,1)S(1)} collective-permute-done((s16[4,208,128]{2,1,0:T(8,128)(2,1)S(1)}, s16[4,208,128]{2,1,0:T(8,128)(2,1)S(1)}, u32[]{:S(2)}, u32[]{:S(2)}) %collective-permute-start.19) | collective-permute-done | bytes 213024 | tf_op jit(solution)/shard_map/ppermute | solution.py:67
  137.4 1.5 %collective-permute-start.20 = (s16[8,32,128]{2,1,0:T(8,128)(2,1)S(1)}, s16[8,32,128]{2,1,0:T(8,128)(2,1)S(1)}, u32[]{:S(2)}, u32[]{:S(2)}) collective-permute-start(s16[8,32,128]{2,1,0:T(8,128)(2,1)S(1)} %get-tuple-element.82.refs_0_), channel_id=1, source_target_pairs={{0,1},{1,0},{2,3},{3,2},{4,5},{5,4},{6,7},{7,6},{8,9},{9,8},{10,11... | collective-permute-start | bytes 196616 | tf_op jit(solution)/shard_map/ppermute | solution.py:67
  139.2 3.9 %finish.1 = (f32[100,4,1024]{2,1,0:T(4,128)}, f32[4,1024]{1,0:T(4,128)}, f32[275,1024]{1,0:T(8,128)}) custom-call(s16[8,208,128]{2,1,0:T(8,128)(2,1)S(1)} %chunk_join1.3.mine_a, s16[8,208,128]{2,1,0:T(8,128)(2,1)S(1)} %get-tuple-element.83.mine_b, s16[8,208,128]{2,1,0:T(8,128)(2,1)S(1)} %collective-permute-done.25.theirs_a, ...), custom_call_target="tpu_custom_call" | custom-call | bytes 12000000 | tf_op jit(solution)/shard_map/finish/pallas_call | solution.py:24
  143.2 1.1 collective-permute-done.27.refs_2_
  144.3 1.4 embed_finish.1
  (95 shorter events, 14.0 us)
Async XLA Ops:
  3.0 24.4 %copy-start.17 = (f32[275]{0:T(512)S(1)}, f32[275]{0:T(512)}, u32[]{:S(2)}) copy-start(f32[275]{0:T(512)} %param.17) | copy-start | bytes 3304
  10.5 16.9 %collective-permute-start.1 = (bf16[2,112,1024]{2,1,0:T(8,128)(2,1)}, bf16[2,112,1024]{2,1,0:T(8,128)(2,1)S(1)}, u32[]{:S(2)}, u32[]{:S(2)}) collective-permute-start(bf16[2,112,1024]{2,1,0:T(8,128)(2,1)} %get-tuple-element.55), channel_id=1, source_target_pairs={{0,1},{1,0},{2,3},{3,2},{4,5},{5,4},{6,7},{7,6},{8,9},{9,8},{10,11... | collective-permute-start | bytes 1376264 | tf_op jit(solution)/shard_map/ppermute | solution.py:683
  13.5 13.9 %all-to-all-start = ((f32[16,2,8,128]{3,2,1,0:T(8,128)}), f32[16,2,8,128]{3,2,1,0:T(8,128)S(1)}, u32[]{:S(2)}, u32[]{:S(2)}) async-start(f32[16,2,8,128]{3,2,1,0:T(8,128)} %get-tuple-element.54), calls=%async_computation | async-start | bytes 262144 | tf_op jit(solution)/shard_map/all_to_all | solution.py:71
  19.5 11.1 %collective-permute-start.4 = (bf16[144,1024]{1,0:T(8,128)(2,1)}, bf16[144,1024]{1,0:T(8,128)(2,1)S(1)}, u32[]{:S(2)}, u32[]{:S(2)}) collective-permute-start(bf16[144,1024]{1,0:T(8,128)(2,1)} %get-tuple-element.57), channel_id=1, source_target_pairs={{0,1},{1,0},{2,3},{3,2},{4,5},{5,4},{6,7},{7,6},{8,9},{9,8},{10,11... | collective-permute-start | bytes 884744 | tf_op jit(solution)/shard_map/ppermute | solution.py:683
  27.4 5.3 %collective-permute-start.2 = (bf16[2,112,1024]{2,1,0:T(8,128)(2,1)S(1)}, bf16[2,112,1024]{2,1,0:T(8,128)(2,1)S(1)}, u32[]{:S(2)}, u32[]{:S(2)}) collective-permute-start(bf16[2,112,1024]{2,1,0:T(8,128)(2,1)S(1)} %collective-permute-done.1.direct), channel_id=1, source_target_pairs={{0,2},{2,0},{4,6},{6,4},{8,10},{10,8},{12,14},{14,12},{16,18},{18,... | collective-permute-start | bytes 1376264 | tf_op jit(solution)/shard_map/ppermute | solution.py:67
  30.6 6.0 %collective-permute-start.5 = (bf16[144,1024]{1,0:T(8,128)(2,1)S(1)}, bf16[144,1024]{1,0:T(8,128)(2,1)S(1)}, u32[]{:S(2)}, u32[]{:S(2)}) collective-permute-start(bf16[144,1024]{1,0:T(8,128)(2,1)S(1)} %collective-permute-done.4.refs_12_), channel_id=1, source_target_pairs={{0,2},{2,0},{4,6},{6,4},{8,10},{10,8},{12,14},{14,12},{16,18},{18,... | collective-permute-start | bytes 884744 | tf_op jit(solution)/shard_map/ppermute | solution.py:67
  30.6 6.0 %collective-permute-start.3 = (f32[16,2,8,128]{3,2,1,0:T(8,128)S(1)}, f32[16,2,8,128]{3,2,1,0:T(8,128)S(1)}, u32[]{:S(2)}, u32[]{:S(2)}) collective-permute-start(f32[16,2,8,128]{3,2,1,0:T(8,128)S(1)} %copy-done.4), channel_id=1, source_target_pairs={{0,1},{1,0},{2,3},{3,2},{4,5},{5,4},{6,7},{7,6},{8,9},{9,8},{10,11... | collective-permute-start | bytes 393224 | tf_op jit(solution)/shard_map/ppermute | solution.py:683
  32.4 4.2 %collective-permute-start = (f32[8,128]{1,0:T(8,128)S(1)}, f32[8,128]{1,0:T(8,128)S(1)}, u32[]{:S(2)}, u32[]{:S(2)}) collective-permute-start(f32[8,128]{1,0:T(8,128)S(1)} %carry.1.refs_8_), channel_id=1, source_target_pairs={{0,1},{1,0},{2,3},{3,2},{4,5},{5,4},{6,7},{7,6},{8,9},{9,8},{10,11... | collective-permute-start | bytes 12296 | tf_op jit(solution)/shard_map/ppermute | solution.py:683
  37.3 37.3 %copy-start.5 = (f32[16,2,8,128]{3,2,1,0:T(8,128)S(1)}, f32[16,2,8,128]{3,2,1,0:T(8,128)}, u32[]{:S(2)}) copy-start(f32[16,2,8,128]{3,2,1,0:T(8,128)} %get-tuple-element.52.refs_3_.seg) | copy-start | bytes 393220
  37.3 37.3 %copy-start.9 = (s32[2048]{0:T(1024)S(1)}, s32[2048]{0:T(1024)}, u32[]{:S(2)}) copy-start(s32[2048]{0:T(1024)} %copy-done.8) | copy-start | bytes 24580
  89.0 3.5 %collective-permute-start.6 = (f32[8,224,128]{2,1,0:T(8,128)S(1)}, f32[8,224,128]{2,1,0:T(8,128)S(1)}, u32[]{:S(2)}, u32[]{:S(2)}) collective-permute-start(f32[8,224,128]{2,1,0:T(8,128)S(1)} %get-tuple-element.71), channel_id=1, source_target_pairs={{0,2},{2,0},{4,6},{6,4},{8,10},{10,8},{12,14},{14,12},{16,18},{18,... | collective-permute-start | bytes 2752520 | tf_op jit(solution)/shard_map/ppermute | solution.py:67
  89.1 3.4 %collective-permute-start.7 = (f32[8,144,128]{2,1,0:T(8,128)S(1)}, f32[8,144,128]{2,1,0:T(8,128)S(1)}, u32[]{:S(2)}, u32[]{:S(2)}) collective-permute-start(f32[8,144,128]{2,1,0:T(8,128)S(1)} %copy-done.18), channel_id=1, source_target_pairs={{0,2},{2,0},{4,6},{6,4},{8,10},{10,8},{12,14},{14,12},{16,18},{18,... | collective-permute-start | bytes 1769480 | tf_op jit(solution)/shard_map/ppermute | solution.py:67
  89.6 2.9 %collective-permute-start.8 = (f32[8,24,128]{2,1,0:T(8,128)S(1)}, f32[8,24,128]{2,1,0:T(8,128)S(1)}, u32[]{:S(2)}, u32[]{:S(2)}) collective-permute-start(f32[8,24,128]{2,1,0:T(8,128)S(1)} %get-tuple-element.73), channel_id=1, source_target_pairs={{0,2},{2,0},{4,6},{6,4},{8,10},{10,8},{12,14},{14,12},{16,18},{18,... | collective-permute-start | bytes 294920 | tf_op jit(solution)/shard_map/ppermute | solution.py:67
  93.8 6.0 %collective-permute-start.9 = (s16[1,416,128]{2,1,0:T(8,128)(2,1)S(1)}, s16[1,416,128]{2,1,0:T(8,128)(2,1)S(1)}, u32[]{:S(2)}, u32[]{:S(2)}) collective-permute-start(s16[1,416,128]{2,1,0:T(8,128)(2,1)S(1)} %get-tuple-element.75), channel_id=1, source_target_pairs={{0,4},{2,6},{4,0},{6,2},{8,12},{10,14},{12,8},{14,10},{16,20},{18,... | collective-permute-start | bytes 319496 | tf_op jit(solution)/shard_map/ppermute | solution.py:67
  94.0 7.0 %collective-permute-start.10 = (s16[1,416,128]{2,1,0:T(8,128)(2,1)S(1)}, s16[1,416,128]{2,1,0:T(8,128)(2,1)S(1)}, u32[]{:S(2)}, u32[]{:S(2)}) collective-permute-start(s16[1,416,128]{2,1,0:T(8,128)(2,1)S(1)} %get-tuple-element.76), channel_id=1, source_target_pairs={{0,8},{2,10},{4,12},{6,14},{8,0},{10,2},{12,4},{14,6},{16,24},{18,... | collective-permute-start | bytes 319496 | tf_op jit(solution)/shard_map/ppermute | solution.py:67
  94.6 10.4 %collective-permute-start.11 = (s16[1,416,128]{2,1,0:T(8,128)(2,1)S(1)}, s16[1,416,128]{2,1,0:T(8,128)(2,1)S(1)}, u32[]{:S(2)}, u32[]{:S(2)}) collective-permute-start(s16[1,416,128]{2,1,0:T(8,128)(2,1)S(1)} %get-tuple-element.77), channel_id=1, source_target_pairs={{0,12},{2,14},{4,8},{6,10},{8,4},{10,6},{12,0},{14,2},{16,28},{18,... | collective-permute-start | bytes 319496 | tf_op jit(solution)/shard_map/ppermute | solution.py:67
  97.4 15.2 %collective-permute-start.12 = (s16[1,416,128]{2,1,0:T(8,128)(2,1)S(1)}, s16[1,416,128]{2,1,0:T(8,128)(2,1)S(1)}, u32[]{:S(2)}, u32[]{:S(2)}) collective-permute-start(s16[1,416,128]{2,1,0:T(8,128)(2,1)S(1)} %get-tuple-element.78), channel_id=1, source_target_pairs={{0,16},{2,18},{4,20},{6,22},{8,24},{10,26},{12,28},{14,30},{16,0},... | collective-permute-start | bytes 319496 | tf_op jit(solution)/shard_map/ppermute | solution.py:67
  97.5 17.3 %collective-permute-start.13 = (s16[1,416,128]{2,1,0:T(8,128)(2,1)S(1)}, s16[1,416,128]{2,1,0:T(8,128)(2,1)S(1)}, u32[]{:S(2)}, u32[]{:S(2)}) collective-permute-start(s16[1,416,128]{2,1,0:T(8,128)(2,1)S(1)} %get-tuple-element.79), channel_id=1, source_target_pairs={{0,20},{2,22},{4,16},{6,18},{8,28},{10,30},{12,24},{14,26},{16,4},... | collective-permute-start | bytes 319496 | tf_op jit(solution)/shard_map/ppermute | solution.py:67
  99.8 15.0 %collective-permute-start.14 = (s16[1,416,128]{2,1,0:T(8,128)(2,1)S(1)}, s16[1,416,128]{2,1,0:T(8,128)(2,1)S(1)}, u32[]{:S(2)}, u32[]{:S(2)}) collective-permute-start(s16[1,416,128]{2,1,0:T(8,128)(2,1)S(1)} %get-tuple-element.80), channel_id=1, source_target_pairs={{0,24},{2,26},{4,28},{6,30},{8,16},{10,18},{12,20},{14,22},{16,8},... | collective-permute-start | bytes 319496 | tf_op jit(solution)/shard_map/ppermute | solution.py:67
  100.9 13.9 %collective-permute-start.15 = (s16[1,416,128]{2,1,0:T(8,128)(2,1)S(1)}, s16[1,416,128]{2,1,0:T(8,128)(2,1)S(1)}, u32[]{:S(2)}, u32[]{:S(2)}) collective-permute-start(s16[1,416,128]{2,1,0:T(8,128)(2,1)S(1)} %get-tuple-element.81), channel_id=1, source_target_pairs={{0,28},{2,30},{4,24},{6,26},{8,20},{10,22},{12,16},{14,18},{16,12}... | collective-permute-start | bytes 319496 | tf_op jit(solution)/shard_map/ppermute | solution.py:67
  115.6 9.0 %collective-permute-start.23 = (s16[1,208,128]{2,1,0:T(8,128)(2,1)S(1)}, s16[1,208,128]{2,1,0:T(8,128)(2,1)S(1)}, u32[]{:S(2)}, u32[]{:S(2)}) collective-permute-start(s16[1,208,128]{2,1,0:T(8,128)(2,1)S(1)} %get-tuple-element.91.refs_0_), channel_id=1, source_target_pairs={{0,24},{2,26},{4,28},{6,30},{8,16},{10,18},{12,20},{14,22},{16,8},... | collective-permute-start | bytes 159752 | tf_op jit(solution)/shard_map/ppermute | solution.py:67
  116.7 9.6 %collective-permute-start.22 = (s16[1,208,128]{2,1,0:T(8,128)(2,1)S(1)}, s16[1,208,128]{2,1,0:T(8,128)(2,1)S(1)}, u32[]{:S(2)}, u32[]{:S(2)}) collective-permute-start(s16[1,208,128]{2,1,0:T(8,128)(2,1)S(1)} %get-tuple-element.91.refs_0_), channel_id=1, source_target_pairs={{0,16},{2,18},{4,20},{6,22},{8,24},{10,26},{12,28},{14,30},{16,0},... | collective-permute-start | bytes 159752 | tf_op jit(solution)/shard_map/ppermute | solution.py:67
  121.1 5.2 %collective-permute-start.21 = (s16[1,208,128]{2,1,0:T(8,128)(2,1)S(1)}, s16[1,208,128]{2,1,0:T(8,128)(2,1)S(1)}, u32[]{:S(2)}, u32[]{:S(2)}) collective-permute-start(s16[1,208,128]{2,1,0:T(8,128)(2,1)S(1)} %get-tuple-element.91.refs_0_), channel_id=1, source_target_pairs={{0,8},{2,10},{4,12},{6,14},{8,0},{10,2},{12,4},{14,6},{16,24},{18,... | collective-permute-start | bytes 159752 | tf_op jit(solution)/shard_map/ppermute | solution.py:67
  121.1 7.8 %collective-permute-start.18 = (s16[1,208,128]{2,1,0:T(8,128)(2,1)S(1)}, s16[1,208,128]{2,1,0:T(8,128)(2,1)S(1)}, u32[]{:S(2)}, u32[]{:S(2)}) collective-permute-start(s16[1,208,128]{2,1,0:T(8,128)(2,1)S(1)} %get-tuple-element.92.refs_0_), channel_id=1, source_target_pairs={{0,24},{2,26},{4,28},{6,30},{8,16},{10,18},{12,20},{14,22},{16,8},... | collective-permute-start | bytes 159752 | tf_op jit(solution)/shard_map/ppermute | solution.py:67
  122.5 6.5 %collective-permute-start.17 = (s16[1,208,128]{2,1,0:T(8,128)(2,1)S(1)}, s16[1,208,128]{2,1,0:T(8,128)(2,1)S(1)}, u32[]{:S(2)}, u32[]{:S(2)}) collective-permute-start(s16[1,208,128]{2,1,0:T(8,128)(2,1)S(1)} %get-tuple-element.92.refs_0_), channel_id=1, source_target_pairs={{0,16},{2,18},{4,20},{6,22},{8,24},{10,26},{12,28},{14,30},{16,0},... | collective-permute-start | bytes 159752 | tf_op jit(solution)/shard_map/ppermute | solution.py:67
  124.6 4.7 %collective-permute-start.16 = (s16[1,208,128]{2,1,0:T(8,128)(2,1)S(1)}, s16[1,208,128]{2,1,0:T(8,128)(2,1)S(1)}, u32[]{:S(2)}, u32[]{:S(2)}) collective-permute-start(s16[1,208,128]{2,1,0:T(8,128)(2,1)S(1)} %get-tuple-element.92.refs_0_), channel_id=1, source_target_pairs={{0,8},{2,10},{4,12},{6,14},{8,0},{10,2},{12,4},{14,6},{16,24},{18,... | collective-permute-start | bytes 159752 | tf_op jit(solution)/shard_map/ppermute | solution.py:67
  126.3 8.2 %collective-permute-start.24 = (s16[4,208,128]{2,1,0:T(8,128)(2,1)S(1)}, s16[4,208,128]{2,1,0:T(8,128)(2,1)S(1)}, u32[]{:S(2)}, u32[]{:S(2)}) collective-permute-start(s16[4,208,128]{2,1,0:T(8,128)(2,1)S(1)} %chunk_join0.3.refs_0_), channel_id=1, source_target_pairs={{0,4},{2,6},{4,0},{6,2},{8,12},{10,14},{12,8},{14,10},{16,20},{18,... | collective-permute-start | bytes 638984 | tf_op jit(solution)/shard_map/ppermute | solution.py:67
  129.3 8.0 %collective-permute-start.19 = (s16[4,208,128]{2,1,0:T(8,128)(2,1)S(1)}, s16[4,208,128]{2,1,0:T(8,128)(2,1)S(1)}, u32[]{:S(2)}, u32[]{:S(2)}) collective-permute-start(s16[4,208,128]{2,1,0:T(8,128)(2,1)S(1)} %chunk_join0.2.refs_0_), channel_id=1, source_target_pairs={{0,4},{2,6},{4,0},{6,2},{8,12},{10,14},{12,8},{14,10},{16,20},{18,... | collective-permute-start | bytes 638984 | tf_op jit(solution)/shard_map/ppermute | solution.py:67
  134.6 4.4 %collective-permute-start.25 = (s16[8,208,128]{2,1,0:T(8,128)(2,1)S(1)}, s16[8,208,128]{2,1,0:T(8,128)(2,1)S(1)}, u32[]{:S(2)}, u32[]{:S(2)}) collective-permute-start(s16[8,208,128]{2,1,0:T(8,128)(2,1)S(1)} %chunk_join1.3.mine_a), channel_id=1, source_target_pairs={{0,2},{2,0},{4,6},{6,4},{8,10},{10,8},{12,14},{14,12},{16,18},{18,... | collective-permute-start | bytes 1277960 | tf_op jit(solution)/shard_map/ppermute | solution.py:67
  137.3 1.8 %collective-permute-start.26 = (s16[8,208,128]{2,1,0:T(8,128)(2,1)S(1)}, s16[8,208,128]{2,1,0:T(8,128)(2,1)S(1)}, u32[]{:S(2)}, u32[]{:S(2)}) collective-permute-start(s16[8,208,128]{2,1,0:T(8,128)(2,1)S(1)} %get-tuple-element.83.mine_b), channel_id=1, source_target_pairs={{0,2},{2,0},{4,6},{6,4},{8,10},{10,8},{12,14},{14,12},{16,18},{18,... | collective-permute-start | bytes 1277960 | tf_op jit(solution)/shard_map/ppermute | solution.py:67
  137.4 5.6 %collective-permute-start.20 = (s16[8,32,128]{2,1,0:T(8,128)(2,1)S(1)}, s16[8,32,128]{2,1,0:T(8,128)(2,1)S(1)}, u32[]{:S(2)}, u32[]{:S(2)}) collective-permute-start(s16[8,32,128]{2,1,0:T(8,128)(2,1)S(1)} %get-tuple-element.82.refs_0_), channel_id=1, source_target_pairs={{0,1},{1,0},{2,3},{3,2},{4,5},{5,4},{6,7},{7,6},{8,9},{9,8},{10,11... | collective-permute-start | bytes 196616 | tf_op jit(solution)/shard_map/ppermute | solution.py:67
  143.0 1.3 collective-permute-start.27
  (16 other events, 98.5 us)

commit v7 on v6

--- a/solution.py
+++ b/solution.py
@@ -47,7 +47,7 @@
 def stages_of(count):
     stages, bit = [[1]], 2
     while bit < count:
-        ways = min(8 if bit == 2 else 4, count // bit)
+        ways = min(4 if bit == 2 else 2, count // bit)
         stages.append([k * bit for k in range(1, ways)])
         bit *= ways
     return stages

time: 147 us -> 143 us (0.973)
  starting transfers between devices: 40.1 us -> 27.9 us
  waiting for transfers between devices: 31.6 us -> 40.2 us
    ppermute x24 -> x21, starting transfers between devices: 28.4 us -> 16.3 us  [swap(): return lax.ppermute(value, axis, [(k, k ^ mask) for k in range(count)])]
    ppermute x24 -> x21, waiting for transfers between devices: 20.8 us -> 29.3 us  [swap(): return lax.ppermute(value, axis, [(k, k ^ mask) for k in range(count)])]
    pallas_call x16 -> x17, Pallas kernels: 55 us -> 55 us  [call(): pl.pallas_call(kernel, grid=(steps,) if blocked else (), in_specs=[spec(p...]
  transfers between devices with their start and end apart: 29 -> 26, of which waited for: 13 -> 15; matrix products, arithmetic and copies ran while one was open for 0% -> 0% of each run, Pallas kernels for 5% -> 5%
where the time goes in v7:
time: 143 us
  Pallas kernels  55 us (38%)
  waiting for transfers between devices  40.2 us (28%)
  starting transfers between devices  27.9 us (20%)
  blocking collectives  13.1 us (9%)
  local copies, waits for them, and re-layouts  3.09 us (2%)
  other arithmetic  2.39 us (2%)
    pallas_call x17, Pallas kernels, call(): pl.pallas_call(kernel, grid=(steps,) if blocked else (), in_specs=[spec(p...  55 us
    ppermute x21, waiting for transfers between devices, swap(): return lax.ppermute(value, axis, [(k, k ^ mask) for k in range(count)])  29.3 us
    ppermute x21, starting transfers between devices, swap(): return lax.ppermute(value, axis, [(k, k ^ mask) for k in range(count)])  16.3 us
    all_to_all x1, blocking collectives, exchange(): return lax.all_to_all(copies, axis, 0, 0, tiled=True)  13.1 us
    all_to_all x1, waiting for transfers between devices, exchange(): return lax.all_to_all(copies, axis, 0, 0, tiled=True)  7.34 us
    all_to_all x1, starting transfers between devices, exchange(): return lax.all_to_all(copies, axis, 0, 0, tiled=True)  5.93 us
    ppermute x4, starting transfers between devices, from_others(): lax.ppermute(value, 'wa', [(k, (k - s) % wa) for k in range(wa)])  5.7 us
    ppermute x4, waiting for transfers between devices, from_others(): lax.ppermute(value, 'wa', [(k, (k - s) % wa) for k in range(wa)])  3.51 us
  transfers between devices with their start and end apart: 26, of which 15 were waited for; matrix products, arithmetic and copies ran while one was open for 0% of the time, Pallas kernels for 5%

profile of v7, /device:TPU:0, one launch (start us, length us, event | category | flops | bytes accessed | tf_op | source)
XLA Modules:
  0.0 142.7 jit_solution(13745877802139847160)
XLA Ops:
  1.6 1.4 copy.36
  3.0 1.0 and_select_fusion.embed.table
  4.8 5.7 %tables_own.1 = (s32[2048]{0:T(1024)S(1)}, s32[4]{0:T(128)S(1)}, f32[4608,128]{1,0:T(8,128)}, f32[16,2,8,128]{3,2,1,0:T(8,128)}, f32[16,2,8,128]{3,2,1,0:T(8,128...) custom-call(s32[4]{0:T(128)S(1)} %copy-done.12, s32[16]{0:T(128)S(1)} %copy-done.11, ...), custom_call_target="tpu_custom_call" | custom-call | bytes 18000000 | tf_op jit(solution)/shard_map/tables_own/pallas_call | solution.py:24
  10.5 3.0 %collective-permute-start.1 = (bf16[2,112,1024]{2,1,0:T(8,128)(2,1)}, bf16[2,112,1024]{2,1,0:T(8,128)(2,1)S(1)}, u32[]{:S(2)}, u32[]{:S(2)}) collective-permute-start(bf16[2,112,1024]{2,1,0:T(8,128)(2,1)} %get-tuple-element.53), channel_id=1, source_target_pairs={{0,1},{1,0},{2,3},{3,2},{4,5},{5,4},{6,7},{7,6},{8,9},{9,8},{10,11... | collective-permute-start | bytes 1376264 | tf_op jit(solution)/shard_map/ppermute | solution.py:683
  13.5 5.9 %all-to-all-start = ((f32[16,2,8,128]{3,2,1,0:T(8,128)}), f32[16,2,8,128]{3,2,1,0:T(8,128)S(1)}, u32[]{:S(2)}, u32[]{:S(2)}) async-start(f32[16,2,8,128]{3,2,1,0:T(8,128)} %get-tuple-element.52), calls=%async_computation | async-start | bytes 262144 | tf_op jit(solution)/shard_map/all_to_all | solution.py:71
  20.1 7.3 %all-to-all-done.ps_all = f32[16,2,8,128]{3,2,1,0:T(8,128)S(1)} async-done(((f32[16,2,8,128]{3,2,1,0:T(8,128)}), f32[16,2,8,128]{3,2,1,0:T(8,128)S(1)}, u32[]{:S(2)}, u32[]{:S(2)}) %all-to-all-start) | async-done | bytes 131104 | tf_op jit(solution)/shard_map/all_to_all | solution.py:71
  27.5 0.9 tables_rest.1._.refs_2_
  28.5 0.9 carry.1.refs_8_
  29.4 1.2 collective-permute-done.4.refs_12_
  30.6 1.8 %collective-permute-start.3 = (f32[16,2,8,128]{3,2,1,0:T(8,128)S(1)}, f32[16,2,8,128]{3,2,1,0:T(8,128)S(1)}, u32[]{:S(2)}, u32[]{:S(2)}) collective-permute-start(f32[16,2,8,128]{3,2,1,0:T(8,128)S(1)} %copy-done.4), channel_id=1, source_target_pairs={{0,1},{1,0},{2,3},{3,2},{4,5},{5,4},{6,7},{7,6},{8,9},{9,8},{10,11... | collective-permute-start | bytes 393224 | tf_op jit(solution)/shard_map/ppermute | solution.py:683
  32.7 1.6 %tables_other.1.refs_10_ = f32[6912,128]{1,0:T(8,128)S(1)} custom-call(s32[4]{0:T(128)S(1)} %get-tuple-element.49.spots, bf16[288,112]{1,0:T(8,128)(2,1)S(1)} %and_select_fusion.embed.table, bf16[2,112,1024]{2,1,0:T(8,128)(2,1)S(1)} %collective-permute-done.1.direct, bf16[2,112,1024]{2,1,0:T(8,128)(2,1)S(1)} %collective-permute-done.2.passed), custom_call_target="tpu_custom_call" | custom-call | bytes 9000000 | tf_op jit(solution)/shard_map/tables_other/pallas_call | solution.py:24
  34.2 2.3 %collective-permute-done.3.refs_11_ = f32[16,2,8,128]{3,2,1,0:T(8,128)S(1)} collective-permute-done((f32[16,2,8,128]{3,2,1,0:T(8,128)S(1)}, f32[16,2,8,128]{3,2,1,0:T(8,128)S(1)}, u32[]{:S(2)}, u32[]{:S(2)}) %collective-permute-start.3) | collective-permute-done | bytes 131104 | tf_op jit(solution)/shard_map/ppermute | solution.py:683
  37.3 24.1 %cells.1 = (bf16[2048,1024]{1,0:T(8,128)(2,1)}, f32[16384,128]{1,0:T(8,128)S(1)}, f32[16384,128]{1,0:T(8,128)}, f32[8,144,128]{2,1,0:T(8,128)}, f32[8,144,128]{2...) custom-call(s32[2048]{0:T(1024)} %copy-done.8, ...), custom_call_target="tpu_custom_call" | custom-call | bytes 78000000 | tf_op jit(solution)/shard_map/cells/pallas_call | solution.py:24
  61.5 13.1 %all_to_all.10.h_all = f32[16,8,128]{2,1,0:T(8,128)S(1)} all-to-all(f32[16,8,128]{2,1,0:T(8,128)} %get-tuple-element.59), channel_id=1, replica_groups=mesh['ctx'=16,'wa'=2] {'ctx'}, dimensions={0} | all-to-all | bytes 131072 | tf_op jit(solution)/shard_map/all_to_all | solution.py:71
  74.6 9.0 %char_sums.1.sums = f32[2,2304,128]{2,1,0:T(8,128)S(1)} custom-call(s32[2048]{0:T(1024)S(1)} %copy-done.9, s32[16]{0:T(128)S(1)} %copy-done.11, f32[4608,128]{1,0:T(8,128)S(1)} %copy-done, f32[16,2,8,128]{3,2,1,0:T(8,128)S(1)} %copy-done.5, f32[128,128]{1,0:T(8,128)S(1)} %get-tuple-element.58.heads, f32[16,8,128]{2,1,0:T(8,128)S(1)} %all_to_all.10.h_all, ...), custom_call_target="tpu_custom_call" | custom-call | bytes 27000000 | tf_op jit(solution)/shard_map/char_sums/pallas_call | solution.py:24
  83.6 4.1 %gate_sums.1 = (bf16[4,288,1024]{2,1,0:T(8,128)(2,1)S(1)}, bf16[4,288,1024]{2,1,0:T(8,128)(2,1)S(1)}, f32[8,24,128]{2,1,0:T(8,128)S(1)}, f32[8,24,128]{2,1,0:T(8,128)S(1)}) custom-call(s32[4]{0:T(128)S(1)} %get-tuple-element.49.spots, f32[2,2304,128]{2,1,0:T(8,128)S(1)} %char_sums.1.sums, f32[288,1024]{1,0:T(8,128)S(1)} %get-tuple-element.62.o_sum, ...), custom_call_target="tpu_custom_call" | custom-call | bytes 9000000 | tf_op jit(solution)/shard_map/gate_sums/pallas_call | solution.py:24
  87.7 1.3 input_grad.1
  89.7 2.9 %collective-permute-done.8.refs_5_ = f32[8,24,128]{2,1,0:T(8,128)S(1)} collective-permute-done((f32[8,24,128]{2,1,0:T(8,128)S(1)}, f32[8,24,128]{2,1,0:T(8,128)S(1)}, u32[]{:S(2)}, u32[]{:S(2)}) %collective-permute-start.8) | collective-permute-done | bytes 98336 | tf_op jit(solution)/shard_map/ppermute | solution.py:67
  92.6 1.1 core_sum.1
  94.5 2.8 %collective-permute-start.11 = (s16[2,416,128]{2,1,0:T(8,128)(2,1)S(1)}, s16[2,416,128]{2,1,0:T(8,128)(2,1)S(1)}, u32[]{:S(2)}, u32[]{:S(2)}) collective-permute-start(s16[2,416,128]{2,1,0:T(8,128)(2,1)S(1)} %get-tuple-element.75), channel_id=1, source_target_pairs={{0,12},{2,14},{4,8},{6,10},{8,4},{10,6},{12,0},{14,2},{16,28},{18,... | collective-permute-start | bytes 638984 | tf_op jit(solution)/shard_map/ppermute | solution.py:67
  97.2 3.8 %collective-permute-done.9.refs_1_ = s16[2,416,128]{2,1,0:T(8,128)(2,1)S(1)} collective-permute-done((s16[2,416,128]{2,1,0:T(8,128)(2,1)S(1)}, s16[2,416,128]{2,1,0:T(8,128)(2,1)S(1)}, u32[]{:S(2)}, u32[]{:S(2)}) %collective-permute-start.9) | collective-permute-done | bytes 213024 | tf_op jit(solution)/shard_map/ppermute | solution.py:67
  101.9 4.9 %collective-permute-done.11.refs_3_ = s16[2,416,128]{2,1,0:T(8,128)(2,1)S(1)} collective-permute-done((s16[2,416,128]{2,1,0:T(8,128)(2,1)S(1)}, s16[2,416,128]{2,1,0:T(8,128)(2,1)S(1)}, u32[]{:S(2)}, u32[]{:S(2)}) %collective-permute-start.11) | collective-permute-done | bytes 213024 | tf_op jit(solution)/shard_map/ppermute | solution.py:67
  107.7 6.8 %collective-permute-done.12.refs_1_ = s16[1,416,128]{2,1,0:T(8,128)(2,1)S(1)} collective-permute-done((s16[1,416,128]{2,1,0:T(8,128)(2,1)S(1)}, s16[1,416,128]{2,1,0:T(8,128)(2,1)S(1)}, u32[]{:S(2)}, u32[]{:S(2)}) %collective-permute-start.12) | collective-permute-done | bytes 106528 | tf_op jit(solution)/shard_map/ppermute | solution.py:67
  115.4 3.8 %collective-permute-start.18 = (s16[1,208,128]{2,1,0:T(8,128)(2,1)S(1)}, s16[1,208,128]{2,1,0:T(8,128)(2,1)S(1)}, u32[]{:S(2)}, u32[]{:S(2)}) collective-permute-start(s16[1,208,128]{2,1,0:T(8,128)(2,1)S(1)} %get-tuple-element.87.refs_0_), channel_id=1, source_target_pairs={{0,8},{2,10},{4,12},{6,14},{8,0},{10,2},{12,4},{14,6},{16,24},{18,... | collective-permute-start | bytes 159752 | tf_op jit(solution)/shard_map/ppermute | solution.py:67
  119.8 0.9 collective-permute-start.14
  120.9 2.7 %collective-permute-start.13 = (s16[1,208,128]{2,1,0:T(8,128)(2,1)S(1)}, s16[1,208,128]{2,1,0:T(8,128)(2,1)S(1)}, u32[]{:S(2)}, u32[]{:S(2)}) collective-permute-start(s16[1,208,128]{2,1,0:T(8,128)(2,1)S(1)} %get-tuple-element.88.refs_0_), channel_id=1, source_target_pairs={{0,8},{2,10},{4,12},{6,14},{8,0},{10,2},{12,4},{14,6},{16,24},{18,... | collective-permute-start | bytes 159752 | tf_op jit(solution)/shard_map/ppermute | solution.py:67
  126.7 4.7 %collective-permute-done.21.refs_1_ = s16[4,208,128]{2,1,0:T(8,128)(2,1)S(1)} collective-permute-done((s16[4,208,128]{2,1,0:T(8,128)(2,1)S(1)}, s16[4,208,128]{2,1,0:T(8,128)(2,1)S(1)}, u32[]{:S(2)}, u32[]{:S(2)}) %collective-permute-start.21) | collective-permute-done | bytes 213024 | tf_op jit(solution)/shard_map/ppermute | solution.py:67
  131.5 2.2 %collective-permute-done.16.refs_1_ = s16[4,208,128]{2,1,0:T(8,128)(2,1)S(1)} collective-permute-done((s16[4,208,128]{2,1,0:T(8,128)(2,1)S(1)}, s16[4,208,128]{2,1,0:T(8,128)(2,1)S(1)}, u32[]{:S(2)}, u32[]{:S(2)}) %collective-permute-start.16) | collective-permute-done | bytes 213024 | tf_op jit(solution)/shard_map/ppermute | solution.py:67
  133.8 1.6 %collective-permute-start.17 = (s16[8,32,128]{2,1,0:T(8,128)(2,1)S(1)}, s16[8,32,128]{2,1,0:T(8,128)(2,1)S(1)}, u32[]{:S(2)}, u32[]{:S(2)}) collective-permute-start(s16[8,32,128]{2,1,0:T(8,128)(2,1)S(1)} %get-tuple-element.78.refs_0_), channel_id=1, source_target_pairs={{0,1},{1,0},{2,3},{3,2},{4,5},{5,4},{6,7},{7,6},{8,9},{9,8},{10,11... | collective-permute-start | bytes 196616 | tf_op jit(solution)/shard_map/ppermute | solution.py:67
  135.6 3.9 %finish.1 = (f32[100,4,1024]{2,1,0:T(4,128)}, f32[4,1024]{1,0:T(4,128)}, f32[275,1024]{1,0:T(8,128)}) custom-call(s16[8,208,128]{2,1,0:T(8,128)(2,1)S(1)} %chunk_join1.3.mine_a, s16[8,208,128]{2,1,0:T(8,128)(2,1)S(1)} %get-tuple-element.79.mine_b, s16[8,208,128]{2,1,0:T(8,128)(2,1)S(1)} %collective-permute-done.22.theirs_a, ...), custom_call_target="tpu_custom_call" | custom-call | bytes 12000000 | tf_op jit(solution)/shard_map/finish/pallas_call | solution.py:24
  139.6 1.1 collective-permute-done.24.refs_2_
  140.7 1.4 embed_finish.1
  (90 shorter events, 12.6 us)
Async XLA Ops:
  3.0 24.5 %copy-start.17 = (f32[275]{0:T(512)S(1)}, f32[275]{0:T(512)}, u32[]{:S(2)}) copy-start(f32[275]{0:T(512)} %param.17) | copy-start | bytes 3304
  10.5 17.0 %copy-start.8 = (s32[2048]{0:T(1024)}, s32[2048]{0:T(1024)S(1)}, u32[]{:S(2)}) copy-start(s32[2048]{0:T(1024)S(1)} %get-tuple-element.47.refs_0_.ids) | copy-start | bytes 24580
  10.5 20.1 %copy-start.4 = (f32[16,2,8,128]{3,2,1,0:T(8,128)S(1)}, f32[16,2,8,128]{3,2,1,0:T(8,128)}, u32[]{:S(2)}) copy-start(f32[16,2,8,128]{3,2,1,0:T(8,128)} %get-tuple-element.50.refs_3_.seg) | copy-start | bytes 393220
  10.5 16.9 %collective-permute-start.1 = (bf16[2,112,1024]{2,1,0:T(8,128)(2,1)}, bf16[2,112,1024]{2,1,0:T(8,128)(2,1)S(1)}, u32[]{:S(2)}, u32[]{:S(2)}) collective-permute-start(bf16[2,112,1024]{2,1,0:T(8,128)(2,1)} %get-tuple-element.53), channel_id=1, source_target_pairs={{0,1},{1,0},{2,3},{3,2},{4,5},{5,4},{6,7},{7,6},{8,9},{9,8},{10,11... | collective-permute-start | bytes 1376264 | tf_op jit(solution)/shard_map/ppermute | solution.py:683
  13.5 13.9 %all-to-all-start = ((f32[16,2,8,128]{3,2,1,0:T(8,128)}), f32[16,2,8,128]{3,2,1,0:T(8,128)S(1)}, u32[]{:S(2)}, u32[]{:S(2)}) async-start(f32[16,2,8,128]{3,2,1,0:T(8,128)} %get-tuple-element.52), calls=%async_computation | async-start | bytes 262144 | tf_op jit(solution)/shard_map/all_to_all | solution.py:71
  19.5 11.1 %collective-permute-start.4 = (bf16[144,1024]{1,0:T(8,128)(2,1)}, bf16[144,1024]{1,0:T(8,128)(2,1)S(1)}, u32[]{:S(2)}, u32[]{:S(2)}) collective-permute-start(bf16[144,1024]{1,0:T(8,128)(2,1)} %get-tuple-element.55), channel_id=1, source_target_pairs={{0,1},{1,0},{2,3},{3,2},{4,5},{5,4},{6,7},{7,6},{8,9},{9,8},{10,11... | collective-permute-start | bytes 884744 | tf_op jit(solution)/shard_map/ppermute | solution.py:683
  27.4 5.3 %collective-permute-start.2 = (bf16[2,112,1024]{2,1,0:T(8,128)(2,1)S(1)}, bf16[2,112,1024]{2,1,0:T(8,128)(2,1)S(1)}, u32[]{:S(2)}, u32[]{:S(2)}) collective-permute-start(bf16[2,112,1024]{2,1,0:T(8,128)(2,1)S(1)} %collective-permute-done.1.direct), channel_id=1, source_target_pairs={{0,2},{2,0},{4,6},{6,4},{8,10},{10,8},{12,14},{14,12},{16,18},{18,... | collective-permute-start | bytes 1376264 | tf_op jit(solution)/shard_map/ppermute | solution.py:67
  30.6 6.0 %collective-permute-start.5 = (bf16[144,1024]{1,0:T(8,128)(2,1)S(1)}, bf16[144,1024]{1,0:T(8,128)(2,1)S(1)}, u32[]{:S(2)}, u32[]{:S(2)}) collective-permute-start(bf16[144,1024]{1,0:T(8,128)(2,1)S(1)} %collective-permute-done.4.refs_12_), channel_id=1, source_target_pairs={{0,2},{2,0},{4,6},{6,4},{8,10},{10,8},{12,14},{14,12},{16,18},{18,... | collective-permute-start | bytes 884744 | tf_op jit(solution)/shard_map/ppermute | solution.py:67
  30.6 6.0 %collective-permute-start.3 = (f32[16,2,8,128]{3,2,1,0:T(8,128)S(1)}, f32[16,2,8,128]{3,2,1,0:T(8,128)S(1)}, u32[]{:S(2)}, u32[]{:S(2)}) collective-permute-start(f32[16,2,8,128]{3,2,1,0:T(8,128)S(1)} %copy-done.4), channel_id=1, source_target_pairs={{0,1},{1,0},{2,3},{3,2},{4,5},{5,4},{6,7},{7,6},{8,9},{9,8},{10,11... | collective-permute-start | bytes 393224 | tf_op jit(solution)/shard_map/ppermute | solution.py:683
  32.4 4.2 %collective-permute-start = (f32[8,128]{1,0:T(8,128)S(1)}, f32[8,128]{1,0:T(8,128)S(1)}, u32[]{:S(2)}, u32[]{:S(2)}) collective-permute-start(f32[8,128]{1,0:T(8,128)S(1)} %carry.1.refs_8_), channel_id=1, source_target_pairs={{0,1},{1,0},{2,3},{3,2},{4,5},{5,4},{6,7},{7,6},{8,9},{9,8},{10,11... | collective-permute-start | bytes 12296 | tf_op jit(solution)/shard_map/ppermute | solution.py:683
  37.3 37.2 %copy-start.5 = (f32[16,2,8,128]{3,2,1,0:T(8,128)S(1)}, f32[16,2,8,128]{3,2,1,0:T(8,128)}, u32[]{:S(2)}) copy-start(f32[16,2,8,128]{3,2,1,0:T(8,128)} %get-tuple-element.50.refs_3_.seg) | copy-start | bytes 393220
  37.3 37.2 %copy-start.9 = (s32[2048]{0:T(1024)S(1)}, s32[2048]{0:T(1024)}, u32[]{:S(2)}) copy-start(s32[2048]{0:T(1024)} %copy-done.8) | copy-start | bytes 24580
  74.6 9.0 %copy-start.6 = (f32[288,128]{1,0:T(8,128)S(1)}, f32[288,128]{1,0:T(8,128)}, u32[]{:S(2)}) copy-start(f32[288,128]{1,0:T(8,128)} %get-tuple-element.63.extra) | copy-start | bytes 442372
  89.0 3.5 %collective-permute-start.6 = (f32[8,224,128]{2,1,0:T(8,128)S(1)}, f32[8,224,128]{2,1,0:T(8,128)S(1)}, u32[]{:S(2)}, u32[]{:S(2)}) collective-permute-start(f32[8,224,128]{2,1,0:T(8,128)S(1)} %get-tuple-element.69), channel_id=1, source_target_pairs={{0,2},{2,0},{4,6},{6,4},{8,10},{10,8},{12,14},{14,12},{16,18},{18,... | collective-permute-start | bytes 2752520 | tf_op jit(solution)/shard_map/ppermute | solution.py:67
  89.1 3.4 %collective-permute-start.7 = (f32[8,144,128]{2,1,0:T(8,128)S(1)}, f32[8,144,128]{2,1,0:T(8,128)S(1)}, u32[]{:S(2)}, u32[]{:S(2)}) collective-permute-start(f32[8,144,128]{2,1,0:T(8,128)S(1)} %copy-done.18), channel_id=1, source_target_pairs={{0,2},{2,0},{4,6},{6,4},{8,10},{10,8},{12,14},{14,12},{16,18},{18,... | collective-permute-start | bytes 1769480 | tf_op jit(solution)/shard_map/ppermute | solution.py:67
  89.6 2.9 %collective-permute-start.8 = (f32[8,24,128]{2,1,0:T(8,128)S(1)}, f32[8,24,128]{2,1,0:T(8,128)S(1)}, u32[]{:S(2)}, u32[]{:S(2)}) collective-permute-start(f32[8,24,128]{2,1,0:T(8,128)S(1)} %get-tuple-element.71), channel_id=1, source_target_pairs={{0,2},{2,0},{4,6},{6,4},{8,10},{10,8},{12,14},{14,12},{16,18},{18,... | collective-permute-start | bytes 294920 | tf_op jit(solution)/shard_map/ppermute | solution.py:67
  93.7 7.4 %collective-permute-start.9 = (s16[2,416,128]{2,1,0:T(8,128)(2,1)S(1)}, s16[2,416,128]{2,1,0:T(8,128)(2,1)S(1)}, u32[]{:S(2)}, u32[]{:S(2)}) collective-permute-start(s16[2,416,128]{2,1,0:T(8,128)(2,1)S(1)} %get-tuple-element.73), channel_id=1, source_target_pairs={{0,4},{2,6},{4,0},{6,2},{8,12},{10,14},{12,8},{14,10},{16,20},{18,... | collective-permute-start | bytes 638984 | tf_op jit(solution)/shard_map/ppermute | solution.py:67
  93.8 8.2 %collective-permute-start.10 = (s16[2,416,128]{2,1,0:T(8,128)(2,1)S(1)}, s16[2,416,128]{2,1,0:T(8,128)(2,1)S(1)}, u32[]{:S(2)}, u32[]{:S(2)}) collective-permute-start(s16[2,416,128]{2,1,0:T(8,128)(2,1)S(1)} %get-tuple-element.74), channel_id=1, source_target_pairs={{0,8},{2,10},{4,12},{6,14},{8,0},{10,2},{12,4},{14,6},{16,24},{18,... | collective-permute-start | bytes 638984 | tf_op jit(solution)/shard_map/ppermute | solution.py:67
  94.5 12.3 %collective-permute-start.11 = (s16[2,416,128]{2,1,0:T(8,128)(2,1)S(1)}, s16[2,416,128]{2,1,0:T(8,128)(2,1)S(1)}, u32[]{:S(2)}, u32[]{:S(2)}) collective-permute-start(s16[2,416,128]{2,1,0:T(8,128)(2,1)S(1)} %get-tuple-element.75), channel_id=1, source_target_pairs={{0,12},{2,14},{4,8},{6,10},{8,4},{10,6},{12,0},{14,2},{16,28},{18,... | collective-permute-start | bytes 638984 | tf_op jit(solution)/shard_map/ppermute | solution.py:67
  107.5 7.0 %collective-permute-start.12 = (s16[1,416,128]{2,1,0:T(8,128)(2,1)S(1)}, s16[1,416,128]{2,1,0:T(8,128)(2,1)S(1)}, u32[]{:S(2)}, u32[]{:S(2)}) collective-permute-start(s16[1,416,128]{2,1,0:T(8,128)(2,1)S(1)} %get-tuple-element.77), channel_id=1, source_target_pairs={{0,16},{2,18},{4,20},{6,22},{8,24},{10,26},{12,28},{14,30},{16,0},... | collective-permute-start | bytes 319496 | tf_op jit(solution)/shard_map/ppermute | solution.py:67
  114.8 6.1 %collective-permute-start.20 = (s16[1,208,128]{2,1,0:T(8,128)(2,1)S(1)}, s16[1,208,128]{2,1,0:T(8,128)(2,1)S(1)}, u32[]{:S(2)}, u32[]{:S(2)}) collective-permute-start(s16[1,208,128]{2,1,0:T(8,128)(2,1)S(1)} %get-tuple-element.87.refs_0_), channel_id=1, source_target_pairs={{0,24},{2,26},{4,28},{6,30},{8,16},{10,18},{12,20},{14,22},{16,8},... | collective-permute-start | bytes 159752 | tf_op jit(solution)/shard_map/ppermute | solution.py:67
  115.4 8.2 %collective-permute-start.19 = (s16[1,208,128]{2,1,0:T(8,128)(2,1)S(1)}, s16[1,208,128]{2,1,0:T(8,128)(2,1)S(1)}, u32[]{:S(2)}, u32[]{:S(2)}) collective-permute-start(s16[1,208,128]{2,1,0:T(8,128)(2,1)S(1)} %get-tuple-element.87.refs_0_), channel_id=1, source_target_pairs={{0,16},{2,18},{4,20},{6,22},{8,24},{10,26},{12,28},{14,30},{16,0},... | collective-permute-start | bytes 159752 | tf_op jit(solution)/shard_map/ppermute | solution.py:67
  115.4 8.2 %collective-permute-start.18 = (s16[1,208,128]{2,1,0:T(8,128)(2,1)S(1)}, s16[1,208,128]{2,1,0:T(8,128)(2,1)S(1)}, u32[]{:S(2)}, u32[]{:S(2)}) collective-permute-start(s16[1,208,128]{2,1,0:T(8,128)(2,1)S(1)} %get-tuple-element.87.refs_0_), channel_id=1, source_target_pairs={{0,8},{2,10},{4,12},{6,14},{8,0},{10,2},{12,4},{14,6},{16,24},{18,... | collective-permute-start | bytes 159752 | tf_op jit(solution)/shard_map/ppermute | solution.py:67
  119.2 6.0 %collective-permute-start.15 = (s16[1,208,128]{2,1,0:T(8,128)(2,1)S(1)}, s16[1,208,128]{2,1,0:T(8,128)(2,1)S(1)}, u32[]{:S(2)}, u32[]{:S(2)}) collective-permute-start(s16[1,208,128]{2,1,0:T(8,128)(2,1)S(1)} %get-tuple-element.88.refs_0_), channel_id=1, source_target_pairs={{0,24},{2,26},{4,28},{6,30},{8,16},{10,18},{12,20},{14,22},{16,8},... | collective-permute-start | bytes 159752 | tf_op jit(solution)/shard_map/ppermute | solution.py:67
  119.8 6.3 %collective-permute-start.14 = (s16[1,208,128]{2,1,0:T(8,128)(2,1)S(1)}, s16[1,208,128]{2,1,0:T(8,128)(2,1)S(1)}, u32[]{:S(2)}, u32[]{:S(2)}) collective-permute-start(s16[1,208,128]{2,1,0:T(8,128)(2,1)S(1)} %get-tuple-element.88.refs_0_), channel_id=1, source_target_pairs={{0,16},{2,18},{4,20},{6,22},{8,24},{10,26},{12,28},{14,30},{16,0},... | collective-permute-start | bytes 159752 | tf_op jit(solution)/shard_map/ppermute | solution.py:67
  120.9 5.2 %collective-permute-start.13 = (s16[1,208,128]{2,1,0:T(8,128)(2,1)S(1)}, s16[1,208,128]{2,1,0:T(8,128)(2,1)S(1)}, u32[]{:S(2)}, u32[]{:S(2)}) collective-permute-start(s16[1,208,128]{2,1,0:T(8,128)(2,1)S(1)} %get-tuple-element.88.refs_0_), channel_id=1, source_target_pairs={{0,8},{2,10},{4,12},{6,14},{8,0},{10,2},{12,4},{14,6},{16,24},{18,... | collective-permute-start | bytes 159752 | tf_op jit(solution)/shard_map/ppermute | solution.py:67
  123.7 7.8 %collective-permute-start.21 = (s16[4,208,128]{2,1,0:T(8,128)(2,1)S(1)}, s16[4,208,128]{2,1,0:T(8,128)(2,1)S(1)}, u32[]{:S(2)}, u32[]{:S(2)}) collective-permute-start(s16[4,208,128]{2,1,0:T(8,128)(2,1)S(1)} %chunk_join0.3.refs_0_), channel_id=1, source_target_pairs={{0,4},{2,6},{4,0},{6,2},{8,12},{10,14},{12,8},{14,10},{16,20},{18,... | collective-permute-start | bytes 638984 | tf_op jit(solution)/shard_map/ppermute | solution.py:67
  126.2 7.5 %collective-permute-start.16 = (s16[4,208,128]{2,1,0:T(8,128)(2,1)S(1)}, s16[4,208,128]{2,1,0:T(8,128)(2,1)S(1)}, u32[]{:S(2)}, u32[]{:S(2)}) collective-permute-start(s16[4,208,128]{2,1,0:T(8,128)(2,1)S(1)} %chunk_join0.2.refs_0_), channel_id=1, source_target_pairs={{0,4},{2,6},{4,0},{6,2},{8,12},{10,14},{12,8},{14,10},{16,20},{18,... | collective-permute-start | bytes 638984 | tf_op jit(solution)/shard_map/ppermute | solution.py:67
  131.5 3.9 %collective-permute-start.22 = (s16[8,208,128]{2,1,0:T(8,128)(2,1)S(1)}, s16[8,208,128]{2,1,0:T(8,128)(2,1)S(1)}, u32[]{:S(2)}, u32[]{:S(2)}) collective-permute-start(s16[8,208,128]{2,1,0:T(8,128)(2,1)S(1)} %chunk_join1.3.mine_a), channel_id=1, source_target_pairs={{0,2},{2,0},{4,6},{6,4},{8,10},{10,8},{12,14},{14,12},{16,18},{18,... | collective-permute-start | bytes 1277960 | tf_op jit(solution)/shard_map/ppermute | solution.py:67
  133.8 1.8 %collective-permute-start.23 = (s16[8,208,128]{2,1,0:T(8,128)(2,1)S(1)}, s16[8,208,128]{2,1,0:T(8,128)(2,1)S(1)}, u32[]{:S(2)}, u32[]{:S(2)}) collective-permute-start(s16[8,208,128]{2,1,0:T(8,128)(2,1)S(1)} %get-tuple-element.79.mine_b), channel_id=1, source_target_pairs={{0,2},{2,0},{4,6},{6,4},{8,10},{10,8},{12,14},{14,12},{16,18},{18,... | collective-permute-start | bytes 1277960 | tf_op jit(solution)/shard_map/ppermute | solution.py:67
  133.8 5.6 %collective-permute-start.17 = (s16[8,32,128]{2,1,0:T(8,128)(2,1)S(1)}, s16[8,32,128]{2,1,0:T(8,128)(2,1)S(1)}, u32[]{:S(2)}, u32[]{:S(2)}) collective-permute-start(s16[8,32,128]{2,1,0:T(8,128)(2,1)S(1)} %get-tuple-element.78.refs_0_), channel_id=1, source_target_pairs={{0,1},{1,0},{2,3},{3,2},{4,5},{5,4},{6,7},{7,6},{8,9},{9,8},{10,11... | collective-permute-start | bytes 196616 | tf_op jit(solution)/shard_map/ppermute | solution.py:67
  139.5 1.3 collective-permute-start.24
  (13 other events, 52.6 us)
